TPU v7x, 512 devices: a whole 4x4x16 slice. The times are simulated.
512 devices in a mesh: dp: 16 (over z), replica: 8 (over y_lo, x), tensor: 4 (over y_hi, core).
Axes of the slice: x: 4, y: 4 (y_hi: 2, y_lo: 2; y = y_hi * 2 + y_lo), z: 16, core: 2. Of those that a mesh axis runs over, the one named last changes fastest.
Arguments:
- image_residual_input: bfloat16 [16384, 1152], P(('dp', 'replica')), may hold values from -6 to 6
- image_hidden_units: bfloat16 [16384, 2176], P(('dp', 'replica'), 'tensor'), may hold values from -12 to 12, as said below
- image_output_weight: bfloat16 [2176, 1152], P('tensor'), may hold values from -0.125 to 0.125
- text_residual_input: bfloat16 [16384, 1152], P(('dp', 'replica')), may hold values from -6 to 6
- text_hidden_units: bfloat16 [16384, 2176], P(('dp', 'replica'), 'tensor'), may hold values from -12 to 12, as said below
- text_output_weight: bfloat16 [2176, 1152], P('tensor'), may hold values from -0.125 to 0.125
- log_logit_scale: float32 [1], replicated, may hold values from 1.8 to 2.6
- pair_logit_bias: float32 [1], replicated, may hold values from -4 to -1
Outputs:
- hidden_grad_image: bfloat16 [16384, 2176], P(('dp', 'replica'), 'tensor')
- hidden_grad_text: bfloat16 [16384, 2176], P(('dp', 'replica'), 'tensor')
- weight_grad_image: float32 [2176, 1152], P('tensor', 'replica')
- weight_grad_text: float32 [2176, 1152], P('tensor', 'replica')
Inputs may be any that keep to these rules, and one draw needn't show every extreme that they name: `image_hidden_units`: post-activation hidden values; each row has its own scale. `text_hidden_units`: post-activation hidden values; each row has its own scale.
All inputs are finite; a program needn't handle non-finite values.
Results may differ from a plain program's by a relative error of at most 0.022.
Values may be sent and summed in bfloat16 or wider, within the bound.
No kernel may reach another device: no remote copies, remote signals or barrier semaphores. Data moves between devices by JAX's collectives and lax.ppermute only.
A program may use at most 64 MiB of HBM per device.

v0:
```python
import jax
import jax.numpy as jnp
from jax import lax
from jax.sharding import PartitionSpec as P


def from_behind(x, axis, by):
    size = lax.axis_size(axis)
    return lax.ppermute(x, axis, [(i, (i + by) % size) for i in range(size)])


def normalize(residual, summed):
    combined = residual.astype(jnp.float32) + summed
    inverse = lax.rsqrt(jnp.sum(combined * combined, axis=1, keepdims=True) + 1e-06)
    return (combined * inverse, inverse)


def retract(normed, inverse, gradient):
    projection = jnp.sum(normed * gradient, axis=1, keepdims=True)
    return ((gradient - normed * projection) * inverse).astype(jnp.bfloat16)


def pairwise_loss_terms(
    image_row_block,
    image_label_index,
    text_row_block,
    text_label_index,
    logit_scale_value,
    shifted_logit_bias,
):
    pair_logit_matrix = (
        logit_scale_value
        * jnp.dot(image_row_block, text_row_block.T, preferred_element_type=jnp.float32)
        + shifted_logit_bias
    )
    matches = image_label_index[:, None] == text_label_index[None, :]
    label_sign_matrix = jnp.where(matches, 1.0, -1.0).astype(jnp.float32)
    pair_coefficients = (
        -label_sign_matrix
        * jax.nn.sigmoid(-label_sign_matrix * pair_logit_matrix)
        * logit_scale_value
    ).astype(jnp.bfloat16)
    image_term = jnp.dot(pair_coefficients, text_row_block, preferred_element_type=jnp.float32)
    text_term = jnp.dot(pair_coefficients.T, image_row_block, preferred_element_type=jnp.float32)
    return (image_term, text_term)


def shards(
    image_residual_input,
    image_hidden_units,
    image_output_weight,
    text_residual_input,
    text_hidden_units,
    text_output_weight,
    log_logit_scale,
    pair_logit_bias,
):
    partial_image = jnp.dot(
        image_hidden_units, image_output_weight, preferred_element_type=jnp.float32
    )
    partial_text = jnp.dot(
        text_hidden_units, text_output_weight, preferred_element_type=jnp.float32
    )
    summed_image, summed_text = (
        lax.psum(partial_image.astype(jnp.bfloat16), "tensor").astype(jnp.float32),
        lax.psum(partial_text.astype(jnp.bfloat16), "tensor").astype(jnp.float32),
    )
    normed_image, inverse_image = normalize(image_residual_input, summed_image)
    normed_text, inverse_text = normalize(text_residual_input, summed_text)
    row_count = image_residual_input.shape[0]
    feature_width = image_residual_input.shape[1]
    piece_rows = row_count // 2
    replicas = lax.axis_size("replica")
    loop_size = lax.axis_size("dp")
    data_parallel_rank = lax.axis_index("dp")
    replica_position = lax.axis_index("replica")
    tensor_position = lax.axis_index("tensor")
    half_image = tensor_position // 2
    half_text = tensor_position % 2
    own_images = lax.dynamic_slice_in_dim(
        normed_image.astype(jnp.bfloat16), half_image * piece_rows, piece_rows, 0
    )
    image_row_block = lax.all_gather(own_images, "replica", axis=0, tiled=True)
    position = jnp.arange(replicas * piece_rows, dtype=jnp.int32)
    image_label_index = (
        (data_parallel_rank * replicas + position // piece_rows) * row_count
        + half_image * piece_rows
        + position % piece_rows
    )
    text_row_block = lax.dynamic_slice_in_dim(
        normed_text.astype(jnp.bfloat16), half_text * piece_rows, piece_rows, 0
    )
    text_offsets = jnp.arange(piece_rows, dtype=jnp.int32)

    def text_label_lookup(anchor_point):
        return (
            (anchor_point * replicas + replica_position) * row_count
            + half_text * piece_rows
            + text_offsets
        )

    logit_scale_value = jnp.exp(log_logit_scale[0])
    shifted_logit_bias = pair_logit_bias[0]
    image_acc, text_acc = pairwise_loss_terms(
        image_row_block,
        image_label_index,
        text_row_block,
        text_label_lookup(data_parallel_rank),
        logit_scale_value,
        shifted_logit_bias,
    )

    def advance(counter, carry_state):
        rotating_texts, carried, image_sum = carry_state
        rotating_texts = from_behind(rotating_texts, "dp", 1)
        carried = from_behind(carried, "dp", 1)
        anchor_point = (data_parallel_rank - counter) % loop_size
        image_term, text_term = pairwise_loss_terms(
            image_row_block,
            image_label_index,
            rotating_texts,
            text_label_lookup(anchor_point),
            logit_scale_value,
            shifted_logit_bias,
        )
        return (rotating_texts, carried + text_term, image_sum + image_term)

    rotating_texts, carried, image_acc = lax.fori_loop(
        1, loop_size, advance, (text_row_block, text_acc, image_acc)
    )
    text_grad = from_behind(carried, "dp", 1)
    image_part = lax.psum_scatter(
        image_acc.astype(jnp.bfloat16), "replica", scatter_dimension=0, tiled=True
    ).astype(jnp.float32)
    image_buffer = lax.dynamic_update_slice_in_dim(
        jnp.zeros((row_count, feature_width), jnp.float32), image_part, half_image * piece_rows, 0
    )
    text_buffer = lax.dynamic_update_slice_in_dim(
        jnp.zeros((row_count, feature_width), jnp.float32), text_grad, half_text * piece_rows, 0
    )
    grad_image, grad_text = lax.psum((image_buffer, text_buffer), "tensor")
    upstream_image = retract(normed_image, inverse_image, grad_image)
    upstream_text = retract(normed_text, inverse_text, grad_text)
    hidden_grad_image = jnp.dot(
        upstream_image, image_output_weight.T, preferred_element_type=jnp.float32
    ).astype(jnp.bfloat16)
    hidden_grad_text = jnp.dot(
        upstream_text, text_output_weight.T, preferred_element_type=jnp.float32
    ).astype(jnp.bfloat16)
    term_image = jnp.dot(image_hidden_units.T, upstream_image, preferred_element_type=jnp.float32)
    term_text = jnp.dot(text_hidden_units.T, upstream_text, preferred_element_type=jnp.float32)
    share_image, share_text = (
        lax.psum_scatter(
            term_image.astype(jnp.bfloat16), "replica", scatter_dimension=1, tiled=True
        ).astype(jnp.float32),
        lax.psum_scatter(
            term_text.astype(jnp.bfloat16), "replica", scatter_dimension=1, tiled=True
        ).astype(jnp.float32),
    )
    total_image, total_text = lax.psum((share_image, share_text), "dp")
    return (hidden_grad_image, hidden_grad_text, total_image, total_text)


def solution(mesh):
    in_specs = (
        P(("dp", "replica"), None),
        P(("dp", "replica"), "tensor"),
        P("tensor", None),
        P(("dp", "replica"), None),
        P(("dp", "replica"), "tensor"),
        P("tensor", None),
        P(),
        P(),
    )
    out_specs = (
        P(("dp", "replica"), "tensor"),
        P(("dp", "replica"), "tensor"),
        P("tensor", "replica"),
        P("tensor", "replica"),
    )
    return jax.shard_map(shards, mesh=mesh, in_specs=in_specs, out_specs=out_specs, check_vma=False)
```

profile of v0, /device:TPU:24, one launch (start us, length us, event | category | flops | bytes accessed | tf_op | source)
XLA Modules:
  0.0 658.9 jit_solution(15720231304251806751)
XLA Ops:
  11.1 61.1 %all-reduce.9.cloned.1.call-done = (bf16[128,1152]{1,0:T(8,128)(2,1)}, bf16[128,1152]{1,0:T(8,128)(2,1)}) async-done(((bf16[128,1152]{1,0:T(8,128)(2,1)}, bf16[128,1152]{1,0:T(8,128)(2,1)}), (bf16[128,1152]{1,0:T(8,128)(2,1)}, bf16[128,1152]{1,0:T(8,128)(2,1)})) %all-reduce.9.cloned.1.call-update) | async-done | bytes 589840 | tf_op jit(solution)/shard_map/psum | solution.py:66
  78.5 44.2 %all-gather.2.cloned.1.call-done = bf16[512,1152]{1,0:T(8,128)(2,1)} async-done(((bf16[64,1152]{1,0:T(8,128)(2,1)}), bf16[512,1152]{1,0:T(8,128)(2,1)}) %all-gather.2.cloned.1.call-update) | async-done | bytes 1179664 | tf_op jit(solution)/shard_map/all_gather | solution.py:83
  128.5 239.9 %while.20 = (s32[]{:T(128)}, bf16[64,1152]{1,0:T(8,128)(2,1)}, f32[64,1152]{1,0:T(8,128)}, f32[512,1152]{1,0:T(8,128)}, s32[]{:T(128)}, /*index=5*/s32[]{:T(128)...) while((s32[]{:T(128)}, bf16[64,1152]{1,0:T(8,128)(2,1)}, ...), condition=%wide.region_5.6_spmd.clone, body=%wide.region_4.5_spmd.clone.sunk | while | flops 227557456 | bytes 10228658 | solution.py:128
  146.1 3.9 collective-permute-start.1
  154.5 3.6 convolution_add_fusion.5
  161.1 5.0 collective-permute-start.1
  169.4 3.6 convolution_add_fusion.5
  174.0 3.8 collective-permute-start
  177.9 4.3 collective-permute-start.1
  184.3 3.6 convolution_add_fusion.5
  201.5 3.6 convolution_add_fusion.5
  212.8 3.6 collective-permute-done
  218.2 3.6 convolution_add_fusion.5
  242.3 4.3 collective-permute-start.1
  259.1 4.4 collective-permute-start.1
  275.9 3.8 collective-permute-start.1
  279.8 4.3 collective-permute-done
  285.8 3.6 convolution_add_fusion.5
  295.3 5.1 collective-permute-done
  311.3 5.5 collective-permute-done
  318.6 3.6 convolution_add_fusion.5
  327.7 4.4 collective-permute-done
  333.9 3.6 convolution_add_fusion.5
  343.3 3.7 collective-permute-done
  358.2 3.7 collective-permute-done
  363.7 3.6 convolution_add_fusion.5
  373.2 7.9 %collective-permute-done.2 = f32[64,1152]{1,0:T(8,128)S(1)} collective-permute-done((f32[64,1152]{1,0:T(8,128)S(1)}, f32[64,1152]{1,0:T(8,128)S(1)}, u32[]{:S(2)}, u32[]{:S(2)}) %collective-permute-start.2) | collective-permute-done | bytes 294944 | tf_op jit(solution)/shard_map/ppermute | solution.py:9
  382.7 29.6 %reduce-scatter.8.cloned.1.call-done = bf16[64,1152]{1,0:T(8,128)(2,1)} async-done(((bf16[512,1152]{1,0:T(8,128)(2,1)}), bf16[64,1152]{1,0:T(8,128)(2,1)}) %reduce-scatter.8.cloned.1.call-update) | async-done | bytes 147472 | tf_op jit(solution)/shard_map/reduce_scatter | solution.py:132
  414.3 61.2 %all-reduce.7.cloned.1.call-done = (f32[128,1152]{1,0:T(8,128)}, f32[128,1152]{1,0:T(8,128)}) async-done(((f32[128,1152]{1,0:T(8,128)}, f32[128,1152]{1,0:T(8,128)}), (f32[128,1152]{1,0:T(8,128)}, f32[128,1152]{1,0:T(8,128)})) %all-reduce.7.cloned.1.call-update) | async-done | bytes 1179664 | tf_op jit(solution)/shard_map/psum | solution.py:141
  485.6 43.3 %reduce-scatter.10.cloned.1.call-done = bf16[144,544]{1,0:T(8,128)(2,1)} async-done(((bf16[1152,544]{1,0:T(8,128)(2,1)}), bf16[144,544]{1,0:T(8,128)(2,1)}) %reduce-scatter.10.cloned.1.call-update) | async-done | bytes 156688
  530.0 48.7 %reduce-scatter.12.cloned.1.call-done = bf16[144,544]{1,0:T(8,128)(2,1)} async-done(((bf16[1152,544]{1,0:T(8,128)(2,1)}), bf16[144,544]{1,0:T(8,128)(2,1)}) %reduce-scatter.12.cloned.1.call-update) | async-done | bytes 156688
  579.7 70.4 %all-reduce.10 = (f32[544,144]{1,0:T(8,128)S(1)}, f32[544,144]{1,0:T(8,128)S(1)}) all-reduce(bf16[544,144]{1,0:T(8,128)(2,1)S(1)} %copy.17, bf16[544,144]{1,0:T(8,128)(2,1)S(1)} %copy.19), channel_id=1, replica_groups=mesh['dp'=16,'replica'=8,'tensor'=4] {'dp'}, use_global_device_ids=true, to_apply=%region_12.13 | all-reduce | flops 156672 | bytes 940032 | tf_op jit(solution)/shard_map/psum | solution.py:160
  (205 shorter events, 183.6 us)
Async XLA Ops:
  7.2 65.1 %all-reduce.9.cloned.1.call-start = ((), (), s32[]{:S(2)}) async-start(), calls=%async_computation.8 | async-start | bytes 1179648 | tf_op jit(solution)/shard_map/psum | solution.py:66
  11.1 111.6 %all-gather.2.cloned.1.call-start = ((), (), s32[]{:S(2)}) async-start(), calls=%async_computation.3 | async-start | bytes 1327104 | tf_op jit(solution)/shard_map/all_gather | solution.py:83
  75.3 337.1 %reduce-scatter.8.cloned.1.call-start = ((), (), s32[]{:S(2)}) async-start(), calls=%async_computation.4 | async-start | bytes 1327104 | tf_op jit(solution)/shard_map/reduce_scatter | solution.py:132
  128.5 9.3 %collective-permute-start = (bf16[64,1152]{1,0:T(8,128)(2,1)}, bf16[64,1152]{1,0:T(8,128)(2,1)S(1)}, u32[]{:S(2)}, u32[]{:S(2)}) collective-permute-start(bf16[64,1152]{1,0:T(8,128)(2,1)} %get-tuple-element.457), channel_id=1, source_target_pairs={{0,32},{32,64},{64,96},{96,128},{128,160},{160,192},{192,224},{224... | collective-permute-start | bytes 442376 | tf_op jit(solution)/shard_map/while/body/eval_jaxpr/ppermute | solution.py:9
  132.0 11.2 %collective-permute-start.1 = (f32[64,1152]{1,0:T(8,128)}, f32[64,1152]{1,0:T(8,128)S(1)}, u32[]{:S(2)}, u32[]{:S(2)}) collective-permute-start(f32[64,1152]{1,0:T(8,128)} %get-tuple-element.458), channel_id=1, source_target_pairs={{0,32},{32,64},{64,96},{96,128},{128,160},{160,192},{192,224},{224... | collective-permute-start | bytes 884744 | tf_op jit(solution)/shard_map/while/body/eval_jaxpr/ppermute | solution.py:9
  144.2 8.4 %collective-permute-start = (bf16[64,1152]{1,0:T(8,128)(2,1)}, bf16[64,1152]{1,0:T(8,128)(2,1)S(1)}, u32[]{:S(2)}, u32[]{:S(2)}) collective-permute-start(bf16[64,1152]{1,0:T(8,128)(2,1)} %get-tuple-element.457), channel_id=1, source_target_pairs={{0,32},{32,64},{64,96},{96,128},{128,160},{160,192},{192,224},{224... | collective-permute-start | bytes 442376 | tf_op jit(solution)/shard_map/while/body/eval_jaxpr/ppermute | solution.py:9
  146.1 11.9 %collective-permute-start.1 = (f32[64,1152]{1,0:T(8,128)}, f32[64,1152]{1,0:T(8,128)S(1)}, u32[]{:S(2)}, u32[]{:S(2)}) collective-permute-start(f32[64,1152]{1,0:T(8,128)} %get-tuple-element.458), channel_id=1, source_target_pairs={{0,32},{32,64},{64,96},{96,128},{128,160},{160,192},{192,224},{224... | collective-permute-start | bytes 884744 | tf_op jit(solution)/shard_map/while/body/eval_jaxpr/ppermute | solution.py:9
  159.1 8.4 %collective-permute-start = (bf16[64,1152]{1,0:T(8,128)(2,1)}, bf16[64,1152]{1,0:T(8,128)(2,1)S(1)}, u32[]{:S(2)}, u32[]{:S(2)}) collective-permute-start(bf16[64,1152]{1,0:T(8,128)(2,1)} %get-tuple-element.457), channel_id=1, source_target_pairs={{0,32},{32,64},{64,96},{96,128},{128,160},{160,192},{192,224},{224... | collective-permute-start | bytes 442376 | tf_op jit(solution)/shard_map/while/body/eval_jaxpr/ppermute | solution.py:9
  161.1 11.9 %collective-permute-start.1 = (f32[64,1152]{1,0:T(8,128)}, f32[64,1152]{1,0:T(8,128)S(1)}, u32[]{:S(2)}, u32[]{:S(2)}) collective-permute-start(f32[64,1152]{1,0:T(8,128)} %get-tuple-element.458), channel_id=1, source_target_pairs={{0,32},{32,64},{64,96},{96,128},{128,160},{160,192},{192,224},{224... | collective-permute-start | bytes 884744 | tf_op jit(solution)/shard_map/while/body/eval_jaxpr/ppermute | solution.py:9
  174.0 8.4 %collective-permute-start = (bf16[64,1152]{1,0:T(8,128)(2,1)}, bf16[64,1152]{1,0:T(8,128)(2,1)S(1)}, u32[]{:S(2)}, u32[]{:S(2)}) collective-permute-start(bf16[64,1152]{1,0:T(8,128)(2,1)} %get-tuple-element.457), channel_id=1, source_target_pairs={{0,32},{32,64},{64,96},{96,128},{128,160},{160,192},{192,224},{224... | collective-permute-start | bytes 442376 | tf_op jit(solution)/shard_map/while/body/eval_jaxpr/ppermute | solution.py:9
  177.9 12.3 %collective-permute-start.1 = (f32[64,1152]{1,0:T(8,128)}, f32[64,1152]{1,0:T(8,128)S(1)}, u32[]{:S(2)}, u32[]{:S(2)}) collective-permute-start(f32[64,1152]{1,0:T(8,128)} %get-tuple-element.458), channel_id=1, source_target_pairs={{0,32},{32,64},{64,96},{96,128},{128,160},{160,192},{192,224},{224... | collective-permute-start | bytes 884744 | tf_op jit(solution)/shard_map/while/body/eval_jaxpr/ppermute | solution.py:9
  194.0 12.9 %collective-permute-start.1 = (f32[64,1152]{1,0:T(8,128)}, f32[64,1152]{1,0:T(8,128)S(1)}, u32[]{:S(2)}, u32[]{:S(2)}) collective-permute-start(f32[64,1152]{1,0:T(8,128)} %get-tuple-element.458), channel_id=1, source_target_pairs={{0,32},{32,64},{64,96},{96,128},{128,160},{160,192},{192,224},{224... | collective-permute-start | bytes 884744 | tf_op jit(solution)/shard_map/while/body/eval_jaxpr/ppermute | solution.py:9
  209.9 13.1 %collective-permute-start.1 = (f32[64,1152]{1,0:T(8,128)}, f32[64,1152]{1,0:T(8,128)S(1)}, u32[]{:S(2)}, u32[]{:S(2)}) collective-permute-start(f32[64,1152]{1,0:T(8,128)} %get-tuple-element.458), channel_id=1, source_target_pairs={{0,32},{32,64},{64,96},{96,128},{128,160},{160,192},{192,224},{224... | collective-permute-start | bytes 884744 | tf_op jit(solution)/shard_map/while/body/eval_jaxpr/ppermute | solution.py:9
  225.9 13.2 %collective-permute-start.1 = (f32[64,1152]{1,0:T(8,128)}, f32[64,1152]{1,0:T(8,128)S(1)}, u32[]{:S(2)}, u32[]{:S(2)}) collective-permute-start(f32[64,1152]{1,0:T(8,128)} %get-tuple-element.458), channel_id=1, source_target_pairs={{0,32},{32,64},{64,96},{96,128},{128,160},{160,192},{192,224},{224... | collective-permute-start | bytes 884744 | tf_op jit(solution)/shard_map/while/body/eval_jaxpr/ppermute | solution.py:9
  240.1 9.2 %collective-permute-start = (bf16[64,1152]{1,0:T(8,128)(2,1)}, bf16[64,1152]{1,0:T(8,128)(2,1)S(1)}, u32[]{:S(2)}, u32[]{:S(2)}) collective-permute-start(bf16[64,1152]{1,0:T(8,128)(2,1)} %get-tuple-element.457), channel_id=1, source_target_pairs={{0,32},{32,64},{64,96},{96,128},{128,160},{160,192},{192,224},{224... | collective-permute-start | bytes 442376 | tf_op jit(solution)/shard_map/while/body/eval_jaxpr/ppermute | solution.py:9
  242.3 13.3 %collective-permute-start.1 = (f32[64,1152]{1,0:T(8,128)}, f32[64,1152]{1,0:T(8,128)S(1)}, u32[]{:S(2)}, u32[]{:S(2)}) collective-permute-start(f32[64,1152]{1,0:T(8,128)} %get-tuple-element.458), channel_id=1, source_target_pairs={{0,32},{32,64},{64,96},{96,128},{128,160},{160,192},{192,224},{224... | collective-permute-start | bytes 884744 | tf_op jit(solution)/shard_map/while/body/eval_jaxpr/ppermute | solution.py:9
  256.7 10.0 %collective-permute-start = (bf16[64,1152]{1,0:T(8,128)(2,1)}, bf16[64,1152]{1,0:T(8,128)(2,1)S(1)}, u32[]{:S(2)}, u32[]{:S(2)}) collective-permute-start(bf16[64,1152]{1,0:T(8,128)(2,1)} %get-tuple-element.457), channel_id=1, source_target_pairs={{0,32},{32,64},{64,96},{96,128},{128,160},{160,192},{192,224},{224... | collective-permute-start | bytes 442376 | tf_op jit(solution)/shard_map/while/body/eval_jaxpr/ppermute | solution.py:9
  259.1 13.9 %collective-permute-start.1 = (f32[64,1152]{1,0:T(8,128)}, f32[64,1152]{1,0:T(8,128)S(1)}, u32[]{:S(2)}, u32[]{:S(2)}) collective-permute-start(f32[64,1152]{1,0:T(8,128)} %get-tuple-element.458), channel_id=1, source_target_pairs={{0,32},{32,64},{64,96},{96,128},{128,160},{160,192},{192,224},{224... | collective-permute-start | bytes 884744 | tf_op jit(solution)/shard_map/while/body/eval_jaxpr/ppermute | solution.py:9
  274.0 10.0 %collective-permute-start = (bf16[64,1152]{1,0:T(8,128)(2,1)}, bf16[64,1152]{1,0:T(8,128)(2,1)S(1)}, u32[]{:S(2)}, u32[]{:S(2)}) collective-permute-start(bf16[64,1152]{1,0:T(8,128)(2,1)} %get-tuple-element.457), channel_id=1, source_target_pairs={{0,32},{32,64},{64,96},{96,128},{128,160},{160,192},{192,224},{224... | collective-permute-start | bytes 442376 | tf_op jit(solution)/shard_map/while/body/eval_jaxpr/ppermute | solution.py:9
  275.9 13.5 %collective-permute-start.1 = (f32[64,1152]{1,0:T(8,128)}, f32[64,1152]{1,0:T(8,128)S(1)}, u32[]{:S(2)}, u32[]{:S(2)}) collective-permute-start(f32[64,1152]{1,0:T(8,128)} %get-tuple-element.458), channel_id=1, source_target_pairs={{0,32},{32,64},{64,96},{96,128},{128,160},{160,192},{192,224},{224... | collective-permute-start | bytes 884744 | tf_op jit(solution)/shard_map/while/body/eval_jaxpr/ppermute | solution.py:9
  290.5 9.8 %collective-permute-start = (bf16[64,1152]{1,0:T(8,128)(2,1)}, bf16[64,1152]{1,0:T(8,128)(2,1)S(1)}, u32[]{:S(2)}, u32[]{:S(2)}) collective-permute-start(bf16[64,1152]{1,0:T(8,128)(2,1)} %get-tuple-element.457), channel_id=1, source_target_pairs={{0,32},{32,64},{64,96},{96,128},{128,160},{160,192},{192,224},{224... | collective-permute-start | bytes 442376 | tf_op jit(solution)/shard_map/while/body/eval_jaxpr/ppermute | solution.py:9
  292.4 13.3 %collective-permute-start.1 = (f32[64,1152]{1,0:T(8,128)}, f32[64,1152]{1,0:T(8,128)S(1)}, u32[]{:S(2)}, u32[]{:S(2)}) collective-permute-start(f32[64,1152]{1,0:T(8,128)} %get-tuple-element.458), channel_id=1, source_target_pairs={{0,32},{32,64},{64,96},{96,128},{128,160},{160,192},{192,224},{224... | collective-permute-start | bytes 884744 | tf_op jit(solution)/shard_map/while/body/eval_jaxpr/ppermute | solution.py:9
  306.8 10.0 %collective-permute-start = (bf16[64,1152]{1,0:T(8,128)(2,1)}, bf16[64,1152]{1,0:T(8,128)(2,1)S(1)}, u32[]{:S(2)}, u32[]{:S(2)}) collective-permute-start(bf16[64,1152]{1,0:T(8,128)(2,1)} %get-tuple-element.457), channel_id=1, source_target_pairs={{0,32},{32,64},{64,96},{96,128},{128,160},{160,192},{192,224},{224... | collective-permute-start | bytes 442376 | tf_op jit(solution)/shard_map/while/body/eval_jaxpr/ppermute | solution.py:9
  308.7 13.5 %collective-permute-start.1 = (f32[64,1152]{1,0:T(8,128)}, f32[64,1152]{1,0:T(8,128)S(1)}, u32[]{:S(2)}, u32[]{:S(2)}) collective-permute-start(f32[64,1152]{1,0:T(8,128)} %get-tuple-element.458), channel_id=1, source_target_pairs={{0,32},{32,64},{64,96},{96,128},{128,160},{160,192},{192,224},{224... | collective-permute-start | bytes 884744 | tf_op jit(solution)/shard_map/while/body/eval_jaxpr/ppermute | solution.py:9
  323.3 8.8 %collective-permute-start = (bf16[64,1152]{1,0:T(8,128)(2,1)}, bf16[64,1152]{1,0:T(8,128)(2,1)S(1)}, u32[]{:S(2)}, u32[]{:S(2)}) collective-permute-start(bf16[64,1152]{1,0:T(8,128)(2,1)} %get-tuple-element.457), channel_id=1, source_target_pairs={{0,32},{32,64},{64,96},{96,128},{128,160},{160,192},{192,224},{224... | collective-permute-start | bytes 442376 | tf_op jit(solution)/shard_map/while/body/eval_jaxpr/ppermute | solution.py:9
  325.2 12.3 %collective-permute-start.1 = (f32[64,1152]{1,0:T(8,128)}, f32[64,1152]{1,0:T(8,128)S(1)}, u32[]{:S(2)}, u32[]{:S(2)}) collective-permute-start(f32[64,1152]{1,0:T(8,128)} %get-tuple-element.458), channel_id=1, source_target_pairs={{0,32},{32,64},{64,96},{96,128},{128,160},{160,192},{192,224},{224... | collective-permute-start | bytes 884744 | tf_op jit(solution)/shard_map/while/body/eval_jaxpr/ppermute | solution.py:9
  340.5 11.9 %collective-permute-start.1 = (f32[64,1152]{1,0:T(8,128)}, f32[64,1152]{1,0:T(8,128)S(1)}, u32[]{:S(2)}, u32[]{:S(2)}) collective-permute-start(f32[64,1152]{1,0:T(8,128)} %get-tuple-element.458), channel_id=1, source_target_pairs={{0,32},{32,64},{64,96},{96,128},{128,160},{160,192},{192,224},{224... | collective-permute-start | bytes 884744 | tf_op jit(solution)/shard_map/while/body/eval_jaxpr/ppermute | solution.py:9
  355.4 11.9 %collective-permute-start.1 = (f32[64,1152]{1,0:T(8,128)}, f32[64,1152]{1,0:T(8,128)S(1)}, u32[]{:S(2)}, u32[]{:S(2)}) collective-permute-start(f32[64,1152]{1,0:T(8,128)} %get-tuple-element.458), channel_id=1, source_target_pairs={{0,32},{32,64},{64,96},{96,128},{128,160},{160,192},{192,224},{224... | collective-permute-start | bytes 884744 | tf_op jit(solution)/shard_map/while/body/eval_jaxpr/ppermute | solution.py:9
  371.3 104.2 %all-reduce.7.cloned.1.call-start = ((), (), s32[]{:S(2)}) async-start(), calls=%async_computation.7 | async-start | bytes 2359296 | tf_op jit(solution)/shard_map/psum | solution.py:141
  371.3 9.8 %collective-permute-start.2 = (f32[64,1152]{1,0:T(8,128)S(1)}, f32[64,1152]{1,0:T(8,128)S(1)}, u32[]{:S(2)}, u32[]{:S(2)}) collective-permute-start(f32[64,1152]{1,0:T(8,128)S(1)} %copy-done.15), channel_id=1, source_target_pairs={{0,32},{32,64},{64,96},{96,128},{128,160},{160,192},{192,224},{224... | collective-permute-start | bytes 884744 | tf_op jit(solution)/shard_map/ppermute | solution.py:9
  414.2 114.7 %reduce-scatter.10.cloned.1.call-start = ((), (), s32[]{:S(2)}) async-start(), calls=%async_computation.5 | async-start | bytes 1658880
  480.1 98.6 %reduce-scatter.12.cloned.1.call-start = ((), (), s32[]{:S(2)}) async-start(), calls=%async_computation.6 | async-start | bytes 1658880
  (21 other events, 258.1 us)
Sparse Core Ops, SparseCore 0:
  11.6 60.6 all-reduce.8
  75.4 47.2 all-gather.1
  371.4 40.9 reduce-scatter.7
  415.2 60.1 all-reduce.6
  480.2 48.7 reduce-scatter.9
  531.7 46.9 reduce-scatter.11
where the time goes:
time: 661 us; the launch traced here: 659 us
  waiting for transfers between devices  352 us (53%)
  matrix products  99.6 us (15%)
  starting transfers between devices  88.3 us (13%)
  blocking collectives  70.4 us (11%)
  local copies, waits for them, and re-layouts  23 us (3%)
  between operations  15.7 us (2%)
  other arithmetic  9 us (1%)
    unnamed x8, waiting for transfers between devices  92.1 us
    ppermute x31, starting transfers between devices, from_behind(): return lax.ppermute(x, axis, [(i, (i + by) % size) for i in range(size)])  88 us
    psum x1, blocking collectives, shards(): total_image, total_text = lax.psum((share_image, share_text), 'dp')  70.4 us
    ppermute x31, waiting for transfers between devices, from_behind(): return lax.ppermute(x, axis, [(i, (i + by) % size) for i in range(size)])  63.7 us
    psum x1, waiting for transfers between devices, shards(): grad_image, grad_text = lax.psum((image_buffer, text_buffer), 'tensor')  61.2 us
    psum x1, waiting for transfers between devices, shards(): lax.psum(partial_text.astype(jnp.bfloat16), 'tensor').astype(jnp.float32)  61.1 us
    dot_general x16, matrix products, pairwise_loss_terms(): jnp.dot(pair_coefficients, text_row_block, preferred_element_type=jnp.flo...  56.7 us
    all_gather x1, waiting for transfers between devices, shards(): image_row_block = lax.all_gather(own_images, 'replica', axis=0, tiled=True)  44.2 us
  transfers between devices with their start and end apart: 37, of which 28 were waited for; matrix products, arithmetic and copies ran while one was open for 14% of the time, Pallas kernels for 0%

commit v1 on v0

v1 whole, which is shorter than its diff:
```python
import jax
import jax.numpy as jnp
from jax import lax
from jax.sharding import PartitionSpec as P

F32 = jnp.float32
BF16 = jnp.bfloat16
PLANE = ("replica", "tensor")


def dot(a, b, contract):
    return lax.dot_general(a, b, (contract, ((), ())), preferred_element_type=F32)


def exchange(x, axis):
    return lax.all_to_all(x, axis, split_axis=0, concat_axis=0, tiled=True)


def spread(x, axis):
    size = lax.axis_size(axis)
    return exchange(jnp.broadcast_to(x[None], (size,) + x.shape), axis)


def after(x, *others):
    return lax.optimization_barrier((x,) + others)[0]


def normalize(residual, summed):
    combined = residual.astype(F32) + summed
    inverse = lax.rsqrt(jnp.sum(combined * combined, axis=1, keepdims=True) + 1e-06)
    return (combined * inverse, inverse)


def retract(normed, inverse, gradient):
    projection = jnp.sum(normed * gradient, axis=1, keepdims=True)
    return ((gradient - normed * projection) * inverse).astype(BF16)


def shards(
    image_residual_input,
    image_hidden_units,
    image_output_weight,
    text_residual_input,
    text_hidden_units,
    text_output_weight,
    log_logit_scale,
    pair_logit_bias,
):
    rows, width = image_residual_input.shape
    hidden = image_hidden_units.shape[1]
    n_dp = lax.axis_size("dp")
    n_replica = lax.axis_size("replica")
    n_tensor = lax.axis_size("tensor")
    dp = lax.axis_index("dp")
    replica = lax.axis_index("replica")
    tensor = lax.axis_index("tensor")
    own = rows // n_tensor
    members = n_replica * n_tensor
    columns = width // n_replica

    terms = jnp.concatenate(
        [
            dot(image_hidden_units, image_output_weight, ((1,), (0,)))
            .astype(BF16)
            .reshape(n_tensor, own, width),
            dot(text_hidden_units, text_output_weight, ((1,), (0,)))
            .astype(BF16)
            .reshape(n_tensor, own, width),
        ],
        axis=1,
    )
    summed = jnp.sum(exchange(terms, "tensor").astype(F32), axis=0)
    image_residual = lax.dynamic_slice_in_dim(image_residual_input, tensor * own, own, 0)
    text_residual = lax.dynamic_slice_in_dim(text_residual_input, tensor * own, own, 0)
    normed_text, inverse_text = normalize(text_residual, summed[own:])
    normed_image, inverse_image = normalize(image_residual, summed[:own])

    texts = lax.all_gather(normed_text.astype(BF16), "dp", axis=0, tiled=True)
    images = spread(normed_image.astype(BF16), PLANE)
    hidden_image = spread(after(image_hidden_units, images), "replica")
    texts, images, hidden_image = lax.optimization_barrier((texts, images, hidden_image))
    images = images.reshape(members * own, width)

    scale = jnp.exp(log_logit_scale[0])
    logits = scale * dot(images, texts, ((1,), (1,))) + pair_logit_bias[0]
    image_index = dp * (members * own) + jnp.arange(members * own, dtype=jnp.int32)
    position = jnp.arange(n_dp * own, dtype=jnp.int32)
    text_index = (
        (position // own) * (members * own)
        + (replica * n_tensor + tensor) * own
        + position % own
    )
    label = jnp.where(image_index[:, None] == text_index[None, :], 1.0, -1.0).astype(F32)
    coefficients = (-label * jax.nn.sigmoid(-label * logits) * scale).astype(BF16)
    text_partial = dot(coefficients, images, ((0,), (0,))).astype(BF16)
    image_partial = dot(coefficients, texts, ((1,), (0,))).astype(BF16)

    text_grad = lax.psum_scatter(text_partial, "dp", scatter_dimension=0, tiled=True).astype(F32)
    image_parts = exchange(image_partial.reshape(members, own, width), PLANE)
    image_grad = jnp.sum(image_parts.astype(F32), axis=0)
    hidden_text = spread(after(text_hidden_units, image_parts), "replica")
    text_grad, image_grad, hidden_text = lax.optimization_barrier(
        (text_grad, image_grad, hidden_text)
    )

    upstream = jnp.concatenate(
        [
            retract(normed_image, inverse_image, image_grad),
            retract(normed_text, inverse_text, text_grad),
        ],
        axis=0,
    )
    group = lax.all_gather(upstream, "tensor", axis=0).reshape(n_tensor, 2, own, width)
    hidden_grad_image = dot(
        group[:, 0].reshape(rows, width), image_output_weight, ((1,), (1,))
    ).astype(BF16)
    hidden_grad_text = dot(
        group[:, 1].reshape(rows, width), text_output_weight, ((1,), (1,))
    ).astype(BF16)

    cut = jnp.transpose(upstream.reshape(2 * own, n_replica, columns), (1, 0, 2))
    cut = jnp.broadcast_to(cut[:, None], (n_replica, n_tensor, 2 * own, columns))
    cut = exchange(cut.reshape(members, 2 * own, columns), PLANE)
    cut_image = cut[:, :own].reshape(members * own, columns)
    cut_text = cut[:, own:].reshape(members * own, columns)
    partial = jnp.concatenate(
        [
            dot(hidden_image.reshape(members * own, hidden), cut_image, ((0,), (0,))),
            dot(hidden_text.reshape(members * own, hidden), cut_text, ((0,), (0,))),
        ],
        axis=1,
    ).astype(BF16)
    pieces = exchange(partial.reshape(n_dp, hidden // n_dp, 2 * columns), "dp")
    share = jnp.sum(pieces.astype(F32), axis=0).astype(BF16)
    total = spread(share, "dp").reshape(hidden, 2 * columns).astype(F32)
    return (hidden_grad_image, hidden_grad_text, total[:, :columns], total[:, columns:])


def solution(mesh):
    in_specs = (
        P(("dp", "replica"), None),
        P(("dp", "replica"), "tensor"),
        P("tensor", None),
        P(("dp", "replica"), None),
        P(("dp", "replica"), "tensor"),
        P("tensor", None),
        P(),
        P(),
    )
    out_specs = (
        P(("dp", "replica"), "tensor"),
        P(("dp", "replica"), "tensor"),
        P("tensor", "replica"),
        P("tensor", "replica"),
    )
    return jax.shard_map(shards, mesh=mesh, in_specs=in_specs, out_specs=out_specs, check_vma=False)
```

time: 661 us -> 312 us (0.47)
  waiting for transfers between devices: 352 us -> 161 us
  matrix products: 99.6 us -> 17.6 us
  starting transfers between devices: 88.3 us -> 48.2 us
  blocking collectives: 70.4 us -> 44 us
    psum x2 -> x0, waiting for transfers between devices: 122 us -> none  [the longest x1 61.2 us: shards(): grad_image, grad_text = lax.psum((image_buffer, text_buffer), 'tensor')]
    all_to_all x0 -> x7, waiting for transfers between devices: none -> 91.6 us  [exchange(): return lax.all_to_all(x, axis, split_axis=0, concat_axis=0, tiled=True)]
    unnamed x8 -> x2, waiting for transfers between devices: 92.1 us -> 0.7 us
    ppermute x31 -> x0, starting transfers between devices: 88 us -> none  [from_behind(): return lax.ppermute(x, axis, [(i, (i + by) % size) for i in range(size)])]
    dot_general x54 -> x9, matrix products: 99.6 us -> 17.6 us  [dot(): lax.dot_general(a, b, (contract, ((), ())), preferred_element_type=F32)]
    psum x1 -> x0, blocking collectives: 70.4 us -> none  [shards(): total_image, total_text = lax.psum((share_image, share_text), 'dp')]
    ppermute x31 -> x0, waiting for transfers between devices: 63.7 us -> none  [from_behind(): return lax.ppermute(x, axis, [(i, (i + by) % size) for i in range(size)])]
    all_to_all x0 -> x7, starting transfers between devices: none -> 48.1 us  [exchange(): return lax.all_to_all(x, axis, split_axis=0, concat_axis=0, tiled=True)]
  transfers between devices with their start and end apart: 37 -> 9, of which waited for: 28 -> 7; matrix products, arithmetic and copies ran while one was open for 14% -> 6% of each run, Pallas kernels for 0% -> 0%
where the time goes in v1:
time: 312 us; the launch traced here: 309 us
  waiting for transfers between devices  161 us (52%)
  starting transfers between devices  48.2 us (15%)
  blocking collectives  44 us (14%)
  matrix products  17.6 us (6%)
  local copies, waits for them, and re-layouts  16.8 us (5%)
  between operations  15.6 us (5%)
  other arithmetic  5.4 us (2%)
    all_to_all x7, waiting for transfers between devices, exchange(): return lax.all_to_all(x, axis, split_axis=0, concat_axis=0, tiled=True)  91.6 us
    all_to_all x7, starting transfers between devices, exchange(): return lax.all_to_all(x, axis, split_axis=0, concat_axis=0, tiled=True)  48.1 us
    all_gather x1, waiting for transfers between devices, shards(): texts = lax.all_gather(normed_text.astype(BF16), 'dp', axis=0, tiled=True)  36.1 us
    all_to_all x1, blocking collectives, exchange(): return lax.all_to_all(x, axis, split_axis=0, concat_axis=0, tiled=True)  35.3 us
    reduce_scatter x1, waiting for transfers between devices, shards(): lax.psum_scatter(text_partial, 'dp', scatter_dimension=0, tiled=True)  32.9 us
    dot_general x9, matrix products, dot(): lax.dot_general(a, b, (contract, ((), ())), preferred_element_type=F32)  17.6 us
    all_gather x1, blocking collectives, shards(): lax.all_gather(upstream, 'tensor', axis=0).reshape(n_tensor, 2, own, width)  8.75 us
  transfers between devices with their start and end apart: 9, of which 7 were waited for; matrix products, arithmetic and copies ran while one was open for 6% of the time, Pallas kernels for 0%

profile of v1, /device:TPU:24, one launch (start us, length us, event | category | flops | bytes accessed | tf_op | source)
XLA Modules:
  0.0 308.9 jit_solution(18119059985383449754)
XLA Ops:
  7.2 1.9 convolution_convert_fusion.3
  10.5 4.9 %all-to-all-start = ((bf16[4,64,1152]{2,1,0:T(8,128)(2,1)}), bf16[4,64,1152]{2,1,0:T(8,128)(2,1)S(1)}, u32[]{:S(2)}, u32[]{:S(2)}) async-start(bf16[4,64,1152]{2,1,0:T(8,128)(2,1)} %pad_maximum_fusion), calls=%async_computation | async-start | bytes 1179648 | tf_op jit(solution)/shard_map/all_to_all | solution.py:16
  15.4 7.9 %all-to-all-done = bf16[4,64,1152]{2,1,0:T(8,128)(2,1)S(1)} async-done(((bf16[4,64,1152]{2,1,0:T(8,128)(2,1)}), bf16[4,64,1152]{2,1,0:T(8,128)(2,1)S(1)}, u32[]{:S(2)}, u32[]{:S(2)}) %all-to-all-start) | async-done | bytes 589856 | tf_op jit(solution)/shard_map/all_to_all | solution.py:16
  24.3 1.6 broadcast_in_dim.20
  25.8 12.0 %all-to-all-start.1 = ((bf16[32,32,1152]{2,1,0:T(8,128)(2,1)}), bf16[32,32,1152]{2,1,0:T(8,128)(2,1)}, u32[]{:S(2)}, u32[]{:S(2)}) async-start(bf16[32,32,1152]{2,1,0:T(8,128)(2,1)} %broadcast_in_dim.20), calls=%async_computation.1 | async-start | bytes 4718592 | tf_op jit(solution)/shard_map/all_to_all | solution.py:16
  38.6 30.9 %all-to-all-done.1 = bf16[32,32,1152]{2,1,0:T(8,128)(2,1)} async-done(((bf16[32,32,1152]{2,1,0:T(8,128)(2,1)}), bf16[32,32,1152]{2,1,0:T(8,128)(2,1)}, u32[]{:S(2)}, u32[]{:S(2)}) %all-to-all-start.1) | async-done | bytes 2359328 | tf_op jit(solution)/shard_map/all_to_all | solution.py:16
  69.6 1.2 broadcast_in_dim.21
  70.7 4.7 %all-to-all-start.2 = ((bf16[8,128,544]{1,2,0:T(8,128)(2,1)}), bf16[8,128,544]{1,2,0:T(8,128)(2,1)S(1)}, u32[]{:S(2)}, u32[]{:S(2)}) async-start(bf16[8,128,544]{1,2,0:T(8,128)(2,1)} %broadcast_in_dim.21), calls=%async_computation.2 | async-start | bytes 2228224 | tf_op jit(solution)/shard_map/all_to_all | solution.py:16
  76.8 36.1 %all-gather.3.cloned.1.call-done = bf16[512,1152]{1,0:T(8,128)(2,1)} async-done(((bf16[32,1152]{1,0:T(8,128)(2,1)}), bf16[512,1152]{1,0:T(8,128)(2,1)}) %all-gather.3.cloned.1.call-update) | async-done | bytes 1179664 | tf_op jit(solution)/shard_map/all_gather | solution.py:78
  113.0 4.3 %multiply_convert_fusion = bf16[1024,512]{1,0:T(8,128)(2,1)S(1)} fusion(bf16[1024,1152]{1,0:T(8,128)(2,1)} %bitcast.3, bf16[512,1152]{1,0:T(8,128)(2,1)} %all-gather.3.cloned.1.call-done, f32[]{:T(128)} %bitcast.49, f32[]{:T(128)} %bitcast, s32[512]{0:T(512)S(1)} %fusion.6, s32[1024]{0:T(1024)S(1)} %iota_add_fusion), kind=kOutput, calls=%fused_computation.5 | convolution fusion | flops 1214251008 | bytes 4593672 | tf_op jit(solution)/shard_map/dot_general | solution.py:12
  117.3 3.0 convolution_convert_fusion
  120.2 7.3 %all-to-all-start.3 = ((bf16[32,32,1152]{2,1,0:T(8,128)(2,1)}), bf16[32,32,1152]{2,1,0:T(8,128)(2,1)}, u32[]{:S(2)}, u32[]{:S(2)}) async-start(bf16[32,32,1152]{2,1,0:T(8,128)(2,1)} %bitcast.51), calls=%async_computation.4 | async-start | bytes 4718592 | tf_op jit(solution)/shard_map/all_to_all | solution.py:16
  127.6 4.6 %convolution_convert_fusion.1 = bf16[512,1152]{1,0:T(8,128)(2,1)} fusion(bf16[1024,512]{1,0:T(8,128)(2,1)} %copy-done.4, bf16[1024,1152]{1,0:T(8,128)(2,1)} %bitcast.3), kind=kOutput, calls=%fused_computation.2 | convolution fusion | flops 1208549376 | bytes 4587520 | tf_op jit(solution)/shard_map/dot_general | solution.py:12
  132.3 26.9 %all-to-all-done.3 = bf16[32,32,1152]{2,1,0:T(8,128)(2,1)} async-done(((bf16[32,32,1152]{2,1,0:T(8,128)(2,1)}), bf16[32,32,1152]{2,1,0:T(8,128)(2,1)}, u32[]{:S(2)}, u32[]{:S(2)}) %all-to-all-start.3) | async-done | bytes 2359328 | tf_op jit(solution)/shard_map/all_to_all | solution.py:16
  159.1 1.2 broadcast_in_dim.22
  160.3 4.9 %all-to-all-start.4 = ((bf16[8,128,544]{1,2,0:T(8,128)(2,1)}), bf16[8,128,544]{1,2,0:T(8,128)(2,1)}, u32[]{:S(2)}, u32[]{:S(2)}) async-start(bf16[8,128,544]{1,2,0:T(8,128)(2,1)} %broadcast_in_dim.22), calls=%async_computation.5 | async-start | bytes 2228224 | tf_op jit(solution)/shard_map/all_to_all | solution.py:16
  165.2 2.0 convert_reduce_fusion
  167.3 32.9 %reduce-scatter.2.cloned.1.call-done = bf16[32,1152]{1,0:T(8,128)(2,1)} async-done(((bf16[512,1152]{1,0:T(8,128)(2,1)}), bf16[32,1152]{1,0:T(8,128)(2,1)}) %reduce-scatter.2.cloned.1.call-update) | async-done | bytes 73744 | tf_op jit(solution)/shard_map/reduce_scatter | solution.py:98
  201.8 1.1 broadcast_in_dim.23
  202.9 7.5 %all-to-all-start.5 = ((bf16[32,64,144]{2,1,0:T(8,128)(2,1)}), bf16[32,64,144]{2,1,0:T(8,128)(2,1)}, u32[]{:S(2)}, u32[]{:S(2)}) async-start(bf16[32,64,144]{2,1,0:T(8,128)(2,1)} %bitcast.50), calls=%async_computation.6 | async-start | bytes 2097152 | tf_op jit(solution)/shard_map/all_to_all | solution.py:16
  210.4 1.1 bitcast_bitcast_fusion.1
  211.6 2.3 dot_general.43
  213.9 1.4 bitcast_bitcast_fusion
  215.3 1.2 dot_general.46
  216.5 9.6 %all-to-all-done.5 = bf16[32,64,144]{2,1,0:T(8,128)(2,1)} async-done(((bf16[32,64,144]{2,1,0:T(8,128)(2,1)}), bf16[32,64,144]{2,1,0:T(8,128)(2,1)}, u32[]{:S(2)}, u32[]{:S(2)}) %all-to-all-start.5) | async-done | bytes 589856 | tf_op jit(solution)/shard_map/all_to_all | solution.py:16
  226.1 1.3 fusion.10
  229.4 35.3 %all_to_all.40 = bf16[16,34,288]{2,1,0:T(8,128)(2,1)S(1)} all-to-all(bf16[16,34,288]{2,1,0:T(8,128)(2,1)S(1)} %pad_maximum_fusion.1), channel_id=1, replica_groups=mesh['dp'=16,'replica'=8,'tensor'=4] {'dp'}, dimensions={0} | all-to-all | bytes 626688 | tf_op jit(solution)/shard_map/all_to_all | solution.py:16
  265.6 6.6 %all-to-all-start.7 = ((bf16[16,34,288]{2,1,0:T(8,128)(2,1)}), bf16[16,34,288]{2,1,0:T(8,128)(2,1)S(1)}, u32[]{:S(2)}, u32[]{:S(2)}) async-start(bf16[16,34,288]{2,1,0:T(8,128)(2,1)} %broadcast_in_dim.24), calls=%async_computation.8 | async-start | bytes 983040 | tf_op jit(solution)/shard_map/all_to_all | solution.py:16
  272.2 8.8 %all-gather = bf16[256,1152]{1,0:T(8,128)(2,1)S(1)} all-gather(bf16[64,1152]{1,0:T(8,128)(2,1)S(1)} %pad_maximum_fusion.2), channel_id=2, replica_groups=mesh['dp'=16,'replica'=8,'tensor'=4] {'tensor'}, dimensions={0}, use_global_device_ids=true | all-gather | bytes 737280 | tf_op jit(solution)/shard_map/all_gather | solution.py:113
  281.0 1.2 convolution_convert_fusion.6
  282.3 1.2 convolution_convert_fusion.7
  283.4 16.3 %all-to-all-done.7 = bf16[16,34,288]{2,1,0:T(8,128)(2,1)S(1)} async-done(((bf16[16,34,288]{2,1,0:T(8,128)(2,1)}), bf16[16,34,288]{2,1,0:T(8,128)(2,1)S(1)}, u32[]{:S(2)}, u32[]{:S(2)}) %all-to-all-start.7) | async-done | bytes 313376 | tf_op jit(solution)/shard_map/all_to_all | solution.py:16
  (50 shorter events, 10.1 us)
Async XLA Ops:
  7.2 1.9 copy-start
  7.2 1.9 copy-start.6
  10.5 12.9 %copy-start.7 = (bf16[128,1152]{1,0:T(8,128)(2,1)S(1)}, bf16[128,1152]{1,0:T(8,128)(2,1)}, u32[]{:S(2)}) copy-start(bf16[128,1152]{1,0:T(8,128)(2,1)} %param.8) | copy-start | bytes 884740
  10.5 12.9 %copy-start.8 = (bf16[128,1152]{1,0:T(8,128)(2,1)S(1)}, bf16[128,1152]{1,0:T(8,128)(2,1)}, u32[]{:S(2)}) copy-start(bf16[128,1152]{1,0:T(8,128)(2,1)} %param.11) | copy-start | bytes 884740
  10.5 12.8 %all-to-all-start = ((bf16[4,64,1152]{2,1,0:T(8,128)(2,1)}), bf16[4,64,1152]{2,1,0:T(8,128)(2,1)S(1)}, u32[]{:S(2)}, u32[]{:S(2)}) async-start(bf16[4,64,1152]{2,1,0:T(8,128)(2,1)} %pad_maximum_fusion), calls=%async_computation | async-start | bytes 1179648 | tf_op jit(solution)/shard_map/all_to_all | solution.py:16
  25.8 43.7 %copy-start.5 = (bf16[128,544]{0,1:T(8,128)(2,1)S(1)}, bf16[128,544]{0,1:T(8,128)(2,1)}, u32[]{:S(2)}) copy-start(bf16[128,544]{0,1:T(8,128)(2,1)} %param.9) | copy-start | bytes 417796
  25.8 43.7 %all-to-all-start.1 = ((bf16[32,32,1152]{2,1,0:T(8,128)(2,1)}), bf16[32,32,1152]{2,1,0:T(8,128)(2,1)}, u32[]{:S(2)}, u32[]{:S(2)}) async-start(bf16[32,32,1152]{2,1,0:T(8,128)(2,1)} %broadcast_in_dim.20), calls=%async_computation.1 | async-start | bytes 4718592 | tf_op jit(solution)/shard_map/all_to_all | solution.py:16
  37.9 75.1 %all-gather.3.cloned.1.call-start = ((), (), s32[]{:S(2)}) async-start(), calls=%async_computation.9 | async-start | bytes 1253376 | tf_op jit(solution)/shard_map/all_gather | solution.py:78
  70.7 42.2 %all-to-all-start.2 = ((bf16[8,128,544]{1,2,0:T(8,128)(2,1)}), bf16[8,128,544]{1,2,0:T(8,128)(2,1)S(1)}, u32[]{:S(2)}, u32[]{:S(2)}) async-start(bf16[8,128,544]{1,2,0:T(8,128)(2,1)} %broadcast_in_dim.21), calls=%async_computation.2 | async-start | bytes 2228224 | tf_op jit(solution)/shard_map/all_to_all | solution.py:16
  113.0 4.3 %copy-start.9 = (bf16[512,1152]{1,0:T(8,128)(2,1)S(1)}, bf16[512,1152]{1,0:T(8,128)(2,1)}, u32[]{:S(2)}) copy-start(bf16[512,1152]{1,0:T(8,128)(2,1)} %all-gather.3.cloned.1.call-done) | copy-start | bytes 3538948
  117.2 3.0 copy-start.4
  120.2 38.9 %all-to-all-start.3 = ((bf16[32,32,1152]{2,1,0:T(8,128)(2,1)}), bf16[32,32,1152]{2,1,0:T(8,128)(2,1)}, u32[]{:S(2)}, u32[]{:S(2)}) async-start(bf16[32,32,1152]{2,1,0:T(8,128)(2,1)} %bitcast.51), calls=%async_computation.4 | async-start | bytes 4718592 | tf_op jit(solution)/shard_map/all_to_all | solution.py:16
  127.6 72.6 %reduce-scatter.2.cloned.1.call-start = ((), (), s32[]{:S(2)}) async-start(), calls=%async_computation.10 | async-start | bytes 1253376 | tf_op jit(solution)/shard_map/reduce_scatter | solution.py:98
  160.3 40.7 %all-to-all-start.4 = ((bf16[8,128,544]{1,2,0:T(8,128)(2,1)}), bf16[8,128,544]{1,2,0:T(8,128)(2,1)}, u32[]{:S(2)}, u32[]{:S(2)}) async-start(bf16[8,128,544]{1,2,0:T(8,128)(2,1)} %broadcast_in_dim.22), calls=%async_computation.5 | async-start | bytes 2228224 | tf_op jit(solution)/shard_map/all_to_all | solution.py:16
  202.9 23.2 %all-to-all-start.5 = ((bf16[32,64,144]{2,1,0:T(8,128)(2,1)}), bf16[32,64,144]{2,1,0:T(8,128)(2,1)}, u32[]{:S(2)}, u32[]{:S(2)}) async-start(bf16[32,64,144]{2,1,0:T(8,128)(2,1)} %bitcast.50), calls=%async_computation.6 | async-start | bytes 2097152 | tf_op jit(solution)/shard_map/all_to_all | solution.py:16
  216.5 10.9 %copy-start.3 = (bf16[16,34,1024]{2,1,0:T(8,128)(2,1)S(1)}, bf16[16,34,1024]{2,1,0:T(8,128)(2,1)}, u32[]{:S(2)}) copy-start(bf16[16,34,1024]{2,1,0:T(8,128)(2,1)} %dot_general.46) | copy-start | bytes 3342340
  227.4 1.3 copy-start.2
  265.6 34.2 %all-to-all-start.7 = ((bf16[16,34,288]{2,1,0:T(8,128)(2,1)}), bf16[16,34,288]{2,1,0:T(8,128)(2,1)S(1)}, u32[]{:S(2)}, u32[]{:S(2)}) async-start(bf16[16,34,288]{2,1,0:T(8,128)(2,1)} %broadcast_in_dim.24), calls=%async_computation.8 | async-start | bytes 983040 | tf_op jit(solution)/shard_map/all_to_all | solution.py:16
  281.0 1.3 copy-start.1
Sparse Core Ops, SparseCore 0:
  41.4 71.5 all-gather.2
  132.4 67.7 reduce-scatter.1

commit v2 on v1

--- a/solution.py
+++ b/solution.py
@@ -23,6 +23,55 @@
 
 def after(x, *others):
     return lax.optimization_barrier((x,) + others)[0]
+
+
+OFFSETS = (0, -4, -8, -12, -1, -5, -9, -13, 1, -3, -7, -11, 2, -2, -6, -10)
+PLACES = tuple([offset % 16 for offset in OFFSETS].index(k) for k in range(16))
+
+
+def shift(x, by):
+    size = lax.axis_size("dp")
+    return lax.ppermute(x, "dp", [(i, (i + by) % size) for i in range(size)])
+
+
+def gather_dp(x):
+    half = x.shape[0] // 16 * 8
+    below = shift(x, 4)
+    above = shift(x, -4)
+    far = jnp.concatenate([shift(above[:half], -4), shift(below[half:], 4)], axis=0)
+    quad = jnp.stack([x, below, far, above])
+    return jnp.concatenate(
+        [quad, shift(quad, 1), shift(quad, -1), shift(quad[0:2], -2), shift(quad[1:3], 2)],
+        axis=0,
+    )
+
+
+def scatter_dp(x):
+    half = x.shape[1] // 16 * 8
+    one = shift(x[4:8], -1)
+    two = shift(x[8:12], 1)
+    three = shift(x[12:14], 2)
+    four = shift(x[14:16], -2)
+    quad = x[0:4].astype(F32) + one.astype(F32) + two.astype(F32)
+    near = quad[0] + three[0].astype(F32)
+    below = quad[1] + three[1].astype(F32) + four[0].astype(F32)
+    far = (quad[2] + four[1].astype(F32)).astype(BF16)
+    above = quad[3]
+    above_half = shift(far[:half], 4).astype(F32)
+    below_half = shift(far[half:], -4).astype(F32)
+    above = jnp.concatenate([above[:half] + above_half, above[half:]], axis=0).astype(BF16)
+    below = jnp.concatenate([below[:half], below[half:] + below_half], axis=0).astype(BF16)
+    return near + shift(above, 4).astype(F32) + shift(below, -4).astype(F32)
+
+
+def chunked(hidden_units, dp, size):
+    rows, hidden = hidden_units.shape
+    chunk = hidden // size
+    slots = -(-chunk // 8) * 8
+    x = hidden_units.T.reshape(size, chunk, rows)
+    x = lax.optimization_barrier(jnp.pad(x, ((0, 0), (0, slots - chunk), (0, 0))))
+    place = (dp + jnp.array(OFFSETS, jnp.int32)) % size
+    return x.at[place].get(mode="promise_in_bounds").reshape(size * slots, rows)
 
 
 def normalize(residual, summed):
@@ -75,64 +124,65 @@
     normed_text, inverse_text = normalize(text_residual, summed[own:])
     normed_image, inverse_image = normalize(image_residual, summed[:own])
 
-    texts = lax.all_gather(normed_text.astype(BF16), "dp", axis=0, tiled=True)
     images = spread(normed_image.astype(BF16), PLANE)
-    hidden_image = spread(after(image_hidden_units, images), "replica")
-    texts, images, hidden_image = lax.optimization_barrier((texts, images, hidden_image))
+    texts = gather_dp(normed_text.astype(BF16))
+    hidden_text = spread(chunked(text_hidden_units, dp, n_dp), "replica")
+    texts, images, hidden_text = lax.optimization_barrier((texts, images, hidden_text))
+    texts = texts.reshape(n_dp * own, width)
     images = images.reshape(members * own, width)
+    hidden_image = spread(after(chunked(image_hidden_units, dp, n_dp), images), "replica")
 
     scale = jnp.exp(log_logit_scale[0])
     logits = scale * dot(images, texts, ((1,), (1,))) + pair_logit_bias[0]
-    image_index = dp * (members * own) + jnp.arange(members * own, dtype=jnp.int32)
+    image_index = jnp.arange(members * own, dtype=jnp.int32)
     position = jnp.arange(n_dp * own, dtype=jnp.int32)
-    text_index = (
-        (position // own) * (members * own)
-        + (replica * n_tensor + tensor) * own
-        + position % own
-    )
+    text_index = jnp.where(position < own, (replica * n_tensor + tensor) * own + position, -1)
     label = jnp.where(image_index[:, None] == text_index[None, :], 1.0, -1.0).astype(F32)
     coefficients = (-label * jax.nn.sigmoid(-label * logits) * scale).astype(BF16)
     text_partial = dot(coefficients, images, ((0,), (0,))).astype(BF16)
-    image_partial = dot(coefficients, texts, ((1,), (0,))).astype(BF16)
-
-    text_grad = lax.psum_scatter(text_partial, "dp", scatter_dimension=0, tiled=True).astype(F32)
+    image_partial = dot(after(coefficients, text_partial), texts, ((1,), (0,))).astype(BF16)
+    image_partial, hidden_image = lax.optimization_barrier((image_partial, hidden_image))
+
+    text_grad = scatter_dp(text_partial.reshape(n_dp, own, width))
     image_parts = exchange(image_partial.reshape(members, own, width), PLANE)
     image_grad = jnp.sum(image_parts.astype(F32), axis=0)
-    hidden_text = spread(after(text_hidden_units, image_parts), "replica")
-    text_grad, image_grad, hidden_text = lax.optimization_barrier(
-        (text_grad, image_grad, hidden_text)
-    )
-
-    upstream = jnp.concatenate(
+
+    upstream_image = retract(normed_image, inverse_image, image_grad)
+    upstream_text = retract(normed_text, inverse_text, text_grad)
+    cut = jnp.concatenate(
         [
-            retract(normed_image, inverse_image, image_grad),
-            retract(normed_text, inverse_text, text_grad),
+            upstream_image.reshape(own, n_replica, columns),
+            upstream_text.reshape(own, n_replica, columns),
         ],
-        axis=0,
-    )
-    group = lax.all_gather(upstream, "tensor", axis=0).reshape(n_tensor, 2, own, width)
+        axis=2,
+    )
+    cut = jnp.transpose(cut, (1, 0, 2))
+    cut = jnp.broadcast_to(cut[:, None], (n_replica, n_tensor, own, 2 * columns))
+    cut = exchange(cut.reshape(members, own, 2 * columns), PLANE)
+    cut = cut.reshape(members * own, 2 * columns)
+    slots = hidden_image.shape[1]
+    hidden_image = jnp.transpose(hidden_image, (1, 0, 2)).reshape(slots, members * own)
+    hidden_text = jnp.transpose(hidden_text, (1, 0, 2)).reshape(slots, members * own)
+    partial = jnp.where(
+        jnp.arange(2 * columns)[None, :] < columns,
+        dot(hidden_image, cut, ((1,), (0,))),
+        dot(hidden_text, cut, ((1,), (0,))),
+    ).astype(BF16)
+    share = scatter_dp(partial.reshape(n_dp, slots // n_dp, 2 * columns)).astype(BF16)
+    total = gather_dp(share)
+
+    group = lax.all_gather(jnp.stack([upstream_image, upstream_text]), "tensor", axis=1)
     hidden_grad_image = dot(
-        group[:, 0].reshape(rows, width), image_output_weight, ((1,), (1,))
+        group[0].reshape(rows, width), image_output_weight, ((1,), (1,))
     ).astype(BF16)
     hidden_grad_text = dot(
-        group[:, 1].reshape(rows, width), text_output_weight, ((1,), (1,))
+        group[1].reshape(rows, width), text_output_weight, ((1,), (1,))
     ).astype(BF16)
 
-    cut = jnp.transpose(upstream.reshape(2 * own, n_replica, columns), (1, 0, 2))
-    cut = jnp.broadcast_to(cut[:, None], (n_replica, n_tensor, 2 * own, columns))
-    cut = exchange(cut.reshape(members, 2 * own, columns), PLANE)
-    cut_image = cut[:, :own].reshape(members * own, columns)
-    cut_text = cut[:, own:].reshape(members * own, columns)
-    partial = jnp.concatenate(
-        [
-            dot(hidden_image.reshape(members * own, hidden), cut_image, ((0,), (0,))),
-            dot(hidden_text.reshape(members * own, hidden), cut_text, ((0,), (0,))),
-        ],
-        axis=1,
-    ).astype(BF16)
-    pieces = exchange(partial.reshape(n_dp, hidden // n_dp, 2 * columns), "dp")
-    share = jnp.sum(pieces.astype(F32), axis=0).astype(BF16)
-    total = spread(share, "dp").reshape(hidden, 2 * columns).astype(F32)
+    place = jnp.array(PLACES, jnp.int32)[(jnp.arange(n_dp, dtype=jnp.int32) - dp) % n_dp]
+    total = lax.optimization_barrier(total).at[place].get(mode="promise_in_bounds")
+    total = total[:, : hidden // n_dp].astype(F32)
+    total = total.reshape(hidden, 2 * columns)
     return (hidden_grad_image, hidden_grad_text, total[:, :columns], total[:, columns:])
 
 

time: 312 us -> 310 us (level)
  starting transfers between devices: 48.2 us -> 180 us
  waiting for transfers between devices: 161 us -> 44.2 us
  blocking collectives: 44 us -> 15.5 us
  between operations: 15.6 us -> 2.94 us
  local copies, waits for them, and re-layouts: 16.8 us -> 27.2 us
  other arithmetic: 5.4 us -> 15.5 us
  matrix products: 17.6 us -> 21.3 us
    ppermute x0 -> x32, starting transfers between devices: none -> 139 us  [shift(): return lax.ppermute(x, 'dp', [(i, (i + by) % size) for i in range(size)])]
    all_to_all x7 -> x6, waiting for transfers between devices: 91.6 us -> 17.1 us  [exchange(): return lax.all_to_all(x, axis, split_axis=0, concat_axis=0, tiled=True)]
    all_gather x1 -> x0, waiting for transfers between devices: 36.1 us -> none  [shards(): texts = lax.all_gather(normed_text.astype(BF16), 'dp', axis=0, tiled=True)]
    all_to_all x1 -> x0, blocking collectives: 35.3 us -> none  [exchange(): return lax.all_to_all(x, axis, split_axis=0, concat_axis=0, tiled=True)]
    reduce_scatter x1 -> x0, waiting for transfers between devices: 32.9 us -> none  [shards(): lax.psum_scatter(text_partial, 'dp', scatter_dimension=0, tiled=True)]
    ppermute x0 -> x32, waiting for transfers between devices: none -> 27.1 us  [shift(): return lax.ppermute(x, 'dp', [(i, (i + by) % size) for i in range(size)])]
    unnamed x22 -> x52, local copies, waits for them, and re-layouts: 2.79 us -> 11.2 us
    all_to_all x7 -> x6, starting transfers between devices: 48.1 us -> 40.6 us  [exchange(): return lax.all_to_all(x, axis, split_axis=0, concat_axis=0, tiled=True)]
  transfers between devices with their start and end apart: 9 -> 38, of which waited for: 7 -> 12; matrix products, arithmetic and copies ran while one was open for 6% -> 11% of each run, Pallas kernels for 0% -> 0%
where the time goes in v2:
time: 310 us; the launch traced here: 307 us
  starting transfers between devices  180 us (58%)
  waiting for transfers between devices  44.2 us (14%)
  local copies, waits for them, and re-layouts  27.2 us (9%)
  matrix products  21.3 us (7%)
  other arithmetic  15.5 us (5%)
  blocking collectives  15.5 us (5%)
    ppermute x32, starting transfers between devices, shift(): return lax.ppermute(x, 'dp', [(i, (i + by) % size) for i in range(size)])  139 us
    all_to_all x6, starting transfers between devices, exchange(): return lax.all_to_all(x, axis, split_axis=0, concat_axis=0, tiled=True)  40.6 us
    ppermute x32, waiting for transfers between devices, shift(): return lax.ppermute(x, 'dp', [(i, (i + by) % size) for i in range(size)])  27.1 us
    dot_general x9, matrix products, dot(): lax.dot_general(a, b, (contract, ((), ())), preferred_element_type=F32)  21.3 us
    all_to_all x6, waiting for transfers between devices, exchange(): return lax.all_to_all(x, axis, split_axis=0, concat_axis=0, tiled=True)  17.1 us
    all_gather x1, blocking collectives, shards(): lax.all_gather(jnp.stack([upstream_image, upstream_text]), 'tensor', axis=1)  15.5 us
    unnamed x52, local copies, waits for them, and re-layouts  11.2 us
  transfers between devices with their start and end apart: 38, of which 12 were waited for; matrix products, arithmetic and copies ran while one was open for 11% of the time, Pallas kernels for 0%

profile of v2, /device:TPU:24, one launch (start us, length us, event | category | flops | bytes accessed | tf_op | source)
XLA Modules:
  0.0 306.7 jit_solution(12807438640997451045)
XLA Ops:
  4.7 4.8 %all-to-all-start = ((bf16[4,64,1152]{2,1,0:T(8,128)(2,1)}), bf16[4,64,1152]{2,1,0:T(8,128)(2,1)S(1)}, u32[]{:S(2)}, u32[]{:S(2)}) async-start(bf16[4,64,1152]{2,1,0:T(8,128)(2,1)} %pad_maximum_fusion), calls=%async_computation | async-start | bytes 1179648 | tf_op jit(solution)/shard_map/all_to_all | solution.py:16
  19.4 9.3 %all-to-all-start.2 = ((bf16[8,640,128]{1,2,0:T(8,128)(2,1)}), bf16[8,640,128]{1,2,0:T(8,128)(2,1)}, u32[]{:S(2)}, u32[]{:S(2)}) async-start(bf16[8,640,128]{1,2,0:T(8,128)(2,1)} %broadcast_in_dim.66), calls=%async_computation.2 | async-start | bytes 2621440 | tf_op jit(solution)/shard_map/all_to_all | solution.py:16
  31.5 9.2 %collective-permute-start.1 = (bf16[32,1152]{1,0:T(8,128)(2,1)S(1)}, bf16[32,1152]{1,0:T(8,128)(2,1)S(1)}, u32[]{:S(2)}, u32[]{:S(2)}) collective-permute-start(bf16[32,1152]{1,0:T(8,128)(2,1)S(1)} %get-tuple-element.33), channel_id=1, source_target_pairs={{0,384},{32,416},{64,448},{96,480},{128,0},{160,32},{192,64},{224,... | collective-permute-start | bytes 221192 | tf_op jit(solution)/shard_map/ppermute | solution.py:34
  45.1 9.7 %collective-permute-start.2 = (bf16[16,1152]{1,0:T(8,128)(2,1)S(1)}, bf16[16,1152]{1,0:T(8,128)(2,1)S(1)}, u32[]{:S(2)}, u32[]{:S(2)}) collective-permute-start(bf16[16,1152]{1,0:T(8,128)(2,1)S(1)} %slice.299), channel_id=1, source_target_pairs={{0,384},{32,416},{64,448},{96,480},{128,0},{160,32},{192,64},{224,... | collective-permute-start | bytes 110600 | tf_op jit(solution)/shard_map/ppermute | solution.py:34
  59.0 7.1 %all-to-all-start.1 = ((bf16[32,32,1152]{2,1,0:T(8,128)(2,1)}), bf16[32,32,1152]{2,1,0:T(8,128)(2,1)}, u32[]{:S(2)}, u32[]{:S(2)}) async-start(bf16[32,32,1152]{2,1,0:T(8,128)(2,1)} %broadcast_in_dim.37), calls=%async_computation.1 | async-start | bytes 4718592 | tf_op jit(solution)/shard_map/all_to_all | solution.py:16
  66.3 6.0 %collective-permute-start.5 = (bf16[4,32,1152]{2,1,0:T(8,128)(2,1)S(1)}, bf16[4,32,1152]{2,1,0:T(8,128)(2,1)S(1)}, u32[]{:S(2)}, u32[]{:S(2)}) collective-permute-start(bf16[4,32,1152]{2,1,0:T(8,128)(2,1)S(1)} %pad_maximum_fusion.1), channel_id=1, source_target_pairs={{0,480},{32,0},{64,32},{96,64},{128,96},{160,128},{192,160},{224,1... | collective-permute-start | bytes 884744 | tf_op jit(solution)/shard_map/ppermute | solution.py:34
  76.2 6.0 %collective-permute-start.6 = (bf16[2,32,1152]{2,1,0:T(8,128)(2,1)S(1)}, bf16[2,32,1152]{2,1,0:T(8,128)(2,1)S(1)}, u32[]{:S(2)}, u32[]{:S(2)}) collective-permute-start(bf16[2,32,1152]{2,1,0:T(8,128)(2,1)S(1)} %get-tuple-element.55), channel_id=1, source_target_pairs={{0,448},{32,480},{64,0},{96,32},{128,64},{160,96},{192,128},{224,1... | collective-permute-start | bytes 442376 | tf_op jit(solution)/shard_map/ppermute | solution.py:34
  83.5 5.0 %collective-permute-done.4 = bf16[4,32,1152]{2,1,0:T(8,128)(2,1)S(1)} collective-permute-done((bf16[4,32,1152]{2,1,0:T(8,128)(2,1)S(1)}, bf16[4,32,1152]{2,1,0:T(8,128)(2,1)S(1)}, u32[]{:S(2)}, u32[]{:S(2)}) %collective-permute-start.4) | collective-permute-done | bytes 294944 | tf_op jit(solution)/shard_map/ppermute | solution.py:34
  91.3 6.4 %all-to-all-done.1 = bf16[32,32,1152]{2,1,0:T(8,128)(2,1)} async-done(((bf16[32,32,1152]{2,1,0:T(8,128)(2,1)}), bf16[32,32,1152]{2,1,0:T(8,128)(2,1)}, u32[]{:S(2)}, u32[]{:S(2)}) %all-to-all-start.1) | async-done | bytes 2359328 | tf_op jit(solution)/shard_map/all_to_all | solution.py:16
  97.7 4.2 %multiply_convert_fusion = bf16[1024,512]{1,0:T(8,128)(2,1)S(1)} fusion(bf16[1024,1152]{1,0:T(8,128)(2,1)} %bitcast.9, bf16[512,1152]{1,0:T(8,128)(2,1)} %bitcast.10, f32[]{:T(128)} %bitcast.142, f32[]{:T(128)} %bitcast, s32[512]{0:T(512)} %add_select_fusion), kind=kOutput, calls=%fused_computation.9 | convolution fusion | flops 1214251008 | bytes 4589576 | tf_op jit(solution)/shard_map/dot_general | solution.py:12
  110.5 4.8 %collective-permute-start.8 = (bf16[4,32,1152]{2,1,0:T(8,128)(2,1)S(1)}, bf16[4,32,1152]{2,1,0:T(8,128)(2,1)}, u32[]{:S(2)}, u32[]{:S(2)}) collective-permute-start(bf16[4,32,1152]{2,1,0:T(8,128)(2,1)S(1)} %bitcast.161), channel_id=1, source_target_pairs={{0,480},{32,0},{64,32},{96,64},{128,96},{160,128},{192,160},{224,1... | collective-permute-start | bytes 884744 | tf_op jit(solution)/shard_map/ppermute | solution.py:34
  116.5 4.9 %all-to-all-start.3 = ((bf16[8,640,128]{1,2,0:T(8,128)(2,1)}), bf16[8,640,128]{1,2,0:T(8,128)(2,1)}, u32[]{:S(2)}, u32[]{:S(2)}) async-start(bf16[8,640,128]{1,2,0:T(8,128)(2,1)} %broadcast_in_dim.68), calls=%async_computation.3 | async-start | bytes 2621440 | tf_op jit(solution)/shard_map/all_to_all | solution.py:16
  121.5 4.6 %convolution_convert_fusion = bf16[1024,1152]{1,0:T(8,128)(2,1)} fusion(bf16[1024,512]{1,0:T(8,128)(2,1)} %copy-done.4, bf16[512,1152]{1,0:T(8,128)(2,1)} %bitcast.10), kind=kOutput, calls=%fused_computation.5 | convolution fusion | flops 1209139200 | bytes 4587520 | tf_op jit(solution)/shard_map/dot_general | solution.py:12
  126.0 4.0 %collective-permute-start.11 = (bf16[2,32,1152]{2,1,0:T(8,128)(2,1)S(1)}, bf16[2,32,1152]{2,1,0:T(8,128)(2,1)S(1)}, u32[]{:S(2)}, u32[]{:S(2)}) collective-permute-start(bf16[2,32,1152]{2,1,0:T(8,128)(2,1)S(1)} %bitcast.167), channel_id=1, source_target_pairs={{0,448},{32,480},{64,0},{96,32},{128,64},{160,96},{192,128},{224,1... | collective-permute-start | bytes 442376 | tf_op jit(solution)/shard_map/ppermute | solution.py:34
  134.8 6.4 %collective-permute-done.10 = bf16[2,32,1152]{2,1,0:T(8,128)(2,1)S(1)} collective-permute-done((bf16[2,32,1152]{2,1,0:T(8,128)(2,1)S(1)}, bf16[2,32,1152]{2,1,0:T(8,128)(2,1)S(1)}, u32[]{:S(2)}, u32[]{:S(2)}) %collective-permute-start.10) | collective-permute-done | bytes 147488 | tf_op jit(solution)/shard_map/ppermute | solution.py:34
  142.5 8.2 %all-to-all-start.4 = ((bf16[32,32,1152]{2,1,0:T(8,128)(2,1)}), bf16[32,32,1152]{2,1,0:T(8,128)(2,1)}, u32[]{:S(2)}, u32[]{:S(2)}) async-start(bf16[32,32,1152]{2,1,0:T(8,128)(2,1)} %bitcast.143), calls=%async_computation.4 | async-start | bytes 4718592 | tf_op jit(solution)/shard_map/all_to_all | solution.py:16
  151.5 4.5 %collective-permute-start.14 = (bf16[16,1152]{1,0:T(8,128)(2,1)S(1)}, bf16[16,1152]{1,0:T(8,128)(2,1)S(1)}, u32[]{:S(2)}, u32[]{:S(2)}) collective-permute-start(bf16[16,1152]{1,0:T(8,128)(2,1)S(1)} %get-tuple-element.53), channel_id=1, source_target_pairs={{0,384},{32,416},{64,448},{96,480},{128,0},{160,32},{192,64},{224,... | collective-permute-start | bytes 110600 | tf_op jit(solution)/shard_map/ppermute | solution.py:34
  156.1 5.2 %collective-permute-start.12 = (bf16[16,1152]{1,0:T(8,128)(2,1)S(1)}, bf16[16,1152]{1,0:T(8,128)(2,1)S(1)}, u32[]{:S(2)}, u32[]{:S(2)}) collective-permute-start(bf16[16,1152]{1,0:T(8,128)(2,1)S(1)} %get-tuple-element.52), channel_id=1, source_target_pairs={{0,128},{32,160},{64,192},{96,224},{128,256},{160,288},{192,320},{... | collective-permute-start | bytes 110600 | tf_op jit(solution)/shard_map/ppermute | solution.py:34
  162.7 5.7 %collective-permute-start.15 = (bf16[32,1152]{1,0:T(8,128)(2,1)}, bf16[32,1152]{1,0:T(8,128)(2,1)}, u32[]{:S(2)}, u32[]{:S(2)}) collective-permute-start(bf16[32,1152]{1,0:T(8,128)(2,1)} %pad_maximum_fusion.7), channel_id=1, source_target_pairs={{0,384},{32,416},{64,448},{96,480},{128,0},{160,32},{192,64},{224,... | collective-permute-start | bytes 221192 | tf_op jit(solution)/shard_map/ppermute | solution.py:34
  169.1 4.1 %collective-permute-start.13 = (bf16[32,1152]{1,0:T(8,128)(2,1)}, bf16[32,1152]{1,0:T(8,128)(2,1)}, u32[]{:S(2)}, u32[]{:S(2)}) collective-permute-start(bf16[32,1152]{1,0:T(8,128)(2,1)} %pad_maximum_fusion.6), channel_id=1, source_target_pairs={{0,128},{32,160},{64,192},{96,224},{128,256},{160,288},{192,320},{... | collective-permute-start | bytes 221192 | tf_op jit(solution)/shard_map/ppermute | solution.py:34
  173.2 9.1 %all-to-all-done.4 = bf16[32,32,1152]{2,1,0:T(8,128)(2,1)} async-done(((bf16[32,32,1152]{2,1,0:T(8,128)(2,1)}), bf16[32,32,1152]{2,1,0:T(8,128)(2,1)}, u32[]{:S(2)}, u32[]{:S(2)}) %all-to-all-start.4) | async-done | bytes 2359328 | tf_op jit(solution)/shard_map/all_to_all | solution.py:16
  188.2 6.3 %all-to-all-start.5 = ((bf16[32,32,288]{2,1,0:T(8,128)(2,1)}), bf16[32,32,288]{2,1,0:T(8,128)(2,1)}, u32[]{:S(2)}, u32[]{:S(2)}) async-start(bf16[32,32,288]{2,1,0:T(8,128)(2,1)} %bitcast.34), calls=%async_computation.5 | async-start | bytes 1572864 | tf_op jit(solution)/shard_map/all_to_all | solution.py:16
  194.6 15.5 %all-gather = bf16[2,128,1152]{2,1,0:T(8,128)(2,1)S(1)} all-gather(bf16[2,32,1152]{2,1,0:T(8,128)(2,1)S(1)} %pad_maximum_fusion.4), channel_id=2, replica_groups=mesh['dp'=16,'replica'=8,'tensor'=4] {'tensor'}, dimensions={1}, use_global_device_ids=true | all-gather | bytes 737280 | tf_op jit(solution)/shard_map/all_gather | solution.py:174
  218.0 4.0 %collective-permute-start.16 = (bf16[4,40,288]{2,1,0:T(8,128)(2,1)S(1)}, bf16[4,40,288]{2,1,0:T(8,128)(2,1)S(1)}, u32[]{:S(2)}, u32[]{:S(2)}) collective-permute-start(bf16[4,40,288]{2,1,0:T(8,128)(2,1)S(1)} %bitcast.168), channel_id=1, source_target_pairs={{0,480},{32,0},{64,32},{96,64},{128,96},{160,128},{192,160},{224,1... | collective-permute-start | bytes 276488 | tf_op jit(solution)/shard_map/ppermute | solution.py:34
  224.7 4.2 %collective-permute-start.18 = (bf16[2,40,288]{2,1,0:T(8,128)(2,1)S(1)}, bf16[2,40,288]{2,1,0:T(8,128)(2,1)S(1)}, u32[]{:S(2)}, u32[]{:S(2)}) collective-permute-start(bf16[2,40,288]{2,1,0:T(8,128)(2,1)S(1)} %bitcast.170), channel_id=1, source_target_pairs={{0,64},{32,96},{64,128},{96,160},{128,192},{160,224},{192,256},{22... | collective-permute-start | bytes 138248 | tf_op jit(solution)/shard_map/ppermute | solution.py:34
  229.2 4.4 %collective-permute-done.18 = bf16[2,40,288]{2,1,0:T(8,128)(2,1)S(1)} collective-permute-done((bf16[2,40,288]{2,1,0:T(8,128)(2,1)S(1)}, bf16[2,40,288]{2,1,0:T(8,128)(2,1)S(1)}, u32[]{:S(2)}, u32[]{:S(2)}) %collective-permute-start.18) | collective-permute-done | bytes 46112 | tf_op jit(solution)/shard_map/ppermute | solution.py:34
  237.4 6.0 %collective-permute-start.22 = (bf16[24,288]{1,0:T(8,128)(2,1)S(1)}, bf16[24,288]{1,0:T(8,128)(2,1)S(1)}, u32[]{:S(2)}, u32[]{:S(2)}) collective-permute-start(bf16[24,288]{1,0:T(8,128)(2,1)S(1)} %slice_bitcast_fusion.10), channel_id=1, source_target_pairs={{0,384},{32,416},{64,448},{96,480},{128,0},{160,32},{192,64},{224,... | collective-permute-start | bytes 41480 | tf_op jit(solution)/shard_map/ppermute | solution.py:34
  247.3 6.0 %collective-permute-start.23 = (bf16[40,288]{1,0:T(8,128)(2,1)S(1)}, bf16[40,288]{1,0:T(8,128)(2,1)S(1)}, u32[]{:S(2)}, u32[]{:S(2)}) collective-permute-start(bf16[40,288]{1,0:T(8,128)(2,1)S(1)} %pad_maximum_fusion.11), channel_id=1, source_target_pairs={{0,384},{32,416},{64,448},{96,480},{128,0},{160,32},{192,64},{224,... | collective-permute-start | bytes 69128 | tf_op jit(solution)/shard_map/ppermute | solution.py:34
  257.6 6.7 %collective-permute-start.25 = (bf16[40,288]{1,0:T(8,128)(2,1)S(1)}, bf16[40,288]{1,0:T(8,128)(2,1)S(1)}, u32[]{:S(2)}, u32[]{:S(2)}) collective-permute-start(bf16[40,288]{1,0:T(8,128)(2,1)S(1)} %get-tuple-element.31), channel_id=1, source_target_pairs={{0,384},{32,416},{64,448},{96,480},{128,0},{160,32},{192,64},{224,... | collective-permute-start | bytes 69128 | tf_op jit(solution)/shard_map/ppermute | solution.py:34
  268.5 6.7 %collective-permute-start.26 = (bf16[16,288]{1,0:T(8,128)(2,1)S(1)}, bf16[16,288]{1,0:T(8,128)(2,1)S(1)}, u32[]{:S(2)}, u32[]{:S(2)}) collective-permute-start(bf16[16,288]{1,0:T(8,128)(2,1)S(1)} %slice.340), channel_id=1, source_target_pairs={{0,384},{32,416},{64,448},{96,480},{128,0},{160,32},{192,64},{224,... | collective-permute-start | bytes 27656 | tf_op jit(solution)/shard_map/ppermute | solution.py:34
  278.9 6.1 %collective-permute-done.27 = bf16[24,288]{1,0:T(8,128)(2,1)S(1)} collective-permute-done((bf16[24,288]{1,0:T(8,128)(2,1)S(1)}, bf16[24,288]{1,0:T(8,128)(2,1)S(1)}, u32[]{:S(2)}, u32[]{:S(2)}) %collective-permute-start.27) | collective-permute-done | bytes 13856 | tf_op jit(solution)/shard_map/ppermute | solution.py:34
  292.9 6.0 %collective-permute-start.30 = (bf16[2,40,288]{2,1,0:T(8,128)(2,1)S(1)}, bf16[2,40,288]{2,1,0:T(8,128)(2,1)S(1)}, u32[]{:S(2)}, u32[]{:S(2)}) collective-permute-start(bf16[2,40,288]{2,1,0:T(8,128)(2,1)S(1)} %get-tuple-element.57), channel_id=1, source_target_pairs={{0,448},{32,480},{64,0},{96,32},{128,64},{160,96},{192,128},{224,1... | collective-permute-start | bytes 138248 | tf_op jit(solution)/shard_map/ppermute | solution.py:34
  (182 shorter events, 102.4 us)
Async XLA Ops:
  4.7 12.7 %all-to-all-start = ((bf16[4,64,1152]{2,1,0:T(8,128)(2,1)}), bf16[4,64,1152]{2,1,0:T(8,128)(2,1)S(1)}, u32[]{:S(2)}, u32[]{:S(2)}) async-start(bf16[4,64,1152]{2,1,0:T(8,128)(2,1)} %pad_maximum_fusion), calls=%async_computation | async-start | bytes 1179648 | tf_op jit(solution)/shard_map/all_to_all | solution.py:16
  19.4 38.0 %all-to-all-start.2 = ((bf16[8,640,128]{1,2,0:T(8,128)(2,1)}), bf16[8,640,128]{1,2,0:T(8,128)(2,1)}, u32[]{:S(2)}, u32[]{:S(2)}) async-start(bf16[8,640,128]{1,2,0:T(8,128)(2,1)} %broadcast_in_dim.66), calls=%async_computation.2 | async-start | bytes 2621440 | tf_op jit(solution)/shard_map/all_to_all | solution.py:16
  31.5 13.6 %collective-permute-start.1 = (bf16[32,1152]{1,0:T(8,128)(2,1)S(1)}, bf16[32,1152]{1,0:T(8,128)(2,1)S(1)}, u32[]{:S(2)}, u32[]{:S(2)}) collective-permute-start(bf16[32,1152]{1,0:T(8,128)(2,1)S(1)} %get-tuple-element.33), channel_id=1, source_target_pairs={{0,384},{32,416},{64,448},{96,480},{128,0},{160,32},{192,64},{224,... | collective-permute-start | bytes 221192 | tf_op jit(solution)/shard_map/ppermute | solution.py:34
  40.7 14.1 %collective-permute-start = (bf16[32,1152]{1,0:T(8,128)(2,1)S(1)}, bf16[32,1152]{1,0:T(8,128)(2,1)S(1)}, u32[]{:S(2)}, u32[]{:S(2)}) collective-permute-start(bf16[32,1152]{1,0:T(8,128)(2,1)S(1)} %get-tuple-element.33), channel_id=1, source_target_pairs={{0,128},{32,160},{64,192},{96,224},{128,256},{160,288},{192,320},{... | collective-permute-start | bytes 221192 | tf_op jit(solution)/shard_map/ppermute | solution.py:34
  45.1 21.0 %collective-permute-start.2 = (bf16[16,1152]{1,0:T(8,128)(2,1)S(1)}, bf16[16,1152]{1,0:T(8,128)(2,1)S(1)}, u32[]{:S(2)}, u32[]{:S(2)}) collective-permute-start(bf16[16,1152]{1,0:T(8,128)(2,1)S(1)} %slice.299), channel_id=1, source_target_pairs={{0,384},{32,416},{64,448},{96,480},{128,0},{160,32},{192,64},{224,... | collective-permute-start | bytes 110600 | tf_op jit(solution)/shard_map/ppermute | solution.py:34
  54.8 11.3 %collective-permute-start.3 = (bf16[16,1152]{1,0:T(8,128)(2,1)S(1)}, bf16[16,1152]{1,0:T(8,128)(2,1)S(1)}, u32[]{:S(2)}, u32[]{:S(2)}) collective-permute-start(bf16[16,1152]{1,0:T(8,128)(2,1)S(1)} %slice.300), channel_id=1, source_target_pairs={{0,128},{32,160},{64,192},{96,224},{128,256},{160,288},{192,320},{... | collective-permute-start | bytes 110600 | tf_op jit(solution)/shard_map/ppermute | solution.py:34
  59.0 38.7 %all-to-all-start.1 = ((bf16[32,32,1152]{2,1,0:T(8,128)(2,1)}), bf16[32,32,1152]{2,1,0:T(8,128)(2,1)}, u32[]{:S(2)}, u32[]{:S(2)}) async-start(bf16[32,32,1152]{2,1,0:T(8,128)(2,1)} %broadcast_in_dim.37), calls=%async_computation.1 | async-start | bytes 4718592 | tf_op jit(solution)/shard_map/all_to_all | solution.py:16
  66.3 22.9 %collective-permute-start.5 = (bf16[4,32,1152]{2,1,0:T(8,128)(2,1)S(1)}, bf16[4,32,1152]{2,1,0:T(8,128)(2,1)S(1)}, u32[]{:S(2)}, u32[]{:S(2)}) collective-permute-start(bf16[4,32,1152]{2,1,0:T(8,128)(2,1)S(1)} %pad_maximum_fusion.1), channel_id=1, source_target_pairs={{0,480},{32,0},{64,32},{96,64},{128,96},{160,128},{192,160},{224,1... | collective-permute-start | bytes 884744 | tf_op jit(solution)/shard_map/ppermute | solution.py:34
  72.3 16.2 %collective-permute-start.4 = (bf16[4,32,1152]{2,1,0:T(8,128)(2,1)S(1)}, bf16[4,32,1152]{2,1,0:T(8,128)(2,1)S(1)}, u32[]{:S(2)}, u32[]{:S(2)}) collective-permute-start(bf16[4,32,1152]{2,1,0:T(8,128)(2,1)S(1)} %pad_maximum_fusion.1), channel_id=1, source_target_pairs={{0,32},{32,64},{64,96},{96,128},{128,160},{160,192},{192,224},{224... | collective-permute-start | bytes 884744 | tf_op jit(solution)/shard_map/ppermute | solution.py:34
  74.3 16.4 %collective-permute-start.7 = (bf16[2,32,1152]{2,1,0:T(8,128)(2,1)S(1)}, bf16[2,32,1152]{2,1,0:T(8,128)(2,1)S(1)}, u32[]{:S(2)}, u32[]{:S(2)}) collective-permute-start(bf16[2,32,1152]{2,1,0:T(8,128)(2,1)S(1)} %get-tuple-element.54), channel_id=1, source_target_pairs={{0,64},{32,96},{64,128},{96,160},{128,192},{160,224},{192,256},{22... | collective-permute-start | bytes 442376 | tf_op jit(solution)/shard_map/ppermute | solution.py:34
  76.2 13.8 %collective-permute-start.6 = (bf16[2,32,1152]{2,1,0:T(8,128)(2,1)S(1)}, bf16[2,32,1152]{2,1,0:T(8,128)(2,1)S(1)}, u32[]{:S(2)}, u32[]{:S(2)}) collective-permute-start(bf16[2,32,1152]{2,1,0:T(8,128)(2,1)S(1)} %get-tuple-element.55), channel_id=1, source_target_pairs={{0,448},{32,480},{64,0},{96,32},{128,64},{160,96},{192,128},{224,1... | collective-permute-start | bytes 442376 | tf_op jit(solution)/shard_map/ppermute | solution.py:34
  107.4 25.4 %collective-permute-start.9 = (bf16[4,32,1152]{2,1,0:T(8,128)(2,1)}, bf16[4,32,1152]{2,1,0:T(8,128)(2,1)S(1)}, u32[]{:S(2)}, u32[]{:S(2)}) collective-permute-start(bf16[4,32,1152]{2,1,0:T(8,128)(2,1)} %bitcast.162), channel_id=1, source_target_pairs={{0,32},{32,64},{64,96},{96,128},{128,160},{160,192},{192,224},{224... | collective-permute-start | bytes 884744 | tf_op jit(solution)/shard_map/ppermute | solution.py:34
  110.5 22.3 %collective-permute-start.8 = (bf16[4,32,1152]{2,1,0:T(8,128)(2,1)S(1)}, bf16[4,32,1152]{2,1,0:T(8,128)(2,1)}, u32[]{:S(2)}, u32[]{:S(2)}) collective-permute-start(bf16[4,32,1152]{2,1,0:T(8,128)(2,1)S(1)} %bitcast.161), channel_id=1, source_target_pairs={{0,480},{32,0},{64,32},{96,64},{128,96},{160,128},{192,160},{224,1... | collective-permute-start | bytes 884744 | tf_op jit(solution)/shard_map/ppermute | solution.py:34
  116.5 26.0 %all-to-all-start.3 = ((bf16[8,640,128]{1,2,0:T(8,128)(2,1)}), bf16[8,640,128]{1,2,0:T(8,128)(2,1)}, u32[]{:S(2)}, u32[]{:S(2)}) async-start(bf16[8,640,128]{1,2,0:T(8,128)(2,1)} %broadcast_in_dim.68), calls=%async_computation.3 | async-start | bytes 2621440 | tf_op jit(solution)/shard_map/all_to_all | solution.py:16
  130.1 11.1 %collective-permute-start.10 = (bf16[2,32,1152]{2,1,0:T(8,128)(2,1)S(1)}, bf16[2,32,1152]{2,1,0:T(8,128)(2,1)S(1)}, u32[]{:S(2)}, u32[]{:S(2)}) collective-permute-start(bf16[2,32,1152]{2,1,0:T(8,128)(2,1)S(1)} %bitcast.166), channel_id=1, source_target_pairs={{0,64},{32,96},{64,128},{96,160},{128,192},{160,224},{192,256},{22... | collective-permute-start | bytes 442376 | tf_op jit(solution)/shard_map/ppermute | solution.py:34
  142.5 39.8 %all-to-all-start.4 = ((bf16[32,32,1152]{2,1,0:T(8,128)(2,1)}), bf16[32,32,1152]{2,1,0:T(8,128)(2,1)}, u32[]{:S(2)}, u32[]{:S(2)}) async-start(bf16[32,32,1152]{2,1,0:T(8,128)(2,1)} %bitcast.143), calls=%async_computation.4 | async-start | bytes 4718592 | tf_op jit(solution)/shard_map/all_to_all | solution.py:16
  151.5 10.5 %collective-permute-start.14 = (bf16[16,1152]{1,0:T(8,128)(2,1)S(1)}, bf16[16,1152]{1,0:T(8,128)(2,1)S(1)}, u32[]{:S(2)}, u32[]{:S(2)}) collective-permute-start(bf16[16,1152]{1,0:T(8,128)(2,1)S(1)} %get-tuple-element.53), channel_id=1, source_target_pairs={{0,384},{32,416},{64,448},{96,480},{128,0},{160,32},{192,64},{224,... | collective-permute-start | bytes 110600 | tf_op jit(solution)/shard_map/ppermute | solution.py:34
  156.1 12.3 %collective-permute-start.12 = (bf16[16,1152]{1,0:T(8,128)(2,1)S(1)}, bf16[16,1152]{1,0:T(8,128)(2,1)S(1)}, u32[]{:S(2)}, u32[]{:S(2)}) collective-permute-start(bf16[16,1152]{1,0:T(8,128)(2,1)S(1)} %get-tuple-element.52), channel_id=1, source_target_pairs={{0,128},{32,160},{64,192},{96,224},{128,256},{160,288},{192,320},{... | collective-permute-start | bytes 110600 | tf_op jit(solution)/shard_map/ppermute | solution.py:34
  162.7 21.7 %collective-permute-start.15 = (bf16[32,1152]{1,0:T(8,128)(2,1)}, bf16[32,1152]{1,0:T(8,128)(2,1)}, u32[]{:S(2)}, u32[]{:S(2)}) collective-permute-start(bf16[32,1152]{1,0:T(8,128)(2,1)} %pad_maximum_fusion.7), channel_id=1, source_target_pairs={{0,384},{32,416},{64,448},{96,480},{128,0},{160,32},{192,64},{224,... | collective-permute-start | bytes 221192 | tf_op jit(solution)/shard_map/ppermute | solution.py:34
  169.1 15.3 %collective-permute-start.13 = (bf16[32,1152]{1,0:T(8,128)(2,1)}, bf16[32,1152]{1,0:T(8,128)(2,1)}, u32[]{:S(2)}, u32[]{:S(2)}) collective-permute-start(bf16[32,1152]{1,0:T(8,128)(2,1)} %pad_maximum_fusion.6), channel_id=1, source_target_pairs={{0,128},{32,160},{64,192},{96,224},{128,256},{160,288},{192,320},{... | collective-permute-start | bytes 221192 | tf_op jit(solution)/shard_map/ppermute | solution.py:34
  188.2 21.9 %all-to-all-start.5 = ((bf16[32,32,288]{2,1,0:T(8,128)(2,1)}), bf16[32,32,288]{2,1,0:T(8,128)(2,1)}, u32[]{:S(2)}, u32[]{:S(2)}) async-start(bf16[32,32,288]{2,1,0:T(8,128)(2,1)} %bitcast.34), calls=%async_computation.5 | async-start | bytes 1572864 | tf_op jit(solution)/shard_map/all_to_all | solution.py:16
  215.0 13.9 %collective-permute-start.17 = (bf16[4,40,288]{2,1,0:T(8,128)(2,1)S(1)}, bf16[4,40,288]{2,1,0:T(8,128)(2,1)S(1)}, u32[]{:S(2)}, u32[]{:S(2)}) collective-permute-start(bf16[4,40,288]{2,1,0:T(8,128)(2,1)S(1)} %bitcast.169), channel_id=1, source_target_pairs={{0,32},{32,64},{64,96},{96,128},{128,160},{160,192},{192,224},{224... | collective-permute-start | bytes 276488 | tf_op jit(solution)/shard_map/ppermute | solution.py:34
  218.0 10.8 %collective-permute-start.16 = (bf16[4,40,288]{2,1,0:T(8,128)(2,1)S(1)}, bf16[4,40,288]{2,1,0:T(8,128)(2,1)S(1)}, u32[]{:S(2)}, u32[]{:S(2)}) collective-permute-start(bf16[4,40,288]{2,1,0:T(8,128)(2,1)S(1)} %bitcast.168), channel_id=1, source_target_pairs={{0,480},{32,0},{64,32},{96,64},{128,96},{160,128},{192,160},{224,1... | collective-permute-start | bytes 276488 | tf_op jit(solution)/shard_map/ppermute | solution.py:34
  233.7 9.8 %collective-permute-start.20 = (bf16[16,288]{1,0:T(8,128)(2,1)S(1)}, bf16[16,288]{1,0:T(8,128)(2,1)S(1)}, u32[]{:S(2)}, u32[]{:S(2)}) collective-permute-start(bf16[16,288]{1,0:T(8,128)(2,1)S(1)} %slice_bitcast_fusion.11), channel_id=1, source_target_pairs={{0,128},{32,160},{64,192},{96,224},{128,256},{160,288},{192,320},{... | collective-permute-start | bytes 27656 | tf_op jit(solution)/shard_map/ppermute | solution.py:34
  237.4 9.8 %collective-permute-start.22 = (bf16[24,288]{1,0:T(8,128)(2,1)S(1)}, bf16[24,288]{1,0:T(8,128)(2,1)S(1)}, u32[]{:S(2)}, u32[]{:S(2)}) collective-permute-start(bf16[24,288]{1,0:T(8,128)(2,1)S(1)} %slice_bitcast_fusion.10), channel_id=1, source_target_pairs={{0,384},{32,416},{64,448},{96,480},{128,0},{160,32},{192,64},{224,... | collective-permute-start | bytes 41480 | tf_op jit(solution)/shard_map/ppermute | solution.py:34
  243.5 11.0 %collective-permute-start.21 = (bf16[40,288]{1,0:T(8,128)(2,1)S(1)}, bf16[40,288]{1,0:T(8,128)(2,1)S(1)}, u32[]{:S(2)}, u32[]{:S(2)}) collective-permute-start(bf16[40,288]{1,0:T(8,128)(2,1)S(1)} %pad_maximum_fusion.10), channel_id=1, source_target_pairs={{0,128},{32,160},{64,192},{96,224},{128,256},{160,288},{192,320},{... | collective-permute-start | bytes 69128 | tf_op jit(solution)/shard_map/ppermute | solution.py:34
  257.6 10.9 %collective-permute-start.25 = (bf16[40,288]{1,0:T(8,128)(2,1)S(1)}, bf16[40,288]{1,0:T(8,128)(2,1)S(1)}, u32[]{:S(2)}, u32[]{:S(2)}) collective-permute-start(bf16[40,288]{1,0:T(8,128)(2,1)S(1)} %get-tuple-element.31), channel_id=1, source_target_pairs={{0,384},{32,416},{64,448},{96,480},{128,0},{160,32},{192,64},{224,... | collective-permute-start | bytes 69128 | tf_op jit(solution)/shard_map/ppermute | solution.py:34
  264.3 10.9 %collective-permute-start.24 = (bf16[40,288]{1,0:T(8,128)(2,1)S(1)}, bf16[40,288]{1,0:T(8,128)(2,1)S(1)}, u32[]{:S(2)}, u32[]{:S(2)}) collective-permute-start(bf16[40,288]{1,0:T(8,128)(2,1)S(1)} %get-tuple-element.31), channel_id=1, source_target_pairs={{0,128},{32,160},{64,192},{96,224},{128,256},{160,288},{192,320},{... | collective-permute-start | bytes 69128 | tf_op jit(solution)/shard_map/ppermute | solution.py:34
  268.5 10.4 %collective-permute-start.26 = (bf16[16,288]{1,0:T(8,128)(2,1)S(1)}, bf16[16,288]{1,0:T(8,128)(2,1)S(1)}, u32[]{:S(2)}, u32[]{:S(2)}) collective-permute-start(bf16[16,288]{1,0:T(8,128)(2,1)S(1)} %slice.340), channel_id=1, source_target_pairs={{0,384},{32,416},{64,448},{96,480},{128,0},{160,32},{192,64},{224,... | collective-permute-start | bytes 27656 | tf_op jit(solution)/shard_map/ppermute | solution.py:34
  285.1 15.7 %collective-permute-start.29 = (bf16[4,40,288]{2,1,0:T(8,128)(2,1)S(1)}, bf16[4,40,288]{2,1,0:T(8,128)(2,1)S(1)}, u32[]{:S(2)}, u32[]{:S(2)}) collective-permute-start(bf16[4,40,288]{2,1,0:T(8,128)(2,1)S(1)} %pad_maximum_fusion.5), channel_id=1, source_target_pairs={{0,480},{32,0},{64,32},{96,64},{128,96},{160,128},{192,160},{224,1... | collective-permute-start | bytes 276488 | tf_op jit(solution)/shard_map/ppermute | solution.py:34
  287.0 13.1 %collective-permute-start.28 = (bf16[4,40,288]{2,1,0:T(8,128)(2,1)S(1)}, bf16[4,40,288]{2,1,0:T(8,128)(2,1)S(1)}, u32[]{:S(2)}, u32[]{:S(2)}) collective-permute-start(bf16[4,40,288]{2,1,0:T(8,128)(2,1)S(1)} %pad_maximum_fusion.5), channel_id=1, source_target_pairs={{0,32},{32,64},{64,96},{96,128},{128,160},{160,192},{192,224},{224... | collective-permute-start | bytes 276488 | tf_op jit(solution)/shard_map/ppermute | solution.py:34
  291.0 11.2 %collective-permute-start.31 = (bf16[2,40,288]{2,1,0:T(8,128)(2,1)S(1)}, bf16[2,40,288]{2,1,0:T(8,128)(2,1)S(1)}, u32[]{:S(2)}, u32[]{:S(2)}) collective-permute-start(bf16[2,40,288]{2,1,0:T(8,128)(2,1)S(1)} %get-tuple-element.56), channel_id=1, source_target_pairs={{0,64},{32,96},{64,128},{96,160},{128,192},{160,224},{192,256},{22... | collective-permute-start | bytes 138248 | tf_op jit(solution)/shard_map/ppermute | solution.py:34
  (26 other events, 177.6 us)

commit v3 on v2

v3 whole, which is shorter than its diff:
```python
import math

import jax
import jax.numpy as jnp
from jax import lax
from jax.sharding import Mesh
from jax.sharding import PartitionSpec as P

F32 = jnp.float32
BF16 = jnp.bfloat16
PLANE = ("replica", "tensor")


def dot(a, b, contract):
    return lax.dot_general(a, b, (contract, ((), ())), preferred_element_type=F32)


def exchange(x, axis):
    return lax.all_to_all(x, axis, split_axis=0, concat_axis=0, tiled=True)


def spread(x, axis):
    size = lax.axis_size(axis)
    return exchange(jnp.broadcast_to(x[None], (size,) + x.shape), axis)


def after(x, *others):
    return lax.optimization_barrier((x,) + others)[0]


def gather_dp(x):
    runs = lax.all_gather(x, "run", axis=0)
    return spread(runs, "place")


def scatter_dp(x):
    runs = jnp.sum(exchange(x, "place").astype(F32), axis=0).astype(BF16)
    return jnp.sum(exchange(runs, "run").astype(F32), axis=0)


def chunked(hidden_units, size):
    rows, hidden = hidden_units.shape
    chunk = hidden // size
    slots = -(-chunk // 8) * 8
    x = hidden_units.T.reshape(size, chunk, rows)
    return jnp.pad(x, ((0, 0), (0, slots - chunk), (0, 0))).reshape(size * slots, rows)


def normalize(residual, summed):
    combined = residual.astype(F32) + summed
    inverse = lax.rsqrt(jnp.sum(combined * combined, axis=1, keepdims=True) + 1e-06)
    return (combined * inverse, inverse)


def retract(normed, inverse, gradient):
    projection = jnp.sum(normed * gradient, axis=1, keepdims=True)
    return ((gradient - normed * projection) * inverse).astype(BF16)


def shards(
    image_residual_input,
    image_hidden_units,
    image_output_weight,
    text_residual_input,
    text_hidden_units,
    text_output_weight,
    log_logit_scale,
    pair_logit_bias,
):
    rows, width = image_residual_input.shape
    hidden = image_hidden_units.shape[1]
    n_run = lax.axis_size("run")
    n_place = lax.axis_size("place")
    n_dp = n_run * n_place
    n_replica = lax.axis_size("replica")
    n_tensor = lax.axis_size("tensor")
    run = lax.axis_index("run")
    place = lax.axis_index("place")
    replica = lax.axis_index("replica")
    tensor = lax.axis_index("tensor")
    own = rows // n_tensor
    members = n_replica * n_tensor
    columns = width // n_replica

    terms = jnp.concatenate(
        [
            dot(image_hidden_units, image_output_weight, ((1,), (0,)))
            .astype(BF16)
            .reshape(n_tensor, own, width),
            dot(text_hidden_units, text_output_weight, ((1,), (0,)))
            .astype(BF16)
            .reshape(n_tensor, own, width),
        ],
        axis=1,
    )
    summed = jnp.sum(exchange(terms, "tensor").astype(F32), axis=0)
    image_residual = lax.dynamic_slice_in_dim(image_residual_input, tensor * own, own, 0)
    text_residual = lax.dynamic_slice_in_dim(text_residual_input, tensor * own, own, 0)
    normed_text, inverse_text = normalize(text_residual, summed[own:])
    normed_image, inverse_image = normalize(image_residual, summed[:own])

    images = spread(normed_image.astype(BF16), PLANE)
    texts = gather_dp(normed_text.astype(BF16))
    texts, images = lax.optimization_barrier((texts, images))
    texts = texts.reshape(n_dp * own, width)
    images = images.reshape(members * own, width)

    scale = jnp.exp(log_logit_scale[0])
    logits = scale * dot(images, texts, ((1,), (1,))) + pair_logit_bias[0]
    image_index = jnp.arange(members * own, dtype=jnp.int32)
    position = jnp.arange(n_dp * own, dtype=jnp.int32)
    text_index = jnp.where(
        position // own == place * n_run + run,
        (replica * n_tensor + tensor) * own + position % own,
        -1,
    )
    label = jnp.where(image_index[:, None] == text_index[None, :], 1.0, -1.0).astype(F32)
    coefficients = (-label * jax.nn.sigmoid(-label * logits) * scale).astype(BF16)
    text_partial = dot(coefficients, images, ((0,), (0,))).astype(BF16)
    hidden_units = jnp.concatenate(
        [chunked(image_hidden_units, n_dp), chunked(text_hidden_units, n_dp)], axis=0
    )
    text_partial, coefficients, hidden_units = lax.optimization_barrier(
        (text_partial, coefficients, hidden_units)
    )
    text_grad = scatter_dp(text_partial.reshape(n_place, n_run, own, width))
    image_partial = dot(coefficients, texts, ((1,), (0,))).astype(BF16)
    image_parts = exchange(image_partial.reshape(members, own, width), PLANE)
    image_grad = jnp.sum(image_parts.astype(F32), axis=0)
    hidden_units = spread(hidden_units, "replica")
    text_grad, image_grad, hidden_units = lax.optimization_barrier(
        (text_grad, image_grad, hidden_units)
    )

    upstream_image = retract(normed_image, inverse_image, image_grad)
    upstream_text = retract(normed_text, inverse_text, text_grad)
    cut = jnp.concatenate(
        [
            upstream_image.reshape(own, n_replica, columns),
            upstream_text.reshape(own, n_replica, columns),
        ],
        axis=2,
    )
    cut = jnp.transpose(cut, (1, 0, 2))
    cut = jnp.broadcast_to(cut[:, None], (n_replica, n_tensor, own, 2 * columns))
    cut = exchange(cut.reshape(members, own, 2 * columns), PLANE)
    cut = cut.reshape(members * own, 2 * columns)
    slots = hidden_units.shape[1] // 2
    hidden_units = jnp.transpose(hidden_units, (1, 0, 2)).reshape(2 * slots, members * own)
    partial = dot(hidden_units, cut, ((1,), (0,)))
    partial = jnp.where(
        jnp.arange(2 * columns)[None, :] < columns, partial[:slots], partial[slots:]
    ).astype(BF16)
    partial = partial.reshape(n_place, n_run, slots // n_dp, 2 * columns)
    share = scatter_dp(partial).astype(BF16)
    total = gather_dp(share).reshape(n_dp, slots // n_dp, 2 * columns)
    total = total[:, : hidden // n_dp].astype(F32).reshape(hidden, 2 * columns)

    group = after(jnp.stack([upstream_image, upstream_text]), cut)
    group = lax.all_gather(group, "tensor", axis=1)
    hidden_grad_image = dot(
        group[0].reshape(rows, width), image_output_weight, ((1,), (1,))
    ).astype(BF16)
    hidden_grad_text = dot(
        group[1].reshape(rows, width), text_output_weight, ((1,), (1,))
    ).astype(BF16)

    return (hidden_grad_image, hidden_grad_text, total[:, :columns], total[:, columns:])


def solution(mesh):
    n_dp, n_replica, n_tensor = mesh.devices.shape
    n_run = math.isqrt(n_dp)
    mesh = Mesh(
        mesh.devices.reshape(n_run, n_dp // n_run, n_replica, n_tensor),
        ("run", "place", "replica", "tensor"),
    )
    rows = ("run", "place", "replica")
    in_specs = (
        P(rows, None),
        P(rows, "tensor"),
        P("tensor", None),
        P(rows, None),
        P(rows, "tensor"),
        P("tensor", None),
        P(),
        P(),
    )
    out_specs = (
        P(rows, "tensor"),
        P(rows, "tensor"),
        P("tensor", "replica"),
        P("tensor", "replica"),
    )
    return jax.shard_map(shards, mesh=mesh, in_specs=in_specs, out_specs=out_specs, check_vma=False)
```

time: 310 us -> 351 us (1.13)
  starting transfers between devices: 180 us -> 62.7 us
  waiting for transfers between devices: 44.2 us -> 150 us
  blocking collectives: 15.5 us -> 91.8 us
  local copies, waits for them, and re-layouts: 27.2 us -> 11.2 us
  other arithmetic: 15.5 us -> 5.07 us
    ppermute x32 -> x0, starting transfers between devices: 139 us -> none  [shift(): return lax.ppermute(x, 'dp', [(i, (i + by) % size) for i in range(size)])]
    all_to_all x6 -> x9, waiting for transfers between devices: 17.1 us -> 150 us  [exchange(): return lax.all_to_all(x, axis, split_axis=0, concat_axis=0, tiled=True)]
    all_to_all x0 -> x2, blocking collectives: none -> 41.8 us  [exchange(): return lax.all_to_all(x, axis, split_axis=0, concat_axis=0, tiled=True)]
    all_gather x1 -> x3, blocking collectives: 15.5 us -> 50 us  [the longest x2 41.7 us: gather_dp(): runs = lax.all_gather(x, 'run', axis=0)]
    ppermute x32 -> x0, waiting for transfers between devices: 27.1 us -> none  [shift(): return lax.ppermute(x, 'dp', [(i, (i + by) % size) for i in range(size)])]
    all_to_all x6 -> x9, starting transfers between devices: 40.6 us -> 62.7 us  [exchange(): return lax.all_to_all(x, axis, split_axis=0, concat_axis=0, tiled=True)]
    unnamed x52 -> x22, local copies, waits for them, and re-layouts: 11.2 us -> 2.99 us
    gather x4 -> x0, local copies, waits for them, and re-layouts: 3.51 us -> none  [the longest x1 1.68 us: shards(): lax.optimization_barrier(total).at[place].get(mode='promise_in_bounds')]
  transfers between devices with their start and end apart: 38 -> 9, of which waited for: 12 -> 8; matrix products, arithmetic and copies ran while one was open for 11% -> 3% of each run, Pallas kernels for 0% -> 0%
where the time goes in v3:
time: 351 us; the launch traced here: 345 us
  waiting for transfers between devices  150 us (43%)
  blocking collectives  91.8 us (26%)
  starting transfers between devices  62.7 us (18%)
  matrix products  21.8 us (6%)
  local copies, waits for them, and re-layouts  11.2 us (3%)
  other arithmetic  5.07 us (1%)
    all_to_all x9, waiting for transfers between devices, exchange(): return lax.all_to_all(x, axis, split_axis=0, concat_axis=0, tiled=True)  150 us
    all_to_all x9, starting transfers between devices, exchange(): return lax.all_to_all(x, axis, split_axis=0, concat_axis=0, tiled=True)  62.7 us
    all_to_all x2, blocking collectives, exchange(): return lax.all_to_all(x, axis, split_axis=0, concat_axis=0, tiled=True)  41.8 us
    all_gather x2, blocking collectives, gather_dp(): runs = lax.all_gather(x, 'run', axis=0)  41.7 us
    dot_general x8, matrix products, dot(): lax.dot_general(a, b, (contract, ((), ())), preferred_element_type=F32)  21.8 us
    all_gather x1, blocking collectives, shards(): group = lax.all_gather(group, 'tensor', axis=1)  8.29 us
  transfers between devices with their start and end apart: 9, of which 8 were waited for; matrix products, arithmetic and copies ran while one was open for 3% of the time, Pallas kernels for 0%

profile of v3, /device:TPU:24, one launch (start us, length us, event | category | flops | bytes accessed | tf_op | source)
XLA Modules:
  0.0 345.4 jit_solution(10714957774693737679)
XLA Ops:
  0.6 1.9 convolution_convert_fusion.2
  2.6 1.4 convolution_convert_fusion.3
  4.9 4.8 %all-to-all-start = ((bf16[4,64,1152]{2,1,0:T(8,128)(2,1)}), bf16[4,64,1152]{2,1,0:T(8,128)(2,1)S(1)}, u32[]{:S(2)}, u32[]{:S(2)}) async-start(bf16[4,64,1152]{2,1,0:T(8,128)(2,1)} %pad_maximum_fusion), calls=%async_computation | async-start | bytes 1179648 | tf_op jit(solution)/shard_map/all_to_all | solution.py:19
  9.7 7.9 %all-to-all-done = bf16[4,64,1152]{2,1,0:T(8,128)(2,1)S(1)} async-done(((bf16[4,64,1152]{2,1,0:T(8,128)(2,1)}), bf16[4,64,1152]{2,1,0:T(8,128)(2,1)S(1)}, u32[]{:S(2)}, u32[]{:S(2)}) %all-to-all-start) | async-done | bytes 589856 | tf_op jit(solution)/shard_map/all_to_all | solution.py:19
  17.9 1.6 broadcast_in_dim.28
  19.5 11.9 %all-to-all-start.2 = ((bf16[32,32,1152]{2,1,0:T(8,128)(2,1)}), bf16[32,32,1152]{2,1,0:T(8,128)(2,1)}, u32[]{:S(2)}, u32[]{:S(2)}) async-start(bf16[32,32,1152]{2,1,0:T(8,128)(2,1)} %broadcast_in_dim.28), calls=%async_computation.2 | async-start | bytes 4718592 | tf_op jit(solution)/shard_map/all_to_all | solution.py:19
  31.5 24.0 %all-gather = bf16[128,1152]{1,0:T(8,128)(2,1)S(1)} all-gather(bf16[32,1152]{1,0:T(8,128)(2,1)S(1)} %get-tuple-element.39), channel_id=2, replica_groups=mesh['run'=4,'place'=4,'replica'=8,'tensor'=4] {'run'}, dimensions={0}, use_global_device_ids=true | all-gather | bytes 368640 | tf_op jit(solution)/shard_map/all_gather | solution.py:32
  55.5 7.6 %all-to-all-done.2 = bf16[32,32,1152]{2,1,0:T(8,128)(2,1)} async-done(((bf16[32,32,1152]{2,1,0:T(8,128)(2,1)}), bf16[32,32,1152]{2,1,0:T(8,128)(2,1)}, u32[]{:S(2)}, u32[]{:S(2)}) %all-to-all-start.2) | async-done | bytes 2359328 | tf_op jit(solution)/shard_map/all_to_all | solution.py:19
  64.2 3.5 %all-to-all-start.1 = ((bf16[4,4,32,1152]{3,2,1,0:T(8,128)(2,1)}), bf16[4,4,32,1152]{3,2,1,0:T(8,128)(2,1)S(1)}, u32[]{:S(2)}, u32[]{:S(2)}) async-start(bf16[4,4,32,1152]{3,2,1,0:T(8,128)(2,1)} %broadcast_in_dim.27), calls=%async_computation.1 | async-start | bytes 2359296 | tf_op jit(solution)/shard_map/all_to_all | solution.py:19
  69.3 25.2 %all-to-all-done.1 = bf16[4,4,32,1152]{3,2,1,0:T(8,128)(2,1)S(1)} async-done(((bf16[4,4,32,1152]{3,2,1,0:T(8,128)(2,1)}), bf16[4,4,32,1152]{3,2,1,0:T(8,128)(2,1)S(1)}, u32[]{:S(2)}, u32[]{:S(2)}) %all-to-all-start.1) | async-done | bytes 1179680 | tf_op jit(solution)/shard_map/all_to_all | solution.py:19
  94.5 4.3 %multiply_convert_fusion = bf16[1024,512]{1,0:T(8,128)(2,1)S(1)} fusion(bf16[1024,1152]{1,0:T(8,128)(2,1)} %bitcast.4, bf16[512,1152]{1,0:T(8,128)(2,1)S(1)} %bitcast.49, f32[]{:T(128)} %bitcast.45, f32[]{:T(128)} %bitcast, s32[512]{0:T(512)S(1)} %fusion.7), kind=kOutput, calls=%fused_computation.5 | convolution fusion | flops 1214251008 | bytes 4589576 | tf_op jit(solution)/shard_map/dot_general | solution.py:15
  98.8 4.6 %convolution_convert_fusion.1 = bf16[512,1152]{1,0:T(8,128)(2,1)} fusion(bf16[1024,512]{1,0:T(8,128)(2,1)S(1)} %multiply_convert_fusion, bf16[1024,1152]{1,0:T(8,128)(2,1)} %bitcast.4), kind=kOutput, calls=%fused_computation.2 | convolution fusion | flops 1208549376 | bytes 4587520 | tf_op jit(solution)/shard_map/dot_general | solution.py:15
  103.5 3.5 %all-to-all-start.3 = ((bf16[4,4,32,1152]{3,2,1,0:T(8,128)(2,1)}), bf16[4,4,32,1152]{3,2,1,0:T(8,128)(2,1)S(1)}, u32[]{:S(2)}, u32[]{:S(2)}) async-start(bf16[4,4,32,1152]{3,2,1,0:T(8,128)(2,1)} %bitcast.11), calls=%async_computation.3 | async-start | bytes 2359296 | tf_op jit(solution)/shard_map/all_to_all | solution.py:19
  107.0 4.5 %convolution_convert_fusion = bf16[1024,1152]{1,0:T(8,128)(2,1)} fusion(bf16[1024,512]{1,0:T(8,128)(2,1)} %copy-done.3, bf16[512,1152]{1,0:T(8,128)(2,1)} %bitcast.50), kind=kOutput, calls=%fused_computation.1 | convolution fusion | flops 1209139200 | bytes 4587520 | tf_op jit(solution)/shard_map/dot_general | solution.py:15
  111.5 23.4 %all-to-all-done.3 = bf16[4,4,32,1152]{3,2,1,0:T(8,128)(2,1)S(1)} async-done(((bf16[4,4,32,1152]{3,2,1,0:T(8,128)(2,1)}), bf16[4,4,32,1152]{3,2,1,0:T(8,128)(2,1)S(1)}, u32[]{:S(2)}, u32[]{:S(2)}) %all-to-all-start.3) | async-done | bytes 1179680 | tf_op jit(solution)/shard_map/all_to_all | solution.py:19
  135.0 8.9 %all-to-all-start.5 = ((bf16[32,32,1152]{2,1,0:T(8,128)(2,1)}), bf16[32,32,1152]{2,1,0:T(8,128)(2,1)}, u32[]{:S(2)}, u32[]{:S(2)}) async-start(bf16[32,32,1152]{2,1,0:T(8,128)(2,1)} %bitcast.46), calls=%async_computation.5 | async-start | bytes 4718592 | tf_op jit(solution)/shard_map/all_to_all | solution.py:19
  144.9 30.7 %all-to-all-done.5 = bf16[32,32,1152]{2,1,0:T(8,128)(2,1)} async-done(((bf16[32,32,1152]{2,1,0:T(8,128)(2,1)}), bf16[32,32,1152]{2,1,0:T(8,128)(2,1)}, u32[]{:S(2)}, u32[]{:S(2)}) %all-to-all-start.5) | async-done | bytes 2359328 | tf_op jit(solution)/shard_map/all_to_all | solution.py:19
  175.6 11.0 %all-to-all-start.4 = ((bf16[4,32,1152]{2,1,0:T(8,128)(2,1)}), bf16[4,32,1152]{2,1,0:T(8,128)(2,1)S(1)}, u32[]{:S(2)}, u32[]{:S(2)}) async-start(bf16[4,32,1152]{2,1,0:T(8,128)(2,1)} %reduce_sum.102), calls=%async_computation.4 | async-start | bytes 589824 | tf_op jit(solution)/shard_map/all_to_all | solution.py:19
  186.8 18.8 %all-to-all-done.4 = bf16[4,32,1152]{2,1,0:T(8,128)(2,1)S(1)} async-done(((bf16[4,32,1152]{2,1,0:T(8,128)(2,1)}), bf16[4,32,1152]{2,1,0:T(8,128)(2,1)S(1)}, u32[]{:S(2)}, u32[]{:S(2)}) %all-to-all-start.4) | async-done | bytes 294944 | tf_op jit(solution)/shard_map/all_to_all | solution.py:19
  205.6 1.7 broadcast_in_dim.29
  207.2 6.1 %all-to-all-start.6 = ((bf16[8,1280,128]{1,2,0:T(8,128)(2,1)}), bf16[8,1280,128]{1,2,0:T(8,128)(2,1)}, u32[]{:S(2)}, u32[]{:S(2)}) async-start(bf16[8,1280,128]{1,2,0:T(8,128)(2,1)} %broadcast_in_dim.29), calls=%async_computation.6 | async-start | bytes 5242880 | tf_op jit(solution)/shard_map/all_to_all | solution.py:19
  213.3 2.1 convert_reduce_fusion
  215.5 23.9 %all-to-all-done.6 = bf16[8,1280,128]{1,2,0:T(8,128)(2,1)} async-done(((bf16[8,1280,128]{1,2,0:T(8,128)(2,1)}), bf16[8,1280,128]{1,2,0:T(8,128)(2,1)}, u32[]{:S(2)}, u32[]{:S(2)}) %all-to-all-start.6) | async-done | bytes 2621472 | tf_op jit(solution)/shard_map/all_to_all | solution.py:19
  241.3 9.3 %all-to-all-start.7 = ((bf16[32,32,288]{2,1,0:T(8,128)(2,1)}), bf16[32,32,288]{2,1,0:T(8,128)(2,1)S(1)}, u32[]{:S(2)}, u32[]{:S(2)}) async-start(bf16[32,32,288]{2,1,0:T(8,128)(2,1)} %bitcast.16), calls=%async_computation.7 | async-start | bytes 1572864 | tf_op jit(solution)/shard_map/all_to_all | solution.py:19
  250.6 12.8 %all-to-all-done.7 = bf16[32,32,288]{2,1,0:T(8,128)(2,1)S(1)} async-done(((bf16[32,32,288]{2,1,0:T(8,128)(2,1)}), bf16[32,32,288]{2,1,0:T(8,128)(2,1)S(1)}, u32[]{:S(2)}, u32[]{:S(2)}) %all-to-all-start.7) | async-done | bytes 589856 | tf_op jit(solution)/shard_map/all_to_all | solution.py:19
  263.4 2.7 fusion.12
  266.5 15.9 %all_to_all.55 = bf16[4,4,40,288]{3,2,1,0:T(8,128)(2,1)S(1)} all-to-all(bf16[4,4,40,288]{3,2,1,0:T(8,128)(2,1)S(1)} %bitcast.48), channel_id=1, replica_groups=mesh['run'=4,'place'=4,'replica'=8,'tensor'=4] {'place'}, dimensions={0} | all-to-all | bytes 737280 | tf_op jit(solution)/shard_map/all_to_all | solution.py:19
  282.5 25.9 %all_to_all.56 = bf16[4,40,288]{2,1,0:T(8,128)(2,1)S(1)} all-to-all(bf16[4,40,288]{2,1,0:T(8,128)(2,1)S(1)} %reduce_sum.107), channel_id=1, replica_groups=mesh['run'=4,'place'=4,'replica'=8,'tensor'=4] {'run'}, dimensions={0} | all-to-all | bytes 184320 | tf_op jit(solution)/shard_map/all_to_all | solution.py:19
  308.5 17.7 %all-gather.2 = bf16[160,288]{1,0:T(8,128)(2,1)S(1)} all-gather(bf16[40,288]{1,0:T(8,128)(2,1)S(1)} %reduce_sum.108), channel_id=4, replica_groups=mesh['run'=4,'place'=4,'replica'=8,'tensor'=4] {'run'}, dimensions={0}, use_global_device_ids=true | all-gather | bytes 115200 | tf_op jit(solution)/shard_map/all_gather | solution.py:32
  327.0 3.7 %all-to-all-start.10 = ((bf16[4,4,40,288]{3,2,1,0:T(8,128)(2,1)}), bf16[4,4,40,288]{3,2,1,0:T(8,128)(2,1)S(1)}, u32[]{:S(2)}, u32[]{:S(2)}) async-start(bf16[4,4,40,288]{3,2,1,0:T(8,128)(2,1)} %broadcast_in_dim.35), calls=%async_computation.10 | async-start | bytes 983040 | tf_op jit(solution)/shard_map/all_to_all | solution.py:19
  330.7 8.3 %all-gather.1 = bf16[2,128,1152]{2,1,0:T(8,128)(2,1)S(1)} all-gather(bf16[2,32,1152]{2,1,0:T(8,128)(2,1)S(1)} %pad_maximum_fusion.2), channel_id=3, replica_groups=mesh['run'=4,'place'=4,'replica'=8,'tensor'=4] {'tensor'}, dimensions={1}, use_global_device_ids=true | all-gather | bytes 737280 | tf_op jit(solution)/shard_map/all_gather | solution.py:160
  342.4 2.0 copy.21
  (56 shorter events, 11.3 us)
Async XLA Ops:
  0.6 1.9 copy-start
  2.6 15.1 %copy-start.6 = (bf16[128,1152]{1,0:T(8,128)(2,1)S(1)}, bf16[128,1152]{1,0:T(8,128)(2,1)}, u32[]{:S(2)}) copy-start(bf16[128,1152]{1,0:T(8,128)(2,1)} %param.8) | copy-start | bytes 884740
  2.6 15.1 %copy-start.8 = (bf16[128,1152]{1,0:T(8,128)(2,1)S(1)}, bf16[128,1152]{1,0:T(8,128)(2,1)}, u32[]{:S(2)}) copy-start(bf16[128,1152]{1,0:T(8,128)(2,1)} %param.11) | copy-start | bytes 884740
  4.9 12.7 %all-to-all-start = ((bf16[4,64,1152]{2,1,0:T(8,128)(2,1)}), bf16[4,64,1152]{2,1,0:T(8,128)(2,1)S(1)}, u32[]{:S(2)}, u32[]{:S(2)}) async-start(bf16[4,64,1152]{2,1,0:T(8,128)(2,1)} %pad_maximum_fusion), calls=%async_computation | async-start | bytes 1179648 | tf_op jit(solution)/shard_map/all_to_all | solution.py:19
  19.5 43.6 %all-to-all-start.2 = ((bf16[32,32,1152]{2,1,0:T(8,128)(2,1)}), bf16[32,32,1152]{2,1,0:T(8,128)(2,1)}, u32[]{:S(2)}, u32[]{:S(2)}) async-start(bf16[32,32,1152]{2,1,0:T(8,128)(2,1)} %broadcast_in_dim.28), calls=%async_computation.2 | async-start | bytes 4718592 | tf_op jit(solution)/shard_map/all_to_all | solution.py:19
  31.4 37.7 %copy-start.4 = (bf16[128,544]{0,1:T(8,128)(2,1)S(1)}, bf16[128,544]{0,1:T(8,128)(2,1)}, u32[]{:S(2)}) copy-start(bf16[128,544]{0,1:T(8,128)(2,1)} %param.12) | copy-start | bytes 417796
  55.5 13.7 %copy-start.5 = (bf16[128,544]{0,1:T(8,128)(2,1)S(1)}, bf16[128,544]{0,1:T(8,128)(2,1)}, u32[]{:S(2)}) copy-start(bf16[128,544]{0,1:T(8,128)(2,1)} %param.9) | copy-start | bytes 417796
  64.2 30.3 %all-to-all-start.1 = ((bf16[4,4,32,1152]{3,2,1,0:T(8,128)(2,1)}), bf16[4,4,32,1152]{3,2,1,0:T(8,128)(2,1)S(1)}, u32[]{:S(2)}, u32[]{:S(2)}) async-start(bf16[4,4,32,1152]{3,2,1,0:T(8,128)(2,1)} %broadcast_in_dim.27), calls=%async_computation.1 | async-start | bytes 2359296 | tf_op jit(solution)/shard_map/all_to_all | solution.py:19
  94.5 4.3 %copy-start.2 = (bf16[4,4,32,1152]{3,2,1,0:T(8,128)(2,1)}, bf16[4,4,32,1152]{3,2,1,0:T(8,128)(2,1)S(1)}, u32[]{:S(2)}) copy-start(bf16[4,4,32,1152]{3,2,1,0:T(8,128)(2,1)S(1)} %all-to-all-done.1) | copy-start | bytes 3538948
  98.8 4.6 %copy-start.3 = (bf16[1024,512]{1,0:T(8,128)(2,1)}, bf16[1024,512]{1,0:T(8,128)(2,1)S(1)}, u32[]{:S(2)}) copy-start(bf16[1024,512]{1,0:T(8,128)(2,1)S(1)} %multiply_convert_fusion) | copy-start | bytes 3145732
  103.5 31.5 %all-to-all-start.3 = ((bf16[4,4,32,1152]{3,2,1,0:T(8,128)(2,1)}), bf16[4,4,32,1152]{3,2,1,0:T(8,128)(2,1)S(1)}, u32[]{:S(2)}, u32[]{:S(2)}) async-start(bf16[4,4,32,1152]{3,2,1,0:T(8,128)(2,1)} %bitcast.11), calls=%async_computation.3 | async-start | bytes 2359296 | tf_op jit(solution)/shard_map/all_to_all | solution.py:19
  135.0 40.6 %all-to-all-start.5 = ((bf16[32,32,1152]{2,1,0:T(8,128)(2,1)}), bf16[32,32,1152]{2,1,0:T(8,128)(2,1)}, u32[]{:S(2)}, u32[]{:S(2)}) async-start(bf16[32,32,1152]{2,1,0:T(8,128)(2,1)} %bitcast.46), calls=%async_computation.5 | async-start | bytes 4718592 | tf_op jit(solution)/shard_map/all_to_all | solution.py:19
  175.6 30.0 %all-to-all-start.4 = ((bf16[4,32,1152]{2,1,0:T(8,128)(2,1)}), bf16[4,32,1152]{2,1,0:T(8,128)(2,1)S(1)}, u32[]{:S(2)}, u32[]{:S(2)}) async-start(bf16[4,32,1152]{2,1,0:T(8,128)(2,1)} %reduce_sum.102), calls=%async_computation.4 | async-start | bytes 589824 | tf_op jit(solution)/shard_map/all_to_all | solution.py:19
  207.2 32.1 %all-to-all-start.6 = ((bf16[8,1280,128]{1,2,0:T(8,128)(2,1)}), bf16[8,1280,128]{1,2,0:T(8,128)(2,1)}, u32[]{:S(2)}, u32[]{:S(2)}) async-start(bf16[8,1280,128]{1,2,0:T(8,128)(2,1)} %broadcast_in_dim.29), calls=%async_computation.6 | async-start | bytes 5242880 | tf_op jit(solution)/shard_map/all_to_all | solution.py:19
  213.3 26.1 %copy-start.7 = (bf16[128,1152]{1,0:T(8,128)(2,1)S(1)}, bf16[128,1152]{1,0:T(8,128)(2,1)}, u32[]{:S(2)}) copy-start(bf16[128,1152]{1,0:T(8,128)(2,1)} %param.8) | copy-start | bytes 884740
  213.3 26.1 %copy-start.9 = (bf16[128,1152]{1,0:T(8,128)(2,1)S(1)}, bf16[128,1152]{1,0:T(8,128)(2,1)}, u32[]{:S(2)}) copy-start(bf16[128,1152]{1,0:T(8,128)(2,1)} %param.11) | copy-start | bytes 884740
  241.3 22.1 %all-to-all-start.7 = ((bf16[32,32,288]{2,1,0:T(8,128)(2,1)}), bf16[32,32,288]{2,1,0:T(8,128)(2,1)S(1)}, u32[]{:S(2)}, u32[]{:S(2)}) async-start(bf16[32,32,288]{2,1,0:T(8,128)(2,1)} %bitcast.16), calls=%async_computation.7 | async-start | bytes 1572864 | tf_op jit(solution)/shard_map/all_to_all | solution.py:19
  326.2 14.0 %copy-start.1 = (bf16[544,1152]{1,0:T(8,128)(2,1)S(1)}, bf16[544,1152]{1,0:T(8,128)(2,1)}, u32[]{:S(2)}) copy-start(bf16[544,1152]{1,0:T(8,128)(2,1)} %param.13) | copy-start | bytes 3760132
  327.0 14.3 %all-to-all-start.10 = ((bf16[4,4,40,288]{3,2,1,0:T(8,128)(2,1)}), bf16[4,4,40,288]{3,2,1,0:T(8,128)(2,1)S(1)}, u32[]{:S(2)}, u32[]{:S(2)}) async-start(bf16[4,4,40,288]{3,2,1,0:T(8,128)(2,1)} %broadcast_in_dim.35), calls=%async_computation.10 | async-start | bytes 983040 | tf_op jit(solution)/shard_map/all_to_all | solution.py:19

commit v4 on v2

--- a/solution.py
+++ b/solution.py
@@ -26,7 +26,6 @@
 
 
 OFFSETS = (0, -4, -8, -12, -1, -5, -9, -13, 1, -3, -7, -11, 2, -2, -6, -10)
-PLACES = tuple([offset % 16 for offset in OFFSETS].index(k) for k in range(16))
 
 
 def shift(x, by):
@@ -64,16 +63,6 @@
     return near + shift(above, 4).astype(F32) + shift(below, -4).astype(F32)
 
 
-def chunked(hidden_units, dp, size):
-    rows, hidden = hidden_units.shape
-    chunk = hidden // size
-    slots = -(-chunk // 8) * 8
-    x = hidden_units.T.reshape(size, chunk, rows)
-    x = lax.optimization_barrier(jnp.pad(x, ((0, 0), (0, slots - chunk), (0, 0))))
-    place = (dp + jnp.array(OFFSETS, jnp.int32)) % size
-    return x.at[place].get(mode="promise_in_bounds").reshape(size * slots, rows)
-
-
 def normalize(residual, summed):
     combined = residual.astype(F32) + summed
     inverse = lax.rsqrt(jnp.sum(combined * combined, axis=1, keepdims=True) + 1e-06)
@@ -96,11 +85,9 @@
     pair_logit_bias,
 ):
     rows, width = image_residual_input.shape
-    hidden = image_hidden_units.shape[1]
     n_dp = lax.axis_size("dp")
     n_replica = lax.axis_size("replica")
     n_tensor = lax.axis_size("tensor")
-    dp = lax.axis_index("dp")
     replica = lax.axis_index("replica")
     tensor = lax.axis_index("tensor")
     own = rows // n_tensor
@@ -124,13 +111,16 @@
     normed_text, inverse_text = normalize(text_residual, summed[own:])
     normed_image, inverse_image = normalize(image_residual, summed[:own])
 
+    hidden_image, hidden_text = (
+        lax.all_gather(after(units, summed), "replica", axis=0, tiled=True)
+        for units in (image_hidden_units, text_hidden_units)
+    )
+
     images = spread(normed_image.astype(BF16), PLANE)
     texts = gather_dp(normed_text.astype(BF16))
-    hidden_text = spread(chunked(text_hidden_units, dp, n_dp), "replica")
-    texts, images, hidden_text = lax.optimization_barrier((texts, images, hidden_text))
+    texts, images = lax.optimization_barrier((texts, images))
     texts = texts.reshape(n_dp * own, width)
     images = images.reshape(members * own, width)
-    hidden_image = spread(after(chunked(image_hidden_units, dp, n_dp), images), "replica")
 
     scale = jnp.exp(log_logit_scale[0])
     logits = scale * dot(images, texts, ((1,), (1,))) + pair_logit_bias[0]
@@ -141,7 +131,6 @@
     coefficients = (-label * jax.nn.sigmoid(-label * logits) * scale).astype(BF16)
     text_partial = dot(coefficients, images, ((0,), (0,))).astype(BF16)
     image_partial = dot(after(coefficients, text_partial), texts, ((1,), (0,))).astype(BF16)
-    image_partial, hidden_image = lax.optimization_barrier((image_partial, hidden_image))
 
     text_grad = scatter_dp(text_partial.reshape(n_dp, own, width))
     image_parts = exchange(image_partial.reshape(members, own, width), PLANE)
@@ -160,17 +149,6 @@
     cut = jnp.broadcast_to(cut[:, None], (n_replica, n_tensor, own, 2 * columns))
     cut = exchange(cut.reshape(members, own, 2 * columns), PLANE)
     cut = cut.reshape(members * own, 2 * columns)
-    slots = hidden_image.shape[1]
-    hidden_image = jnp.transpose(hidden_image, (1, 0, 2)).reshape(slots, members * own)
-    hidden_text = jnp.transpose(hidden_text, (1, 0, 2)).reshape(slots, members * own)
-    partial = jnp.where(
-        jnp.arange(2 * columns)[None, :] < columns,
-        dot(hidden_image, cut, ((1,), (0,))),
-        dot(hidden_text, cut, ((1,), (0,))),
-    ).astype(BF16)
-    share = scatter_dp(partial.reshape(n_dp, slots // n_dp, 2 * columns)).astype(BF16)
-    total = gather_dp(share)
-
     group = lax.all_gather(jnp.stack([upstream_image, upstream_text]), "tensor", axis=1)
     hidden_grad_image = dot(
         group[0].reshape(rows, width), image_output_weight, ((1,), (1,))
@@ -179,10 +157,15 @@
         group[1].reshape(rows, width), text_output_weight, ((1,), (1,))
     ).astype(BF16)
 
-    place = jnp.array(PLACES, jnp.int32)[(jnp.arange(n_dp, dtype=jnp.int32) - dp) % n_dp]
-    total = lax.optimization_barrier(total).at[place].get(mode="promise_in_bounds")
-    total = total[:, : hidden // n_dp].astype(F32)
-    total = total.reshape(hidden, 2 * columns)
+    partial = jnp.where(
+        jnp.arange(2 * columns)[None, :] < columns,
+        dot(hidden_image, cut, ((0,), (0,))),
+        dot(hidden_text, cut, ((0,), (0,))),
+    ).astype(BF16)
+    partial, hidden_grad_image, hidden_grad_text = lax.optimization_barrier(
+        (partial, hidden_grad_image, hidden_grad_text)
+    )
+    total = lax.psum(partial, "dp").astype(F32)
     return (hidden_grad_image, hidden_grad_text, total[:, :columns], total[:, columns:])
 
 

time: 310 us -> 335 us (1.081)
  waiting for transfers between devices: 44.2 us -> 160 us
  starting transfers between devices: 180 us -> 92.7 us
  local copies, waits for them, and re-layouts: 27.2 us -> 9.92 us
  between operations: 2.94 us -> 15.6 us
  blocking collectives: 15.5 us -> 28.1 us
  other arithmetic: 15.5 us -> 6.36 us
    psum x0 -> x1, waiting for transfers between devices: none -> 135 us  [shards(): total = lax.psum(partial, 'dp').astype(F32)]
    ppermute x32 -> x16, starting transfers between devices: 139 us -> 71.5 us  [shift(): return lax.ppermute(x, 'dp', [(i, (i + by) % size) for i in range(size)])]
    all_to_all x6 -> x3, starting transfers between devices: 40.6 us -> 21.2 us  [exchange(): return lax.all_to_all(x, axis, split_axis=0, concat_axis=0, tiled=True)]
    ppermute x32 -> x16, waiting for transfers between devices: 27.1 us -> 12.8 us  [shift(): return lax.ppermute(x, 'dp', [(i, (i + by) % size) for i in range(size)])]
    all_to_all x0 -> x1, blocking collectives: none -> 12.6 us  [exchange(): return lax.all_to_all(x, axis, split_axis=0, concat_axis=0, tiled=True)]
    unnamed x52 -> x15, local copies, waits for them, and re-layouts: 11.2 us -> 3.48 us
    all_to_all x6 -> x3, waiting for transfers between devices: 17.1 us -> 11.2 us  [exchange(): return lax.all_to_all(x, axis, split_axis=0, concat_axis=0, tiled=True)]
    broadcast_in_dim x4 -> x1, local copies, waits for them, and re-layouts: 5.71 us -> 1.61 us  [spread(): return exchange(jnp.broadcast_to(x[None], (size,) + x.shape), axis)]
  transfers between devices with their start and end apart: 38 -> 22, of which waited for: 12 -> 8; matrix products, arithmetic and copies ran while one was open for 11% -> 9% of each run, Pallas kernels for 0% -> 0%
where the time goes in v4:
time: 335 us; the launch traced here: 333 us
  waiting for transfers between devices  160 us (48%)
  starting transfers between devices  92.7 us (28%)
  blocking collectives  28.1 us (8%)
  matrix products  21 us (6%)
  between operations  15.6 us (5%)
  local copies, waits for them, and re-layouts  9.92 us (3%)
  other arithmetic  6.36 us (2%)
    psum x1, waiting for transfers between devices, shards(): total = lax.psum(partial, 'dp').astype(F32)  135 us
    ppermute x16, starting transfers between devices, shift(): return lax.ppermute(x, 'dp', [(i, (i + by) % size) for i in range(size)])  71.5 us
    all_to_all x3, starting transfers between devices, exchange(): return lax.all_to_all(x, axis, split_axis=0, concat_axis=0, tiled=True)  21.2 us
    dot_general x9, matrix products, dot(): lax.dot_general(a, b, (contract, ((), ())), preferred_element_type=F32)  21 us
    all_gather x1, blocking collectives, shards(): lax.all_gather(jnp.stack([upstream_image, upstream_text]), 'tensor', axis=1)  15.5 us
    ppermute x16, waiting for transfers between devices, shift(): return lax.ppermute(x, 'dp', [(i, (i + by) % size) for i in range(size)])  12.8 us
    all_to_all x1, blocking collectives, exchange(): return lax.all_to_all(x, axis, split_axis=0, concat_axis=0, tiled=True)  12.6 us
    all_to_all x3, waiting for transfers between devices, exchange(): return lax.all_to_all(x, axis, split_axis=0, concat_axis=0, tiled=True)  11.2 us
  transfers between devices with their start and end apart: 22, of which 8 were waited for; matrix products, arithmetic and copies ran while one was open for 9% of the time, Pallas kernels for 0%

profile of v4, /device:TPU:24, one launch (start us, length us, event | category | flops | bytes accessed | tf_op | source)
XLA Modules:
  0.0 333.3 jit_solution(11048982385715041985)
XLA Ops:
  7.2 1.9 convolution_convert_fusion.3
  9.7 12.6 %all_to_all.20 = bf16[4,64,1152]{2,1,0:T(8,128)(2,1)S(1)} all-to-all(bf16[4,64,1152]{2,1,0:T(8,128)(2,1)S(1)} %pad_maximum_fusion), channel_id=1, replica_groups=mesh['dp'=16,'replica'=8,'tensor'=4] {'tensor'}, dimensions={0} | all-to-all | bytes 1179648 | tf_op jit(solution)/shard_map/all_to_all | solution.py:16
  24.7 12.7 %collective-permute-start.1 = (bf16[32,1152]{1,0:T(8,128)(2,1)S(1)}, bf16[32,1152]{1,0:T(8,128)(2,1)S(1)}, u32[]{:S(2)}, u32[]{:S(2)}) collective-permute-start(bf16[32,1152]{1,0:T(8,128)(2,1)S(1)} %get-tuple-element.25), channel_id=1, source_target_pairs={{0,384},{32,416},{64,448},{96,480},{128,0},{160,32},{192,64},{224,... | collective-permute-start | bytes 221192 | tf_op jit(solution)/shard_map/ppermute | solution.py:33
  37.4 1.9 collective-permute-start
  41.1 7.7 %all-to-all-start.1 = ((bf16[32,32,1152]{2,1,0:T(8,128)(2,1)}), bf16[32,32,1152]{2,1,0:T(8,128)(2,1)}, u32[]{:S(2)}, u32[]{:S(2)}) async-start(bf16[32,32,1152]{2,1,0:T(8,128)(2,1)} %broadcast_in_dim.43), calls=%async_computation.1 | async-start | bytes 4718592 | tf_op jit(solution)/shard_map/all_to_all | solution.py:16
  49.5 7.8 %collective-permute-start.2 = (bf16[16,1152]{1,0:T(8,128)(2,1)S(1)}, bf16[16,1152]{1,0:T(8,128)(2,1)S(1)}, u32[]{:S(2)}, u32[]{:S(2)}) collective-permute-start(bf16[16,1152]{1,0:T(8,128)(2,1)S(1)} %slice.157), channel_id=1, source_target_pairs={{0,384},{32,416},{64,448},{96,480},{128,0},{160,32},{192,64},{224,... | collective-permute-start | bytes 110600 | tf_op jit(solution)/shard_map/ppermute | solution.py:33
  57.4 1.9 collective-permute-start.3
  61.4 5.8 %collective-permute-done.3 = bf16[16,1152]{1,0:T(8,128)(2,1)S(1)} collective-permute-done((bf16[16,1152]{1,0:T(8,128)(2,1)S(1)}, bf16[16,1152]{1,0:T(8,128)(2,1)S(1)}, u32[]{:S(2)}, u32[]{:S(2)}) %collective-permute-start.3) | collective-permute-done | bytes 36896 | tf_op jit(solution)/shard_map/ppermute | solution.py:33
  67.2 2.9 collective-permute-start.4
  70.2 4.1 %collective-permute-start.5 = (bf16[4,32,1152]{2,1,0:T(8,128)(2,1)S(1)}, bf16[4,32,1152]{2,1,0:T(8,128)(2,1)S(1)}, u32[]{:S(2)}, u32[]{:S(2)}) collective-permute-start(bf16[4,32,1152]{2,1,0:T(8,128)(2,1)S(1)} %pad_maximum_fusion.1), channel_id=1, source_target_pairs={{0,480},{32,0},{64,32},{96,64},{128,96},{160,128},{192,160},{224,1... | collective-permute-start | bytes 884744 | tf_op jit(solution)/shard_map/ppermute | solution.py:33
  74.4 3.8 %collective-permute-start.6 = (bf16[2,32,1152]{2,1,0:T(8,128)(2,1)S(1)}, bf16[2,32,1152]{2,1,0:T(8,128)(2,1)S(1)}, u32[]{:S(2)}, u32[]{:S(2)}) collective-permute-start(bf16[2,32,1152]{2,1,0:T(8,128)(2,1)S(1)} %get-tuple-element.40), channel_id=1, source_target_pairs={{0,448},{32,480},{64,0},{96,32},{128,64},{160,96},{192,128},{224,1... | collective-permute-start | bytes 442376 | tf_op jit(solution)/shard_map/ppermute | solution.py:33
  78.2 2.9 collective-permute-start.7
  89.6 4.2 %multiply_convert_fusion = bf16[1024,512]{1,0:T(8,128)(2,1)S(1)} fusion(bf16[1024,1152]{1,0:T(8,128)(2,1)} %bitcast.7, bf16[512,1152]{1,0:T(8,128)(2,1)} %bitcast.8, f32[]{:T(128)} %bitcast.81, f32[]{:T(128)} %bitcast.2, s32[512]{0:T(512)S(1)} %add_select_fusion), kind=kOutput, calls=%fused_computation.5 | convolution fusion | flops 1214251008 | bytes 4589576 | tf_op jit(solution)/shard_map/dot_general | solution.py:12
  93.8 3.2 convolution_convert_fusion.1
  97.8 2.4 collective-permute-start.8
  100.2 3.4 %collective-permute-start.9 = (bf16[4,32,1152]{2,1,0:T(8,128)(2,1)S(1)}, bf16[4,32,1152]{2,1,0:T(8,128)(2,1)}, u32[]{:S(2)}, u32[]{:S(2)}) collective-permute-start(bf16[4,32,1152]{2,1,0:T(8,128)(2,1)S(1)} %bitcast.95), channel_id=1, source_target_pairs={{0,32},{32,64},{64,96},{96,128},{128,160},{160,192},{192,224},{224... | collective-permute-start | bytes 884744 | tf_op jit(solution)/shard_map/ppermute | solution.py:33
  103.7 2.6 collective-permute-start.10
  106.3 5.3 %collective-permute-start.11 = (bf16[2,32,1152]{2,1,0:T(8,128)(2,1)}, bf16[2,32,1152]{2,1,0:T(8,128)(2,1)}, u32[]{:S(2)}, u32[]{:S(2)}) collective-permute-start(bf16[2,32,1152]{2,1,0:T(8,128)(2,1)} %bitcast.17), channel_id=1, source_target_pairs={{0,448},{32,480},{64,0},{96,32},{128,64},{160,96},{192,128},{224,1... | collective-permute-start | bytes 442376 | tf_op jit(solution)/shard_map/ppermute | solution.py:33
  111.6 4.2 %convolution_convert_fusion = bf16[1024,1152]{1,0:T(8,128)(2,1)} fusion(bf16[1024,512]{1,0:T(8,128)(2,1)S(1)} %multiply_convert_fusion, bf16[512,1152]{1,0:T(8,128)(2,1)} %bitcast.8), kind=kOutput, calls=%fused_computation.1 | convolution fusion | flops 1209139200 | bytes 4587520 | tf_op jit(solution)/shard_map/dot_general | solution.py:12
  115.9 7.4 %all-to-all-start.2 = ((bf16[32,32,1152]{2,1,0:T(8,128)(2,1)}), bf16[32,32,1152]{2,1,0:T(8,128)(2,1)}, u32[]{:S(2)}, u32[]{:S(2)}) async-start(bf16[32,32,1152]{2,1,0:T(8,128)(2,1)} %bitcast.82), calls=%async_computation.2 | async-start | bytes 4718592 | tf_op jit(solution)/shard_map/all_to_all | solution.py:16
  125.3 4.5 %collective-permute-start.12 = (bf16[16,1152]{1,0:T(8,128)(2,1)S(1)}, bf16[16,1152]{1,0:T(8,128)(2,1)S(1)}, u32[]{:S(2)}, u32[]{:S(2)}) collective-permute-start(bf16[16,1152]{1,0:T(8,128)(2,1)S(1)} %get-tuple-element.37), channel_id=1, source_target_pairs={{0,128},{32,160},{64,192},{96,224},{128,256},{160,288},{192,320},{... | collective-permute-start | bytes 110600 | tf_op jit(solution)/shard_map/ppermute | solution.py:33
  129.8 5.3 %collective-permute-start.14 = (bf16[16,1152]{1,0:T(8,128)(2,1)S(1)}, bf16[16,1152]{1,0:T(8,128)(2,1)S(1)}, u32[]{:S(2)}, u32[]{:S(2)}) collective-permute-start(bf16[16,1152]{1,0:T(8,128)(2,1)S(1)} %get-tuple-element.38), channel_id=1, source_target_pairs={{0,384},{32,416},{64,448},{96,480},{128,0},{160,32},{192,64},{224,... | collective-permute-start | bytes 110600 | tf_op jit(solution)/shard_map/ppermute | solution.py:33
  136.4 4.5 %collective-permute-start.13 = (bf16[32,1152]{1,0:T(8,128)(2,1)S(1)}, bf16[32,1152]{1,0:T(8,128)(2,1)S(1)}, u32[]{:S(2)}, u32[]{:S(2)}) collective-permute-start(bf16[32,1152]{1,0:T(8,128)(2,1)S(1)} %pad_maximum_fusion.5), channel_id=1, source_target_pairs={{0,128},{32,160},{64,192},{96,224},{128,256},{160,288},{192,320},{... | collective-permute-start | bytes 221192 | tf_op jit(solution)/shard_map/ppermute | solution.py:33
  140.9 5.3 %collective-permute-start.15 = (bf16[32,1152]{1,0:T(8,128)(2,1)S(1)}, bf16[32,1152]{1,0:T(8,128)(2,1)S(1)}, u32[]{:S(2)}, u32[]{:S(2)}) collective-permute-start(bf16[32,1152]{1,0:T(8,128)(2,1)S(1)} %pad_maximum_fusion.6), channel_id=1, source_target_pairs={{0,384},{32,416},{64,448},{96,480},{128,0},{160,32},{192,64},{224,... | collective-permute-start | bytes 221192 | tf_op jit(solution)/shard_map/ppermute | solution.py:33
  146.2 11.2 %all-to-all-done.2 = bf16[32,32,1152]{2,1,0:T(8,128)(2,1)} async-done(((bf16[32,32,1152]{2,1,0:T(8,128)(2,1)}), bf16[32,32,1152]{2,1,0:T(8,128)(2,1)}, u32[]{:S(2)}, u32[]{:S(2)}) %all-to-all-start.2) | async-done | bytes 2359328 | tf_op jit(solution)/shard_map/all_to_all | solution.py:16
  157.4 2.0 convert_reduce_fusion
  161.3 6.1 %all-to-all-start.3 = ((bf16[32,32,288]{2,1,0:T(8,128)(2,1)}), bf16[32,32,288]{2,1,0:T(8,128)(2,1)S(1)}, u32[]{:S(2)}, u32[]{:S(2)}) async-start(bf16[32,32,288]{2,1,0:T(8,128)(2,1)} %bitcast.24), calls=%async_computation.3 | async-start | bytes 1572864 | tf_op jit(solution)/shard_map/all_to_all | solution.py:16
  167.5 15.5 %all-gather = bf16[2,128,1152]{2,1,0:T(8,128)(2,1)S(1)} all-gather(bf16[2,32,1152]{2,1,0:T(8,128)(2,1)S(1)} %pad_maximum_fusion.4), channel_id=2, replica_groups=mesh['dp'=16,'replica'=8,'tensor'=4] {'tensor'}, dimensions={1}, use_global_device_ids=true | all-gather | bytes 737280 | tf_op jit(solution)/shard_map/all_gather | solution.py:152
  185.3 2.0 fusion.16
  187.3 2.7 fusion
  190.1 134.8 %all-reduce.2.cloned.1.call-done = bf16[544,288]{0,1:T(8,128)(2,1)} async-done(((bf16[544,288]{0,1:T(8,128)(2,1)}), bf16[544,288]{0,1:T(8,128)(2,1)}) %all-reduce.2.cloned.1.call-update) | async-done | bytes 313360 | tf_op jit(solution)/shard_map/psum | solution.py:168
  324.8 1.9 fusion.15
  (78 shorter events, 23.0 us)
Async XLA Ops:
  7.2 2.0 copy-start
  7.2 2.0 copy-start.2
  7.2 178.2 %all-gather.4.cloned.1.call-start = ((), (), s32[]{:S(2)}) async-start(), calls=%async_computation.4 | async-start | bytes 1253376 | tf_op jit(solution)/shard_map/all_gather | solution.py:115
  9.7 14.1 %copy-start.3 = (bf16[128,1152]{1,0:T(8,128)(2,1)S(1)}, bf16[128,1152]{1,0:T(8,128)(2,1)}, u32[]{:S(2)}) copy-start(bf16[128,1152]{1,0:T(8,128)(2,1)} %param.8) | copy-start | bytes 884740
  9.7 14.1 %copy-start.4 = (bf16[128,1152]{1,0:T(8,128)(2,1)S(1)}, bf16[128,1152]{1,0:T(8,128)(2,1)}, u32[]{:S(2)}) copy-start(bf16[128,1152]{1,0:T(8,128)(2,1)} %param.11) | copy-start | bytes 884740
  24.7 24.8 %collective-permute-start.1 = (bf16[32,1152]{1,0:T(8,128)(2,1)S(1)}, bf16[32,1152]{1,0:T(8,128)(2,1)S(1)}, u32[]{:S(2)}, u32[]{:S(2)}) collective-permute-start(bf16[32,1152]{1,0:T(8,128)(2,1)S(1)} %get-tuple-element.25), channel_id=1, source_target_pairs={{0,384},{32,416},{64,448},{96,480},{128,0},{160,32},{192,64},{224,... | collective-permute-start | bytes 221192 | tf_op jit(solution)/shard_map/ppermute | solution.py:33
  37.4 19.9 %collective-permute-start = (bf16[32,1152]{1,0:T(8,128)(2,1)S(1)}, bf16[32,1152]{1,0:T(8,128)(2,1)S(1)}, u32[]{:S(2)}, u32[]{:S(2)}) collective-permute-start(bf16[32,1152]{1,0:T(8,128)(2,1)S(1)} %get-tuple-element.25), channel_id=1, source_target_pairs={{0,128},{32,160},{64,192},{96,224},{128,256},{160,288},{192,320},{... | collective-permute-start | bytes 221192 | tf_op jit(solution)/shard_map/ppermute | solution.py:33
  41.1 48.5 %all-to-all-start.1 = ((bf16[32,32,1152]{2,1,0:T(8,128)(2,1)}), bf16[32,32,1152]{2,1,0:T(8,128)(2,1)}, u32[]{:S(2)}, u32[]{:S(2)}) async-start(bf16[32,32,1152]{2,1,0:T(8,128)(2,1)} %broadcast_in_dim.43), calls=%async_computation.1 | async-start | bytes 4718592 | tf_op jit(solution)/shard_map/all_to_all | solution.py:16
  48.7 138.6 %all-gather.6.cloned.1.call-start = ((), (), s32[]{:S(2)}) async-start(), calls=%async_computation.5 | async-start | bytes 1253376 | tf_op jit(solution)/shard_map/all_gather | solution.py:115
  49.5 11.9 %collective-permute-start.2 = (bf16[16,1152]{1,0:T(8,128)(2,1)S(1)}, bf16[16,1152]{1,0:T(8,128)(2,1)S(1)}, u32[]{:S(2)}, u32[]{:S(2)}) collective-permute-start(bf16[16,1152]{1,0:T(8,128)(2,1)S(1)} %slice.157), channel_id=1, source_target_pairs={{0,384},{32,416},{64,448},{96,480},{128,0},{160,32},{192,64},{224,... | collective-permute-start | bytes 110600 | tf_op jit(solution)/shard_map/ppermute | solution.py:33
  57.4 9.8 %collective-permute-start.3 = (bf16[16,1152]{1,0:T(8,128)(2,1)S(1)}, bf16[16,1152]{1,0:T(8,128)(2,1)S(1)}, u32[]{:S(2)}, u32[]{:S(2)}) collective-permute-start(bf16[16,1152]{1,0:T(8,128)(2,1)S(1)} %slice.158), channel_id=1, source_target_pairs={{0,128},{32,160},{64,192},{96,224},{128,256},{160,288},{192,320},{... | collective-permute-start | bytes 110600 | tf_op jit(solution)/shard_map/ppermute | solution.py:33
  67.2 15.1 %collective-permute-start.4 = (bf16[4,32,1152]{2,1,0:T(8,128)(2,1)S(1)}, bf16[4,32,1152]{2,1,0:T(8,128)(2,1)S(1)}, u32[]{:S(2)}, u32[]{:S(2)}) collective-permute-start(bf16[4,32,1152]{2,1,0:T(8,128)(2,1)S(1)} %pad_maximum_fusion.1), channel_id=1, source_target_pairs={{0,32},{32,64},{64,96},{96,128},{128,160},{160,192},{192,224},{224... | collective-permute-start | bytes 884744 | tf_op jit(solution)/shard_map/ppermute | solution.py:33
  70.2 14.1 %collective-permute-start.5 = (bf16[4,32,1152]{2,1,0:T(8,128)(2,1)S(1)}, bf16[4,32,1152]{2,1,0:T(8,128)(2,1)S(1)}, u32[]{:S(2)}, u32[]{:S(2)}) collective-permute-start(bf16[4,32,1152]{2,1,0:T(8,128)(2,1)S(1)} %pad_maximum_fusion.1), channel_id=1, source_target_pairs={{0,480},{32,0},{64,32},{96,64},{128,96},{160,128},{192,160},{224,1... | collective-permute-start | bytes 884744 | tf_op jit(solution)/shard_map/ppermute | solution.py:33
  74.4 12.2 %collective-permute-start.6 = (bf16[2,32,1152]{2,1,0:T(8,128)(2,1)S(1)}, bf16[2,32,1152]{2,1,0:T(8,128)(2,1)S(1)}, u32[]{:S(2)}, u32[]{:S(2)}) collective-permute-start(bf16[2,32,1152]{2,1,0:T(8,128)(2,1)S(1)} %get-tuple-element.40), channel_id=1, source_target_pairs={{0,448},{32,480},{64,0},{96,32},{128,64},{160,96},{192,128},{224,1... | collective-permute-start | bytes 442376 | tf_op jit(solution)/shard_map/ppermute | solution.py:33
  78.2 10.7 %collective-permute-start.7 = (bf16[2,32,1152]{2,1,0:T(8,128)(2,1)S(1)}, bf16[2,32,1152]{2,1,0:T(8,128)(2,1)S(1)}, u32[]{:S(2)}, u32[]{:S(2)}) collective-permute-start(bf16[2,32,1152]{2,1,0:T(8,128)(2,1)S(1)} %get-tuple-element.39), channel_id=1, source_target_pairs={{0,64},{32,96},{64,128},{96,160},{128,192},{160,224},{192,256},{22... | collective-permute-start | bytes 442376 | tf_op jit(solution)/shard_map/ppermute | solution.py:33
  97.8 25.4 %collective-permute-start.8 = (bf16[4,32,1152]{2,1,0:T(8,128)(2,1)S(1)}, bf16[4,32,1152]{2,1,0:T(8,128)(2,1)S(1)}, u32[]{:S(2)}, u32[]{:S(2)}) collective-permute-start(bf16[4,32,1152]{2,1,0:T(8,128)(2,1)S(1)} %bitcast.96), channel_id=1, source_target_pairs={{0,480},{32,0},{64,32},{96,64},{128,96},{160,128},{192,160},{224,1... | collective-permute-start | bytes 884744 | tf_op jit(solution)/shard_map/ppermute | solution.py:33
  100.2 23.0 %collective-permute-start.9 = (bf16[4,32,1152]{2,1,0:T(8,128)(2,1)S(1)}, bf16[4,32,1152]{2,1,0:T(8,128)(2,1)}, u32[]{:S(2)}, u32[]{:S(2)}) collective-permute-start(bf16[4,32,1152]{2,1,0:T(8,128)(2,1)S(1)} %bitcast.95), channel_id=1, source_target_pairs={{0,32},{32,64},{64,96},{96,128},{128,160},{160,192},{192,224},{224... | collective-permute-start | bytes 884744 | tf_op jit(solution)/shard_map/ppermute | solution.py:33
  103.7 20.7 %collective-permute-start.10 = (bf16[2,32,1152]{2,1,0:T(8,128)(2,1)}, bf16[2,32,1152]{2,1,0:T(8,128)(2,1)S(1)}, u32[]{:S(2)}, u32[]{:S(2)}) collective-permute-start(bf16[2,32,1152]{2,1,0:T(8,128)(2,1)} %bitcast.14), channel_id=1, source_target_pairs={{0,64},{32,96},{64,128},{96,160},{128,192},{160,224},{192,256},{22... | collective-permute-start | bytes 442376 | tf_op jit(solution)/shard_map/ppermute | solution.py:33
  106.3 18.0 %collective-permute-start.11 = (bf16[2,32,1152]{2,1,0:T(8,128)(2,1)}, bf16[2,32,1152]{2,1,0:T(8,128)(2,1)}, u32[]{:S(2)}, u32[]{:S(2)}) collective-permute-start(bf16[2,32,1152]{2,1,0:T(8,128)(2,1)} %bitcast.17), channel_id=1, source_target_pairs={{0,448},{32,480},{64,0},{96,32},{128,64},{160,96},{192,128},{224,1... | collective-permute-start | bytes 442376 | tf_op jit(solution)/shard_map/ppermute | solution.py:33
  115.9 41.5 %all-to-all-start.2 = ((bf16[32,32,1152]{2,1,0:T(8,128)(2,1)}), bf16[32,32,1152]{2,1,0:T(8,128)(2,1)}, u32[]{:S(2)}, u32[]{:S(2)}) async-start(bf16[32,32,1152]{2,1,0:T(8,128)(2,1)} %bitcast.82), calls=%async_computation.2 | async-start | bytes 4718592 | tf_op jit(solution)/shard_map/all_to_all | solution.py:16
  125.3 11.0 %collective-permute-start.12 = (bf16[16,1152]{1,0:T(8,128)(2,1)S(1)}, bf16[16,1152]{1,0:T(8,128)(2,1)S(1)}, u32[]{:S(2)}, u32[]{:S(2)}) collective-permute-start(bf16[16,1152]{1,0:T(8,128)(2,1)S(1)} %get-tuple-element.37), channel_id=1, source_target_pairs={{0,128},{32,160},{64,192},{96,224},{128,256},{160,288},{192,320},{... | collective-permute-start | bytes 110600 | tf_op jit(solution)/shard_map/ppermute | solution.py:33
  129.8 11.0 %collective-permute-start.14 = (bf16[16,1152]{1,0:T(8,128)(2,1)S(1)}, bf16[16,1152]{1,0:T(8,128)(2,1)S(1)}, u32[]{:S(2)}, u32[]{:S(2)}) collective-permute-start(bf16[16,1152]{1,0:T(8,128)(2,1)S(1)} %get-tuple-element.38), channel_id=1, source_target_pairs={{0,384},{32,416},{64,448},{96,480},{128,0},{160,32},{192,64},{224,... | collective-permute-start | bytes 110600 | tf_op jit(solution)/shard_map/ppermute | solution.py:33
  136.4 23.0 %collective-permute-start.13 = (bf16[32,1152]{1,0:T(8,128)(2,1)S(1)}, bf16[32,1152]{1,0:T(8,128)(2,1)S(1)}, u32[]{:S(2)}, u32[]{:S(2)}) collective-permute-start(bf16[32,1152]{1,0:T(8,128)(2,1)S(1)} %pad_maximum_fusion.5), channel_id=1, source_target_pairs={{0,128},{32,160},{64,192},{96,224},{128,256},{160,288},{192,320},{... | collective-permute-start | bytes 221192 | tf_op jit(solution)/shard_map/ppermute | solution.py:33
  140.9 18.5 %collective-permute-start.15 = (bf16[32,1152]{1,0:T(8,128)(2,1)S(1)}, bf16[32,1152]{1,0:T(8,128)(2,1)S(1)}, u32[]{:S(2)}, u32[]{:S(2)}) collective-permute-start(bf16[32,1152]{1,0:T(8,128)(2,1)S(1)} %pad_maximum_fusion.6), channel_id=1, source_target_pairs={{0,384},{32,416},{64,448},{96,480},{128,0},{160,32},{192,64},{224,... | collective-permute-start | bytes 221192 | tf_op jit(solution)/shard_map/ppermute | solution.py:33
  161.3 24.0 %all-to-all-start.3 = ((bf16[32,32,288]{2,1,0:T(8,128)(2,1)}), bf16[32,32,288]{2,1,0:T(8,128)(2,1)S(1)}, u32[]{:S(2)}, u32[]{:S(2)}) async-start(bf16[32,32,288]{2,1,0:T(8,128)(2,1)} %bitcast.24), calls=%async_computation.3 | async-start | bytes 1572864 | tf_op jit(solution)/shard_map/all_to_all | solution.py:16
  167.4 157.4 %all-reduce.2.cloned.1.call-start = ((), (), s32[]{:S(2)}) async-start(), calls=%async_computation.6 | async-start | bytes 737280 | tf_op jit(solution)/shard_map/psum | solution.py:168
  167.5 16.7 %copy-start.1 = (bf16[544,1152]{1,0:T(8,128)(2,1)S(1)}, bf16[544,1152]{1,0:T(8,128)(2,1)}, u32[]{:S(2)}) copy-start(bf16[544,1152]{1,0:T(8,128)(2,1)} %param.10) | copy-start | bytes 3760132
Sparse Core Ops, SparseCore 0:
  22.5 63.5 all-gather.3
  88.2 58.7 all-gather.5
  190.2 134.6 all-reduce.1

commit v5 on v4

--- a/solution.py
+++ b/solution.py
@@ -63,6 +63,14 @@
     return near + shift(above, 4).astype(F32) + shift(below, -4).astype(F32)
 
 
+def chunked(hidden_units, size):
+    rows, hidden = hidden_units.shape
+    chunk = hidden // size
+    slots = -(-chunk // 8) * 8
+    x = hidden_units.T.reshape(size, chunk, rows)
+    return jnp.pad(x, ((0, 0), (0, slots - chunk), (0, 0))).reshape(size * slots, rows).T
+
+
 def normalize(residual, summed):
     combined = residual.astype(F32) + summed
     inverse = lax.rsqrt(jnp.sum(combined * combined, axis=1, keepdims=True) + 1e-06)
@@ -112,7 +120,7 @@
     normed_image, inverse_image = normalize(image_residual, summed[:own])
 
     hidden_image, hidden_text = (
-        lax.all_gather(after(units, summed), "replica", axis=0, tiled=True)
+        lax.all_gather(after(chunked(units, n_dp), summed), "replica", axis=0, tiled=True)
         for units in (image_hidden_units, text_hidden_units)
     )
 
@@ -129,11 +137,11 @@
     text_index = jnp.where(position < own, (replica * n_tensor + tensor) * own + position, -1)
     label = jnp.where(image_index[:, None] == text_index[None, :], 1.0, -1.0).astype(F32)
     coefficients = (-label * jax.nn.sigmoid(-label * logits) * scale).astype(BF16)
+    image_partial = dot(coefficients, texts, ((1,), (0,))).astype(BF16)
+    coefficients, image_partial = lax.optimization_barrier((coefficients, image_partial))
+    image_parts = exchange(image_partial.reshape(members, own, width), PLANE)
     text_partial = dot(coefficients, images, ((0,), (0,))).astype(BF16)
-    image_partial = dot(after(coefficients, text_partial), texts, ((1,), (0,))).astype(BF16)
-
     text_grad = scatter_dp(text_partial.reshape(n_dp, own, width))
-    image_parts = exchange(image_partial.reshape(members, own, width), PLANE)
     image_grad = jnp.sum(image_parts.astype(F32), axis=0)
 
     upstream_image = retract(normed_image, inverse_image, image_grad)
@@ -149,7 +157,8 @@
     cut = jnp.broadcast_to(cut[:, None], (n_replica, n_tensor, own, 2 * columns))
     cut = exchange(cut.reshape(members, own, 2 * columns), PLANE)
     cut = cut.reshape(members * own, 2 * columns)
-    group = lax.all_gather(jnp.stack([upstream_image, upstream_text]), "tensor", axis=1)
+    group = after(jnp.stack([upstream_image, upstream_text]), cut)
+    group = lax.all_gather(group, "tensor", axis=1)
     hidden_grad_image = dot(
         group[0].reshape(rows, width), image_output_weight, ((1,), (1,))
     ).astype(BF16)
@@ -162,10 +171,11 @@
         dot(hidden_image, cut, ((0,), (0,))),
         dot(hidden_text, cut, ((0,), (0,))),
     ).astype(BF16)
-    partial, hidden_grad_image, hidden_grad_text = lax.optimization_barrier(
-        (partial, hidden_grad_image, hidden_grad_text)
-    )
-    total = lax.psum(partial, "dp").astype(F32)
+    chunk = image_hidden_units.shape[1] // n_dp
+    pieces = exchange(partial.reshape(n_dp, -1, 2 * columns), "dp")
+    share = jnp.sum(pieces.astype(F32), axis=0).astype(BF16)
+    total = lax.all_gather(share, "dp", axis=0)[:, :chunk].astype(F32)
+    total = total.reshape(n_dp * chunk, 2 * columns)
     return (hidden_grad_image, hidden_grad_text, total[:, :columns], total[:, columns:])
 
 

time: 335 us -> 272 us (0.81)
  waiting for transfers between devices: 160 us -> 62.9 us
  starting transfers between devices: 92.7 us -> 107 us
  blocking collectives: 28.1 us -> 41.6 us
  local copies, waits for them, and re-layouts: 9.92 us -> 14.6 us
    psum x1 -> x0, waiting for transfers between devices: 135 us -> none  [shards(): total = lax.psum(partial, 'dp').astype(F32)]
    all_to_all x3 -> x5, waiting for transfers between devices: 11.2 us -> 49.4 us  [exchange(): return lax.all_to_all(x, axis, split_axis=0, concat_axis=0, tiled=True)]
    all_gather x1 -> x2, blocking collectives: 15.5 us -> 41.6 us  [the longest x1 33.3 us: shards(): total = lax.all_gather(share, 'dp', axis=0)[:, :chunk].astype(F32)]
    all_to_all x3 -> x5, starting transfers between devices: 21.2 us -> 35.3 us  [exchange(): return lax.all_to_all(x, axis, split_axis=0, concat_axis=0, tiled=True)]
    all_to_all x1 -> x0, blocking collectives: 12.6 us -> none  [exchange(): return lax.all_to_all(x, axis, split_axis=0, concat_axis=0, tiled=True)]
  transfers between devices with their start and end apart: 22 -> 23, of which waited for: 8 -> 10; matrix products, arithmetic and copies ran while one was open for 9% -> 12% of each run, Pallas kernels for 0% -> 0%
where the time goes in v5:
time: 272 us; the launch traced here: 270 us
  starting transfers between devices  107 us (39%)
  waiting for transfers between devices  62.9 us (23%)
  blocking collectives  41.6 us (15%)
  matrix products  20.4 us (7%)
  between operations  15.9 us (6%)
  local copies, waits for them, and re-layouts  14.6 us (5%)
  other arithmetic  7.41 us (3%)
    ppermute x16, starting transfers between devices, shift(): return lax.ppermute(x, 'dp', [(i, (i + by) % size) for i in range(size)])  71.5 us
    all_to_all x5, waiting for transfers between devices, exchange(): return lax.all_to_all(x, axis, split_axis=0, concat_axis=0, tiled=True)  49.4 us
    all_to_all x5, starting transfers between devices, exchange(): return lax.all_to_all(x, axis, split_axis=0, concat_axis=0, tiled=True)  35.3 us
    all_gather x1, blocking collectives, shards(): total = lax.all_gather(share, 'dp', axis=0)[:, :chunk].astype(F32)  33.3 us
    dot_general x9, matrix products, dot(): lax.dot_general(a, b, (contract, ((), ())), preferred_element_type=F32)  20.4 us
    ppermute x16, waiting for transfers between devices, shift(): return lax.ppermute(x, 'dp', [(i, (i + by) % size) for i in range(size)])  12.8 us
    all_gather x1, blocking collectives, shards(): group = lax.all_gather(group, 'tensor', axis=1)  8.33 us
    unnamed x19, local copies, waits for them, and re-layouts  6.42 us
  transfers between devices with their start and end apart: 23, of which 10 were waited for; matrix products, arithmetic and copies ran while one was open for 12% of the time, Pallas kernels for 0%

profile of v5, /device:TPU:24, one launch (start us, length us, event | category | flops | bytes accessed | tf_op | source)
XLA Modules:
  0.0 269.6 jit_solution(7543420874623375101)
XLA Ops:
  10.5 4.8 %all-to-all-start = ((bf16[4,64,1152]{2,1,0:T(8,128)(2,1)}), bf16[4,64,1152]{2,1,0:T(8,128)(2,1)S(1)}, u32[]{:S(2)}, u32[]{:S(2)}) async-start(bf16[4,64,1152]{2,1,0:T(8,128)(2,1)} %pad_maximum_fusion), calls=%async_computation | async-start | bytes 1179648 | tf_op jit(solution)/shard_map/all_to_all | solution.py:16
  16.0 7.1 %all-to-all-done = bf16[4,64,1152]{2,1,0:T(8,128)(2,1)S(1)} async-done(((bf16[4,64,1152]{2,1,0:T(8,128)(2,1)}), bf16[4,64,1152]{2,1,0:T(8,128)(2,1)S(1)}, u32[]{:S(2)}, u32[]{:S(2)}) %all-to-all-start) | async-done | bytes 589856 | tf_op jit(solution)/shard_map/all_to_all | solution.py:16
  26.3 12.7 %collective-permute-start.1 = (bf16[32,1152]{1,0:T(8,128)(2,1)S(1)}, bf16[32,1152]{1,0:T(8,128)(2,1)S(1)}, u32[]{:S(2)}, u32[]{:S(2)}) collective-permute-start(bf16[32,1152]{1,0:T(8,128)(2,1)S(1)} %get-tuple-element.27), channel_id=1, source_target_pairs={{0,384},{32,416},{64,448},{96,480},{128,0},{160,32},{192,64},{224,... | collective-permute-start | bytes 221192 | tf_op jit(solution)/shard_map/ppermute | solution.py:33
  42.6 7.7 %all-to-all-start.1 = ((bf16[32,32,1152]{2,1,0:T(8,128)(2,1)}), bf16[32,32,1152]{2,1,0:T(8,128)(2,1)}, u32[]{:S(2)}, u32[]{:S(2)}) async-start(bf16[32,32,1152]{2,1,0:T(8,128)(2,1)} %broadcast_in_dim.42), calls=%async_computation.1 | async-start | bytes 4718592 | tf_op jit(solution)/shard_map/all_to_all | solution.py:16
  51.1 7.8 %collective-permute-start.2 = (bf16[16,1152]{1,0:T(8,128)(2,1)S(1)}, bf16[16,1152]{1,0:T(8,128)(2,1)S(1)}, u32[]{:S(2)}, u32[]{:S(2)}) collective-permute-start(bf16[16,1152]{1,0:T(8,128)(2,1)S(1)} %slice.161), channel_id=1, source_target_pairs={{0,384},{32,416},{64,448},{96,480},{128,0},{160,32},{192,64},{224,... | collective-permute-start | bytes 110600 | tf_op jit(solution)/shard_map/ppermute | solution.py:33
  62.9 5.8 %collective-permute-done.3 = bf16[16,1152]{1,0:T(8,128)(2,1)S(1)} collective-permute-done((bf16[16,1152]{1,0:T(8,128)(2,1)S(1)}, bf16[16,1152]{1,0:T(8,128)(2,1)S(1)}, u32[]{:S(2)}, u32[]{:S(2)}) %collective-permute-start.3) | collective-permute-done | bytes 36896 | tf_op jit(solution)/shard_map/ppermute | solution.py:33
  68.8 2.9 %collective-permute-start.4 = (bf16[4,32,1152]{2,1,0:T(8,128)(2,1)S(1)}, bf16[4,32,1152]{2,1,0:T(8,128)(2,1)S(1)}, u32[]{:S(2)}, u32[]{:S(2)}) collective-permute-start(bf16[4,32,1152]{2,1,0:T(8,128)(2,1)S(1)} %pad_maximum_fusion.1), channel_id=1, source_target_pairs={{0,32},{32,64},{64,96},{96,128},{128,160},{160,192},{192,224},{224... | collective-permute-start | bytes 884744 | tf_op jit(solution)/shard_map/ppermute | solution.py:33
  71.7 4.1 %collective-permute-start.5 = (bf16[4,32,1152]{2,1,0:T(8,128)(2,1)S(1)}, bf16[4,32,1152]{2,1,0:T(8,128)(2,1)S(1)}, u32[]{:S(2)}, u32[]{:S(2)}) collective-permute-start(bf16[4,32,1152]{2,1,0:T(8,128)(2,1)S(1)} %pad_maximum_fusion.1), channel_id=1, source_target_pairs={{0,480},{32,0},{64,32},{96,64},{128,96},{160,128},{192,160},{224,1... | collective-permute-start | bytes 884744 | tf_op jit(solution)/shard_map/ppermute | solution.py:33
  75.9 3.8 %collective-permute-start.6 = (bf16[2,32,1152]{2,1,0:T(8,128)(2,1)S(1)}, bf16[2,32,1152]{2,1,0:T(8,128)(2,1)S(1)}, u32[]{:S(2)}, u32[]{:S(2)}) collective-permute-start(bf16[2,32,1152]{2,1,0:T(8,128)(2,1)S(1)} %get-tuple-element.42), channel_id=1, source_target_pairs={{0,448},{32,480},{64,0},{96,32},{128,64},{160,96},{192,128},{224,1... | collective-permute-start | bytes 442376 | tf_op jit(solution)/shard_map/ppermute | solution.py:33
  79.7 2.9 %collective-permute-start.7 = (bf16[2,32,1152]{2,1,0:T(8,128)(2,1)S(1)}, bf16[2,32,1152]{2,1,0:T(8,128)(2,1)S(1)}, u32[]{:S(2)}, u32[]{:S(2)}) collective-permute-start(bf16[2,32,1152]{2,1,0:T(8,128)(2,1)S(1)} %get-tuple-element.41), channel_id=1, source_target_pairs={{0,64},{32,96},{64,128},{96,160},{128,192},{160,224},{192,256},{22... | collective-permute-start | bytes 442376 | tf_op jit(solution)/shard_map/ppermute | solution.py:33
  91.2 4.2 %multiply_convert_fusion = bf16[1024,512]{1,0:T(8,128)(2,1)S(1)} fusion(bf16[1024,1152]{1,0:T(8,128)(2,1)} %bitcast.7, bf16[512,1152]{1,0:T(8,128)(2,1)} %bitcast.8, f32[]{:T(128)} %bitcast.91, f32[]{:T(128)} %bitcast, s32[512]{0:T(512)S(1)} %add_select_fusion), kind=kOutput, calls=%fused_computation.5 | convolution fusion | flops 1214251008 | bytes 4589576 | tf_op jit(solution)/shard_map/dot_general | solution.py:12
  95.3 4.2 %convolution_convert_fusion = bf16[1024,1152]{1,0:T(8,128)(2,1)} fusion(bf16[1024,512]{1,0:T(8,128)(2,1)S(1)} %multiply_convert_fusion, bf16[512,1152]{1,0:T(8,128)(2,1)} %bitcast.8), kind=kOutput, calls=%fused_computation.1 | convolution fusion | flops 1209139200 | bytes 4587520 | tf_op jit(solution)/shard_map/dot_general | solution.py:12
  99.6 3.2 %convolution_convert_fusion.1 = bf16[512,1152]{1,0:T(8,128)(2,1)S(1)} fusion(bf16[1024,512]{1,0:T(8,128)(2,1)S(1)} %multiply_convert_fusion, bf16[1024,1152]{1,0:T(8,128)(2,1)} %bitcast.7), kind=kOutput, calls=%fused_computation.2 | convolution fusion | flops 1208549376 | bytes 4587520 | tf_op jit(solution)/shard_map/dot_general | solution.py:12
  102.9 3.1 %collective-permute-start.8 = (bf16[4,32,1152]{2,1,0:T(8,128)(2,1)S(1)}, bf16[4,32,1152]{2,1,0:T(8,128)(2,1)S(1)}, u32[]{:S(2)}, u32[]{:S(2)}) collective-permute-start(bf16[4,32,1152]{2,1,0:T(8,128)(2,1)S(1)} %bitcast.111), channel_id=1, source_target_pairs={{0,480},{32,0},{64,32},{96,64},{128,96},{160,128},{192,160},{224,1... | collective-permute-start | bytes 884744 | tf_op jit(solution)/shard_map/ppermute | solution.py:33
  106.0 2.7 %collective-permute-start.9 = (bf16[4,32,1152]{2,1,0:T(8,128)(2,1)S(1)}, bf16[4,32,1152]{2,1,0:T(8,128)(2,1)}, u32[]{:S(2)}, u32[]{:S(2)}) collective-permute-start(bf16[4,32,1152]{2,1,0:T(8,128)(2,1)S(1)} %bitcast.110), channel_id=1, source_target_pairs={{0,32},{32,64},{64,96},{96,128},{128,160},{160,192},{192,224},{224... | collective-permute-start | bytes 884744 | tf_op jit(solution)/shard_map/ppermute | solution.py:33
  109.5 2.6 collective-permute-start.10
  112.1 5.3 %collective-permute-start.11 = (bf16[2,32,1152]{2,1,0:T(8,128)(2,1)}, bf16[2,32,1152]{2,1,0:T(8,128)(2,1)}, u32[]{:S(2)}, u32[]{:S(2)}) collective-permute-start(bf16[2,32,1152]{2,1,0:T(8,128)(2,1)} %bitcast.18), channel_id=1, source_target_pairs={{0,448},{32,480},{64,0},{96,32},{128,64},{160,96},{192,128},{224,1... | collective-permute-start | bytes 442376 | tf_op jit(solution)/shard_map/ppermute | solution.py:33
  117.5 7.4 %all-to-all-start.2 = ((bf16[32,32,1152]{2,1,0:T(8,128)(2,1)}), bf16[32,32,1152]{2,1,0:T(8,128)(2,1)}, u32[]{:S(2)}, u32[]{:S(2)}) async-start(bf16[32,32,1152]{2,1,0:T(8,128)(2,1)} %bitcast.94), calls=%async_computation.2 | async-start | bytes 4718592 | tf_op jit(solution)/shard_map/all_to_all | solution.py:16
  126.9 4.5 %collective-permute-start.12 = (bf16[16,1152]{1,0:T(8,128)(2,1)S(1)}, bf16[16,1152]{1,0:T(8,128)(2,1)S(1)}, u32[]{:S(2)}, u32[]{:S(2)}) collective-permute-start(bf16[16,1152]{1,0:T(8,128)(2,1)S(1)} %get-tuple-element.39), channel_id=1, source_target_pairs={{0,128},{32,160},{64,192},{96,224},{128,256},{160,288},{192,320},{... | collective-permute-start | bytes 110600 | tf_op jit(solution)/shard_map/ppermute | solution.py:33
  131.4 5.3 %collective-permute-start.14 = (bf16[16,1152]{1,0:T(8,128)(2,1)S(1)}, bf16[16,1152]{1,0:T(8,128)(2,1)S(1)}, u32[]{:S(2)}, u32[]{:S(2)}) collective-permute-start(bf16[16,1152]{1,0:T(8,128)(2,1)S(1)} %get-tuple-element.40), channel_id=1, source_target_pairs={{0,384},{32,416},{64,448},{96,480},{128,0},{160,32},{192,64},{224,... | collective-permute-start | bytes 110600 | tf_op jit(solution)/shard_map/ppermute | solution.py:33
  138.0 4.5 %collective-permute-start.13 = (bf16[32,1152]{1,0:T(8,128)(2,1)S(1)}, bf16[32,1152]{1,0:T(8,128)(2,1)S(1)}, u32[]{:S(2)}, u32[]{:S(2)}) collective-permute-start(bf16[32,1152]{1,0:T(8,128)(2,1)S(1)} %pad_maximum_fusion.5), channel_id=1, source_target_pairs={{0,128},{32,160},{64,192},{96,224},{128,256},{160,288},{192,320},{... | collective-permute-start | bytes 221192 | tf_op jit(solution)/shard_map/ppermute | solution.py:33
  142.5 5.3 %collective-permute-start.15 = (bf16[32,1152]{1,0:T(8,128)(2,1)S(1)}, bf16[32,1152]{1,0:T(8,128)(2,1)S(1)}, u32[]{:S(2)}, u32[]{:S(2)}) collective-permute-start(bf16[32,1152]{1,0:T(8,128)(2,1)S(1)} %pad_maximum_fusion.6), channel_id=1, source_target_pairs={{0,384},{32,416},{64,448},{96,480},{128,0},{160,32},{192,64},{224,... | collective-permute-start | bytes 221192 | tf_op jit(solution)/shard_map/ppermute | solution.py:33
  147.8 13.1 %all-to-all-done.2 = bf16[32,32,1152]{2,1,0:T(8,128)(2,1)} async-done(((bf16[32,32,1152]{2,1,0:T(8,128)(2,1)}), bf16[32,32,1152]{2,1,0:T(8,128)(2,1)}, u32[]{:S(2)}, u32[]{:S(2)}) %all-to-all-start.2) | async-done | bytes 2359328 | tf_op jit(solution)/shard_map/all_to_all | solution.py:16
  160.9 2.0 convert_reduce_fusion
  164.8 7.0 %all-to-all-start.3 = ((bf16[32,32,288]{2,1,0:T(8,128)(2,1)}), bf16[32,32,288]{2,1,0:T(8,128)(2,1)S(1)}, u32[]{:S(2)}, u32[]{:S(2)}) async-start(bf16[32,32,288]{2,1,0:T(8,128)(2,1)} %bitcast.26), calls=%async_computation.3 | async-start | bytes 1572864 | tf_op jit(solution)/shard_map/all_to_all | solution.py:16
  171.9 12.8 %all-to-all-done.3 = bf16[32,32,288]{2,1,0:T(8,128)(2,1)S(1)} async-done(((bf16[32,32,288]{2,1,0:T(8,128)(2,1)}), bf16[32,32,288]{2,1,0:T(8,128)(2,1)S(1)}, u32[]{:S(2)}, u32[]{:S(2)}) %all-to-all-start.3) | async-done | bytes 589856 | tf_op jit(solution)/shard_map/all_to_all | solution.py:16
  184.7 2.0 fusion.16
  186.8 2.0 fusion
  189.8 8.5 %all-to-all-start.4 = ((bf16[16,40,288]{2,1,0:T(8,128)(2,1)}), bf16[16,40,288]{2,1,0:T(8,128)(2,1)S(1)}, u32[]{:S(2)}, u32[]{:S(2)}) async-start(bf16[16,40,288]{2,1,0:T(8,128)(2,1)} %bitcast.36), calls=%async_computation.4 | async-start | bytes 983040 | tf_op jit(solution)/shard_map/all_to_all | solution.py:16
  198.3 8.3 %all-gather = bf16[2,128,1152]{2,1,0:T(8,128)(2,1)S(1)} all-gather(bf16[2,32,1152]{2,1,0:T(8,128)(2,1)S(1)} %pad_maximum_fusion.4), channel_id=2, replica_groups=mesh['dp'=16,'replica'=8,'tensor'=4] {'tensor'}, dimensions={1}, use_global_device_ids=true | all-gather | bytes 737280 | tf_op jit(solution)/shard_map/all_gather | solution.py:161
  209.0 16.3 %all-to-all-done.4 = bf16[16,40,288]{2,1,0:T(8,128)(2,1)S(1)} async-done(((bf16[16,40,288]{2,1,0:T(8,128)(2,1)}), bf16[16,40,288]{2,1,0:T(8,128)(2,1)S(1)}, u32[]{:S(2)}, u32[]{:S(2)}) %all-to-all-start.4) | async-done | bytes 368672 | tf_op jit(solution)/shard_map/all_to_all | solution.py:16
  225.3 33.3 %all-gather.1 = bf16[640,288]{1,0:T(8,128)(2,1)S(1)} all-gather(bf16[40,288]{1,0:T(8,128)(2,1)S(1)} %reduce_sum.72), channel_id=3, replica_groups=mesh['dp'=16,'replica'=8,'tensor'=4] {'dp'}, dimensions={0}, use_global_device_ids=true | all-gather | bytes 391680 | tf_op jit(solution)/shard_map/all_gather | solution.py:177
  (91 shorter events, 36.3 us)
Async XLA Ops:
  7.2 1.9 copy-start
  7.2 1.9 copy-start.3
  9.6 5.7 %copy-start.2 = (bf16[128,544]{0,1:T(8,128)(2,1)S(1)}, bf16[128,544]{0,1:T(8,128)(2,1)}, u32[]{:S(2)}) copy-start(bf16[128,544]{0,1:T(8,128)(2,1)} %param.9) | copy-start | bytes 417796
  10.5 12.7 %all-to-all-start = ((bf16[4,64,1152]{2,1,0:T(8,128)(2,1)}), bf16[4,64,1152]{2,1,0:T(8,128)(2,1)S(1)}, u32[]{:S(2)}, u32[]{:S(2)}) async-start(bf16[4,64,1152]{2,1,0:T(8,128)(2,1)} %pad_maximum_fusion), calls=%async_computation | async-start | bytes 1179648 | tf_op jit(solution)/shard_map/all_to_all | solution.py:16
  15.3 10.1 %copy-start.4 = (bf16[128,1152]{1,0:T(8,128)(2,1)S(1)}, bf16[128,1152]{1,0:T(8,128)(2,1)}, u32[]{:S(2)}) copy-start(bf16[128,1152]{1,0:T(8,128)(2,1)} %param.8) | copy-start | bytes 884740
  15.3 10.1 %copy-start.5 = (bf16[128,1152]{1,0:T(8,128)(2,1)S(1)}, bf16[128,1152]{1,0:T(8,128)(2,1)}, u32[]{:S(2)}) copy-start(bf16[128,1152]{1,0:T(8,128)(2,1)} %param.11) | copy-start | bytes 884740
  15.3 156.6 %all-gather.5.cloned.1.call-start = ((), (), s32[]{:S(2)}) async-start(), calls=%async_computation.5 | async-start | bytes 1474560 | tf_op jit(solution)/shard_map/all_gather | solution.py:123
  26.3 24.8 %collective-permute-start.1 = (bf16[32,1152]{1,0:T(8,128)(2,1)S(1)}, bf16[32,1152]{1,0:T(8,128)(2,1)S(1)}, u32[]{:S(2)}, u32[]{:S(2)}) collective-permute-start(bf16[32,1152]{1,0:T(8,128)(2,1)S(1)} %get-tuple-element.27), channel_id=1, source_target_pairs={{0,384},{32,416},{64,448},{96,480},{128,0},{160,32},{192,64},{224,... | collective-permute-start | bytes 221192 | tf_op jit(solution)/shard_map/ppermute | solution.py:33
  39.0 19.9 %collective-permute-start = (bf16[32,1152]{1,0:T(8,128)(2,1)S(1)}, bf16[32,1152]{1,0:T(8,128)(2,1)S(1)}, u32[]{:S(2)}, u32[]{:S(2)}) collective-permute-start(bf16[32,1152]{1,0:T(8,128)(2,1)S(1)} %get-tuple-element.27), channel_id=1, source_target_pairs={{0,128},{32,160},{64,192},{96,224},{128,256},{160,288},{192,320},{... | collective-permute-start | bytes 221192 | tf_op jit(solution)/shard_map/ppermute | solution.py:33
  42.6 48.5 %all-to-all-start.1 = ((bf16[32,32,1152]{2,1,0:T(8,128)(2,1)}), bf16[32,32,1152]{2,1,0:T(8,128)(2,1)}, u32[]{:S(2)}, u32[]{:S(2)}) async-start(bf16[32,32,1152]{2,1,0:T(8,128)(2,1)} %broadcast_in_dim.42), calls=%async_computation.1 | async-start | bytes 4718592 | tf_op jit(solution)/shard_map/all_to_all | solution.py:16
  50.3 136.4 %all-gather.7.cloned.1.call-start = ((), (), s32[]{:S(2)}) async-start(), calls=%async_computation.6 | async-start | bytes 1474560 | tf_op jit(solution)/shard_map/all_gather | solution.py:123
  51.1 11.9 %collective-permute-start.2 = (bf16[16,1152]{1,0:T(8,128)(2,1)S(1)}, bf16[16,1152]{1,0:T(8,128)(2,1)S(1)}, u32[]{:S(2)}, u32[]{:S(2)}) collective-permute-start(bf16[16,1152]{1,0:T(8,128)(2,1)S(1)} %slice.161), channel_id=1, source_target_pairs={{0,384},{32,416},{64,448},{96,480},{128,0},{160,32},{192,64},{224,... | collective-permute-start | bytes 110600 | tf_op jit(solution)/shard_map/ppermute | solution.py:33
  58.9 9.8 %collective-permute-start.3 = (bf16[16,1152]{1,0:T(8,128)(2,1)S(1)}, bf16[16,1152]{1,0:T(8,128)(2,1)S(1)}, u32[]{:S(2)}, u32[]{:S(2)}) collective-permute-start(bf16[16,1152]{1,0:T(8,128)(2,1)S(1)} %slice.162), channel_id=1, source_target_pairs={{0,128},{32,160},{64,192},{96,224},{128,256},{160,288},{192,320},{... | collective-permute-start | bytes 110600 | tf_op jit(solution)/shard_map/ppermute | solution.py:33
  68.8 15.1 %collective-permute-start.4 = (bf16[4,32,1152]{2,1,0:T(8,128)(2,1)S(1)}, bf16[4,32,1152]{2,1,0:T(8,128)(2,1)S(1)}, u32[]{:S(2)}, u32[]{:S(2)}) collective-permute-start(bf16[4,32,1152]{2,1,0:T(8,128)(2,1)S(1)} %pad_maximum_fusion.1), channel_id=1, source_target_pairs={{0,32},{32,64},{64,96},{96,128},{128,160},{160,192},{192,224},{224... | collective-permute-start | bytes 884744 | tf_op jit(solution)/shard_map/ppermute | solution.py:33
  71.7 13.8 %collective-permute-start.5 = (bf16[4,32,1152]{2,1,0:T(8,128)(2,1)S(1)}, bf16[4,32,1152]{2,1,0:T(8,128)(2,1)S(1)}, u32[]{:S(2)}, u32[]{:S(2)}) collective-permute-start(bf16[4,32,1152]{2,1,0:T(8,128)(2,1)S(1)} %pad_maximum_fusion.1), channel_id=1, source_target_pairs={{0,480},{32,0},{64,32},{96,64},{128,96},{160,128},{192,160},{224,1... | collective-permute-start | bytes 884744 | tf_op jit(solution)/shard_map/ppermute | solution.py:33
  75.9 12.2 %collective-permute-start.6 = (bf16[2,32,1152]{2,1,0:T(8,128)(2,1)S(1)}, bf16[2,32,1152]{2,1,0:T(8,128)(2,1)S(1)}, u32[]{:S(2)}, u32[]{:S(2)}) collective-permute-start(bf16[2,32,1152]{2,1,0:T(8,128)(2,1)S(1)} %get-tuple-element.42), channel_id=1, source_target_pairs={{0,448},{32,480},{64,0},{96,32},{128,64},{160,96},{192,128},{224,1... | collective-permute-start | bytes 442376 | tf_op jit(solution)/shard_map/ppermute | solution.py:33
  79.7 10.7 %collective-permute-start.7 = (bf16[2,32,1152]{2,1,0:T(8,128)(2,1)S(1)}, bf16[2,32,1152]{2,1,0:T(8,128)(2,1)S(1)}, u32[]{:S(2)}, u32[]{:S(2)}) collective-permute-start(bf16[2,32,1152]{2,1,0:T(8,128)(2,1)S(1)} %get-tuple-element.41), channel_id=1, source_target_pairs={{0,64},{32,96},{64,128},{96,160},{128,192},{160,224},{192,256},{22... | collective-permute-start | bytes 442376 | tf_op jit(solution)/shard_map/ppermute | solution.py:33
  102.9 21.9 %collective-permute-start.8 = (bf16[4,32,1152]{2,1,0:T(8,128)(2,1)S(1)}, bf16[4,32,1152]{2,1,0:T(8,128)(2,1)S(1)}, u32[]{:S(2)}, u32[]{:S(2)}) collective-permute-start(bf16[4,32,1152]{2,1,0:T(8,128)(2,1)S(1)} %bitcast.111), channel_id=1, source_target_pairs={{0,480},{32,0},{64,32},{96,64},{128,96},{160,128},{192,160},{224,1... | collective-permute-start | bytes 884744 | tf_op jit(solution)/shard_map/ppermute | solution.py:33
  106.0 18.8 %collective-permute-start.9 = (bf16[4,32,1152]{2,1,0:T(8,128)(2,1)S(1)}, bf16[4,32,1152]{2,1,0:T(8,128)(2,1)}, u32[]{:S(2)}, u32[]{:S(2)}) collective-permute-start(bf16[4,32,1152]{2,1,0:T(8,128)(2,1)S(1)} %bitcast.110), channel_id=1, source_target_pairs={{0,32},{32,64},{64,96},{96,128},{128,160},{160,192},{192,224},{224... | collective-permute-start | bytes 884744 | tf_op jit(solution)/shard_map/ppermute | solution.py:33
  109.5 16.4 %collective-permute-start.10 = (bf16[2,32,1152]{2,1,0:T(8,128)(2,1)}, bf16[2,32,1152]{2,1,0:T(8,128)(2,1)S(1)}, u32[]{:S(2)}, u32[]{:S(2)}) collective-permute-start(bf16[2,32,1152]{2,1,0:T(8,128)(2,1)} %bitcast.15), channel_id=1, source_target_pairs={{0,64},{32,96},{64,128},{96,160},{128,192},{160,224},{192,256},{22... | collective-permute-start | bytes 442376 | tf_op jit(solution)/shard_map/ppermute | solution.py:33
  112.1 13.8 %collective-permute-start.11 = (bf16[2,32,1152]{2,1,0:T(8,128)(2,1)}, bf16[2,32,1152]{2,1,0:T(8,128)(2,1)}, u32[]{:S(2)}, u32[]{:S(2)}) collective-permute-start(bf16[2,32,1152]{2,1,0:T(8,128)(2,1)} %bitcast.18), channel_id=1, source_target_pairs={{0,448},{32,480},{64,0},{96,32},{128,64},{160,96},{192,128},{224,1... | collective-permute-start | bytes 442376 | tf_op jit(solution)/shard_map/ppermute | solution.py:33
  117.5 43.5 %all-to-all-start.2 = ((bf16[32,32,1152]{2,1,0:T(8,128)(2,1)}), bf16[32,32,1152]{2,1,0:T(8,128)(2,1)}, u32[]{:S(2)}, u32[]{:S(2)}) async-start(bf16[32,32,1152]{2,1,0:T(8,128)(2,1)} %bitcast.94), calls=%async_computation.2 | async-start | bytes 4718592 | tf_op jit(solution)/shard_map/all_to_all | solution.py:16
  126.9 11.0 %collective-permute-start.12 = (bf16[16,1152]{1,0:T(8,128)(2,1)S(1)}, bf16[16,1152]{1,0:T(8,128)(2,1)S(1)}, u32[]{:S(2)}, u32[]{:S(2)}) collective-permute-start(bf16[16,1152]{1,0:T(8,128)(2,1)S(1)} %get-tuple-element.39), channel_id=1, source_target_pairs={{0,128},{32,160},{64,192},{96,224},{128,256},{160,288},{192,320},{... | collective-permute-start | bytes 110600 | tf_op jit(solution)/shard_map/ppermute | solution.py:33
  131.4 11.0 %collective-permute-start.14 = (bf16[16,1152]{1,0:T(8,128)(2,1)S(1)}, bf16[16,1152]{1,0:T(8,128)(2,1)S(1)}, u32[]{:S(2)}, u32[]{:S(2)}) collective-permute-start(bf16[16,1152]{1,0:T(8,128)(2,1)S(1)} %get-tuple-element.40), channel_id=1, source_target_pairs={{0,384},{32,416},{64,448},{96,480},{128,0},{160,32},{192,64},{224,... | collective-permute-start | bytes 110600 | tf_op jit(solution)/shard_map/ppermute | solution.py:33
  138.0 24.9 %collective-permute-start.13 = (bf16[32,1152]{1,0:T(8,128)(2,1)S(1)}, bf16[32,1152]{1,0:T(8,128)(2,1)S(1)}, u32[]{:S(2)}, u32[]{:S(2)}) collective-permute-start(bf16[32,1152]{1,0:T(8,128)(2,1)S(1)} %pad_maximum_fusion.5), channel_id=1, source_target_pairs={{0,128},{32,160},{64,192},{96,224},{128,256},{160,288},{192,320},{... | collective-permute-start | bytes 221192 | tf_op jit(solution)/shard_map/ppermute | solution.py:33
  142.5 20.4 %collective-permute-start.15 = (bf16[32,1152]{1,0:T(8,128)(2,1)S(1)}, bf16[32,1152]{1,0:T(8,128)(2,1)S(1)}, u32[]{:S(2)}, u32[]{:S(2)}) collective-permute-start(bf16[32,1152]{1,0:T(8,128)(2,1)S(1)} %pad_maximum_fusion.6), channel_id=1, source_target_pairs={{0,384},{32,416},{64,448},{96,480},{128,0},{160,32},{192,64},{224,... | collective-permute-start | bytes 221192 | tf_op jit(solution)/shard_map/ppermute | solution.py:33
  164.8 19.9 %all-to-all-start.3 = ((bf16[32,32,288]{2,1,0:T(8,128)(2,1)}), bf16[32,32,288]{2,1,0:T(8,128)(2,1)S(1)}, u32[]{:S(2)}, u32[]{:S(2)}) async-start(bf16[32,32,288]{2,1,0:T(8,128)(2,1)} %bitcast.26), calls=%async_computation.3 | async-start | bytes 1572864 | tf_op jit(solution)/shard_map/all_to_all | solution.py:16
  189.8 35.4 %all-to-all-start.4 = ((bf16[16,40,288]{2,1,0:T(8,128)(2,1)}), bf16[16,40,288]{2,1,0:T(8,128)(2,1)S(1)}, u32[]{:S(2)}, u32[]{:S(2)}) async-start(bf16[16,40,288]{2,1,0:T(8,128)(2,1)} %bitcast.36), calls=%async_computation.4 | async-start | bytes 983040 | tf_op jit(solution)/shard_map/all_to_all | solution.py:16
  198.3 9.5 %copy-start.1 = (bf16[544,1152]{1,0:T(8,128)(2,1)S(1)}, bf16[544,1152]{1,0:T(8,128)(2,1)}, u32[]{:S(2)}) copy-start(bf16[544,1152]{1,0:T(8,128)(2,1)} %param.10) | copy-start | bytes 3760132
Sparse Core Ops, SparseCore 0:
  23.4 65.5 all-gather.4
  91.6 63.5 all-gather.6

commit v6 on v4

--- a/solution.py
+++ b/solution.py
@@ -1,11 +1,16 @@
+import math
+
 import jax
 import jax.numpy as jnp
 from jax import lax
+from jax.sharding import Mesh
 from jax.sharding import PartitionSpec as P
 
 F32 = jnp.float32
 BF16 = jnp.bfloat16
 PLANE = ("replica", "tensor")
+DP = ("run", "place")
+LANES = 128
 
 
 def dot(a, b, contract):
@@ -25,37 +30,32 @@
     return lax.optimization_barrier((x,) + others)[0]
 
 
-OFFSETS = (0, -4, -8, -12, -1, -5, -9, -13, 1, -3, -7, -11, 2, -2, -6, -10)
-
-
 def shift(x, by):
-    size = lax.axis_size("dp")
-    return lax.ppermute(x, "dp", [(i, (i + by) % size) for i in range(size)])
+    size = lax.axis_size(DP)
+    return lax.ppermute(x, DP, [(i, (i + by) % size) for i in range(size)])
 
 
 def gather_dp(x):
-    half = x.shape[0] // 16 * 8
-    below = shift(x, 4)
-    above = shift(x, -4)
-    far = jnp.concatenate([shift(above[:half], -4), shift(below[half:], 4)], axis=0)
-    quad = jnp.stack([x, below, far, above])
+    quad = lax.all_gather(x, "run", axis=0)
     return jnp.concatenate(
-        [quad, shift(quad, 1), shift(quad, -1), shift(quad[0:2], -2), shift(quad[1:3], 2)],
+        [quad, shift(quad, 1), shift(quad, -1), shift(quad[0:2], -2), shift(quad[2:4], 2)],
         axis=0,
     )
 
 
 def scatter_dp(x):
     half = x.shape[1] // 16 * 8
+    run = lax.axis_index("run")
     one = shift(x[4:8], -1)
     two = shift(x[8:12], 1)
     three = shift(x[12:14], 2)
     four = shift(x[14:16], -2)
     quad = x[0:4].astype(F32) + one.astype(F32) + two.astype(F32)
-    near = quad[0] + three[0].astype(F32)
-    below = quad[1] + three[1].astype(F32) + four[0].astype(F32)
-    far = (quad[2] + four[1].astype(F32)).astype(BF16)
-    above = quad[3]
+    quad = quad + jnp.concatenate([three, four], axis=0).astype(F32)
+    near, above, far, below = (
+        lax.dynamic_index_in_dim(quad, (run + k) % 4, 0, keepdims=False) for k in range(4)
+    )
+    far = far.astype(BF16)
     above_half = shift(far[:half], 4).astype(F32)
     below_half = shift(far[half:], -4).astype(F32)
     above = jnp.concatenate([above[:half] + above_half, above[half:]], axis=0).astype(BF16)
@@ -85,7 +85,7 @@
     pair_logit_bias,
 ):
     rows, width = image_residual_input.shape
-    n_dp = lax.axis_size("dp")
+    n_dp = lax.axis_size(DP)
     n_replica = lax.axis_size("replica")
     n_tensor = lax.axis_size("tensor")
     replica = lax.axis_index("replica")
@@ -126,14 +126,18 @@
     logits = scale * dot(images, texts, ((1,), (1,))) + pair_logit_bias[0]
     image_index = jnp.arange(members * own, dtype=jnp.int32)
     position = jnp.arange(n_dp * own, dtype=jnp.int32)
-    text_index = jnp.where(position < own, (replica * n_tensor + tensor) * own + position, -1)
+    text_index = jnp.where(
+        position // own == lax.axis_index("run"),
+        (replica * n_tensor + tensor) * own + position % own,
+        -1,
+    )
     label = jnp.where(image_index[:, None] == text_index[None, :], 1.0, -1.0).astype(F32)
     coefficients = (-label * jax.nn.sigmoid(-label * logits) * scale).astype(BF16)
+    image_partial = dot(coefficients, texts, ((1,), (0,))).astype(BF16)
+    coefficients, image_partial = lax.optimization_barrier((coefficients, image_partial))
+    image_parts = exchange(image_partial.reshape(members, own, width), PLANE)
     text_partial = dot(coefficients, images, ((0,), (0,))).astype(BF16)
-    image_partial = dot(after(coefficients, text_partial), texts, ((1,), (0,))).astype(BF16)
-
     text_grad = scatter_dp(text_partial.reshape(n_dp, own, width))
-    image_parts = exchange(image_partial.reshape(members, own, width), PLANE)
     image_grad = jnp.sum(image_parts.astype(F32), axis=0)
 
     upstream_image = retract(normed_image, inverse_image, image_grad)
@@ -149,7 +153,8 @@
     cut = jnp.broadcast_to(cut[:, None], (n_replica, n_tensor, own, 2 * columns))
     cut = exchange(cut.reshape(members, own, 2 * columns), PLANE)
     cut = cut.reshape(members * own, 2 * columns)
-    group = lax.all_gather(jnp.stack([upstream_image, upstream_text]), "tensor", axis=1)
+    group = after(jnp.stack([upstream_image, upstream_text]), cut)
+    group = lax.all_gather(group, "tensor", axis=1)
     hidden_grad_image = dot(
         group[0].reshape(rows, width), image_output_weight, ((1,), (1,))
     ).astype(BF16)
@@ -157,32 +162,69 @@
         group[1].reshape(rows, width), text_output_weight, ((1,), (1,))
     ).astype(BF16)
 
-    partial = jnp.where(
-        jnp.arange(2 * columns)[None, :] < columns,
-        dot(hidden_image, cut, ((0,), (0,))),
-        dot(hidden_text, cut, ((0,), (0,))),
+    hidden = image_hidden_units.shape[1]
+    side = lax.axis_size("run")
+    partial = jnp.concatenate(
+        [
+            dot(cut, hidden_image, ((0,), (0,)))[:columns],
+            dot(cut, hidden_text, ((0,), (0,)))[columns:],
+        ],
+        axis=0,
     ).astype(BF16)
-    partial, hidden_grad_image, hidden_grad_text = lax.optimization_barrier(
-        (partial, hidden_grad_image, hidden_grad_text)
-    )
-    total = lax.psum(partial, "dp").astype(F32)
-    return (hidden_grad_image, hidden_grad_text, total[:, :columns], total[:, columns:])
+    pieces = exchange(pack(partial, side), DP)
+    share = jnp.sum(pieces.astype(F32), axis=0).astype(BF16)
+    total = unpack(spread(share, DP), side, hidden).astype(F32)
+    return (hidden_grad_image, hidden_grad_text, total[:columns].T, total[columns:].T)
+
+
+def pack(x, side):
+    high = x.shape[0] // side
+    low = high // (side - 1)
+    whole = x.shape[1] // LANES * LANES
+    left = x.shape[1] - whole
+    blocks = [
+        x[:, k * LANES : (k + 1) * LANES].reshape(side, high, LANES) for k in range(side)
+    ]
+    rest = jnp.pad(x[:, whole:], ((0, 0), (0, LANES - left))).reshape(side, high, LANES)
+    rests = [rest[:, k * low : (k + 1) * low] for k in range(side - 1)]
+    rests.append(jnp.zeros_like(rests[0]))
+    return jnp.concatenate(
+        [jnp.concatenate(blocks, axis=0), jnp.concatenate(rests, axis=0)], axis=1
+    )
+
+
+def unpack(x, side, lanes):
+    low = x.shape[1] // side
+    high = x.shape[1] - low
+    blocks = [
+        x[k * side : (k + 1) * side, :high].reshape(side * high, LANES) for k in range(side)
+    ]
+    rest = [x[k * side : (k + 1) * side, high:] for k in range(side - 1)]
+    rest = jnp.concatenate(rest, axis=1).reshape(side * high, LANES)
+    return jnp.concatenate(blocks + [rest[:, : lanes - side * LANES]], axis=1)
 
 
 def solution(mesh):
+    n_dp, n_replica, n_tensor = mesh.devices.shape
+    n_run = math.isqrt(n_dp)
+    mesh = Mesh(
+        mesh.devices.reshape(n_run, n_dp // n_run, n_replica, n_tensor),
+        ("run", "place", "replica", "tensor"),
+    )
+    rows = ("run", "place", "replica")
     in_specs = (
-        P(("dp", "replica"), None),
-        P(("dp", "replica"), "tensor"),
+        P(rows, None),
+        P(rows, "tensor"),
         P("tensor", None),
-        P(("dp", "replica"), None),
-        P(("dp", "replica"), "tensor"),
+        P(rows, None),
+        P(rows, "tensor"),
         P("tensor", None),
         P(),
         P(),
     )
     out_specs = (
-        P(("dp", "replica"), "tensor"),
-        P(("dp", "replica"), "tensor"),
+        P(rows, "tensor"),
+        P(rows, "tensor"),
         P("tensor", "replica"),
         P("tensor", "replica"),
     )

time: 335 us -> 251 us (0.75)
  waiting for transfers between devices: 160 us -> 48.1 us
  blocking collectives: 28.1 us -> 64.9 us
  starting transfers between devices: 92.7 us -> 86.1 us
    psum x1 -> x0, waiting for transfers between devices: 135 us -> none  [shards(): total = lax.psum(partial, 'dp').astype(F32)]
    all_to_all x3 -> x5, waiting for transfers between devices: 11.2 us -> 38.5 us  [exchange(): return lax.all_to_all(x, axis, split_axis=0, concat_axis=0, tiled=True)]
    ppermute x16 -> x12, starting transfers between devices: 71.5 us -> 47.9 us  [shift(): return lax.ppermute(x, DP, [(i, (i + by) % size) for i in range(size)])]
    all_to_all x1, blocking collectives: 12.6 us -> 32.4 us  [exchange(): return lax.all_to_all(x, axis, split_axis=0, concat_axis=0, tiled=True)]
    all_gather x1 -> x2, blocking collectives: 15.5 us -> 32.5 us  [the longest x1 24.1 us: gather_dp(): quad = lax.all_gather(x, 'run', axis=0)]
    all_to_all x3 -> x5, starting transfers between devices: 21.2 us -> 38.1 us  [exchange(): return lax.all_to_all(x, axis, split_axis=0, concat_axis=0, tiled=True)]
    ppermute x16 -> x12, waiting for transfers between devices: 12.8 us -> 8.71 us  [shift(): return lax.ppermute(x, DP, [(i, (i + by) % size) for i in range(size)])]
  transfers between devices with their start and end apart: 22 -> 19, of which waited for: 8 -> 9; matrix products, arithmetic and copies ran while one was open for 9% -> 10% of each run, Pallas kernels for 0% -> 0%
where the time goes in v6:
time: 251 us; the launch traced here: 249 us
  starting transfers between devices  86.1 us (34%)
  blocking collectives  64.9 us (26%)
  waiting for transfers between devices  48.1 us (19%)
  matrix products  19.3 us (8%)
  between operations  16 us (6%)
  local copies, waits for them, and re-layouts  9.55 us (4%)
  other arithmetic  5.24 us (2%)
    ppermute x12, starting transfers between devices, shift(): return lax.ppermute(x, DP, [(i, (i + by) % size) for i in range(size)])  47.9 us
    all_to_all x5, waiting for transfers between devices, exchange(): return lax.all_to_all(x, axis, split_axis=0, concat_axis=0, tiled=True)  38.5 us
    all_to_all x5, starting transfers between devices, exchange(): return lax.all_to_all(x, axis, split_axis=0, concat_axis=0, tiled=True)  38.1 us
    all_to_all x1, blocking collectives, exchange(): return lax.all_to_all(x, axis, split_axis=0, concat_axis=0, tiled=True)  32.4 us
    all_gather x1, blocking collectives, gather_dp(): quad = lax.all_gather(x, 'run', axis=0)  24.1 us
    dot_general x9, matrix products, dot(): lax.dot_general(a, b, (contract, ((), ())), preferred_element_type=F32)  19.3 us
    ppermute x12, waiting for transfers between devices, shift(): return lax.ppermute(x, DP, [(i, (i + by) % size) for i in range(size)])  8.71 us
    all_gather x1, blocking collectives, shards(): group = lax.all_gather(group, 'tensor', axis=1)  8.33 us
  transfers between devices with their start and end apart: 19, of which 9 were waited for; matrix products, arithmetic and copies ran while one was open for 10% of the time, Pallas kernels for 0%

profile of v6, /device:TPU:24, one launch (start us, length us, event | category | flops | bytes accessed | tf_op | source)
XLA Modules:
  0.0 249.0 jit_solution(5770217918052899190)
XLA Ops:
  7.2 1.9 convolution_convert_fusion.3
  10.5 4.9 %all-to-all-start = ((bf16[4,64,1152]{2,1,0:T(8,128)(2,1)}), bf16[4,64,1152]{2,1,0:T(8,128)(2,1)S(1)}, u32[]{:S(2)}, u32[]{:S(2)}) async-start(bf16[4,64,1152]{2,1,0:T(8,128)(2,1)} %pad_maximum_fusion), calls=%async_computation | async-start | bytes 1179648 | tf_op jit(solution)/shard_map/all_to_all | solution.py:21
  15.4 7.9 %all-to-all-done = bf16[4,64,1152]{2,1,0:T(8,128)(2,1)S(1)} async-done(((bf16[4,64,1152]{2,1,0:T(8,128)(2,1)}), bf16[4,64,1152]{2,1,0:T(8,128)(2,1)S(1)}, u32[]{:S(2)}, u32[]{:S(2)}) %all-to-all-start) | async-done | bytes 589856 | tf_op jit(solution)/shard_map/all_to_all | solution.py:21
  25.3 11.9 %all-to-all-start.1 = ((bf16[32,32,1152]{2,1,0:T(8,128)(2,1)}), bf16[32,32,1152]{2,1,0:T(8,128)(2,1)}, u32[]{:S(2)}, u32[]{:S(2)}) async-start(bf16[32,32,1152]{2,1,0:T(8,128)(2,1)} %broadcast_in_dim.20), calls=%async_computation.1 | async-start | bytes 4718592 | tf_op jit(solution)/shard_map/all_to_all | solution.py:21
  38.6 24.1 %all-gather = bf16[128,1152]{1,0:T(8,128)(2,1)S(1)} all-gather(bf16[32,1152]{1,0:T(8,128)(2,1)S(1)} %get-tuple-element.48), channel_id=2, replica_groups=mesh['run'=4,'place'=4,'replica'=8,'tensor'=4] {'run'}, dimensions={0}, use_global_device_ids=true | all-gather | bytes 368640 | tf_op jit(solution)/shard_map/all_gather | solution.py:39
  62.7 2.2 collective-permute-start
  65.0 4.8 %collective-permute-start.1 = (bf16[4,32,1152]{2,1,0:T(8,128)(2,1)S(1)}, bf16[4,32,1152]{2,1,0:T(8,128)(2,1)S(1)}, u32[]{:S(2)}, u32[]{:S(2)}) collective-permute-start(bf16[4,32,1152]{2,1,0:T(8,128)(2,1)S(1)} %bitcast.88), channel_id=1, source_target_pairs={{0,480},{32,0},{64,32},{96,64},{128,96},{160,128},{192,160},{224,1... | collective-permute-start | bytes 884744 | tf_op jit(solution)/shard_map/ppermute | solution.py:35
  70.6 2.2 collective-permute-start.2
  72.8 4.6 %collective-permute-start.3 = (bf16[2,32,1152]{2,1,0:T(8,128)(2,1)S(1)}, bf16[2,32,1152]{2,1,0:T(8,128)(2,1)S(1)}, u32[]{:S(2)}, u32[]{:S(2)}) collective-permute-start(bf16[2,32,1152]{2,1,0:T(8,128)(2,1)S(1)} %bitcast.110), channel_id=1, source_target_pairs={{0,64},{32,96},{64,128},{96,160},{128,192},{160,224},{192,256},{22... | collective-permute-start | bytes 442376 | tf_op jit(solution)/shard_map/ppermute | solution.py:35
  83.2 4.3 %multiply_convert_fusion = bf16[1024,512]{1,0:T(8,128)(2,1)S(1)} fusion(bf16[1024,1152]{1,0:T(8,128)(2,1)} %bitcast.6, bf16[512,1152]{1,0:T(8,128)(2,1)} %bitcast.112, f32[]{:T(128)} %bitcast.86, f32[]{:T(128)} %bitcast, s32[512]{0:T(512)S(1)} %fusion.22), kind=kOutput, calls=%fused_computation.5 | convolution fusion | flops 1214251008 | bytes 4589576 | tf_op jit(solution)/shard_map/dot_general | solution.py:17
  87.5 3.0 %convolution_convert_fusion = bf16[1024,1152]{1,0:T(8,128)(2,1)} fusion(bf16[1024,512]{1,0:T(8,128)(2,1)S(1)} %multiply_convert_fusion, bf16[512,1152]{1,0:T(8,128)(2,1)S(1)} %bitcast.113), kind=kOutput, calls=%fused_computation.1 | convolution fusion | flops 1209139200 | bytes 4587520 | tf_op jit(solution)/shard_map/dot_general | solution.py:17
  90.4 3.2 %convolution_convert_fusion.1 = bf16[512,1152]{1,0:T(8,128)(2,1)S(1)} fusion(bf16[1024,512]{1,0:T(8,128)(2,1)S(1)} %multiply_convert_fusion, bf16[1024,1152]{1,0:T(8,128)(2,1)} %bitcast.6), kind=kOutput, calls=%fused_computation.2 | convolution fusion | flops 1208549376 | bytes 4587520 | tf_op jit(solution)/shard_map/dot_general | solution.py:17
  93.8 2.7 %collective-permute-start.4 = (bf16[4,32,1152]{2,1,0:T(8,128)(2,1)S(1)}, bf16[4,32,1152]{2,1,0:T(8,128)(2,1)S(1)}, u32[]{:S(2)}, u32[]{:S(2)}) collective-permute-start(bf16[4,32,1152]{2,1,0:T(8,128)(2,1)S(1)} %bitcast.108), channel_id=1, source_target_pairs={{0,480},{32,0},{64,32},{96,64},{128,96},{160,128},{192,160},{224,1... | collective-permute-start | bytes 884744 | tf_op jit(solution)/shard_map/ppermute | solution.py:35
  96.5 3.8 %collective-permute-start.5 = (bf16[4,32,1152]{2,1,0:T(8,128)(2,1)S(1)}, bf16[4,32,1152]{2,1,0:T(8,128)(2,1)S(1)}, u32[]{:S(2)}, u32[]{:S(2)}) collective-permute-start(bf16[4,32,1152]{2,1,0:T(8,128)(2,1)S(1)} %bitcast.107), channel_id=1, source_target_pairs={{0,32},{32,64},{64,96},{96,128},{128,160},{160,192},{192,224},{224... | collective-permute-start | bytes 884744 | tf_op jit(solution)/shard_map/ppermute | solution.py:35
  101.1 3.4 %collective-permute-start.6 = (bf16[2,32,1152]{2,1,0:T(8,128)(2,1)}, bf16[2,32,1152]{2,1,0:T(8,128)(2,1)S(1)}, u32[]{:S(2)}, u32[]{:S(2)}) collective-permute-start(bf16[2,32,1152]{2,1,0:T(8,128)(2,1)} %bitcast.14), channel_id=1, source_target_pairs={{0,64},{32,96},{64,128},{96,160},{128,192},{160,224},{192,256},{22... | collective-permute-start | bytes 442376 | tf_op jit(solution)/shard_map/ppermute | solution.py:35
  104.4 4.6 %collective-permute-start.7 = (bf16[2,32,1152]{2,1,0:T(8,128)(2,1)}, bf16[2,32,1152]{2,1,0:T(8,128)(2,1)}, u32[]{:S(2)}, u32[]{:S(2)}) collective-permute-start(bf16[2,32,1152]{2,1,0:T(8,128)(2,1)} %bitcast.15), channel_id=1, source_target_pairs={{0,448},{32,480},{64,0},{96,32},{128,64},{160,96},{192,128},{224,1... | collective-permute-start | bytes 442376 | tf_op jit(solution)/shard_map/ppermute | solution.py:35
  109.1 7.4 %all-to-all-start.2 = ((bf16[32,32,1152]{2,1,0:T(8,128)(2,1)}), bf16[32,32,1152]{2,1,0:T(8,128)(2,1)}, u32[]{:S(2)}, u32[]{:S(2)}) async-start(bf16[32,32,1152]{2,1,0:T(8,128)(2,1)} %bitcast.90), calls=%async_computation.2 | async-start | bytes 4718592 | tf_op jit(solution)/shard_map/all_to_all | solution.py:21
  117.6 4.9 %collective-permute-start.10 = (bf16[16,1152]{1,0:T(8,128)(2,1)S(1)}, bf16[16,1152]{1,0:T(8,128)(2,1)S(1)}, u32[]{:S(2)}, u32[]{:S(2)}) collective-permute-start(bf16[16,1152]{1,0:T(8,128)(2,1)S(1)} %get-tuple-element.55), channel_id=1, source_target_pairs={{0,384},{32,416},{64,448},{96,480},{128,0},{160,32},{192,64},{224,... | collective-permute-start | bytes 110600 | tf_op jit(solution)/shard_map/ppermute | solution.py:35
  122.5 4.9 %collective-permute-start.8 = (bf16[16,1152]{1,0:T(8,128)(2,1)S(1)}, bf16[16,1152]{1,0:T(8,128)(2,1)S(1)}, u32[]{:S(2)}, u32[]{:S(2)}) collective-permute-start(bf16[16,1152]{1,0:T(8,128)(2,1)S(1)} %get-tuple-element.54), channel_id=1, source_target_pairs={{0,128},{32,160},{64,192},{96,224},{128,256},{160,288},{192,320},{... | collective-permute-start | bytes 110600 | tf_op jit(solution)/shard_map/ppermute | solution.py:35
  128.8 4.4 %collective-permute-done.8 = bf16[16,1152]{1,0:T(8,128)(2,1)S(1)} collective-permute-done((bf16[16,1152]{1,0:T(8,128)(2,1)S(1)}, bf16[16,1152]{1,0:T(8,128)(2,1)S(1)}, u32[]{:S(2)}, u32[]{:S(2)}) %collective-permute-start.8) | collective-permute-done | bytes 36896 | tf_op jit(solution)/shard_map/ppermute | solution.py:35
  133.3 4.9 %collective-permute-start.9 = (bf16[32,1152]{1,0:T(8,128)(2,1)S(1)}, bf16[32,1152]{1,0:T(8,128)(2,1)S(1)}, u32[]{:S(2)}, u32[]{:S(2)}) collective-permute-start(bf16[32,1152]{1,0:T(8,128)(2,1)S(1)} %pad_maximum_fusion.2), channel_id=1, source_target_pairs={{0,128},{32,160},{64,192},{96,224},{128,256},{160,288},{192,320},{... | collective-permute-start | bytes 221192 | tf_op jit(solution)/shard_map/ppermute | solution.py:35
  138.2 5.0 %collective-permute-start.11 = (bf16[32,1152]{1,0:T(8,128)(2,1)S(1)}, bf16[32,1152]{1,0:T(8,128)(2,1)S(1)}, u32[]{:S(2)}, u32[]{:S(2)}) collective-permute-start(bf16[32,1152]{1,0:T(8,128)(2,1)S(1)} %pad_maximum_fusion.3), channel_id=1, source_target_pairs={{0,384},{32,416},{64,448},{96,480},{128,0},{160,32},{192,64},{224,... | collective-permute-start | bytes 221192 | tf_op jit(solution)/shard_map/ppermute | solution.py:35
  143.2 4.9 %all-to-all-done.2 = bf16[32,32,1152]{2,1,0:T(8,128)(2,1)} async-done(((bf16[32,32,1152]{2,1,0:T(8,128)(2,1)}), bf16[32,32,1152]{2,1,0:T(8,128)(2,1)}, u32[]{:S(2)}, u32[]{:S(2)}) %all-to-all-start.2) | async-done | bytes 2359328 | tf_op jit(solution)/shard_map/all_to_all | solution.py:21
  148.1 2.0 convert_reduce_fusion
  152.0 7.2 %all-to-all-start.3 = ((bf16[32,32,288]{2,1,0:T(8,128)(2,1)}), bf16[32,32,288]{2,1,0:T(8,128)(2,1)S(1)}, u32[]{:S(2)}, u32[]{:S(2)}) async-start(bf16[32,32,288]{2,1,0:T(8,128)(2,1)} %bitcast.25), calls=%async_computation.3 | async-start | bytes 1572864 | tf_op jit(solution)/shard_map/all_to_all | solution.py:21
  159.3 15.8 %all-to-all-done.3 = bf16[32,32,288]{2,1,0:T(8,128)(2,1)S(1)} async-done(((bf16[32,32,288]{2,1,0:T(8,128)(2,1)}), bf16[32,32,288]{2,1,0:T(8,128)(2,1)S(1)}, u32[]{:S(2)}, u32[]{:S(2)}) %all-to-all-start.3) | async-done | bytes 589856 | tf_op jit(solution)/shard_map/all_to_all | solution.py:21
  175.1 2.1 fusion.33
  178.1 2.1 fusion.32
  180.5 32.4 %all_to_all.30 = bf16[16,96,128]{2,1,0:T(8,128)(2,1)S(1)} all-to-all(bf16[16,96,128]{2,1,0:T(8,128)(2,1)S(1)} %maximum_maximum_fusion), channel_id=1, replica_groups=mesh['run'=4,'place'=4,'replica'=8,'tensor'=4] {'run','place'}, dimensions={0} | all-to-all | bytes 786432 | tf_op jit(solution)/shard_map/all_to_all | solution.py:21
  213.8 6.6 %all-to-all-start.5 = ((bf16[16,96,128]{2,1,0:T(8,128)(2,1)}), bf16[16,96,128]{2,1,0:T(8,128)(2,1)S(1)}, u32[]{:S(2)}, u32[]{:S(2)}) async-start(bf16[16,96,128]{2,1,0:T(8,128)(2,1)} %broadcast_in_dim.23), calls=%async_computation.5 | async-start | bytes 786432 | tf_op jit(solution)/shard_map/all_to_all | solution.py:21
  220.5 8.3 %all-gather.1 = bf16[2,128,1152]{2,1,0:T(8,128)(2,1)S(1)} all-gather(bf16[2,32,1152]{2,1,0:T(8,128)(2,1)S(1)} %pad_maximum_fusion.1), channel_id=3, replica_groups=mesh['run'=4,'place'=4,'replica'=8,'tensor'=4] {'tensor'}, dimensions={1}, use_global_device_ids=true | all-gather | bytes 737280 | tf_op jit(solution)/shard_map/all_gather | solution.py:157
  231.1 9.9 %all-to-all-done.5 = bf16[16,96,128]{2,1,0:T(8,128)(2,1)S(1)} async-done(((bf16[16,96,128]{2,1,0:T(8,128)(2,1)}), bf16[16,96,128]{2,1,0:T(8,128)(2,1)S(1)}, u32[]{:S(2)}, u32[]{:S(2)}) %all-to-all-start.5) | async-done | bytes 393248 | tf_op jit(solution)/shard_map/all_to_all | solution.py:21
  (84 shorter events, 20.8 us)
Async XLA Ops:
  7.2 1.9 copy-start
  7.2 1.9 copy-start.2
  10.5 12.9 %copy-start.3 = (bf16[128,1152]{1,0:T(8,128)(2,1)S(1)}, bf16[128,1152]{1,0:T(8,128)(2,1)}, u32[]{:S(2)}) copy-start(bf16[128,1152]{1,0:T(8,128)(2,1)} %param.8) | copy-start | bytes 884740
  10.5 12.9 %copy-start.4 = (bf16[128,1152]{1,0:T(8,128)(2,1)S(1)}, bf16[128,1152]{1,0:T(8,128)(2,1)}, u32[]{:S(2)}) copy-start(bf16[128,1152]{1,0:T(8,128)(2,1)} %param.11) | copy-start | bytes 884740
  10.5 12.8 %all-to-all-start = ((bf16[4,64,1152]{2,1,0:T(8,128)(2,1)}), bf16[4,64,1152]{2,1,0:T(8,128)(2,1)S(1)}, u32[]{:S(2)}, u32[]{:S(2)}) async-start(bf16[4,64,1152]{2,1,0:T(8,128)(2,1)} %pad_maximum_fusion), calls=%async_computation | async-start | bytes 1179648 | tf_op jit(solution)/shard_map/all_to_all | solution.py:21
  25.3 57.9 %all-to-all-start.1 = ((bf16[32,32,1152]{2,1,0:T(8,128)(2,1)}), bf16[32,32,1152]{2,1,0:T(8,128)(2,1)}, u32[]{:S(2)}, u32[]{:S(2)}) async-start(bf16[32,32,1152]{2,1,0:T(8,128)(2,1)} %broadcast_in_dim.20), calls=%async_computation.1 | async-start | bytes 4718592 | tf_op jit(solution)/shard_map/all_to_all | solution.py:21
  37.2 122.1 %all-gather.7.cloned.1.call-start = ((), (), s32[]{:S(2)}) async-start(), calls=%async_computation.7 | async-start | bytes 1253376 | tf_op jit(solution)/shard_map/all_gather | solution.py:115
  62.7 14.7 %collective-permute-start = (bf16[4,32,1152]{2,1,0:T(8,128)(2,1)S(1)}, bf16[4,32,1152]{2,1,0:T(8,128)(2,1)S(1)}, u32[]{:S(2)}, u32[]{:S(2)}) collective-permute-start(bf16[4,32,1152]{2,1,0:T(8,128)(2,1)S(1)} %bitcast.87), channel_id=1, source_target_pairs={{0,32},{32,64},{64,96},{96,128},{128,160},{160,192},{192,224},{224... | collective-permute-start | bytes 884744 | tf_op jit(solution)/shard_map/ppermute | solution.py:35
  65.0 13.2 %collective-permute-start.1 = (bf16[4,32,1152]{2,1,0:T(8,128)(2,1)S(1)}, bf16[4,32,1152]{2,1,0:T(8,128)(2,1)S(1)}, u32[]{:S(2)}, u32[]{:S(2)}) collective-permute-start(bf16[4,32,1152]{2,1,0:T(8,128)(2,1)S(1)} %bitcast.88), channel_id=1, source_target_pairs={{0,480},{32,0},{64,32},{96,64},{128,96},{160,128},{192,160},{224,1... | collective-permute-start | bytes 884744 | tf_op jit(solution)/shard_map/ppermute | solution.py:35
  70.6 10.1 %collective-permute-start.2 = (bf16[2,32,1152]{2,1,0:T(8,128)(2,1)S(1)}, bf16[2,32,1152]{2,1,0:T(8,128)(2,1)S(1)}, u32[]{:S(2)}, u32[]{:S(2)}) collective-permute-start(bf16[2,32,1152]{2,1,0:T(8,128)(2,1)S(1)} %bitcast.111), channel_id=1, source_target_pairs={{0,448},{32,480},{64,0},{96,32},{128,64},{160,96},{192,128},{224,1... | collective-permute-start | bytes 442376 | tf_op jit(solution)/shard_map/ppermute | solution.py:35
  72.8 9.8 %collective-permute-start.3 = (bf16[2,32,1152]{2,1,0:T(8,128)(2,1)S(1)}, bf16[2,32,1152]{2,1,0:T(8,128)(2,1)S(1)}, u32[]{:S(2)}, u32[]{:S(2)}) collective-permute-start(bf16[2,32,1152]{2,1,0:T(8,128)(2,1)S(1)} %bitcast.110), channel_id=1, source_target_pairs={{0,64},{32,96},{64,128},{96,160},{128,192},{160,224},{192,256},{22... | collective-permute-start | bytes 442376 | tf_op jit(solution)/shard_map/ppermute | solution.py:35
  77.4 100.7 %all-gather.5.cloned.1.call-start = ((), (), s32[]{:S(2)}) async-start(), calls=%async_computation.6 | async-start | bytes 1253376 | tf_op jit(solution)/shard_map/all_gather | solution.py:115
  83.2 4.3 %copy-start.6 = (bf16[16,32,1152]{2,1,0:T(8,128)(2,1)S(1)}, bf16[16,32,1152]{2,1,0:T(8,128)(2,1)}, u32[]{:S(2)}) copy-start(bf16[16,32,1152]{2,1,0:T(8,128)(2,1)} %constant_dynamic-update-slice_fusion) | copy-start | bytes 3538948
  93.8 22.8 %collective-permute-start.4 = (bf16[4,32,1152]{2,1,0:T(8,128)(2,1)S(1)}, bf16[4,32,1152]{2,1,0:T(8,128)(2,1)S(1)}, u32[]{:S(2)}, u32[]{:S(2)}) collective-permute-start(bf16[4,32,1152]{2,1,0:T(8,128)(2,1)S(1)} %bitcast.108), channel_id=1, source_target_pairs={{0,480},{32,0},{64,32},{96,64},{128,96},{160,128},{192,160},{224,1... | collective-permute-start | bytes 884744 | tf_op jit(solution)/shard_map/ppermute | solution.py:35
  96.5 20.1 %collective-permute-start.5 = (bf16[4,32,1152]{2,1,0:T(8,128)(2,1)S(1)}, bf16[4,32,1152]{2,1,0:T(8,128)(2,1)S(1)}, u32[]{:S(2)}, u32[]{:S(2)}) collective-permute-start(bf16[4,32,1152]{2,1,0:T(8,128)(2,1)S(1)} %bitcast.107), channel_id=1, source_target_pairs={{0,32},{32,64},{64,96},{96,128},{128,160},{160,192},{192,224},{224... | collective-permute-start | bytes 884744 | tf_op jit(solution)/shard_map/ppermute | solution.py:35
  101.1 15.4 %collective-permute-start.6 = (bf16[2,32,1152]{2,1,0:T(8,128)(2,1)}, bf16[2,32,1152]{2,1,0:T(8,128)(2,1)S(1)}, u32[]{:S(2)}, u32[]{:S(2)}) collective-permute-start(bf16[2,32,1152]{2,1,0:T(8,128)(2,1)} %bitcast.14), channel_id=1, source_target_pairs={{0,64},{32,96},{64,128},{96,160},{128,192},{160,224},{192,256},{22... | collective-permute-start | bytes 442376 | tf_op jit(solution)/shard_map/ppermute | solution.py:35
  104.4 12.1 %collective-permute-start.7 = (bf16[2,32,1152]{2,1,0:T(8,128)(2,1)}, bf16[2,32,1152]{2,1,0:T(8,128)(2,1)}, u32[]{:S(2)}, u32[]{:S(2)}) collective-permute-start(bf16[2,32,1152]{2,1,0:T(8,128)(2,1)} %bitcast.15), channel_id=1, source_target_pairs={{0,448},{32,480},{64,0},{96,32},{128,64},{160,96},{192,128},{224,1... | collective-permute-start | bytes 442376 | tf_op jit(solution)/shard_map/ppermute | solution.py:35
  109.1 39.0 %all-to-all-start.2 = ((bf16[32,32,1152]{2,1,0:T(8,128)(2,1)}), bf16[32,32,1152]{2,1,0:T(8,128)(2,1)}, u32[]{:S(2)}, u32[]{:S(2)}) async-start(bf16[32,32,1152]{2,1,0:T(8,128)(2,1)} %bitcast.90), calls=%async_computation.2 | async-start | bytes 4718592 | tf_op jit(solution)/shard_map/all_to_all | solution.py:21
  117.6 11.2 %collective-permute-start.10 = (bf16[16,1152]{1,0:T(8,128)(2,1)S(1)}, bf16[16,1152]{1,0:T(8,128)(2,1)S(1)}, u32[]{:S(2)}, u32[]{:S(2)}) collective-permute-start(bf16[16,1152]{1,0:T(8,128)(2,1)S(1)} %get-tuple-element.55), channel_id=1, source_target_pairs={{0,384},{32,416},{64,448},{96,480},{128,0},{160,32},{192,64},{224,... | collective-permute-start | bytes 110600 | tf_op jit(solution)/shard_map/ppermute | solution.py:35
  122.5 10.7 %collective-permute-start.8 = (bf16[16,1152]{1,0:T(8,128)(2,1)S(1)}, bf16[16,1152]{1,0:T(8,128)(2,1)S(1)}, u32[]{:S(2)}, u32[]{:S(2)}) collective-permute-start(bf16[16,1152]{1,0:T(8,128)(2,1)S(1)} %get-tuple-element.54), channel_id=1, source_target_pairs={{0,128},{32,160},{64,192},{96,224},{128,256},{160,288},{192,320},{... | collective-permute-start | bytes 110600 | tf_op jit(solution)/shard_map/ppermute | solution.py:35
  133.3 16.8 %collective-permute-start.9 = (bf16[32,1152]{1,0:T(8,128)(2,1)S(1)}, bf16[32,1152]{1,0:T(8,128)(2,1)S(1)}, u32[]{:S(2)}, u32[]{:S(2)}) collective-permute-start(bf16[32,1152]{1,0:T(8,128)(2,1)S(1)} %pad_maximum_fusion.2), channel_id=1, source_target_pairs={{0,128},{32,160},{64,192},{96,224},{128,256},{160,288},{192,320},{... | collective-permute-start | bytes 221192 | tf_op jit(solution)/shard_map/ppermute | solution.py:35
  138.2 11.9 %copy-start.5 = (bf16[128,1152]{1,0:T(8,128)(2,1)S(1)}, bf16[128,1152]{1,0:T(8,128)(2,1)}, u32[]{:S(2)}) copy-start(bf16[128,1152]{1,0:T(8,128)(2,1)} %param.11) | copy-start | bytes 884740
  138.2 11.9 %collective-permute-start.11 = (bf16[32,1152]{1,0:T(8,128)(2,1)S(1)}, bf16[32,1152]{1,0:T(8,128)(2,1)S(1)}, u32[]{:S(2)}, u32[]{:S(2)}) collective-permute-start(bf16[32,1152]{1,0:T(8,128)(2,1)S(1)} %pad_maximum_fusion.3), channel_id=1, source_target_pairs={{0,384},{32,416},{64,448},{96,480},{128,0},{160,32},{192,64},{224,... | collective-permute-start | bytes 221192 | tf_op jit(solution)/shard_map/ppermute | solution.py:35
  152.0 23.1 %all-to-all-start.3 = ((bf16[32,32,288]{2,1,0:T(8,128)(2,1)}), bf16[32,32,288]{2,1,0:T(8,128)(2,1)S(1)}, u32[]{:S(2)}, u32[]{:S(2)}) async-start(bf16[32,32,288]{2,1,0:T(8,128)(2,1)} %bitcast.25), calls=%async_computation.3 | async-start | bytes 1572864 | tf_op jit(solution)/shard_map/all_to_all | solution.py:21
  213.8 27.2 %all-to-all-start.5 = ((bf16[16,96,128]{2,1,0:T(8,128)(2,1)}), bf16[16,96,128]{2,1,0:T(8,128)(2,1)S(1)}, u32[]{:S(2)}, u32[]{:S(2)}) async-start(bf16[16,96,128]{2,1,0:T(8,128)(2,1)} %broadcast_in_dim.23), calls=%async_computation.5 | async-start | bytes 786432 | tf_op jit(solution)/shard_map/all_to_all | solution.py:21
  220.5 9.5 %copy-start.1 = (bf16[544,1152]{1,0:T(8,128)(2,1)S(1)}, bf16[544,1152]{1,0:T(8,128)(2,1)}, u32[]{:S(2)}) copy-start(bf16[544,1152]{1,0:T(8,128)(2,1)} %param.10) | copy-start | bytes 3760132
Sparse Core Ops, SparseCore 0:
  77.5 40.9 all-gather.6
  120.5 57.4 all-gather.4

commit v7 on v6

--- a/solution.py
+++ b/solution.py
@@ -43,7 +43,7 @@
     )
 
 
-def scatter_dp(x):
+def scatter_dp(x, meanwhile):
     half = x.shape[1] // 16 * 8
     run = lax.axis_index("run")
     one = shift(x[4:8], -1)
@@ -60,7 +60,9 @@
     below_half = shift(far[half:], -4).astype(F32)
     above = jnp.concatenate([above[:half] + above_half, above[half:]], axis=0).astype(BF16)
     below = jnp.concatenate([below[:half], below[half:] + below_half], axis=0).astype(BF16)
-    return near + shift(above, 4).astype(F32) + shift(below, -4).astype(F32)
+    above, below, meanwhile = lax.optimization_barrier((above, below, meanwhile))
+    total = near + shift(above, 4).astype(F32) + shift(below, -4).astype(F32)
+    return (total, meanwhile)
 
 
 def normalize(residual, summed):
@@ -137,8 +139,10 @@
     coefficients, image_partial = lax.optimization_barrier((coefficients, image_partial))
     image_parts = exchange(image_partial.reshape(members, own, width), PLANE)
     text_partial = dot(coefficients, images, ((0,), (0,))).astype(BF16)
-    text_grad = scatter_dp(text_partial.reshape(n_dp, own, width))
+    text_partial, hidden_text = lax.optimization_barrier((text_partial, hidden_text))
+    text_grad, image_parts = scatter_dp(text_partial.reshape(n_dp, own, width), image_parts)
     image_grad = jnp.sum(image_parts.astype(F32), axis=0)
+    image_grad, hidden_image = lax.optimization_barrier((image_grad, hidden_image))
 
     upstream_image = retract(normed_image, inverse_image, image_grad)
     upstream_text = retract(normed_text, inverse_text, text_grad)
@@ -178,30 +182,27 @@
 
 
 def pack(x, side):
+    size = side * side
     high = x.shape[0] // side
-    low = high // (side - 1)
-    whole = x.shape[1] // LANES * LANES
-    left = x.shape[1] - whole
+    whole = side * LANES
     blocks = [
         x[:, k * LANES : (k + 1) * LANES].reshape(side, high, LANES) for k in range(side)
     ]
-    rest = jnp.pad(x[:, whole:], ((0, 0), (0, LANES - left))).reshape(side, high, LANES)
-    rests = [rest[:, k * low : (k + 1) * low] for k in range(side - 1)]
-    rests.append(jnp.zeros_like(rests[0]))
-    return jnp.concatenate(
-        [jnp.concatenate(blocks, axis=0), jnp.concatenate(rests, axis=0)], axis=1
-    )
+    rest = [x[k * high : (k + 1) * high, whole:] for k in range(side)]
+    rest = jnp.concatenate(rest, axis=1).reshape(high // 8, 8, LANES)
+    rest = jnp.pad(rest, ((0, size - high // 8), (0, 0), (0, 0)))
+    return jnp.concatenate([jnp.concatenate(blocks, axis=0), rest], axis=1)
 
 
 def unpack(x, side, lanes):
-    low = x.shape[1] // side
-    high = x.shape[1] - low
+    high = x.shape[1] - 8
+    left = lanes - side * LANES
     blocks = [
         x[k * side : (k + 1) * side, :high].reshape(side * high, LANES) for k in range(side)
     ]
-    rest = [x[k * side : (k + 1) * side, high:] for k in range(side - 1)]
-    rest = jnp.concatenate(rest, axis=1).reshape(side * high, LANES)
-    return jnp.concatenate(blocks + [rest[:, : lanes - side * LANES]], axis=1)
+    rest = x[: high // 8, high:].reshape(high, LANES)
+    rest = [rest[:, k * left : (k + 1) * left] for k in range(side)]
+    return jnp.concatenate(blocks + [jnp.concatenate(rest, axis=0)], axis=1)
 
 
 def solution(mesh):

time: 251 us -> 288 us (1.15)
  waiting for transfers between devices: 48.1 us -> 76.5 us
  blocking collectives: 64.9 us -> 80.8 us
  starting transfers between devices: 86.1 us -> 79.8 us
    all_gather x2, waiting for transfers between devices: 0.87 us -> 25.3 us  [shards(): lax.all_gather(after(units, summed), 'replica', axis=0, tiled=True)]
    all_to_all x1 -> x2, blocking collectives: 32.4 us -> 48 us  [exchange(): return lax.all_to_all(x, axis, split_axis=0, concat_axis=0, tiled=True)]
    all_to_all x5 -> x4, starting transfers between devices: 38.1 us -> 30.6 us  [exchange(): return lax.all_to_all(x, axis, split_axis=0, concat_axis=0, tiled=True)]
    ppermute x12, waiting for transfers between devices: 8.71 us -> 14.5 us  [shift(): return lax.ppermute(x, DP, [(i, (i + by) % size) for i in range(size)])]
    all_to_all x5 -> x4, waiting for transfers between devices: 38.5 us -> 36.7 us  [exchange(): return lax.all_to_all(x, axis, split_axis=0, concat_axis=0, tiled=True)]
  transfers between devices with their start and end apart: 19 -> 18, of which waited for: 9 -> 10; matrix products, arithmetic and copies ran while one was open for 10% -> 7% of each run, Pallas kernels for 0% -> 0%
where the time goes in v7:
time: 288 us; the launch traced here: 285 us
  blocking collectives  80.8 us (28%)
  starting transfers between devices  79.8 us (28%)
  waiting for transfers between devices  76.5 us (27%)
  matrix products  16.8 us (6%)
  between operations  16 us (6%)
  local copies, waits for them, and re-layouts  9.69 us (3%)
  other arithmetic  5.18 us (2%)
    ppermute x12, starting transfers between devices, shift(): return lax.ppermute(x, DP, [(i, (i + by) % size) for i in range(size)])  49.1 us
    all_to_all x2, blocking collectives, exchange(): return lax.all_to_all(x, axis, split_axis=0, concat_axis=0, tiled=True)  48 us
    all_to_all x4, waiting for transfers between devices, exchange(): return lax.all_to_all(x, axis, split_axis=0, concat_axis=0, tiled=True)  36.7 us
    all_to_all x4, starting transfers between devices, exchange(): return lax.all_to_all(x, axis, split_axis=0, concat_axis=0, tiled=True)  30.6 us
    all_gather x2, waiting for transfers between devices, shards(): lax.all_gather(after(units, summed), 'replica', axis=0, tiled=True)  25.3 us
    all_gather x1, blocking collectives, gather_dp(): quad = lax.all_gather(x, 'run', axis=0)  24.1 us
    dot_general x9, matrix products, dot(): lax.dot_general(a, b, (contract, ((), ())), preferred_element_type=F32)  16.8 us
    ppermute x12, waiting for transfers between devices, shift(): return lax.ppermute(x, DP, [(i, (i + by) % size) for i in range(size)])  14.5 us
  transfers between devices with their start and end apart: 18, of which 10 were waited for; matrix products, arithmetic and copies ran while one was open for 7% of the time, Pallas kernels for 0%

profile of v7, /device:TPU:24, one launch (start us, length us, event | category | flops | bytes accessed | tf_op | source)
XLA Modules:
  0.0 284.6 jit_solution(15920435950089781182)
XLA Ops:
  7.2 1.9 convolution_convert_fusion.3
  10.5 4.9 %all-to-all-start = ((bf16[4,64,1152]{2,1,0:T(8,128)(2,1)}), bf16[4,64,1152]{2,1,0:T(8,128)(2,1)S(1)}, u32[]{:S(2)}, u32[]{:S(2)}) async-start(bf16[4,64,1152]{2,1,0:T(8,128)(2,1)} %pad_maximum_fusion), calls=%async_computation | async-start | bytes 1179648 | tf_op jit(solution)/shard_map/all_to_all | solution.py:21
  15.4 7.9 %all-to-all-done = bf16[4,64,1152]{2,1,0:T(8,128)(2,1)S(1)} async-done(((bf16[4,64,1152]{2,1,0:T(8,128)(2,1)}), bf16[4,64,1152]{2,1,0:T(8,128)(2,1)S(1)}, u32[]{:S(2)}, u32[]{:S(2)}) %all-to-all-start) | async-done | bytes 589856 | tf_op jit(solution)/shard_map/all_to_all | solution.py:21
  25.3 11.9 %all-to-all-start.1 = ((bf16[32,32,1152]{2,1,0:T(8,128)(2,1)}), bf16[32,32,1152]{2,1,0:T(8,128)(2,1)}, u32[]{:S(2)}, u32[]{:S(2)}) async-start(bf16[32,32,1152]{2,1,0:T(8,128)(2,1)} %broadcast_in_dim.18), calls=%async_computation.1 | async-start | bytes 4718592 | tf_op jit(solution)/shard_map/all_to_all | solution.py:21
  38.6 24.1 %all-gather = bf16[128,1152]{1,0:T(8,128)(2,1)S(1)} all-gather(bf16[32,1152]{1,0:T(8,128)(2,1)S(1)} %get-tuple-element.62), channel_id=2, replica_groups=mesh['run'=4,'place'=4,'replica'=8,'tensor'=4] {'run'}, dimensions={0}, use_global_device_ids=true | all-gather | bytes 368640 | tf_op jit(solution)/shard_map/all_gather | solution.py:39
  62.7 2.2 collective-permute-start
  65.0 4.8 %collective-permute-start.1 = (bf16[4,32,1152]{2,1,0:T(8,128)(2,1)S(1)}, bf16[4,32,1152]{2,1,0:T(8,128)(2,1)S(1)}, u32[]{:S(2)}, u32[]{:S(2)}) collective-permute-start(bf16[4,32,1152]{2,1,0:T(8,128)(2,1)S(1)} %bitcast.91), channel_id=1, source_target_pairs={{0,480},{32,0},{64,32},{96,64},{128,96},{160,128},{192,160},{224,1... | collective-permute-start | bytes 884744 | tf_op jit(solution)/shard_map/ppermute | solution.py:35
  70.6 2.2 collective-permute-start.2
  72.7 4.6 %collective-permute-start.3 = (bf16[2,32,1152]{2,1,0:T(8,128)(2,1)S(1)}, bf16[2,32,1152]{2,1,0:T(8,128)(2,1)S(1)}, u32[]{:S(2)}, u32[]{:S(2)}) collective-permute-start(bf16[2,32,1152]{2,1,0:T(8,128)(2,1)S(1)} %bitcast.110), channel_id=1, source_target_pairs={{0,64},{32,96},{64,128},{96,160},{128,192},{160,224},{192,256},{22... | collective-permute-start | bytes 442376 | tf_op jit(solution)/shard_map/ppermute | solution.py:35
  78.9 1.8 collective-permute-done.2
  83.2 4.3 %multiply_convert_fusion = bf16[1024,512]{1,0:T(8,128)(2,1)S(1)} fusion(bf16[1024,1152]{1,0:T(8,128)(2,1)} %bitcast.6, bf16[512,1152]{1,0:T(8,128)(2,1)} %bitcast.112, f32[]{:T(128)} %bitcast.88, f32[]{:T(128)} %bitcast, s32[512]{0:T(512)S(1)} %fusion.17), kind=kOutput, calls=%fused_computation.5 | convolution fusion | flops 1214251008 | bytes 4589576 | tf_op jit(solution)/shard_map/dot_general | solution.py:17
  87.5 3.0 %convolution_convert_fusion = bf16[1024,1152]{1,0:T(8,128)(2,1)} fusion(bf16[1024,512]{1,0:T(8,128)(2,1)S(1)} %multiply_convert_fusion, bf16[512,1152]{1,0:T(8,128)(2,1)S(1)} %bitcast.113), kind=kOutput, calls=%fused_computation.1 | convolution fusion | flops 1209139200 | bytes 4587520 | tf_op jit(solution)/shard_map/dot_general | solution.py:17
  90.4 3.2 %convolution_convert_fusion.1 = bf16[512,1152]{1,0:T(8,128)(2,1)S(1)} fusion(bf16[1024,512]{1,0:T(8,128)(2,1)S(1)} %multiply_convert_fusion, bf16[1024,1152]{1,0:T(8,128)(2,1)} %bitcast.6), kind=kOutput, calls=%fused_computation.2 | convolution fusion | flops 1208549376 | bytes 4587520 | tf_op jit(solution)/shard_map/dot_general | solution.py:17
  93.7 24.9 %all-gather.5.cloned.1.call-done = bf16[1024,544]{0,1:T(8,128)(2,1)} async-done(((bf16[128,544]{0,1:T(8,128)(2,1)}), bf16[1024,544]{0,1:T(8,128)(2,1)}) %all-gather.5.cloned.1.call-update) | async-done | bytes 1114128 | tf_op jit(solution)/shard_map/all_gather | solution.py:117
  119.4 5.9 %collective-permute-start.4 = (bf16[4,32,1152]{2,1,0:T(8,128)(2,1)}, bf16[4,32,1152]{2,1,0:T(8,128)(2,1)S(1)}, u32[]{:S(2)}, u32[]{:S(2)}) collective-permute-start(bf16[4,32,1152]{2,1,0:T(8,128)(2,1)} %bitcast.10), channel_id=1, source_target_pairs={{0,480},{32,0},{64,32},{96,64},{128,96},{160,128},{192,160},{224,1... | collective-permute-start | bytes 884744 | tf_op jit(solution)/shard_map/ppermute | solution.py:35
  125.4 1.9 collective-permute-start.5
  128.0 2.4 collective-permute-start.6
  130.4 5.5 %collective-permute-start.7 = (bf16[2,32,1152]{2,1,0:T(8,128)(2,1)S(1)}, bf16[2,32,1152]{2,1,0:T(8,128)(2,1)S(1)}, u32[]{:S(2)}, u32[]{:S(2)}) collective-permute-start(bf16[2,32,1152]{2,1,0:T(8,128)(2,1)S(1)} %bitcast.109), channel_id=1, source_target_pairs={{0,448},{32,480},{64,0},{96,32},{128,64},{160,96},{192,128},{224,1... | collective-permute-start | bytes 442376 | tf_op jit(solution)/shard_map/ppermute | solution.py:35
  136.0 7.8 %all-to-all-start.2 = ((bf16[32,32,1152]{2,1,0:T(8,128)(2,1)}), bf16[32,32,1152]{2,1,0:T(8,128)(2,1)}, u32[]{:S(2)}, u32[]{:S(2)}) async-start(bf16[32,32,1152]{2,1,0:T(8,128)(2,1)} %bitcast.93), calls=%async_computation.2 | async-start | bytes 4718592 | tf_op jit(solution)/shard_map/all_to_all | solution.py:21
  145.0 5.6 %collective-permute-start.8 = (bf16[16,1152]{1,0:T(8,128)(2,1)S(1)}, bf16[16,1152]{1,0:T(8,128)(2,1)S(1)}, u32[]{:S(2)}, u32[]{:S(2)}) collective-permute-start(bf16[16,1152]{1,0:T(8,128)(2,1)S(1)} %get-tuple-element.66), channel_id=1, source_target_pairs={{0,128},{32,160},{64,192},{96,224},{128,256},{160,288},{192,320},{... | collective-permute-start | bytes 110600 | tf_op jit(solution)/shard_map/ppermute | solution.py:35
  150.6 4.1 %collective-permute-start.9 = (bf16[16,1152]{1,0:T(8,128)(2,1)S(1)}, bf16[16,1152]{1,0:T(8,128)(2,1)S(1)}, u32[]{:S(2)}, u32[]{:S(2)}) collective-permute-start(bf16[16,1152]{1,0:T(8,128)(2,1)S(1)} %get-tuple-element.65), channel_id=1, source_target_pairs={{0,384},{32,416},{64,448},{96,480},{128,0},{160,32},{192,64},{224,... | collective-permute-start | bytes 110600 | tf_op jit(solution)/shard_map/ppermute | solution.py:35
  156.3 5.1 %collective-permute-done.9 = bf16[16,1152]{1,0:T(8,128)(2,1)S(1)} collective-permute-done((bf16[16,1152]{1,0:T(8,128)(2,1)S(1)}, bf16[16,1152]{1,0:T(8,128)(2,1)S(1)}, u32[]{:S(2)}, u32[]{:S(2)}) %collective-permute-start.9) | collective-permute-done | bytes 36896 | tf_op jit(solution)/shard_map/ppermute | solution.py:35
  161.5 19.3 %all-to-all-done.2 = bf16[32,32,1152]{2,1,0:T(8,128)(2,1)} async-done(((bf16[32,32,1152]{2,1,0:T(8,128)(2,1)}), bf16[32,32,1152]{2,1,0:T(8,128)(2,1)}, u32[]{:S(2)}, u32[]{:S(2)}) %all-to-all-start.2) | async-done | bytes 2359328 | tf_op jit(solution)/shard_map/all_to_all | solution.py:21
  180.8 5.6 %collective-permute-start.10 = (bf16[32,1152]{1,0:T(8,128)(2,1)S(1)}, bf16[32,1152]{1,0:T(8,128)(2,1)S(1)}, u32[]{:S(2)}, u32[]{:S(2)}) collective-permute-start(bf16[32,1152]{1,0:T(8,128)(2,1)S(1)} %pad_maximum_fusion.6), channel_id=1, source_target_pairs={{0,128},{32,160},{64,192},{96,224},{128,256},{160,288},{192,320},{... | collective-permute-start | bytes 221192 | tf_op jit(solution)/shard_map/ppermute | solution.py:35
  186.4 4.2 %collective-permute-start.11 = (bf16[32,1152]{1,0:T(8,128)(2,1)S(1)}, bf16[32,1152]{1,0:T(8,128)(2,1)S(1)}, u32[]{:S(2)}, u32[]{:S(2)}) collective-permute-start(bf16[32,1152]{1,0:T(8,128)(2,1)S(1)} %pad_maximum_fusion.7), channel_id=1, source_target_pairs={{0,384},{32,416},{64,448},{96,480},{128,0},{160,32},{192,64},{224,... | collective-permute-start | bytes 221192 | tf_op jit(solution)/shard_map/ppermute | solution.py:35
  190.5 2.0 convert_reduce_fusion
  193.0 4.9 %collective-permute-done.11 = bf16[32,1152]{1,0:T(8,128)(2,1)S(1)} collective-permute-done((bf16[32,1152]{1,0:T(8,128)(2,1)S(1)}, bf16[32,1152]{1,0:T(8,128)(2,1)S(1)}, u32[]{:S(2)}, u32[]{:S(2)}) %collective-permute-start.11) | collective-permute-done | bytes 73760 | tf_op jit(solution)/shard_map/ppermute | solution.py:35
  198.9 21.0 %all_to_all.30 = bf16[32,32,288]{2,1,0:T(8,128)(2,1)S(1)} all-to-all(bf16[32,32,288]{2,1,0:T(8,128)(2,1)S(1)} %bitcast.89), channel_id=1, replica_groups=mesh['run'=4,'place'=4,'replica'=8,'tensor'=4] {'replica','tensor'}, dimensions={0} | all-to-all | bytes 1179648 | tf_op jit(solution)/shard_map/all_to_all | solution.py:21
  222.2 27.0 %all_to_all.31 = bf16[16,80,128]{2,1,0:T(8,128)(2,1)S(1)} all-to-all(bf16[16,80,128]{2,1,0:T(8,128)(2,1)S(1)} %fusion.3), channel_id=1, replica_groups=mesh['run'=4,'place'=4,'replica'=8,'tensor'=4] {'run','place'}, dimensions={0} | all-to-all | bytes 655360 | tf_op jit(solution)/shard_map/all_to_all | solution.py:21
  250.0 6.0 %all-to-all-start.5 = ((bf16[16,80,128]{2,1,0:T(8,128)(2,1)}), bf16[16,80,128]{2,1,0:T(8,128)(2,1)S(1)}, u32[]{:S(2)}, u32[]{:S(2)}) async-start(bf16[16,80,128]{2,1,0:T(8,128)(2,1)} %broadcast_in_dim.20), calls=%async_computation.5 | async-start | bytes 655360 | tf_op jit(solution)/shard_map/all_to_all | solution.py:21
  256.0 8.7 %all-gather.1 = bf16[2,128,1152]{2,1,0:T(8,128)(2,1)S(1)} all-gather(bf16[2,32,1152]{2,1,0:T(8,128)(2,1)S(1)} %pad_maximum_fusion.1), channel_id=3, replica_groups=mesh['run'=4,'place'=4,'replica'=8,'tensor'=4] {'tensor'}, dimensions={1}, use_global_device_ids=true | all-gather | bytes 737280 | tf_op jit(solution)/shard_map/all_gather | solution.py:161
  267.0 9.5 %all-to-all-done.5 = bf16[16,80,128]{2,1,0:T(8,128)(2,1)S(1)} async-done(((bf16[16,80,128]{2,1,0:T(8,128)(2,1)}), bf16[16,80,128]{2,1,0:T(8,128)(2,1)S(1)}, u32[]{:S(2)}, u32[]{:S(2)}) %all-to-all-start.5) | async-done | bytes 327712 | tf_op jit(solution)/shard_map/all_to_all | solution.py:21
  (89 shorter events, 20.4 us)
Async XLA Ops:
  7.2 1.9 copy-start
  7.2 1.9 copy-start.2
  10.5 12.9 %copy-start.3 = (bf16[128,1152]{1,0:T(8,128)(2,1)S(1)}, bf16[128,1152]{1,0:T(8,128)(2,1)}, u32[]{:S(2)}) copy-start(bf16[128,1152]{1,0:T(8,128)(2,1)} %param.8) | copy-start | bytes 884740
  10.5 12.9 %copy-start.5 = (bf16[128,1152]{1,0:T(8,128)(2,1)S(1)}, bf16[128,1152]{1,0:T(8,128)(2,1)}, u32[]{:S(2)}) copy-start(bf16[128,1152]{1,0:T(8,128)(2,1)} %param.11) | copy-start | bytes 884740
  10.5 12.8 %all-to-all-start = ((bf16[4,64,1152]{2,1,0:T(8,128)(2,1)}), bf16[4,64,1152]{2,1,0:T(8,128)(2,1)S(1)}, u32[]{:S(2)}, u32[]{:S(2)}) async-start(bf16[4,64,1152]{2,1,0:T(8,128)(2,1)} %pad_maximum_fusion), calls=%async_computation | async-start | bytes 1179648 | tf_op jit(solution)/shard_map/all_to_all | solution.py:21
  25.3 57.9 %all-to-all-start.1 = ((bf16[32,32,1152]{2,1,0:T(8,128)(2,1)}), bf16[32,32,1152]{2,1,0:T(8,128)(2,1)}, u32[]{:S(2)}, u32[]{:S(2)}) async-start(bf16[32,32,1152]{2,1,0:T(8,128)(2,1)} %broadcast_in_dim.18), calls=%async_computation.1 | async-start | bytes 4718592 | tf_op jit(solution)/shard_map/all_to_all | solution.py:21
  37.2 81.3 %all-gather.5.cloned.1.call-start = ((), (), s32[]{:S(2)}) async-start(), calls=%async_computation.6 | async-start | bytes 1253376 | tf_op jit(solution)/shard_map/all_gather | solution.py:117
  62.7 14.7 %collective-permute-start = (bf16[4,32,1152]{2,1,0:T(8,128)(2,1)S(1)}, bf16[4,32,1152]{2,1,0:T(8,128)(2,1)S(1)}, u32[]{:S(2)}, u32[]{:S(2)}) collective-permute-start(bf16[4,32,1152]{2,1,0:T(8,128)(2,1)S(1)} %bitcast.90), channel_id=1, source_target_pairs={{0,32},{32,64},{64,96},{96,128},{128,160},{160,192},{192,224},{224... | collective-permute-start | bytes 884744 | tf_op jit(solution)/shard_map/ppermute | solution.py:35
  65.0 13.2 %collective-permute-start.1 = (bf16[4,32,1152]{2,1,0:T(8,128)(2,1)S(1)}, bf16[4,32,1152]{2,1,0:T(8,128)(2,1)S(1)}, u32[]{:S(2)}, u32[]{:S(2)}) collective-permute-start(bf16[4,32,1152]{2,1,0:T(8,128)(2,1)S(1)} %bitcast.91), channel_id=1, source_target_pairs={{0,480},{32,0},{64,32},{96,64},{128,96},{160,128},{192,160},{224,1... | collective-permute-start | bytes 884744 | tf_op jit(solution)/shard_map/ppermute | solution.py:35
  70.6 10.1 %collective-permute-start.2 = (bf16[2,32,1152]{2,1,0:T(8,128)(2,1)S(1)}, bf16[2,32,1152]{2,1,0:T(8,128)(2,1)S(1)}, u32[]{:S(2)}, u32[]{:S(2)}) collective-permute-start(bf16[2,32,1152]{2,1,0:T(8,128)(2,1)S(1)} %bitcast.111), channel_id=1, source_target_pairs={{0,448},{32,480},{64,0},{96,32},{128,64},{160,96},{192,128},{224,1... | collective-permute-start | bytes 442376 | tf_op jit(solution)/shard_map/ppermute | solution.py:35
  72.7 9.8 %collective-permute-start.3 = (bf16[2,32,1152]{2,1,0:T(8,128)(2,1)S(1)}, bf16[2,32,1152]{2,1,0:T(8,128)(2,1)S(1)}, u32[]{:S(2)}, u32[]{:S(2)}) collective-permute-start(bf16[2,32,1152]{2,1,0:T(8,128)(2,1)S(1)} %bitcast.110), channel_id=1, source_target_pairs={{0,64},{32,96},{64,128},{96,160},{128,192},{160,224},{192,256},{22... | collective-permute-start | bytes 442376 | tf_op jit(solution)/shard_map/ppermute | solution.py:35
  77.3 115.6 %all-gather.7.cloned.1.call-start = ((), (), s32[]{:S(2)}) async-start(), calls=%async_computation.7 | async-start | bytes 1253376 | tf_op jit(solution)/shard_map/all_gather | solution.py:117
  83.2 4.3 %copy-start.7 = (bf16[16,32,1152]{2,1,0:T(8,128)(2,1)S(1)}, bf16[16,32,1152]{2,1,0:T(8,128)(2,1)}, u32[]{:S(2)}) copy-start(bf16[16,32,1152]{2,1,0:T(8,128)(2,1)} %constant_dynamic-update-slice_fusion) | copy-start | bytes 3538948
  119.4 24.4 %collective-permute-start.4 = (bf16[4,32,1152]{2,1,0:T(8,128)(2,1)}, bf16[4,32,1152]{2,1,0:T(8,128)(2,1)S(1)}, u32[]{:S(2)}, u32[]{:S(2)}) collective-permute-start(bf16[4,32,1152]{2,1,0:T(8,128)(2,1)} %bitcast.10), channel_id=1, source_target_pairs={{0,480},{32,0},{64,32},{96,64},{128,96},{160,128},{192,160},{224,1... | collective-permute-start | bytes 884744 | tf_op jit(solution)/shard_map/ppermute | solution.py:35
  125.4 18.4 %collective-permute-start.5 = (bf16[4,32,1152]{2,1,0:T(8,128)(2,1)}, bf16[4,32,1152]{2,1,0:T(8,128)(2,1)}, u32[]{:S(2)}, u32[]{:S(2)}) collective-permute-start(bf16[4,32,1152]{2,1,0:T(8,128)(2,1)} %bitcast.11), channel_id=1, source_target_pairs={{0,32},{32,64},{64,96},{96,128},{128,160},{160,192},{192,224},{224... | collective-permute-start | bytes 884744 | tf_op jit(solution)/shard_map/ppermute | solution.py:35
  128.0 15.8 %collective-permute-start.6 = (bf16[2,32,1152]{2,1,0:T(8,128)(2,1)}, bf16[2,32,1152]{2,1,0:T(8,128)(2,1)S(1)}, u32[]{:S(2)}, u32[]{:S(2)}) collective-permute-start(bf16[2,32,1152]{2,1,0:T(8,128)(2,1)} %bitcast.12), channel_id=1, source_target_pairs={{0,64},{32,96},{64,128},{96,160},{128,192},{160,224},{192,256},{22... | collective-permute-start | bytes 442376 | tf_op jit(solution)/shard_map/ppermute | solution.py:35
  130.4 13.4 %collective-permute-start.7 = (bf16[2,32,1152]{2,1,0:T(8,128)(2,1)S(1)}, bf16[2,32,1152]{2,1,0:T(8,128)(2,1)S(1)}, u32[]{:S(2)}, u32[]{:S(2)}) collective-permute-start(bf16[2,32,1152]{2,1,0:T(8,128)(2,1)S(1)} %bitcast.109), channel_id=1, source_target_pairs={{0,448},{32,480},{64,0},{96,32},{128,64},{160,96},{192,128},{224,1... | collective-permute-start | bytes 442376 | tf_op jit(solution)/shard_map/ppermute | solution.py:35
  136.0 44.8 %all-to-all-start.2 = ((bf16[32,32,1152]{2,1,0:T(8,128)(2,1)}), bf16[32,32,1152]{2,1,0:T(8,128)(2,1)}, u32[]{:S(2)}, u32[]{:S(2)}) async-start(bf16[32,32,1152]{2,1,0:T(8,128)(2,1)} %bitcast.93), calls=%async_computation.2 | async-start | bytes 4718592 | tf_op jit(solution)/shard_map/all_to_all | solution.py:21
  145.0 11.3 %collective-permute-start.8 = (bf16[16,1152]{1,0:T(8,128)(2,1)S(1)}, bf16[16,1152]{1,0:T(8,128)(2,1)S(1)}, u32[]{:S(2)}, u32[]{:S(2)}) collective-permute-start(bf16[16,1152]{1,0:T(8,128)(2,1)S(1)} %get-tuple-element.66), channel_id=1, source_target_pairs={{0,128},{32,160},{64,192},{96,224},{128,256},{160,288},{192,320},{... | collective-permute-start | bytes 110600 | tf_op jit(solution)/shard_map/ppermute | solution.py:35
  150.6 10.8 %collective-permute-start.9 = (bf16[16,1152]{1,0:T(8,128)(2,1)S(1)}, bf16[16,1152]{1,0:T(8,128)(2,1)S(1)}, u32[]{:S(2)}, u32[]{:S(2)}) collective-permute-start(bf16[16,1152]{1,0:T(8,128)(2,1)S(1)} %get-tuple-element.65), channel_id=1, source_target_pairs={{0,384},{32,416},{64,448},{96,480},{128,0},{160,32},{192,64},{224,... | collective-permute-start | bytes 110600 | tf_op jit(solution)/shard_map/ppermute | solution.py:35
  161.5 36.4 %copy-start.4 = (bf16[128,1152]{1,0:T(8,128)(2,1)S(1)}, bf16[128,1152]{1,0:T(8,128)(2,1)}, u32[]{:S(2)}) copy-start(bf16[128,1152]{1,0:T(8,128)(2,1)} %param.8) | copy-start | bytes 884740
  161.5 36.4 %copy-start.6 = (bf16[128,1152]{1,0:T(8,128)(2,1)S(1)}, bf16[128,1152]{1,0:T(8,128)(2,1)}, u32[]{:S(2)}) copy-start(bf16[128,1152]{1,0:T(8,128)(2,1)} %param.11) | copy-start | bytes 884740
  180.8 12.2 %collective-permute-start.10 = (bf16[32,1152]{1,0:T(8,128)(2,1)S(1)}, bf16[32,1152]{1,0:T(8,128)(2,1)S(1)}, u32[]{:S(2)}, u32[]{:S(2)}) collective-permute-start(bf16[32,1152]{1,0:T(8,128)(2,1)S(1)} %pad_maximum_fusion.6), channel_id=1, source_target_pairs={{0,128},{32,160},{64,192},{96,224},{128,256},{160,288},{192,320},{... | collective-permute-start | bytes 221192 | tf_op jit(solution)/shard_map/ppermute | solution.py:35
  186.4 11.5 %collective-permute-start.11 = (bf16[32,1152]{1,0:T(8,128)(2,1)S(1)}, bf16[32,1152]{1,0:T(8,128)(2,1)S(1)}, u32[]{:S(2)}, u32[]{:S(2)}) collective-permute-start(bf16[32,1152]{1,0:T(8,128)(2,1)S(1)} %pad_maximum_fusion.7), channel_id=1, source_target_pairs={{0,384},{32,416},{64,448},{96,480},{128,0},{160,32},{192,64},{224,... | collective-permute-start | bytes 221192 | tf_op jit(solution)/shard_map/ppermute | solution.py:35
  198.8 21.1 %copy-start.9 = (bf16[1024,544]{0,1:T(8,128)(2,1)S(1)}, bf16[1024,544]{0,1:T(8,128)(2,1)}, u32[]{:S(2)}) copy-start(bf16[1024,544]{0,1:T(8,128)(2,1)} %all-gather.7.cloned.1.call-done) | copy-start | bytes 3342340
  219.9 1.2 copy-start.8
  250.0 26.5 %all-to-all-start.5 = ((bf16[16,80,128]{2,1,0:T(8,128)(2,1)}), bf16[16,80,128]{2,1,0:T(8,128)(2,1)S(1)}, u32[]{:S(2)}, u32[]{:S(2)}) async-start(bf16[16,80,128]{2,1,0:T(8,128)(2,1)} %broadcast_in_dim.20), calls=%async_computation.5 | async-start | bytes 655360 | tf_op jit(solution)/shard_map/all_to_all | solution.py:21
  256.0 9.8 %copy-start.1 = (bf16[544,1152]{1,0:T(8,128)(2,1)S(1)}, bf16[544,1152]{1,0:T(8,128)(2,1)}, u32[]{:S(2)}) copy-start(bf16[544,1152]{1,0:T(8,128)(2,1)} %param.10) | copy-start | bytes 3760132
Sparse Core Ops, SparseCore 0:
  77.4 41.0 all-gather.4
  136.1 56.7 all-gather.6

commit v8 on v7

--- a/solution.py
+++ b/solution.py
@@ -43,7 +43,7 @@
     )
 
 
-def scatter_dp(x, meanwhile):
+def scatter_dp(x):
     half = x.shape[1] // 16 * 8
     run = lax.axis_index("run")
     one = shift(x[4:8], -1)
@@ -60,9 +60,7 @@
     below_half = shift(far[half:], -4).astype(F32)
     above = jnp.concatenate([above[:half] + above_half, above[half:]], axis=0).astype(BF16)
     below = jnp.concatenate([below[:half], below[half:] + below_half], axis=0).astype(BF16)
-    above, below, meanwhile = lax.optimization_barrier((above, below, meanwhile))
-    total = near + shift(above, 4).astype(F32) + shift(below, -4).astype(F32)
-    return (total, meanwhile)
+    return near + shift(above, 4).astype(F32) + shift(below, -4).astype(F32)
 
 
 def normalize(residual, summed):
@@ -139,10 +137,8 @@
     coefficients, image_partial = lax.optimization_barrier((coefficients, image_partial))
     image_parts = exchange(image_partial.reshape(members, own, width), PLANE)
     text_partial = dot(coefficients, images, ((0,), (0,))).astype(BF16)
-    text_partial, hidden_text = lax.optimization_barrier((text_partial, hidden_text))
-    text_grad, image_parts = scatter_dp(text_partial.reshape(n_dp, own, width), image_parts)
+    text_grad = scatter_dp(text_partial.reshape(n_dp, own, width))
     image_grad = jnp.sum(image_parts.astype(F32), axis=0)
-    image_grad, hidden_image = lax.optimization_barrier((image_grad, hidden_image))
 
     upstream_image = retract(normed_image, inverse_image, image_grad)
     upstream_text = retract(normed_text, inverse_text, text_grad)
@@ -153,10 +149,8 @@
         ],
         axis=2,
     )
-    cut = jnp.transpose(cut, (1, 0, 2))
-    cut = jnp.broadcast_to(cut[:, None], (n_replica, n_tensor, own, 2 * columns))
-    cut = exchange(cut.reshape(members, own, 2 * columns), PLANE)
-    cut = cut.reshape(members * own, 2 * columns)
+    cut = exchange(jnp.transpose(cut, (1, 0, 2)), "replica")
+    cut = lax.all_gather(cut, "tensor", axis=1).reshape(members * own, 2 * columns)
     group = after(jnp.stack([upstream_image, upstream_text]), cut)
     group = lax.all_gather(group, "tensor", axis=1)
     hidden_grad_image = dot(

time: 288 us -> 247 us (0.86)
  waiting for transfers between devices: 76.5 us -> 31.3 us
  blocking collectives: 80.8 us -> 86.2 us
    all_gather x2, waiting for transfers between devices: 25.3 us -> 0.04 us  [shards(): lax.all_gather(after(units, summed), 'replica', axis=0, tiled=True)]
    all_to_all x4, waiting for transfers between devices: 36.7 us -> 22.5 us  [exchange(): return lax.all_to_all(x, axis, split_axis=0, concat_axis=0, tiled=True)]
    all_gather x0 -> x1, blocking collectives: none -> 12.6 us  [shards(): lax.all_gather(cut, 'tensor', axis=1).reshape(members * own, 2 * columns)]
    all_to_all x2, blocking collectives: 48 us -> 41.1 us  [exchange(): return lax.all_to_all(x, axis, split_axis=0, concat_axis=0, tiled=True)]
    ppermute x12, waiting for transfers between devices: 14.5 us -> 8.72 us  [shift(): return lax.ppermute(x, DP, [(i, (i + by) % size) for i in range(size)])]
  transfers between devices with their start and end apart: 18 -> 18, of which waited for: 10 -> 7; matrix products, arithmetic and copies ran while one was open for 7% -> 10% of each run, Pallas kernels for 0% -> 0%
where the time goes in v8:
time: 247 us; the launch traced here: 245 us
  blocking collectives  86.2 us (35%)
  starting transfers between devices  78.2 us (32%)
  waiting for transfers between devices  31.3 us (13%)
  matrix products  18.9 us (8%)
  between operations  16 us (6%)
  local copies, waits for them, and re-layouts  9.19 us (4%)
  other arithmetic  5.09 us (2%)
    ppermute x12, starting transfers between devices, shift(): return lax.ppermute(x, DP, [(i, (i + by) % size) for i in range(size)])  47.9 us
    all_to_all x2, blocking collectives, exchange(): return lax.all_to_all(x, axis, split_axis=0, concat_axis=0, tiled=True)  41.1 us
    all_to_all x4, starting transfers between devices, exchange(): return lax.all_to_all(x, axis, split_axis=0, concat_axis=0, tiled=True)  30.2 us
    all_gather x1, blocking collectives, gather_dp(): quad = lax.all_gather(x, 'run', axis=0)  24.1 us
    all_to_all x4, waiting for transfers between devices, exchange(): return lax.all_to_all(x, axis, split_axis=0, concat_axis=0, tiled=True)  22.5 us
    dot_general x9, matrix products, dot(): lax.dot_general(a, b, (contract, ((), ())), preferred_element_type=F32)  18.9 us
    all_gather x1, blocking collectives, shards(): lax.all_gather(cut, 'tensor', axis=1).reshape(members * own, 2 * columns)  12.6 us
    ppermute x12, waiting for transfers between devices, shift(): return lax.ppermute(x, DP, [(i, (i + by) % size) for i in range(size)])  8.72 us
  transfers between devices with their start and end apart: 18, of which 7 were waited for; matrix products, arithmetic and copies ran while one was open for 10% of the time, Pallas kernels for 0%

profile of v8, /device:TPU:24, one launch (start us, length us, event | category | flops | bytes accessed | tf_op | source)
XLA Modules:
  0.0 245.0 jit_solution(12491688170623886623)
XLA Ops:
  7.2 1.9 convolution_convert_fusion.3
  10.5 4.9 %all-to-all-start = ((bf16[4,64,1152]{2,1,0:T(8,128)(2,1)}), bf16[4,64,1152]{2,1,0:T(8,128)(2,1)S(1)}, u32[]{:S(2)}, u32[]{:S(2)}) async-start(bf16[4,64,1152]{2,1,0:T(8,128)(2,1)} %pad_maximum_fusion), calls=%async_computation | async-start | bytes 1179648 | tf_op jit(solution)/shard_map/all_to_all | solution.py:21
  15.4 7.9 %all-to-all-done = bf16[4,64,1152]{2,1,0:T(8,128)(2,1)S(1)} async-done(((bf16[4,64,1152]{2,1,0:T(8,128)(2,1)}), bf16[4,64,1152]{2,1,0:T(8,128)(2,1)S(1)}, u32[]{:S(2)}, u32[]{:S(2)}) %all-to-all-start) | async-done | bytes 589856 | tf_op jit(solution)/shard_map/all_to_all | solution.py:21
  25.3 11.9 %all-to-all-start.1 = ((bf16[32,32,1152]{2,1,0:T(8,128)(2,1)}), bf16[32,32,1152]{2,1,0:T(8,128)(2,1)}, u32[]{:S(2)}, u32[]{:S(2)}) async-start(bf16[32,32,1152]{2,1,0:T(8,128)(2,1)} %broadcast_in_dim.16), calls=%async_computation.1 | async-start | bytes 4718592 | tf_op jit(solution)/shard_map/all_to_all | solution.py:21
  38.6 24.1 %all-gather = bf16[128,1152]{1,0:T(8,128)(2,1)S(1)} all-gather(bf16[32,1152]{1,0:T(8,128)(2,1)S(1)} %get-tuple-element.48), channel_id=2, replica_groups=mesh['run'=4,'place'=4,'replica'=8,'tensor'=4] {'run'}, dimensions={0}, use_global_device_ids=true | all-gather | bytes 368640 | tf_op jit(solution)/shard_map/all_gather | solution.py:39
  62.7 2.2 collective-permute-start
  65.0 4.8 %collective-permute-start.1 = (bf16[4,32,1152]{2,1,0:T(8,128)(2,1)S(1)}, bf16[4,32,1152]{2,1,0:T(8,128)(2,1)S(1)}, u32[]{:S(2)}, u32[]{:S(2)}) collective-permute-start(bf16[4,32,1152]{2,1,0:T(8,128)(2,1)S(1)} %bitcast.94), channel_id=1, source_target_pairs={{0,480},{32,0},{64,32},{96,64},{128,96},{160,128},{192,160},{224,1... | collective-permute-start | bytes 884744 | tf_op jit(solution)/shard_map/ppermute | solution.py:35
  70.6 2.2 collective-permute-start.2
  72.7 4.6 %collective-permute-start.3 = (bf16[2,32,1152]{2,1,0:T(8,128)(2,1)S(1)}, bf16[2,32,1152]{2,1,0:T(8,128)(2,1)S(1)}, u32[]{:S(2)}, u32[]{:S(2)}) collective-permute-start(bf16[2,32,1152]{2,1,0:T(8,128)(2,1)S(1)} %bitcast.115), channel_id=1, source_target_pairs={{0,64},{32,96},{64,128},{96,160},{128,192},{160,224},{192,256},{22... | collective-permute-start | bytes 442376 | tf_op jit(solution)/shard_map/ppermute | solution.py:35
  83.2 4.3 %multiply_convert_fusion = bf16[1024,512]{1,0:T(8,128)(2,1)S(1)} fusion(bf16[1024,1152]{1,0:T(8,128)(2,1)} %bitcast.6, bf16[512,1152]{1,0:T(8,128)(2,1)} %bitcast.117, f32[]{:T(128)} %bitcast.92, f32[]{:T(128)} %bitcast, s32[512]{0:T(512)S(1)} %fusion.17), kind=kOutput, calls=%fused_computation.5 | convolution fusion | flops 1214251008 | bytes 4589576 | tf_op jit(solution)/shard_map/dot_general | solution.py:17
  87.5 3.0 %convolution_convert_fusion = bf16[1024,1152]{1,0:T(8,128)(2,1)} fusion(bf16[1024,512]{1,0:T(8,128)(2,1)S(1)} %multiply_convert_fusion, bf16[512,1152]{1,0:T(8,128)(2,1)S(1)} %bitcast.118), kind=kOutput, calls=%fused_computation.1 | convolution fusion | flops 1209139200 | bytes 4587520 | tf_op jit(solution)/shard_map/dot_general | solution.py:17
  90.4 3.2 %convolution_convert_fusion.1 = bf16[512,1152]{1,0:T(8,128)(2,1)S(1)} fusion(bf16[1024,512]{1,0:T(8,128)(2,1)S(1)} %multiply_convert_fusion, bf16[1024,1152]{1,0:T(8,128)(2,1)} %bitcast.6), kind=kOutput, calls=%fused_computation.2 | convolution fusion | flops 1208549376 | bytes 4587520 | tf_op jit(solution)/shard_map/dot_general | solution.py:17
  93.7 2.7 %collective-permute-start.4 = (bf16[4,32,1152]{2,1,0:T(8,128)(2,1)S(1)}, bf16[4,32,1152]{2,1,0:T(8,128)(2,1)S(1)}, u32[]{:S(2)}, u32[]{:S(2)}) collective-permute-start(bf16[4,32,1152]{2,1,0:T(8,128)(2,1)S(1)} %bitcast.110), channel_id=1, source_target_pairs={{0,480},{32,0},{64,32},{96,64},{128,96},{160,128},{192,160},{224,1... | collective-permute-start | bytes 884744 | tf_op jit(solution)/shard_map/ppermute | solution.py:35
  96.5 3.8 %collective-permute-start.5 = (bf16[4,32,1152]{2,1,0:T(8,128)(2,1)S(1)}, bf16[4,32,1152]{2,1,0:T(8,128)(2,1)S(1)}, u32[]{:S(2)}, u32[]{:S(2)}) collective-permute-start(bf16[4,32,1152]{2,1,0:T(8,128)(2,1)S(1)} %bitcast.109), channel_id=1, source_target_pairs={{0,32},{32,64},{64,96},{96,128},{128,160},{160,192},{192,224},{224... | collective-permute-start | bytes 884744 | tf_op jit(solution)/shard_map/ppermute | solution.py:35
  101.0 3.4 %collective-permute-start.6 = (bf16[2,32,1152]{2,1,0:T(8,128)(2,1)}, bf16[2,32,1152]{2,1,0:T(8,128)(2,1)S(1)}, u32[]{:S(2)}, u32[]{:S(2)}) collective-permute-start(bf16[2,32,1152]{2,1,0:T(8,128)(2,1)} %bitcast.14), channel_id=1, source_target_pairs={{0,64},{32,96},{64,128},{96,160},{128,192},{160,224},{192,256},{22... | collective-permute-start | bytes 442376 | tf_op jit(solution)/shard_map/ppermute | solution.py:35
  104.4 4.6 %collective-permute-start.7 = (bf16[2,32,1152]{2,1,0:T(8,128)(2,1)}, bf16[2,32,1152]{2,1,0:T(8,128)(2,1)}, u32[]{:S(2)}, u32[]{:S(2)}) collective-permute-start(bf16[2,32,1152]{2,1,0:T(8,128)(2,1)} %bitcast.15), channel_id=1, source_target_pairs={{0,448},{32,480},{64,0},{96,32},{128,64},{160,96},{192,128},{224,1... | collective-permute-start | bytes 442376 | tf_op jit(solution)/shard_map/ppermute | solution.py:35
  109.1 7.4 %all-to-all-start.2 = ((bf16[32,32,1152]{2,1,0:T(8,128)(2,1)}), bf16[32,32,1152]{2,1,0:T(8,128)(2,1)}, u32[]{:S(2)}, u32[]{:S(2)}) async-start(bf16[32,32,1152]{2,1,0:T(8,128)(2,1)} %bitcast.96), calls=%async_computation.2 | async-start | bytes 4718592 | tf_op jit(solution)/shard_map/all_to_all | solution.py:21
  117.6 4.9 %collective-permute-start.10 = (bf16[16,1152]{1,0:T(8,128)(2,1)S(1)}, bf16[16,1152]{1,0:T(8,128)(2,1)S(1)}, u32[]{:S(2)}, u32[]{:S(2)}) collective-permute-start(bf16[16,1152]{1,0:T(8,128)(2,1)S(1)} %get-tuple-element.52), channel_id=1, source_target_pairs={{0,384},{32,416},{64,448},{96,480},{128,0},{160,32},{192,64},{224,... | collective-permute-start | bytes 110600 | tf_op jit(solution)/shard_map/ppermute | solution.py:35
  122.5 4.9 %collective-permute-start.8 = (bf16[16,1152]{1,0:T(8,128)(2,1)S(1)}, bf16[16,1152]{1,0:T(8,128)(2,1)S(1)}, u32[]{:S(2)}, u32[]{:S(2)}) collective-permute-start(bf16[16,1152]{1,0:T(8,128)(2,1)S(1)} %get-tuple-element.51), channel_id=1, source_target_pairs={{0,128},{32,160},{64,192},{96,224},{128,256},{160,288},{192,320},{... | collective-permute-start | bytes 110600 | tf_op jit(solution)/shard_map/ppermute | solution.py:35
  128.8 4.4 %collective-permute-done.8 = bf16[16,1152]{1,0:T(8,128)(2,1)S(1)} collective-permute-done((bf16[16,1152]{1,0:T(8,128)(2,1)S(1)}, bf16[16,1152]{1,0:T(8,128)(2,1)S(1)}, u32[]{:S(2)}, u32[]{:S(2)}) %collective-permute-start.8) | collective-permute-done | bytes 36896 | tf_op jit(solution)/shard_map/ppermute | solution.py:35
  133.2 4.9 %collective-permute-start.9 = (bf16[32,1152]{1,0:T(8,128)(2,1)S(1)}, bf16[32,1152]{1,0:T(8,128)(2,1)S(1)}, u32[]{:S(2)}, u32[]{:S(2)}) collective-permute-start(bf16[32,1152]{1,0:T(8,128)(2,1)S(1)} %pad_maximum_fusion.7), channel_id=1, source_target_pairs={{0,128},{32,160},{64,192},{96,224},{128,256},{160,288},{192,320},{... | collective-permute-start | bytes 221192 | tf_op jit(solution)/shard_map/ppermute | solution.py:35
  138.2 5.0 %collective-permute-start.11 = (bf16[32,1152]{1,0:T(8,128)(2,1)S(1)}, bf16[32,1152]{1,0:T(8,128)(2,1)S(1)}, u32[]{:S(2)}, u32[]{:S(2)}) collective-permute-start(bf16[32,1152]{1,0:T(8,128)(2,1)S(1)} %pad_maximum_fusion.8), channel_id=1, source_target_pairs={{0,384},{32,416},{64,448},{96,480},{128,0},{160,32},{192,64},{224,... | collective-permute-start | bytes 221192 | tf_op jit(solution)/shard_map/ppermute | solution.py:35
  143.2 4.9 %all-to-all-done.2 = bf16[32,32,1152]{2,1,0:T(8,128)(2,1)} async-done(((bf16[32,32,1152]{2,1,0:T(8,128)(2,1)}), bf16[32,32,1152]{2,1,0:T(8,128)(2,1)}, u32[]{:S(2)}, u32[]{:S(2)}) %all-to-all-start.2) | async-done | bytes 2359328 | tf_op jit(solution)/shard_map/all_to_all | solution.py:21
  148.1 2.0 convert_reduce_fusion
  151.0 10.9 %all_to_all.30 = bf16[8,32,288]{2,1,0:T(8,128)(2,1)S(1)} all-to-all(bf16[8,32,288]{2,1,0:T(8,128)(2,1)S(1)} %bitcast.100), channel_id=1, replica_groups=mesh['run'=4,'place'=4,'replica'=8,'tensor'=4] {'replica'}, dimensions={0} | all-to-all | bytes 294912 | tf_op jit(solution)/shard_map/all_to_all | solution.py:21
  162.0 12.6 %all-gather.1 = bf16[8,128,288]{2,0,1:T(8,128)(2,1)S(1)} all-gather(bf16[8,32,288]{2,0,1:T(8,128)(2,1)S(1)} %copy.31), channel_id=3, replica_groups=mesh['run'=4,'place'=4,'replica'=8,'tensor'=4] {'tensor'}, dimensions={1}, use_global_device_ids=true | all-gather | bytes 737280 | tf_op jit(solution)/shard_map/all_gather | solution.py:153
  175.3 1.9 convolution_convert_fusion.5
  177.3 1.9 convolution_convert_fusion.4
  179.4 30.2 %all_to_all.31 = bf16[16,80,128]{2,1,0:T(8,128)(2,1)S(1)} all-to-all(bf16[16,80,128]{2,1,0:T(8,128)(2,1)S(1)} %fusion.3), channel_id=1, replica_groups=mesh['run'=4,'place'=4,'replica'=8,'tensor'=4] {'run','place'}, dimensions={0} | all-to-all | bytes 655360 | tf_op jit(solution)/shard_map/all_to_all | solution.py:21
  210.5 5.9 %all-to-all-start.5 = ((bf16[16,80,128]{2,1,0:T(8,128)(2,1)}), bf16[16,80,128]{2,1,0:T(8,128)(2,1)S(1)}, u32[]{:S(2)}, u32[]{:S(2)}) async-start(bf16[16,80,128]{2,1,0:T(8,128)(2,1)} %broadcast_in_dim.17), calls=%async_computation.5 | async-start | bytes 655360 | tf_op jit(solution)/shard_map/all_to_all | solution.py:21
  216.5 8.3 %all-gather.2 = bf16[2,128,1152]{2,1,0:T(8,128)(2,1)S(1)} all-gather(bf16[2,32,1152]{2,1,0:T(8,128)(2,1)S(1)} %pad_maximum_fusion.2), channel_id=4, replica_groups=mesh['run'=4,'place'=4,'replica'=8,'tensor'=4] {'tensor'}, dimensions={1}, use_global_device_ids=true | all-gather | bytes 737280 | tf_op jit(solution)/shard_map/all_gather | solution.py:155
  227.1 9.7 %all-to-all-done.5 = bf16[16,80,128]{2,1,0:T(8,128)(2,1)S(1)} async-done(((bf16[16,80,128]{2,1,0:T(8,128)(2,1)}), bf16[16,80,128]{2,1,0:T(8,128)(2,1)S(1)}, u32[]{:S(2)}, u32[]{:S(2)}) %all-to-all-start.5) | async-done | bytes 327712 | tf_op jit(solution)/shard_map/all_to_all | solution.py:21
  (85 shorter events, 19.5 us)
Async XLA Ops:
  7.2 1.9 copy-start
  7.2 1.9 copy-start.2
  10.5 12.9 %copy-start.3 = (bf16[128,1152]{1,0:T(8,128)(2,1)S(1)}, bf16[128,1152]{1,0:T(8,128)(2,1)}, u32[]{:S(2)}) copy-start(bf16[128,1152]{1,0:T(8,128)(2,1)} %param.8) | copy-start | bytes 884740
  10.5 12.9 %copy-start.4 = (bf16[128,1152]{1,0:T(8,128)(2,1)S(1)}, bf16[128,1152]{1,0:T(8,128)(2,1)}, u32[]{:S(2)}) copy-start(bf16[128,1152]{1,0:T(8,128)(2,1)} %param.11) | copy-start | bytes 884740
  10.5 12.8 %all-to-all-start = ((bf16[4,64,1152]{2,1,0:T(8,128)(2,1)}), bf16[4,64,1152]{2,1,0:T(8,128)(2,1)S(1)}, u32[]{:S(2)}, u32[]{:S(2)}) async-start(bf16[4,64,1152]{2,1,0:T(8,128)(2,1)} %pad_maximum_fusion), calls=%async_computation | async-start | bytes 1179648 | tf_op jit(solution)/shard_map/all_to_all | solution.py:21
  25.3 57.9 %all-to-all-start.1 = ((bf16[32,32,1152]{2,1,0:T(8,128)(2,1)}), bf16[32,32,1152]{2,1,0:T(8,128)(2,1)}, u32[]{:S(2)}, u32[]{:S(2)}) async-start(bf16[32,32,1152]{2,1,0:T(8,128)(2,1)} %broadcast_in_dim.16), calls=%async_computation.1 | async-start | bytes 4718592 | tf_op jit(solution)/shard_map/all_to_all | solution.py:21
  37.2 138.1 %all-gather.6.cloned.1.call-start = ((), (), s32[]{:S(2)}) async-start(), calls=%async_computation.6 | async-start | bytes 1253376 | tf_op jit(solution)/shard_map/all_gather | solution.py:115
  62.7 14.7 %collective-permute-start = (bf16[4,32,1152]{2,1,0:T(8,128)(2,1)S(1)}, bf16[4,32,1152]{2,1,0:T(8,128)(2,1)S(1)}, u32[]{:S(2)}, u32[]{:S(2)}) collective-permute-start(bf16[4,32,1152]{2,1,0:T(8,128)(2,1)S(1)} %bitcast.93), channel_id=1, source_target_pairs={{0,32},{32,64},{64,96},{96,128},{128,160},{160,192},{192,224},{224... | collective-permute-start | bytes 884744 | tf_op jit(solution)/shard_map/ppermute | solution.py:35
  65.0 13.2 %collective-permute-start.1 = (bf16[4,32,1152]{2,1,0:T(8,128)(2,1)S(1)}, bf16[4,32,1152]{2,1,0:T(8,128)(2,1)S(1)}, u32[]{:S(2)}, u32[]{:S(2)}) collective-permute-start(bf16[4,32,1152]{2,1,0:T(8,128)(2,1)S(1)} %bitcast.94), channel_id=1, source_target_pairs={{0,480},{32,0},{64,32},{96,64},{128,96},{160,128},{192,160},{224,1... | collective-permute-start | bytes 884744 | tf_op jit(solution)/shard_map/ppermute | solution.py:35
  70.6 10.1 %collective-permute-start.2 = (bf16[2,32,1152]{2,1,0:T(8,128)(2,1)S(1)}, bf16[2,32,1152]{2,1,0:T(8,128)(2,1)S(1)}, u32[]{:S(2)}, u32[]{:S(2)}) collective-permute-start(bf16[2,32,1152]{2,1,0:T(8,128)(2,1)S(1)} %bitcast.116), channel_id=1, source_target_pairs={{0,448},{32,480},{64,0},{96,32},{128,64},{160,96},{192,128},{224,1... | collective-permute-start | bytes 442376 | tf_op jit(solution)/shard_map/ppermute | solution.py:35
  72.7 9.8 %collective-permute-start.3 = (bf16[2,32,1152]{2,1,0:T(8,128)(2,1)S(1)}, bf16[2,32,1152]{2,1,0:T(8,128)(2,1)S(1)}, u32[]{:S(2)}, u32[]{:S(2)}) collective-permute-start(bf16[2,32,1152]{2,1,0:T(8,128)(2,1)S(1)} %bitcast.115), channel_id=1, source_target_pairs={{0,64},{32,96},{64,128},{96,160},{128,192},{160,224},{192,256},{22... | collective-permute-start | bytes 442376 | tf_op jit(solution)/shard_map/ppermute | solution.py:35
  77.3 100.0 %all-gather.8.cloned.1.call-start = ((), (), s32[]{:S(2)}) async-start(), calls=%async_computation.7 | async-start | bytes 1253376 | tf_op jit(solution)/shard_map/all_gather | solution.py:115
  83.2 4.3 %copy-start.6 = (bf16[16,32,1152]{2,1,0:T(8,128)(2,1)S(1)}, bf16[16,32,1152]{2,1,0:T(8,128)(2,1)}, u32[]{:S(2)}) copy-start(bf16[16,32,1152]{2,1,0:T(8,128)(2,1)} %constant_dynamic-update-slice_fusion) | copy-start | bytes 3538948
  93.7 22.8 %collective-permute-start.4 = (bf16[4,32,1152]{2,1,0:T(8,128)(2,1)S(1)}, bf16[4,32,1152]{2,1,0:T(8,128)(2,1)S(1)}, u32[]{:S(2)}, u32[]{:S(2)}) collective-permute-start(bf16[4,32,1152]{2,1,0:T(8,128)(2,1)S(1)} %bitcast.110), channel_id=1, source_target_pairs={{0,480},{32,0},{64,32},{96,64},{128,96},{160,128},{192,160},{224,1... | collective-permute-start | bytes 884744 | tf_op jit(solution)/shard_map/ppermute | solution.py:35
  96.5 20.1 %collective-permute-start.5 = (bf16[4,32,1152]{2,1,0:T(8,128)(2,1)S(1)}, bf16[4,32,1152]{2,1,0:T(8,128)(2,1)S(1)}, u32[]{:S(2)}, u32[]{:S(2)}) collective-permute-start(bf16[4,32,1152]{2,1,0:T(8,128)(2,1)S(1)} %bitcast.109), channel_id=1, source_target_pairs={{0,32},{32,64},{64,96},{96,128},{128,160},{160,192},{192,224},{224... | collective-permute-start | bytes 884744 | tf_op jit(solution)/shard_map/ppermute | solution.py:35
  101.0 15.4 %collective-permute-start.6 = (bf16[2,32,1152]{2,1,0:T(8,128)(2,1)}, bf16[2,32,1152]{2,1,0:T(8,128)(2,1)S(1)}, u32[]{:S(2)}, u32[]{:S(2)}) collective-permute-start(bf16[2,32,1152]{2,1,0:T(8,128)(2,1)} %bitcast.14), channel_id=1, source_target_pairs={{0,64},{32,96},{64,128},{96,160},{128,192},{160,224},{192,256},{22... | collective-permute-start | bytes 442376 | tf_op jit(solution)/shard_map/ppermute | solution.py:35
  104.4 12.1 %collective-permute-start.7 = (bf16[2,32,1152]{2,1,0:T(8,128)(2,1)}, bf16[2,32,1152]{2,1,0:T(8,128)(2,1)}, u32[]{:S(2)}, u32[]{:S(2)}) collective-permute-start(bf16[2,32,1152]{2,1,0:T(8,128)(2,1)} %bitcast.15), channel_id=1, source_target_pairs={{0,448},{32,480},{64,0},{96,32},{128,64},{160,96},{192,128},{224,1... | collective-permute-start | bytes 442376 | tf_op jit(solution)/shard_map/ppermute | solution.py:35
  109.1 39.0 %all-to-all-start.2 = ((bf16[32,32,1152]{2,1,0:T(8,128)(2,1)}), bf16[32,32,1152]{2,1,0:T(8,128)(2,1)}, u32[]{:S(2)}, u32[]{:S(2)}) async-start(bf16[32,32,1152]{2,1,0:T(8,128)(2,1)} %bitcast.96), calls=%async_computation.2 | async-start | bytes 4718592 | tf_op jit(solution)/shard_map/all_to_all | solution.py:21
  117.6 11.2 %collective-permute-start.10 = (bf16[16,1152]{1,0:T(8,128)(2,1)S(1)}, bf16[16,1152]{1,0:T(8,128)(2,1)S(1)}, u32[]{:S(2)}, u32[]{:S(2)}) collective-permute-start(bf16[16,1152]{1,0:T(8,128)(2,1)S(1)} %get-tuple-element.52), channel_id=1, source_target_pairs={{0,384},{32,416},{64,448},{96,480},{128,0},{160,32},{192,64},{224,... | collective-permute-start | bytes 110600 | tf_op jit(solution)/shard_map/ppermute | solution.py:35
  122.5 10.7 %collective-permute-start.8 = (bf16[16,1152]{1,0:T(8,128)(2,1)S(1)}, bf16[16,1152]{1,0:T(8,128)(2,1)S(1)}, u32[]{:S(2)}, u32[]{:S(2)}) collective-permute-start(bf16[16,1152]{1,0:T(8,128)(2,1)S(1)} %get-tuple-element.51), channel_id=1, source_target_pairs={{0,128},{32,160},{64,192},{96,224},{128,256},{160,288},{192,320},{... | collective-permute-start | bytes 110600 | tf_op jit(solution)/shard_map/ppermute | solution.py:35
  133.2 16.8 %collective-permute-start.9 = (bf16[32,1152]{1,0:T(8,128)(2,1)S(1)}, bf16[32,1152]{1,0:T(8,128)(2,1)S(1)}, u32[]{:S(2)}, u32[]{:S(2)}) collective-permute-start(bf16[32,1152]{1,0:T(8,128)(2,1)S(1)} %pad_maximum_fusion.7), channel_id=1, source_target_pairs={{0,128},{32,160},{64,192},{96,224},{128,256},{160,288},{192,320},{... | collective-permute-start | bytes 221192 | tf_op jit(solution)/shard_map/ppermute | solution.py:35
  138.2 11.9 %copy-start.5 = (bf16[128,1152]{1,0:T(8,128)(2,1)S(1)}, bf16[128,1152]{1,0:T(8,128)(2,1)}, u32[]{:S(2)}) copy-start(bf16[128,1152]{1,0:T(8,128)(2,1)} %param.11) | copy-start | bytes 884740
  138.2 11.9 %collective-permute-start.11 = (bf16[32,1152]{1,0:T(8,128)(2,1)S(1)}, bf16[32,1152]{1,0:T(8,128)(2,1)S(1)}, u32[]{:S(2)}, u32[]{:S(2)}) collective-permute-start(bf16[32,1152]{1,0:T(8,128)(2,1)S(1)} %pad_maximum_fusion.8), channel_id=1, source_target_pairs={{0,384},{32,416},{64,448},{96,480},{128,0},{160,32},{192,64},{224,... | collective-permute-start | bytes 221192 | tf_op jit(solution)/shard_map/ppermute | solution.py:35
  210.5 26.4 %all-to-all-start.5 = ((bf16[16,80,128]{2,1,0:T(8,128)(2,1)}), bf16[16,80,128]{2,1,0:T(8,128)(2,1)S(1)}, u32[]{:S(2)}, u32[]{:S(2)}) async-start(bf16[16,80,128]{2,1,0:T(8,128)(2,1)} %broadcast_in_dim.17), calls=%async_computation.5 | async-start | bytes 655360 | tf_op jit(solution)/shard_map/all_to_all | solution.py:21
  216.5 9.5 %copy-start.1 = (bf16[544,1152]{1,0:T(8,128)(2,1)S(1)}, bf16[544,1152]{1,0:T(8,128)(2,1)}, u32[]{:S(2)}) copy-start(bf16[544,1152]{1,0:T(8,128)(2,1)} %param.10) | copy-start | bytes 3760132
Sparse Core Ops, SparseCore 0:
  77.4 41.0 all-gather.5
  120.5 54.9 all-gather.7

commit v9 on v8

--- a/solution.py
+++ b/solution.py
@@ -37,19 +37,19 @@
 
 def gather_dp(x):
     quad = lax.all_gather(x, "run", axis=0)
-    return jnp.concatenate(
-        [quad, shift(quad, 1), shift(quad, -1), shift(quad[0:2], -2), shift(quad[2:4], 2)],
-        axis=0,
-    )
-
-
-def scatter_dp(x):
+    return (
+        jnp.concatenate([quad, shift(quad, 1), shift(quad, -1)], axis=0),
+        jnp.concatenate([shift(quad[0:2], -2), shift(quad[2:4], 2)], axis=0),
+    )
+
+
+def scatter_dp(x, y):
     half = x.shape[1] // 16 * 8
     run = lax.axis_index("run")
     one = shift(x[4:8], -1)
     two = shift(x[8:12], 1)
-    three = shift(x[12:14], 2)
-    four = shift(x[14:16], -2)
+    three = shift(y[0:2], 2)
+    four = shift(y[2:4], -2)
     quad = x[0:4].astype(F32) + one.astype(F32) + two.astype(F32)
     quad = quad + jnp.concatenate([three, four], axis=0).astype(F32)
     near, above, far, below = (
@@ -117,27 +117,38 @@
     )
 
     images = spread(normed_image.astype(BF16), PLANE)
-    texts = gather_dp(normed_text.astype(BF16))
-    texts, images = lax.optimization_barrier((texts, images))
-    texts = texts.reshape(n_dp * own, width)
+    near, next_near = gather_dp(normed_text.astype(BF16))
+    near = near.reshape(-1, width)
+    next_near = next_near.reshape(-1, width)
     images = images.reshape(members * own, width)
 
     scale = jnp.exp(log_logit_scale[0])
-    logits = scale * dot(images, texts, ((1,), (1,))) + pair_logit_bias[0]
+
     image_index = jnp.arange(members * own, dtype=jnp.int32)
-    position = jnp.arange(n_dp * own, dtype=jnp.int32)
+    position = jnp.arange(near.shape[0], dtype=jnp.int32)
     text_index = jnp.where(
         position // own == lax.axis_index("run"),
         (replica * n_tensor + tensor) * own + position % own,
         -1,
     )
+    logits = scale * dot(images, near, ((1,), (1,))) + pair_logit_bias[0]
     label = jnp.where(image_index[:, None] == text_index[None, :], 1.0, -1.0).astype(F32)
-    coefficients = (-label * jax.nn.sigmoid(-label * logits) * scale).astype(BF16)
-    image_partial = dot(coefficients, texts, ((1,), (0,))).astype(BF16)
-    coefficients, image_partial = lax.optimization_barrier((coefficients, image_partial))
+    near_pairs = (-label * jax.nn.sigmoid(-label * logits) * scale).astype(BF16)
+    logits = scale * dot(images, next_near, ((1,), (1,))) + pair_logit_bias[0]
+    next_pairs = (jax.nn.sigmoid(logits) * scale).astype(BF16)
+    image_partial = dot(
+        jnp.concatenate([near_pairs, next_pairs], axis=1),
+        jnp.concatenate([near, next_near], axis=0),
+        ((1,), (0,)),
+    ).astype(BF16)
+    near_pairs, next_pairs, image_partial = lax.optimization_barrier(
+        (near_pairs, next_pairs, image_partial)
+    )
     image_parts = exchange(image_partial.reshape(members, own, width), PLANE)
-    text_partial = dot(coefficients, images, ((0,), (0,))).astype(BF16)
-    text_grad = scatter_dp(text_partial.reshape(n_dp, own, width))
+    text_grad = scatter_dp(
+        dot(near_pairs, images, ((0,), (0,))).astype(BF16).reshape(-1, own, width),
+        dot(next_pairs, images, ((0,), (0,))).astype(BF16).reshape(-1, own, width),
+    )
     image_grad = jnp.sum(image_parts.astype(F32), axis=0)
 
     upstream_image = retract(normed_image, inverse_image, image_grad)
@@ -149,8 +160,10 @@
         ],
         axis=2,
     )
-    cut = exchange(jnp.transpose(cut, (1, 0, 2)), "replica")
-    cut = lax.all_gather(cut, "tensor", axis=1).reshape(members * own, 2 * columns)
+    cut = jnp.transpose(cut, (1, 0, 2))
+    cut = jnp.broadcast_to(cut[:, None], (n_replica, n_tensor, own, 2 * columns))
+    cut = exchange(cut.reshape(members, own, 2 * columns), PLANE)
+    cut = cut.reshape(members * own, 2 * columns)
     group = after(jnp.stack([upstream_image, upstream_text]), cut)
     group = lax.all_gather(group, "tensor", axis=1)
     hidden_grad_image = dot(

time: 247 us -> 249 us (level)
  blocking collectives: 86.2 us -> 59.7 us
  waiting for transfers between devices: 31.3 us -> 50.2 us
  starting transfers between devices: 78.2 us -> 85.2 us
  matrix products: 18.9 us -> 22.9 us
  local copies, waits for them, and re-layouts: 9.19 us -> 5.81 us
    all_to_all x4 -> x5, waiting for transfers between devices: 22.5 us -> 40.5 us  [exchange(): return lax.all_to_all(x, axis, split_axis=0, concat_axis=0, tiled=True)]
    all_to_all x2 -> x1, blocking collectives: 41.1 us -> 27.1 us  [exchange(): return lax.all_to_all(x, axis, split_axis=0, concat_axis=0, tiled=True)]
    all_gather x1 -> x0, blocking collectives: 12.6 us -> none  [shards(): lax.all_gather(cut, 'tensor', axis=1).reshape(members * own, 2 * columns)]
    all_to_all x4 -> x5, starting transfers between devices: 30.2 us -> 37.6 us  [exchange(): return lax.all_to_all(x, axis, split_axis=0, concat_axis=0, tiled=True)]
    dot_general x9 -> x11, matrix products: 18.9 us -> 22.9 us  [dot(): lax.dot_general(a, b, (contract, ((), ())), preferred_element_type=F32)]
    unnamed x22 -> x20, local copies, waits for them, and re-layouts: 3.05 us -> 0.13 us
  transfers between devices with their start and end apart: 18 -> 19, of which waited for: 7 -> 7; matrix products, arithmetic and copies ran while one was open for 10% -> 10% of each run, Pallas kernels for 0% -> 0%
where the time goes in v9:
time: 249 us; the launch traced here: 245 us
  starting transfers between devices  85.2 us (34%)
  blocking collectives  59.7 us (24%)
  waiting for transfers between devices  50.2 us (20%)
  matrix products  22.9 us (9%)
  between operations  16.1 us (6%)
  local copies, waits for them, and re-layouts  5.81 us (2%)
  other arithmetic  5.05 us (2%)
    ppermute x12, starting transfers between devices, shift(): return lax.ppermute(x, DP, [(i, (i + by) % size) for i in range(size)])  47.6 us
    all_to_all x5, waiting for transfers between devices, exchange(): return lax.all_to_all(x, axis, split_axis=0, concat_axis=0, tiled=True)  40.5 us
    all_to_all x5, starting transfers between devices, exchange(): return lax.all_to_all(x, axis, split_axis=0, concat_axis=0, tiled=True)  37.6 us
    all_to_all x1, blocking collectives, exchange(): return lax.all_to_all(x, axis, split_axis=0, concat_axis=0, tiled=True)  27.1 us
    all_gather x1, blocking collectives, gather_dp(): quad = lax.all_gather(x, 'run', axis=0)  23.8 us
    dot_general x11, matrix products, dot(): lax.dot_general(a, b, (contract, ((), ())), preferred_element_type=F32)  22.9 us
    ppermute x12, waiting for transfers between devices, shift(): return lax.ppermute(x, DP, [(i, (i + by) % size) for i in range(size)])  9.6 us
    all_gather x1, blocking collectives, shards(): group = lax.all_gather(group, 'tensor', axis=1)  8.8 us
  transfers between devices with their start and end apart: 19, of which 7 were waited for; matrix products, arithmetic and copies ran while one was open for 10% of the time, Pallas kernels for 0%

profile of v9, /device:TPU:24, one launch (start us, length us, event | category | flops | bytes accessed | tf_op | source)
XLA Modules:
  0.0 245.0 jit_solution(7907815142225340635)
XLA Ops:
  10.5 4.8 %all-to-all-start = ((bf16[4,64,1152]{2,1,0:T(8,128)(2,1)}), bf16[4,64,1152]{2,1,0:T(8,128)(2,1)S(1)}, u32[]{:S(2)}, u32[]{:S(2)}) async-start(bf16[4,64,1152]{2,1,0:T(8,128)(2,1)} %pad_maximum_fusion.1), calls=%async_computation | async-start | bytes 1179648 | tf_op jit(solution)/shard_map/all_to_all | solution.py:21
  15.3 7.9 %all-to-all-done = bf16[4,64,1152]{2,1,0:T(8,128)(2,1)S(1)} async-done(((bf16[4,64,1152]{2,1,0:T(8,128)(2,1)}), bf16[4,64,1152]{2,1,0:T(8,128)(2,1)S(1)}, u32[]{:S(2)}, u32[]{:S(2)}) %all-to-all-start) | async-done | bytes 589856 | tf_op jit(solution)/shard_map/all_to_all | solution.py:21
  25.2 11.9 %all-to-all-start.1 = ((bf16[32,32,1152]{2,1,0:T(8,128)(2,1)}), bf16[32,32,1152]{2,1,0:T(8,128)(2,1)}, u32[]{:S(2)}, u32[]{:S(2)}) async-start(bf16[32,32,1152]{2,1,0:T(8,128)(2,1)} %broadcast_in_dim.18), calls=%async_computation.1 | async-start | bytes 4718592 | tf_op jit(solution)/shard_map/all_to_all | solution.py:21
  37.1 23.8 %all-gather = bf16[128,1152]{1,0:T(8,128)(2,1)S(1)} all-gather(bf16[32,1152]{1,0:T(8,128)(2,1)S(1)} %get-tuple-element.47), channel_id=2, replica_groups=mesh['run'=4,'place'=4,'replica'=8,'tensor'=4] {'run'}, dimensions={0}, use_global_device_ids=true | all-gather | bytes 368640 | tf_op jit(solution)/shard_map/all_gather | solution.py:39
  61.0 3.3 %collective-permute-start.2 = (bf16[2,32,1152]{2,1,0:T(8,128)(2,1)S(1)}, bf16[2,32,1152]{2,1,0:T(8,128)(2,1)S(1)}, u32[]{:S(2)}, u32[]{:S(2)}) collective-permute-start(bf16[2,32,1152]{2,1,0:T(8,128)(2,1)S(1)} %bitcast.120), channel_id=1, source_target_pairs={{0,448},{32,480},{64,0},{96,32},{128,64},{160,96},{192,128},{224,1... | collective-permute-start | bytes 442376 | tf_op jit(solution)/shard_map/ppermute | solution.py:35
  64.3 3.5 %collective-permute-start.3 = (bf16[2,32,1152]{2,1,0:T(8,128)(2,1)S(1)}, bf16[2,32,1152]{2,1,0:T(8,128)(2,1)S(1)}, u32[]{:S(2)}, u32[]{:S(2)}) collective-permute-start(bf16[2,32,1152]{2,1,0:T(8,128)(2,1)S(1)} %bitcast.119), channel_id=1, source_target_pairs={{0,64},{32,96},{64,128},{96,160},{128,192},{160,224},{192,256},{22... | collective-permute-start | bytes 442376 | tf_op jit(solution)/shard_map/ppermute | solution.py:35
  69.1 2.3 collective-permute-start
  71.4 4.8 %collective-permute-start.1 = (bf16[4,32,1152]{2,1,0:T(8,128)(2,1)S(1)}, bf16[4,32,1152]{2,1,0:T(8,128)(2,1)S(1)}, u32[]{:S(2)}, u32[]{:S(2)}) collective-permute-start(bf16[4,32,1152]{2,1,0:T(8,128)(2,1)S(1)} %bitcast.94), channel_id=1, source_target_pairs={{0,480},{32,0},{64,32},{96,64},{128,96},{160,128},{192,160},{224,1... | collective-permute-start | bytes 884744 | tf_op jit(solution)/shard_map/ppermute | solution.py:35
  77.0 4.5 %collective-permute-done = bf16[4,32,1152]{2,1,0:T(8,128)(2,1)S(1)} collective-permute-done((bf16[4,32,1152]{2,1,0:T(8,128)(2,1)S(1)}, bf16[4,32,1152]{2,1,0:T(8,128)(2,1)S(1)}, u32[]{:S(2)}, u32[]{:S(2)}) %collective-permute-start) | collective-permute-done | bytes 294944 | tf_op jit(solution)/shard_map/ppermute | solution.py:35
  81.7 2.6 %fusion.6 = bf16[1024,128]{0,1:T(8,128)(2,1)S(1)} fusion(bf16[1024,1152]{1,0:T(8,128)(2,1)} %bitcast.3, bf16[128,1152]{1,0:T(8,128)(2,1)} %bitcast.116, f32[]{:T(128)} %bitcast.92, f32[]{:T(128)} %bitcast), kind=kOutput, calls=%fused_computation.17 | convolution fusion | flops 302907392 | bytes 2916360 | tf_op jit(solution)/shard_map/dot_general | solution.py:17
  84.4 3.4 %multiply_convert_fusion = bf16[1024,384]{0,1:T(8,128)(2,1)S(1)} fusion(bf16[1024,1152]{1,0:T(8,128)(2,1)} %bitcast.3, bf16[384,1152]{1,0:T(8,128)(2,1)S(1)} %bitcast.100, f32[]{:T(128)} %bitcast.91, f32[]{:T(128)} %bitcast, s32[384]{0:T(512)S(1)} %fusion.30), kind=kOutput, calls=%fused_computation.6 | convolution fusion | flops 910688256 | bytes 4032008 | tf_op jit(solution)/shard_map/dot_general | solution.py:17
  87.8 3.0 %convolution_convert_fusion = bf16[1024,1152]{1,0:T(8,128)(2,1)} fusion(bf16[128,1152]{1,0:T(8,128)(2,1)S(1)} %bitcast.117, bf16[384,1152]{1,0:T(8,128)(2,1)S(1)} %bitcast.101, bf16[1024,128]{0,1:T(8,128)(2,1)S(1)} %fusion.6, bf16[1024,384]{0,1:T(8,128)(2,1)S(1)} %multiply_convert_fusion), kind=kOutput, calls=%fused_computation.1 | convolution fusion | flops 1213595648 | bytes 4587520 | tf_op jit(solution)/shard_map/dot_general | solution.py:17
  90.8 2.9 %convolution_convert_fusion.1 = bf16[384,1152]{1,0:T(8,128)(2,1)S(1)} fusion(bf16[1024,384]{0,1:T(8,128)(2,1)S(1)} %multiply_convert_fusion, bf16[1024,1152]{1,0:T(8,128)(2,1)} %bitcast.3), kind=kOutput, calls=%fused_computation.2 | convolution fusion | flops 906412032 | bytes 4030464 | tf_op jit(solution)/shard_map/dot_general | solution.py:17
  93.7 4.4 %collective-permute-start.4 = (bf16[4,32,1152]{2,1,0:T(8,128)(2,1)S(1)}, bf16[4,32,1152]{2,1,0:T(8,128)(2,1)S(1)}, u32[]{:S(2)}, u32[]{:S(2)}) collective-permute-start(bf16[4,32,1152]{2,1,0:T(8,128)(2,1)S(1)} %bitcast.111), channel_id=1, source_target_pairs={{0,480},{32,0},{64,32},{96,64},{128,96},{160,128},{192,160},{224,1... | collective-permute-start | bytes 884744 | tf_op jit(solution)/shard_map/ppermute | solution.py:35
  100.1 2.2 convolution_convert_fusion.2
  103.0 3.5 %collective-permute-start.6 = (bf16[2,32,1152]{2,1,0:T(8,128)(2,1)}, bf16[2,32,1152]{2,1,0:T(8,128)(2,1)S(1)}, u32[]{:S(2)}, u32[]{:S(2)}) collective-permute-start(bf16[2,32,1152]{2,1,0:T(8,128)(2,1)} %bitcast.15), channel_id=1, source_target_pairs={{0,64},{32,96},{64,128},{96,160},{128,192},{160,224},{192,256},{22... | collective-permute-start | bytes 442376 | tf_op jit(solution)/shard_map/ppermute | solution.py:35
  106.5 4.5 %collective-permute-start.7 = (bf16[2,32,1152]{2,1,0:T(8,128)(2,1)S(1)}, bf16[2,32,1152]{2,1,0:T(8,128)(2,1)S(1)}, u32[]{:S(2)}, u32[]{:S(2)}) collective-permute-start(bf16[2,32,1152]{2,1,0:T(8,128)(2,1)S(1)} %bitcast.118), channel_id=1, source_target_pairs={{0,448},{32,480},{64,0},{96,32},{128,64},{160,96},{192,128},{224,1... | collective-permute-start | bytes 442376 | tf_op jit(solution)/shard_map/ppermute | solution.py:35
  111.0 7.4 %all-to-all-start.2 = ((bf16[32,32,1152]{2,1,0:T(8,128)(2,1)}), bf16[32,32,1152]{2,1,0:T(8,128)(2,1)}, u32[]{:S(2)}, u32[]{:S(2)}) async-start(bf16[32,32,1152]{2,1,0:T(8,128)(2,1)} %bitcast.96), calls=%async_computation.2 | async-start | bytes 4718592 | tf_op jit(solution)/shard_map/all_to_all | solution.py:21
  118.7 5.1 %collective-permute-start.10 = (bf16[16,1152]{1,0:T(8,128)(2,1)S(1)}, bf16[16,1152]{1,0:T(8,128)(2,1)S(1)}, u32[]{:S(2)}, u32[]{:S(2)}) collective-permute-start(bf16[16,1152]{1,0:T(8,128)(2,1)S(1)} %get-tuple-element.50), channel_id=1, source_target_pairs={{0,384},{32,416},{64,448},{96,480},{128,0},{160,32},{192,64},{224,... | collective-permute-start | bytes 110600 | tf_op jit(solution)/shard_map/ppermute | solution.py:35
  123.8 4.7 %collective-permute-start.8 = (bf16[16,1152]{1,0:T(8,128)(2,1)S(1)}, bf16[16,1152]{1,0:T(8,128)(2,1)S(1)}, u32[]{:S(2)}, u32[]{:S(2)}) collective-permute-start(bf16[16,1152]{1,0:T(8,128)(2,1)S(1)} %get-tuple-element.49), channel_id=1, source_target_pairs={{0,128},{32,160},{64,192},{96,224},{128,256},{160,288},{192,320},{... | collective-permute-start | bytes 110600 | tf_op jit(solution)/shard_map/ppermute | solution.py:35
  129.4 4.1 %collective-permute-done.8 = bf16[16,1152]{1,0:T(8,128)(2,1)S(1)} collective-permute-done((bf16[16,1152]{1,0:T(8,128)(2,1)S(1)}, bf16[16,1152]{1,0:T(8,128)(2,1)S(1)}, u32[]{:S(2)}, u32[]{:S(2)}) %collective-permute-start.8) | collective-permute-done | bytes 36896 | tf_op jit(solution)/shard_map/ppermute | solution.py:35
  133.6 4.7 %collective-permute-start.9 = (bf16[32,1152]{1,0:T(8,128)(2,1)S(1)}, bf16[32,1152]{1,0:T(8,128)(2,1)S(1)}, u32[]{:S(2)}, u32[]{:S(2)}) collective-permute-start(bf16[32,1152]{1,0:T(8,128)(2,1)S(1)} %pad_maximum_fusion.8), channel_id=1, source_target_pairs={{0,128},{32,160},{64,192},{96,224},{128,256},{160,288},{192,320},{... | collective-permute-start | bytes 221192 | tf_op jit(solution)/shard_map/ppermute | solution.py:35
  138.3 5.0 %collective-permute-start.11 = (bf16[32,1152]{1,0:T(8,128)(2,1)S(1)}, bf16[32,1152]{1,0:T(8,128)(2,1)S(1)}, u32[]{:S(2)}, u32[]{:S(2)}) collective-permute-start(bf16[32,1152]{1,0:T(8,128)(2,1)S(1)} %pad_maximum_fusion.9), channel_id=1, source_target_pairs={{0,384},{32,416},{64,448},{96,480},{128,0},{160,32},{192,64},{224,... | collective-permute-start | bytes 221192 | tf_op jit(solution)/shard_map/ppermute | solution.py:35
  143.4 8.5 %all-to-all-done.2 = bf16[32,32,1152]{2,1,0:T(8,128)(2,1)} async-done(((bf16[32,32,1152]{2,1,0:T(8,128)(2,1)}), bf16[32,32,1152]{2,1,0:T(8,128)(2,1)}, u32[]{:S(2)}, u32[]{:S(2)}) %all-to-all-start.2) | async-done | bytes 2359328 | tf_op jit(solution)/shard_map/all_to_all | solution.py:21
  155.9 7.5 %all-to-all-start.3 = ((bf16[32,32,288]{2,1,0:T(8,128)(2,1)}), bf16[32,32,288]{2,1,0:T(8,128)(2,1)S(1)}, u32[]{:S(2)}, u32[]{:S(2)}) async-start(bf16[32,32,288]{2,1,0:T(8,128)(2,1)} %bitcast.26), calls=%async_computation.3 | async-start | bytes 1572864 | tf_op jit(solution)/shard_map/all_to_all | solution.py:21
  163.4 14.9 %all-to-all-done.3 = bf16[32,32,288]{2,1,0:T(8,128)(2,1)S(1)} async-done(((bf16[32,32,288]{2,1,0:T(8,128)(2,1)}), bf16[32,32,288]{2,1,0:T(8,128)(2,1)S(1)}, u32[]{:S(2)}, u32[]{:S(2)}) %all-to-all-start.3) | async-done | bytes 589856 | tf_op jit(solution)/shard_map/all_to_all | solution.py:21
  178.2 2.1 convolution_convert_fusion.6
  180.4 2.1 convolution_convert_fusion.5
  182.7 27.1 %all_to_all.30 = bf16[16,80,128]{2,1,0:T(8,128)(2,1)S(1)} all-to-all(bf16[16,80,128]{2,1,0:T(8,128)(2,1)S(1)} %fusion.16), channel_id=1, replica_groups=mesh['run'=4,'place'=4,'replica'=8,'tensor'=4] {'run','place'}, dimensions={0} | all-to-all | bytes 655360 | tf_op jit(solution)/shard_map/all_to_all | solution.py:21
  210.6 5.9 %all-to-all-start.5 = ((bf16[16,80,128]{2,1,0:T(8,128)(2,1)}), bf16[16,80,128]{2,1,0:T(8,128)(2,1)S(1)}, u32[]{:S(2)}, u32[]{:S(2)}) async-start(bf16[16,80,128]{2,1,0:T(8,128)(2,1)} %broadcast_in_dim.20), calls=%async_computation.5 | async-start | bytes 655360 | tf_op jit(solution)/shard_map/all_to_all | solution.py:21
  216.6 8.8 %all-gather.1 = bf16[2,128,1152]{2,1,0:T(8,128)(2,1)S(1)} all-gather(bf16[2,32,1152]{2,1,0:T(8,128)(2,1)S(1)} %pad_maximum_fusion.3), channel_id=3, replica_groups=mesh['run'=4,'place'=4,'replica'=8,'tensor'=4] {'tensor'}, dimensions={1}, use_global_device_ids=true | all-gather | bytes 737280 | tf_op jit(solution)/shard_map/all_gather | solution.py:168
  227.7 9.2 %all-to-all-done.5 = bf16[16,80,128]{2,1,0:T(8,128)(2,1)S(1)} async-done(((bf16[16,80,128]{2,1,0:T(8,128)(2,1)}), bf16[16,80,128]{2,1,0:T(8,128)(2,1)S(1)}, u32[]{:S(2)}, u32[]{:S(2)}) %all-to-all-start.5) | async-done | bytes 327712 | tf_op jit(solution)/shard_map/all_to_all | solution.py:21
  (85 shorter events, 18.5 us)
Async XLA Ops:
  7.2 1.9 copy-start
  7.2 1.9 copy-start.2
  9.6 13.7 %copy-start.3 = (bf16[128,1152]{1,0:T(8,128)(2,1)S(1)}, bf16[128,1152]{1,0:T(8,128)(2,1)}, u32[]{:S(2)}) copy-start(bf16[128,1152]{1,0:T(8,128)(2,1)} %param.8) | copy-start | bytes 884740
  9.6 13.7 %copy-start.5 = (bf16[128,1152]{1,0:T(8,128)(2,1)S(1)}, bf16[128,1152]{1,0:T(8,128)(2,1)}, u32[]{:S(2)}) copy-start(bf16[128,1152]{1,0:T(8,128)(2,1)} %param.11) | copy-start | bytes 884740
  10.5 12.7 %all-to-all-start = ((bf16[4,64,1152]{2,1,0:T(8,128)(2,1)}), bf16[4,64,1152]{2,1,0:T(8,128)(2,1)S(1)}, u32[]{:S(2)}, u32[]{:S(2)}) async-start(bf16[4,64,1152]{2,1,0:T(8,128)(2,1)} %pad_maximum_fusion.1), calls=%async_computation | async-start | bytes 1179648 | tf_op jit(solution)/shard_map/all_to_all | solution.py:21
  25.2 56.6 %all-to-all-start.1 = ((bf16[32,32,1152]{2,1,0:T(8,128)(2,1)}), bf16[32,32,1152]{2,1,0:T(8,128)(2,1)}, u32[]{:S(2)}, u32[]{:S(2)}) async-start(bf16[32,32,1152]{2,1,0:T(8,128)(2,1)} %broadcast_in_dim.18), calls=%async_computation.1 | async-start | bytes 4718592 | tf_op jit(solution)/shard_map/all_to_all | solution.py:21
  37.1 126.3 %all-gather.5.cloned.1.call-start = ((), (), s32[]{:S(2)}) async-start(), calls=%async_computation.6 | async-start | bytes 1253376 | tf_op jit(solution)/shard_map/all_gather | solution.py:115
  61.0 15.3 %collective-permute-start.2 = (bf16[2,32,1152]{2,1,0:T(8,128)(2,1)S(1)}, bf16[2,32,1152]{2,1,0:T(8,128)(2,1)S(1)}, u32[]{:S(2)}, u32[]{:S(2)}) collective-permute-start(bf16[2,32,1152]{2,1,0:T(8,128)(2,1)S(1)} %bitcast.120), channel_id=1, source_target_pairs={{0,448},{32,480},{64,0},{96,32},{128,64},{160,96},{192,128},{224,1... | collective-permute-start | bytes 442376 | tf_op jit(solution)/shard_map/ppermute | solution.py:35
  64.3 12.0 %collective-permute-start.3 = (bf16[2,32,1152]{2,1,0:T(8,128)(2,1)S(1)}, bf16[2,32,1152]{2,1,0:T(8,128)(2,1)S(1)}, u32[]{:S(2)}, u32[]{:S(2)}) collective-permute-start(bf16[2,32,1152]{2,1,0:T(8,128)(2,1)S(1)} %bitcast.119), channel_id=1, source_target_pairs={{0,64},{32,96},{64,128},{96,160},{128,192},{160,224},{192,256},{22... | collective-permute-start | bytes 442376 | tf_op jit(solution)/shard_map/ppermute | solution.py:35
  69.1 12.5 %collective-permute-start = (bf16[4,32,1152]{2,1,0:T(8,128)(2,1)S(1)}, bf16[4,32,1152]{2,1,0:T(8,128)(2,1)S(1)}, u32[]{:S(2)}, u32[]{:S(2)}) collective-permute-start(bf16[4,32,1152]{2,1,0:T(8,128)(2,1)S(1)} %bitcast.93), channel_id=1, source_target_pairs={{0,32},{32,64},{64,96},{96,128},{128,160},{160,192},{192,224},{224... | collective-permute-start | bytes 884744 | tf_op jit(solution)/shard_map/ppermute | solution.py:35
  71.4 10.2 %collective-permute-start.1 = (bf16[4,32,1152]{2,1,0:T(8,128)(2,1)S(1)}, bf16[4,32,1152]{2,1,0:T(8,128)(2,1)S(1)}, u32[]{:S(2)}, u32[]{:S(2)}) collective-permute-start(bf16[4,32,1152]{2,1,0:T(8,128)(2,1)S(1)} %bitcast.94), channel_id=1, source_target_pairs={{0,480},{32,0},{64,32},{96,64},{128,96},{160,128},{192,160},{224,1... | collective-permute-start | bytes 884744 | tf_op jit(solution)/shard_map/ppermute | solution.py:35
  76.2 104.2 %all-gather.7.cloned.1.call-start = ((), (), s32[]{:S(2)}) async-start(), calls=%async_computation.7 | async-start | bytes 1253376 | tf_op jit(solution)/shard_map/all_gather | solution.py:115
  84.3 3.4 %copy-start.7 = (bf16[4,32,1152]{2,1,0:T(8,128)(2,1)S(1)}, bf16[4,32,1152]{2,1,0:T(8,128)(2,1)}, u32[]{:S(2)}) copy-start(bf16[4,32,1152]{2,1,0:T(8,128)(2,1)} %pad_maximum_fusion.2) | copy-start | bytes 884740
  93.7 24.8 %collective-permute-start.4 = (bf16[4,32,1152]{2,1,0:T(8,128)(2,1)S(1)}, bf16[4,32,1152]{2,1,0:T(8,128)(2,1)S(1)}, u32[]{:S(2)}, u32[]{:S(2)}) collective-permute-start(bf16[4,32,1152]{2,1,0:T(8,128)(2,1)S(1)} %bitcast.111), channel_id=1, source_target_pairs={{0,480},{32,0},{64,32},{96,64},{128,96},{160,128},{192,160},{224,1... | collective-permute-start | bytes 884744 | tf_op jit(solution)/shard_map/ppermute | solution.py:35
  98.2 20.3 %collective-permute-start.5 = (bf16[4,32,1152]{2,1,0:T(8,128)(2,1)S(1)}, bf16[4,32,1152]{2,1,0:T(8,128)(2,1)S(1)}, u32[]{:S(2)}, u32[]{:S(2)}) collective-permute-start(bf16[4,32,1152]{2,1,0:T(8,128)(2,1)S(1)} %bitcast.110), channel_id=1, source_target_pairs={{0,32},{32,64},{64,96},{96,128},{128,160},{160,192},{192,224},{224... | collective-permute-start | bytes 884744 | tf_op jit(solution)/shard_map/ppermute | solution.py:35
  103.0 15.5 %collective-permute-start.6 = (bf16[2,32,1152]{2,1,0:T(8,128)(2,1)}, bf16[2,32,1152]{2,1,0:T(8,128)(2,1)S(1)}, u32[]{:S(2)}, u32[]{:S(2)}) collective-permute-start(bf16[2,32,1152]{2,1,0:T(8,128)(2,1)} %bitcast.15), channel_id=1, source_target_pairs={{0,64},{32,96},{64,128},{96,160},{128,192},{160,224},{192,256},{22... | collective-permute-start | bytes 442376 | tf_op jit(solution)/shard_map/ppermute | solution.py:35
  106.5 12.0 %collective-permute-start.7 = (bf16[2,32,1152]{2,1,0:T(8,128)(2,1)S(1)}, bf16[2,32,1152]{2,1,0:T(8,128)(2,1)S(1)}, u32[]{:S(2)}, u32[]{:S(2)}) collective-permute-start(bf16[2,32,1152]{2,1,0:T(8,128)(2,1)S(1)} %bitcast.118), channel_id=1, source_target_pairs={{0,448},{32,480},{64,0},{96,32},{128,64},{160,96},{192,128},{224,1... | collective-permute-start | bytes 442376 | tf_op jit(solution)/shard_map/ppermute | solution.py:35
  111.0 40.9 %all-to-all-start.2 = ((bf16[32,32,1152]{2,1,0:T(8,128)(2,1)}), bf16[32,32,1152]{2,1,0:T(8,128)(2,1)}, u32[]{:S(2)}, u32[]{:S(2)}) async-start(bf16[32,32,1152]{2,1,0:T(8,128)(2,1)} %bitcast.96), calls=%async_computation.2 | async-start | bytes 4718592 | tf_op jit(solution)/shard_map/all_to_all | solution.py:21
  118.7 10.7 %collective-permute-start.10 = (bf16[16,1152]{1,0:T(8,128)(2,1)S(1)}, bf16[16,1152]{1,0:T(8,128)(2,1)S(1)}, u32[]{:S(2)}, u32[]{:S(2)}) collective-permute-start(bf16[16,1152]{1,0:T(8,128)(2,1)S(1)} %get-tuple-element.50), channel_id=1, source_target_pairs={{0,384},{32,416},{64,448},{96,480},{128,0},{160,32},{192,64},{224,... | collective-permute-start | bytes 110600 | tf_op jit(solution)/shard_map/ppermute | solution.py:35
  123.8 9.8 %collective-permute-start.8 = (bf16[16,1152]{1,0:T(8,128)(2,1)S(1)}, bf16[16,1152]{1,0:T(8,128)(2,1)S(1)}, u32[]{:S(2)}, u32[]{:S(2)}) collective-permute-start(bf16[16,1152]{1,0:T(8,128)(2,1)S(1)} %get-tuple-element.49), channel_id=1, source_target_pairs={{0,128},{32,160},{64,192},{96,224},{128,256},{160,288},{192,320},{... | collective-permute-start | bytes 110600 | tf_op jit(solution)/shard_map/ppermute | solution.py:35
  128.5 25.5 %copy-start.4 = (bf16[128,1152]{1,0:T(8,128)(2,1)S(1)}, bf16[128,1152]{1,0:T(8,128)(2,1)}, u32[]{:S(2)}) copy-start(bf16[128,1152]{1,0:T(8,128)(2,1)} %param.8) | copy-start | bytes 884740
  128.5 25.5 %copy-start.6 = (bf16[128,1152]{1,0:T(8,128)(2,1)S(1)}, bf16[128,1152]{1,0:T(8,128)(2,1)}, u32[]{:S(2)}) copy-start(bf16[128,1152]{1,0:T(8,128)(2,1)} %param.11) | copy-start | bytes 884740
  133.6 20.3 %collective-permute-start.9 = (bf16[32,1152]{1,0:T(8,128)(2,1)S(1)}, bf16[32,1152]{1,0:T(8,128)(2,1)S(1)}, u32[]{:S(2)}, u32[]{:S(2)}) collective-permute-start(bf16[32,1152]{1,0:T(8,128)(2,1)S(1)} %pad_maximum_fusion.8), channel_id=1, source_target_pairs={{0,128},{32,160},{64,192},{96,224},{128,256},{160,288},{192,320},{... | collective-permute-start | bytes 221192 | tf_op jit(solution)/shard_map/ppermute | solution.py:35
  138.3 15.6 %collective-permute-start.11 = (bf16[32,1152]{1,0:T(8,128)(2,1)S(1)}, bf16[32,1152]{1,0:T(8,128)(2,1)S(1)}, u32[]{:S(2)}, u32[]{:S(2)}) collective-permute-start(bf16[32,1152]{1,0:T(8,128)(2,1)S(1)} %pad_maximum_fusion.9), channel_id=1, source_target_pairs={{0,384},{32,416},{64,448},{96,480},{128,0},{160,32},{192,64},{224,... | collective-permute-start | bytes 221192 | tf_op jit(solution)/shard_map/ppermute | solution.py:35
  155.9 22.4 %all-to-all-start.3 = ((bf16[32,32,288]{2,1,0:T(8,128)(2,1)}), bf16[32,32,288]{2,1,0:T(8,128)(2,1)S(1)}, u32[]{:S(2)}, u32[]{:S(2)}) async-start(bf16[32,32,288]{2,1,0:T(8,128)(2,1)} %bitcast.26), calls=%async_computation.3 | async-start | bytes 1572864 | tf_op jit(solution)/shard_map/all_to_all | solution.py:21
  210.6 15.9 %copy-start.1 = (bf16[544,1152]{1,0:T(8,128)(2,1)S(1)}, bf16[544,1152]{1,0:T(8,128)(2,1)}, u32[]{:S(2)}) copy-start(bf16[544,1152]{1,0:T(8,128)(2,1)} %param.10) | copy-start | bytes 3760132
  210.6 26.3 %all-to-all-start.5 = ((bf16[16,80,128]{2,1,0:T(8,128)(2,1)}), bf16[16,80,128]{2,1,0:T(8,128)(2,1)S(1)}, u32[]{:S(2)}, u32[]{:S(2)}) async-start(bf16[16,80,128]{2,1,0:T(8,128)(2,1)} %broadcast_in_dim.20), calls=%async_computation.5 | async-start | bytes 655360 | tf_op jit(solution)/shard_map/all_to_all | solution.py:21
Sparse Core Ops, SparseCore 0:
  76.3 41.0 all-gather.4
  119.5 58.8 all-gather.6

commit v10 on v8

--- a/solution.py
+++ b/solution.py
@@ -48,10 +48,8 @@
     run = lax.axis_index("run")
     one = shift(x[4:8], -1)
     two = shift(x[8:12], 1)
-    three = shift(x[12:14], 2)
-    four = shift(x[14:16], -2)
-    quad = x[0:4].astype(F32) + one.astype(F32) + two.astype(F32)
-    quad = quad + jnp.concatenate([three, four], axis=0).astype(F32)
+    three = shift(x[12:16], 2)
+    quad = x[0:4].astype(F32) + one.astype(F32) + two.astype(F32) + three.astype(F32)
     near, above, far, below = (
         lax.dynamic_index_in_dim(quad, (run + k) % 4, 0, keepdims=False) for k in range(4)
     )

time: 247 us -> 247 us (level)
  waiting for transfers between devices: 31.3 us -> 37.5 us
  starting transfers between devices: 78.2 us -> 73.5 us
    all_gather x2, waiting for transfers between devices: 0.04 us -> 5.91 us  [shards(): lax.all_gather(after(units, summed), 'replica', axis=0, tiled=True)]
    ppermute x12 -> x11, waiting for transfers between devices: 8.72 us -> 13.9 us  [shift(): return lax.ppermute(x, DP, [(i, (i + by) % size) for i in range(size)])]
    all_to_all x4, waiting for transfers between devices: 22.5 us -> 17.6 us  [exchange(): return lax.all_to_all(x, axis, split_axis=0, concat_axis=0, tiled=True)]
    ppermute x12 -> x11, starting transfers between devices: 47.9 us -> 43.3 us  [shift(): return lax.ppermute(x, DP, [(i, (i + by) % size) for i in range(size)])]
    all_gather x1, blocking collectives: 12.6 us -> 10 us  [shards(): lax.all_gather(cut, 'tensor', axis=1).reshape(members * own, 2 * columns)]
  transfers between devices with their start and end apart: 18 -> 17, of which waited for: 7 -> 10; matrix products, arithmetic and copies ran while one was open for 10% -> 9% of each run, Pallas kernels for 0% -> 0%
where the time goes in v10:
time: 247 us; the launch traced here: 246 us
  blocking collectives  86 us (35%)
  starting transfers between devices  73.5 us (30%)
  waiting for transfers between devices  37.5 us (15%)
  matrix products  19 us (8%)
  between operations  16 us (6%)
  local copies, waits for them, and re-layouts  8.49 us (3%)
  other arithmetic  5.16 us (2%)
    all_to_all x2, blocking collectives, exchange(): return lax.all_to_all(x, axis, split_axis=0, concat_axis=0, tiled=True)  43.4 us
    ppermute x11, starting transfers between devices, shift(): return lax.ppermute(x, DP, [(i, (i + by) % size) for i in range(size)])  43.3 us
    all_to_all x4, starting transfers between devices, exchange(): return lax.all_to_all(x, axis, split_axis=0, concat_axis=0, tiled=True)  30.1 us
    all_gather x1, blocking collectives, gather_dp(): quad = lax.all_gather(x, 'run', axis=0)  24.1 us
    dot_general x9, matrix products, dot(): lax.dot_general(a, b, (contract, ((), ())), preferred_element_type=F32)  19 us
    all_to_all x4, waiting for transfers between devices, exchange(): return lax.all_to_all(x, axis, split_axis=0, concat_axis=0, tiled=True)  17.6 us
    ppermute x11, waiting for transfers between devices, shift(): return lax.ppermute(x, DP, [(i, (i + by) % size) for i in range(size)])  13.9 us
    all_gather x1, blocking collectives, shards(): lax.all_gather(cut, 'tensor', axis=1).reshape(members * own, 2 * columns)  10 us
  transfers between devices with their start and end apart: 17, of which 10 were waited for; matrix products, arithmetic and copies ran while one was open for 9% of the time, Pallas kernels for 0%

profile of v10, /device:TPU:24, one launch (start us, length us, event | category | flops | bytes accessed | tf_op | source)
XLA Modules:
  0.0 245.5 jit_solution(11714360661759661229)
XLA Ops:
  7.2 1.9 convolution_convert_fusion.3
  10.5 4.9 %all-to-all-start = ((bf16[4,64,1152]{2,1,0:T(8,128)(2,1)}), bf16[4,64,1152]{2,1,0:T(8,128)(2,1)S(1)}, u32[]{:S(2)}, u32[]{:S(2)}) async-start(bf16[4,64,1152]{2,1,0:T(8,128)(2,1)} %pad_maximum_fusion), calls=%async_computation | async-start | bytes 1179648 | tf_op jit(solution)/shard_map/all_to_all | solution.py:21
  15.4 7.9 %all-to-all-done = bf16[4,64,1152]{2,1,0:T(8,128)(2,1)S(1)} async-done(((bf16[4,64,1152]{2,1,0:T(8,128)(2,1)}), bf16[4,64,1152]{2,1,0:T(8,128)(2,1)S(1)}, u32[]{:S(2)}, u32[]{:S(2)}) %all-to-all-start) | async-done | bytes 589856 | tf_op jit(solution)/shard_map/all_to_all | solution.py:21
  25.3 11.9 %all-to-all-start.1 = ((bf16[32,32,1152]{2,1,0:T(8,128)(2,1)}), bf16[32,32,1152]{2,1,0:T(8,128)(2,1)}, u32[]{:S(2)}, u32[]{:S(2)}) async-start(bf16[32,32,1152]{2,1,0:T(8,128)(2,1)} %broadcast_in_dim.16), calls=%async_computation.1 | async-start | bytes 4718592 | tf_op jit(solution)/shard_map/all_to_all | solution.py:21
  38.6 24.1 %all-gather = bf16[128,1152]{1,0:T(8,128)(2,1)S(1)} all-gather(bf16[32,1152]{1,0:T(8,128)(2,1)S(1)} %get-tuple-element.47), channel_id=2, replica_groups=mesh['run'=4,'place'=4,'replica'=8,'tensor'=4] {'run'}, dimensions={0}, use_global_device_ids=true | all-gather | bytes 368640 | tf_op jit(solution)/shard_map/all_gather | solution.py:39
  62.7 2.2 collective-permute-start
  65.0 4.8 %collective-permute-start.1 = (bf16[4,32,1152]{2,1,0:T(8,128)(2,1)S(1)}, bf16[4,32,1152]{2,1,0:T(8,128)(2,1)S(1)}, u32[]{:S(2)}, u32[]{:S(2)}) collective-permute-start(bf16[4,32,1152]{2,1,0:T(8,128)(2,1)S(1)} %bitcast.93), channel_id=1, source_target_pairs={{0,480},{32,0},{64,32},{96,64},{128,96},{160,128},{192,160},{224,1... | collective-permute-start | bytes 884744 | tf_op jit(solution)/shard_map/ppermute | solution.py:35
  70.6 2.2 collective-permute-start.2
  72.8 4.6 %collective-permute-start.3 = (bf16[2,32,1152]{2,1,0:T(8,128)(2,1)S(1)}, bf16[2,32,1152]{2,1,0:T(8,128)(2,1)S(1)}, u32[]{:S(2)}, u32[]{:S(2)}) collective-permute-start(bf16[2,32,1152]{2,1,0:T(8,128)(2,1)S(1)} %bitcast.115), channel_id=1, source_target_pairs={{0,64},{32,96},{64,128},{96,160},{128,192},{160,224},{192,256},{22... | collective-permute-start | bytes 442376 | tf_op jit(solution)/shard_map/ppermute | solution.py:35
  83.2 4.3 %multiply_convert_fusion = bf16[1024,512]{1,0:T(8,128)(2,1)S(1)} fusion(bf16[1024,1152]{1,0:T(8,128)(2,1)} %bitcast.6, bf16[512,1152]{1,0:T(8,128)(2,1)} %bitcast.117, f32[]{:T(128)} %bitcast.91, f32[]{:T(128)} %bitcast, s32[512]{0:T(512)S(1)} %fusion.17), kind=kOutput, calls=%fused_computation.5 | convolution fusion | flops 1214251008 | bytes 4589576 | tf_op jit(solution)/shard_map/dot_general | solution.py:17
  87.5 3.0 %convolution_convert_fusion = bf16[1024,1152]{1,0:T(8,128)(2,1)} fusion(bf16[1024,512]{1,0:T(8,128)(2,1)S(1)} %multiply_convert_fusion, bf16[512,1152]{1,0:T(8,128)(2,1)S(1)} %bitcast.118), kind=kOutput, calls=%fused_computation.1 | convolution fusion | flops 1209139200 | bytes 4587520 | tf_op jit(solution)/shard_map/dot_general | solution.py:17
  90.4 3.2 %convolution_convert_fusion.1 = bf16[512,1152]{1,0:T(8,128)(2,1)S(1)} fusion(bf16[1024,512]{1,0:T(8,128)(2,1)S(1)} %multiply_convert_fusion, bf16[1024,1152]{1,0:T(8,128)(2,1)} %bitcast.6), kind=kOutput, calls=%fused_computation.2 | convolution fusion | flops 1208549376 | bytes 4587520 | tf_op jit(solution)/shard_map/dot_general | solution.py:17
  93.8 2.7 %collective-permute-start.4 = (bf16[4,32,1152]{2,1,0:T(8,128)(2,1)S(1)}, bf16[4,32,1152]{2,1,0:T(8,128)(2,1)S(1)}, u32[]{:S(2)}, u32[]{:S(2)}) collective-permute-start(bf16[4,32,1152]{2,1,0:T(8,128)(2,1)S(1)} %bitcast.106), channel_id=1, source_target_pairs={{0,480},{32,0},{64,32},{96,64},{128,96},{160,128},{192,160},{224,1... | collective-permute-start | bytes 884744 | tf_op jit(solution)/shard_map/ppermute | solution.py:35
  96.5 3.8 %collective-permute-start.5 = (bf16[4,32,1152]{2,1,0:T(8,128)(2,1)S(1)}, bf16[4,32,1152]{2,1,0:T(8,128)(2,1)S(1)}, u32[]{:S(2)}, u32[]{:S(2)}) collective-permute-start(bf16[4,32,1152]{2,1,0:T(8,128)(2,1)S(1)} %bitcast.105), channel_id=1, source_target_pairs={{0,32},{32,64},{64,96},{96,128},{128,160},{160,192},{192,224},{224... | collective-permute-start | bytes 884744 | tf_op jit(solution)/shard_map/ppermute | solution.py:35
  100.4 3.4 %collective-permute-start.6 = (bf16[4,32,1152]{2,1,0:T(8,128)(2,1)S(1)}, bf16[4,32,1152]{2,1,0:T(8,128)(2,1)}, u32[]{:S(2)}, u32[]{:S(2)}) collective-permute-start(bf16[4,32,1152]{2,1,0:T(8,128)(2,1)S(1)} %bitcast.104), channel_id=1, source_target_pairs={{0,64},{32,96},{64,128},{96,160},{128,192},{160,224},{192,256},{22... | collective-permute-start | bytes 884744 | tf_op jit(solution)/shard_map/ppermute | solution.py:35
  103.8 7.4 %all-to-all-start.2 = ((bf16[32,32,1152]{2,1,0:T(8,128)(2,1)}), bf16[32,32,1152]{2,1,0:T(8,128)(2,1)}, u32[]{:S(2)}, u32[]{:S(2)}) async-start(bf16[32,32,1152]{2,1,0:T(8,128)(2,1)} %bitcast.95), calls=%async_computation.2 | async-start | bytes 4718592 | tf_op jit(solution)/shard_map/all_to_all | solution.py:21
  111.2 6.8 %collective-permute-done.6 = bf16[4,32,1152]{2,1,0:T(8,128)(2,1)} collective-permute-done((bf16[4,32,1152]{2,1,0:T(8,128)(2,1)S(1)}, bf16[4,32,1152]{2,1,0:T(8,128)(2,1)}, u32[]{:S(2)}, u32[]{:S(2)}) %collective-permute-start.6) | collective-permute-done | bytes 294944 | tf_op jit(solution)/shard_map/ppermute | solution.py:35
  119.2 2.5 %collective-permute-start.7 = (bf16[16,1152]{1,0:T(8,128)(2,1)S(1)}, bf16[16,1152]{1,0:T(8,128)(2,1)S(1)}, u32[]{:S(2)}, u32[]{:S(2)}) collective-permute-start(bf16[16,1152]{1,0:T(8,128)(2,1)S(1)} %get-tuple-element.50), channel_id=1, source_target_pairs={{0,128},{32,160},{64,192},{96,224},{128,256},{160,288},{192,320},{... | collective-permute-start | bytes 110600 | tf_op jit(solution)/shard_map/ppermute | solution.py:35
  121.7 7.3 %collective-permute-start.9 = (bf16[16,1152]{1,0:T(8,128)(2,1)S(1)}, bf16[16,1152]{1,0:T(8,128)(2,1)S(1)}, u32[]{:S(2)}, u32[]{:S(2)}) collective-permute-start(bf16[16,1152]{1,0:T(8,128)(2,1)S(1)} %get-tuple-element.51), channel_id=1, source_target_pairs={{0,384},{32,416},{64,448},{96,480},{128,0},{160,32},{192,64},{224,... | collective-permute-start | bytes 110600 | tf_op jit(solution)/shard_map/ppermute | solution.py:35
  129.2 2.4 collective-permute-done.9
  131.6 3.8 %collective-permute-start.8 = (bf16[32,1152]{1,0:T(8,128)(2,1)S(1)}, bf16[32,1152]{1,0:T(8,128)(2,1)S(1)}, u32[]{:S(2)}, u32[]{:S(2)}) collective-permute-start(bf16[32,1152]{1,0:T(8,128)(2,1)S(1)} %pad_maximum_fusion.7), channel_id=1, source_target_pairs={{0,128},{32,160},{64,192},{96,224},{128,256},{160,288},{192,320},{... | collective-permute-start | bytes 221192 | tf_op jit(solution)/shard_map/ppermute | solution.py:35
  135.4 6.1 %collective-permute-start.10 = (bf16[32,1152]{1,0:T(8,128)(2,1)S(1)}, bf16[32,1152]{1,0:T(8,128)(2,1)S(1)}, u32[]{:S(2)}, u32[]{:S(2)}) collective-permute-start(bf16[32,1152]{1,0:T(8,128)(2,1)S(1)} %pad_maximum_fusion.8), channel_id=1, source_target_pairs={{0,384},{32,416},{64,448},{96,480},{128,0},{160,32},{192,64},{224,... | collective-permute-start | bytes 221192 | tf_op jit(solution)/shard_map/ppermute | solution.py:35
  143.0 2.0 convert_reduce_fusion
  147.5 14.6 %all_to_all.30 = bf16[8,32,288]{2,1,0:T(8,128)(2,1)S(1)} all-to-all(bf16[8,32,288]{2,1,0:T(8,128)(2,1)S(1)} %bitcast.99), channel_id=1, replica_groups=mesh['run'=4,'place'=4,'replica'=8,'tensor'=4] {'replica'}, dimensions={0} | all-to-all | bytes 294912 | tf_op jit(solution)/shard_map/all_to_all | solution.py:21
  162.1 10.0 %all-gather.1 = bf16[8,128,288]{2,0,1:T(8,128)(2,1)S(1)} all-gather(bf16[8,32,288]{2,0,1:T(8,128)(2,1)S(1)} %copy.31), channel_id=3, replica_groups=mesh['run'=4,'place'=4,'replica'=8,'tensor'=4] {'tensor'}, dimensions={1}, use_global_device_ids=true | all-gather | bytes 737280 | tf_op jit(solution)/shard_map/all_gather | solution.py:151
  172.8 1.9 convolution_convert_fusion.5
  174.8 5.9 %all-gather.8.cloned.1.call-done = bf16[1024,544]{0,1:T(8,128)(2,1)} async-done(((bf16[128,544]{0,1:T(8,128)(2,1)}), bf16[1024,544]{0,1:T(8,128)(2,1)}) %all-gather.8.cloned.1.call-update) | async-done | bytes 1114128 | tf_op jit(solution)/shard_map/all_gather | solution.py:113
  180.7 1.9 convolution_convert_fusion.4
  182.8 28.9 %all_to_all.31 = bf16[16,80,128]{2,1,0:T(8,128)(2,1)S(1)} all-to-all(bf16[16,80,128]{2,1,0:T(8,128)(2,1)S(1)} %fusion.3), channel_id=1, replica_groups=mesh['run'=4,'place'=4,'replica'=8,'tensor'=4] {'run','place'}, dimensions={0} | all-to-all | bytes 655360 | tf_op jit(solution)/shard_map/all_to_all | solution.py:21
  212.5 5.9 %all-to-all-start.5 = ((bf16[16,80,128]{2,1,0:T(8,128)(2,1)}), bf16[16,80,128]{2,1,0:T(8,128)(2,1)S(1)}, u32[]{:S(2)}, u32[]{:S(2)}) async-start(bf16[16,80,128]{2,1,0:T(8,128)(2,1)} %broadcast_in_dim.17), calls=%async_computation.5 | async-start | bytes 655360 | tf_op jit(solution)/shard_map/all_to_all | solution.py:21
  218.4 8.4 %all-gather.2 = bf16[2,128,1152]{2,1,0:T(8,128)(2,1)S(1)} all-gather(bf16[2,32,1152]{2,1,0:T(8,128)(2,1)S(1)} %pad_maximum_fusion.2), channel_id=4, replica_groups=mesh['run'=4,'place'=4,'replica'=8,'tensor'=4] {'tensor'}, dimensions={1}, use_global_device_ids=true | all-gather | bytes 737280 | tf_op jit(solution)/shard_map/all_gather | solution.py:153
  229.2 8.3 %all-to-all-done.5 = bf16[16,80,128]{2,1,0:T(8,128)(2,1)S(1)} async-done(((bf16[16,80,128]{2,1,0:T(8,128)(2,1)}), bf16[16,80,128]{2,1,0:T(8,128)(2,1)S(1)}, u32[]{:S(2)}, u32[]{:S(2)}) %all-to-all-start.5) | async-done | bytes 327712 | tf_op jit(solution)/shard_map/all_to_all | solution.py:21
  (84 shorter events, 20.7 us)
Async XLA Ops:
  7.2 1.9 copy-start
  7.2 1.9 copy-start.2
  10.5 12.9 %copy-start.3 = (bf16[128,1152]{1,0:T(8,128)(2,1)S(1)}, bf16[128,1152]{1,0:T(8,128)(2,1)}, u32[]{:S(2)}) copy-start(bf16[128,1152]{1,0:T(8,128)(2,1)} %param.8) | copy-start | bytes 884740
  10.5 12.9 %copy-start.5 = (bf16[128,1152]{1,0:T(8,128)(2,1)S(1)}, bf16[128,1152]{1,0:T(8,128)(2,1)}, u32[]{:S(2)}) copy-start(bf16[128,1152]{1,0:T(8,128)(2,1)} %param.11) | copy-start | bytes 884740
  10.5 12.8 %all-to-all-start = ((bf16[4,64,1152]{2,1,0:T(8,128)(2,1)}), bf16[4,64,1152]{2,1,0:T(8,128)(2,1)S(1)}, u32[]{:S(2)}, u32[]{:S(2)}) async-start(bf16[4,64,1152]{2,1,0:T(8,128)(2,1)} %pad_maximum_fusion), calls=%async_computation | async-start | bytes 1179648 | tf_op jit(solution)/shard_map/all_to_all | solution.py:21
  25.3 57.9 %all-to-all-start.1 = ((bf16[32,32,1152]{2,1,0:T(8,128)(2,1)}), bf16[32,32,1152]{2,1,0:T(8,128)(2,1)}, u32[]{:S(2)}, u32[]{:S(2)}) async-start(bf16[32,32,1152]{2,1,0:T(8,128)(2,1)} %broadcast_in_dim.16), calls=%async_computation.1 | async-start | bytes 4718592 | tf_op jit(solution)/shard_map/all_to_all | solution.py:21
  37.2 135.6 %all-gather.6.cloned.1.call-start = ((), (), s32[]{:S(2)}) async-start(), calls=%async_computation.6 | async-start | bytes 1253376 | tf_op jit(solution)/shard_map/all_gather | solution.py:113
  62.7 14.7 %collective-permute-start = (bf16[4,32,1152]{2,1,0:T(8,128)(2,1)S(1)}, bf16[4,32,1152]{2,1,0:T(8,128)(2,1)S(1)}, u32[]{:S(2)}, u32[]{:S(2)}) collective-permute-start(bf16[4,32,1152]{2,1,0:T(8,128)(2,1)S(1)} %bitcast.92), channel_id=1, source_target_pairs={{0,32},{32,64},{64,96},{96,128},{128,160},{160,192},{192,224},{224... | collective-permute-start | bytes 884744 | tf_op jit(solution)/shard_map/ppermute | solution.py:35
  65.0 13.2 %collective-permute-start.1 = (bf16[4,32,1152]{2,1,0:T(8,128)(2,1)S(1)}, bf16[4,32,1152]{2,1,0:T(8,128)(2,1)S(1)}, u32[]{:S(2)}, u32[]{:S(2)}) collective-permute-start(bf16[4,32,1152]{2,1,0:T(8,128)(2,1)S(1)} %bitcast.93), channel_id=1, source_target_pairs={{0,480},{32,0},{64,32},{96,64},{128,96},{160,128},{192,160},{224,1... | collective-permute-start | bytes 884744 | tf_op jit(solution)/shard_map/ppermute | solution.py:35
  70.6 10.1 %collective-permute-start.2 = (bf16[2,32,1152]{2,1,0:T(8,128)(2,1)S(1)}, bf16[2,32,1152]{2,1,0:T(8,128)(2,1)S(1)}, u32[]{:S(2)}, u32[]{:S(2)}) collective-permute-start(bf16[2,32,1152]{2,1,0:T(8,128)(2,1)S(1)} %bitcast.116), channel_id=1, source_target_pairs={{0,448},{32,480},{64,0},{96,32},{128,64},{160,96},{192,128},{224,1... | collective-permute-start | bytes 442376 | tf_op jit(solution)/shard_map/ppermute | solution.py:35
  72.8 9.8 %collective-permute-start.3 = (bf16[2,32,1152]{2,1,0:T(8,128)(2,1)S(1)}, bf16[2,32,1152]{2,1,0:T(8,128)(2,1)S(1)}, u32[]{:S(2)}, u32[]{:S(2)}) collective-permute-start(bf16[2,32,1152]{2,1,0:T(8,128)(2,1)S(1)} %bitcast.115), channel_id=1, source_target_pairs={{0,64},{32,96},{64,128},{96,160},{128,192},{160,224},{192,256},{22... | collective-permute-start | bytes 442376 | tf_op jit(solution)/shard_map/ppermute | solution.py:35
  77.4 103.3 %all-gather.8.cloned.1.call-start = ((), (), s32[]{:S(2)}) async-start(), calls=%async_computation.7 | async-start | bytes 1253376 | tf_op jit(solution)/shard_map/all_gather | solution.py:113
  83.2 4.3 %copy-start.7 = (bf16[16,32,1152]{2,1,0:T(8,128)(2,1)S(1)}, bf16[16,32,1152]{2,1,0:T(8,128)(2,1)}, u32[]{:S(2)}) copy-start(bf16[16,32,1152]{2,1,0:T(8,128)(2,1)} %constant_dynamic-update-slice_fusion) | copy-start | bytes 3538948
  93.8 17.4 %collective-permute-start.4 = (bf16[4,32,1152]{2,1,0:T(8,128)(2,1)S(1)}, bf16[4,32,1152]{2,1,0:T(8,128)(2,1)S(1)}, u32[]{:S(2)}, u32[]{:S(2)}) collective-permute-start(bf16[4,32,1152]{2,1,0:T(8,128)(2,1)S(1)} %bitcast.106), channel_id=1, source_target_pairs={{0,480},{32,0},{64,32},{96,64},{128,96},{160,128},{192,160},{224,1... | collective-permute-start | bytes 884744 | tf_op jit(solution)/shard_map/ppermute | solution.py:35
  96.5 14.7 %collective-permute-start.5 = (bf16[4,32,1152]{2,1,0:T(8,128)(2,1)S(1)}, bf16[4,32,1152]{2,1,0:T(8,128)(2,1)S(1)}, u32[]{:S(2)}, u32[]{:S(2)}) collective-permute-start(bf16[4,32,1152]{2,1,0:T(8,128)(2,1)S(1)} %bitcast.105), channel_id=1, source_target_pairs={{0,32},{32,64},{64,96},{96,128},{128,160},{160,192},{192,224},{224... | collective-permute-start | bytes 884744 | tf_op jit(solution)/shard_map/ppermute | solution.py:35
  100.4 17.7 %collective-permute-start.6 = (bf16[4,32,1152]{2,1,0:T(8,128)(2,1)S(1)}, bf16[4,32,1152]{2,1,0:T(8,128)(2,1)}, u32[]{:S(2)}, u32[]{:S(2)}) collective-permute-start(bf16[4,32,1152]{2,1,0:T(8,128)(2,1)S(1)} %bitcast.104), channel_id=1, source_target_pairs={{0,64},{32,96},{64,128},{96,160},{128,192},{160,224},{192,256},{22... | collective-permute-start | bytes 884744 | tf_op jit(solution)/shard_map/ppermute | solution.py:35
  103.8 39.2 %all-to-all-start.2 = ((bf16[32,32,1152]{2,1,0:T(8,128)(2,1)}), bf16[32,32,1152]{2,1,0:T(8,128)(2,1)}, u32[]{:S(2)}, u32[]{:S(2)}) async-start(bf16[32,32,1152]{2,1,0:T(8,128)(2,1)} %bitcast.95), calls=%async_computation.2 | async-start | bytes 4718592 | tf_op jit(solution)/shard_map/all_to_all | solution.py:21
  119.2 10.0 %collective-permute-start.7 = (bf16[16,1152]{1,0:T(8,128)(2,1)S(1)}, bf16[16,1152]{1,0:T(8,128)(2,1)S(1)}, u32[]{:S(2)}, u32[]{:S(2)}) collective-permute-start(bf16[16,1152]{1,0:T(8,128)(2,1)S(1)} %get-tuple-element.50), channel_id=1, source_target_pairs={{0,128},{32,160},{64,192},{96,224},{128,256},{160,288},{192,320},{... | collective-permute-start | bytes 110600 | tf_op jit(solution)/shard_map/ppermute | solution.py:35
  121.7 9.9 %collective-permute-start.9 = (bf16[16,1152]{1,0:T(8,128)(2,1)S(1)}, bf16[16,1152]{1,0:T(8,128)(2,1)S(1)}, u32[]{:S(2)}, u32[]{:S(2)}) collective-permute-start(bf16[16,1152]{1,0:T(8,128)(2,1)S(1)} %get-tuple-element.51), channel_id=1, source_target_pairs={{0,384},{32,416},{64,448},{96,480},{128,0},{160,32},{192,64},{224,... | collective-permute-start | bytes 110600 | tf_op jit(solution)/shard_map/ppermute | solution.py:35
  131.6 13.4 %collective-permute-start.8 = (bf16[32,1152]{1,0:T(8,128)(2,1)S(1)}, bf16[32,1152]{1,0:T(8,128)(2,1)S(1)}, u32[]{:S(2)}, u32[]{:S(2)}) collective-permute-start(bf16[32,1152]{1,0:T(8,128)(2,1)S(1)} %pad_maximum_fusion.7), channel_id=1, source_target_pairs={{0,128},{32,160},{64,192},{96,224},{128,256},{160,288},{192,320},{... | collective-permute-start | bytes 221192 | tf_op jit(solution)/shard_map/ppermute | solution.py:35
  135.4 11.1 %copy-start.4 = (bf16[128,1152]{1,0:T(8,128)(2,1)S(1)}, bf16[128,1152]{1,0:T(8,128)(2,1)}, u32[]{:S(2)}) copy-start(bf16[128,1152]{1,0:T(8,128)(2,1)} %param.8) | copy-start | bytes 884740
  135.4 11.1 %copy-start.6 = (bf16[128,1152]{1,0:T(8,128)(2,1)S(1)}, bf16[128,1152]{1,0:T(8,128)(2,1)}, u32[]{:S(2)}) copy-start(bf16[128,1152]{1,0:T(8,128)(2,1)} %param.11) | copy-start | bytes 884740
  135.4 11.1 %collective-permute-start.10 = (bf16[32,1152]{1,0:T(8,128)(2,1)S(1)}, bf16[32,1152]{1,0:T(8,128)(2,1)S(1)}, u32[]{:S(2)}, u32[]{:S(2)}) collective-permute-start(bf16[32,1152]{1,0:T(8,128)(2,1)S(1)} %pad_maximum_fusion.8), channel_id=1, source_target_pairs={{0,384},{32,416},{64,448},{96,480},{128,0},{160,32},{192,64},{224,... | collective-permute-start | bytes 221192 | tf_op jit(solution)/shard_map/ppermute | solution.py:35
  212.5 24.9 %all-to-all-start.5 = ((bf16[16,80,128]{2,1,0:T(8,128)(2,1)}), bf16[16,80,128]{2,1,0:T(8,128)(2,1)S(1)}, u32[]{:S(2)}, u32[]{:S(2)}) async-start(bf16[16,80,128]{2,1,0:T(8,128)(2,1)} %broadcast_in_dim.17), calls=%async_computation.5 | async-start | bytes 655360 | tf_op jit(solution)/shard_map/all_to_all | solution.py:21
  218.4 9.6 %copy-start.1 = (bf16[544,1152]{1,0:T(8,128)(2,1)S(1)}, bf16[544,1152]{1,0:T(8,128)(2,1)}, u32[]{:S(2)}) copy-start(bf16[544,1152]{1,0:T(8,128)(2,1)} %param.10) | copy-start | bytes 3760132
Sparse Core Ops, SparseCore 0:
  77.5 44.6 all-gather.5
  124.1 56.5 all-gather.7

commit v11 on v10

--- a/solution.py
+++ b/solution.py
@@ -148,6 +148,7 @@
         axis=2,
     )
     cut = exchange(jnp.transpose(cut, (1, 0, 2)), "replica")
+    cut, hidden_image, hidden_text = lax.optimization_barrier((cut, hidden_image, hidden_text))
     cut = lax.all_gather(cut, "tensor", axis=1).reshape(members * own, 2 * columns)
     group = after(jnp.stack([upstream_image, upstream_text]), cut)
     group = lax.all_gather(group, "tensor", axis=1)

time: 247 us -> 265 us (1.073)
  waiting for transfers between devices: 37.5 us -> 58.1 us
  blocking collectives: 86 us -> 73.9 us
  starting transfers between devices: 73.5 us -> 82.4 us
    all_gather x2, waiting for transfers between devices: 5.91 us -> 24.7 us  [shards(): lax.all_gather(after(units, summed), 'replica', axis=0, tiled=True)]
    all_to_all x2 -> x1, blocking collectives: 43.4 us -> 32.4 us  [exchange(): return lax.all_to_all(x, axis, split_axis=0, concat_axis=0, tiled=True)]
    all_to_all x4 -> x5, starting transfers between devices: 30.1 us -> 39 us  [exchange(): return lax.all_to_all(x, axis, split_axis=0, concat_axis=0, tiled=True)]
    all_to_all x4 -> x5, waiting for transfers between devices: 17.6 us -> 19.4 us  [exchange(): return lax.all_to_all(x, axis, split_axis=0, concat_axis=0, tiled=True)]
  transfers between devices with their start and end apart: 17 -> 18, of which waited for: 10 -> 10; matrix products, arithmetic and copies ran while one was open for 9% -> 8% of each run, Pallas kernels for 0% -> 0%
where the time goes in v11:
time: 265 us; the launch traced here: 262 us
  starting transfers between devices  82.4 us (31%)
  blocking collectives  73.9 us (28%)
  waiting for transfers between devices  58.1 us (22%)
  matrix products  17.8 us (7%)
  between operations  16 us (6%)
  local copies, waits for them, and re-layouts  9.14 us (3%)
  other arithmetic  5.13 us (2%)
    ppermute x11, starting transfers between devices, shift(): return lax.ppermute(x, DP, [(i, (i + by) % size) for i in range(size)])  43.3 us
    all_to_all x5, starting transfers between devices, exchange(): return lax.all_to_all(x, axis, split_axis=0, concat_axis=0, tiled=True)  39 us
    all_to_all x1, blocking collectives, exchange(): return lax.all_to_all(x, axis, split_axis=0, concat_axis=0, tiled=True)  32.4 us
    all_gather x2, waiting for transfers between devices, shards(): lax.all_gather(after(units, summed), 'replica', axis=0, tiled=True)  24.7 us
    all_gather x1, blocking collectives, gather_dp(): quad = lax.all_gather(x, 'run', axis=0)  24.1 us
    all_to_all x5, waiting for transfers between devices, exchange(): return lax.all_to_all(x, axis, split_axis=0, concat_axis=0, tiled=True)  19.4 us
    dot_general x9, matrix products, dot(): lax.dot_general(a, b, (contract, ((), ())), preferred_element_type=F32)  17.8 us
    ppermute x11, waiting for transfers between devices, shift(): return lax.ppermute(x, DP, [(i, (i + by) % size) for i in range(size)])  13.9 us
  transfers between devices with their start and end apart: 18, of which 10 were waited for; matrix products, arithmetic and copies ran while one was open for 8% of the time, Pallas kernels for 0%

profile of v11, /device:TPU:24, one launch (start us, length us, event | category | flops | bytes accessed | tf_op | source)
XLA Modules:
  0.0 262.5 jit_solution(17227612808600297218)
XLA Ops:
  7.2 1.9 convolution_convert_fusion.3
  10.4 4.9 %all-to-all-start = ((bf16[4,64,1152]{2,1,0:T(8,128)(2,1)}), bf16[4,64,1152]{2,1,0:T(8,128)(2,1)S(1)}, u32[]{:S(2)}, u32[]{:S(2)}) async-start(bf16[4,64,1152]{2,1,0:T(8,128)(2,1)} %pad_maximum_fusion), calls=%async_computation | async-start | bytes 1179648 | tf_op jit(solution)/shard_map/all_to_all | solution.py:21
  15.4 7.9 %all-to-all-done = bf16[4,64,1152]{2,1,0:T(8,128)(2,1)S(1)} async-done(((bf16[4,64,1152]{2,1,0:T(8,128)(2,1)}), bf16[4,64,1152]{2,1,0:T(8,128)(2,1)S(1)}, u32[]{:S(2)}, u32[]{:S(2)}) %all-to-all-start) | async-done | bytes 589856 | tf_op jit(solution)/shard_map/all_to_all | solution.py:21
  25.3 11.9 %all-to-all-start.1 = ((bf16[32,32,1152]{2,1,0:T(8,128)(2,1)}), bf16[32,32,1152]{2,1,0:T(8,128)(2,1)}, u32[]{:S(2)}, u32[]{:S(2)}) async-start(bf16[32,32,1152]{2,1,0:T(8,128)(2,1)} %broadcast_in_dim.16), calls=%async_computation.1 | async-start | bytes 4718592 | tf_op jit(solution)/shard_map/all_to_all | solution.py:21
  38.6 24.1 %all-gather = bf16[128,1152]{1,0:T(8,128)(2,1)S(1)} all-gather(bf16[32,1152]{1,0:T(8,128)(2,1)S(1)} %get-tuple-element.53), channel_id=2, replica_groups=mesh['run'=4,'place'=4,'replica'=8,'tensor'=4] {'run'}, dimensions={0}, use_global_device_ids=true | all-gather | bytes 368640 | tf_op jit(solution)/shard_map/all_gather | solution.py:39
  62.7 2.2 collective-permute-start
  65.0 4.8 %collective-permute-start.1 = (bf16[4,32,1152]{2,1,0:T(8,128)(2,1)S(1)}, bf16[4,32,1152]{2,1,0:T(8,128)(2,1)S(1)}, u32[]{:S(2)}, u32[]{:S(2)}) collective-permute-start(bf16[4,32,1152]{2,1,0:T(8,128)(2,1)S(1)} %bitcast.93), channel_id=1, source_target_pairs={{0,480},{32,0},{64,32},{96,64},{128,96},{160,128},{192,160},{224,1... | collective-permute-start | bytes 884744 | tf_op jit(solution)/shard_map/ppermute | solution.py:35
  70.6 2.2 collective-permute-start.2
  72.7 4.6 %collective-permute-start.3 = (bf16[2,32,1152]{2,1,0:T(8,128)(2,1)S(1)}, bf16[2,32,1152]{2,1,0:T(8,128)(2,1)S(1)}, u32[]{:S(2)}, u32[]{:S(2)}) collective-permute-start(bf16[2,32,1152]{2,1,0:T(8,128)(2,1)S(1)} %bitcast.114), channel_id=1, source_target_pairs={{0,64},{32,96},{64,128},{96,160},{128,192},{160,224},{192,256},{22... | collective-permute-start | bytes 442376 | tf_op jit(solution)/shard_map/ppermute | solution.py:35
  78.9 1.8 collective-permute-done.2
  83.2 4.3 %multiply_convert_fusion = bf16[1024,512]{1,0:T(8,128)(2,1)S(1)} fusion(bf16[1024,1152]{1,0:T(8,128)(2,1)} %bitcast.6, bf16[512,1152]{1,0:T(8,128)(2,1)} %bitcast.116, f32[]{:T(128)} %bitcast.91, f32[]{:T(128)} %bitcast, s32[512]{0:T(512)S(1)} %fusion.17), kind=kOutput, calls=%fused_computation.5 | convolution fusion | flops 1214251008 | bytes 4589576 | tf_op jit(solution)/shard_map/dot_general | solution.py:17
  87.4 3.0 %convolution_convert_fusion = bf16[1024,1152]{1,0:T(8,128)(2,1)} fusion(bf16[1024,512]{1,0:T(8,128)(2,1)S(1)} %multiply_convert_fusion, bf16[512,1152]{1,0:T(8,128)(2,1)S(1)} %bitcast.117), kind=kOutput, calls=%fused_computation.1 | convolution fusion | flops 1209139200 | bytes 4587520 | tf_op jit(solution)/shard_map/dot_general | solution.py:17
  90.4 3.2 %convolution_convert_fusion.1 = bf16[512,1152]{1,0:T(8,128)(2,1)S(1)} fusion(bf16[1024,512]{1,0:T(8,128)(2,1)S(1)} %multiply_convert_fusion, bf16[1024,1152]{1,0:T(8,128)(2,1)} %bitcast.6), kind=kOutput, calls=%fused_computation.2 | convolution fusion | flops 1208549376 | bytes 4587520 | tf_op jit(solution)/shard_map/dot_general | solution.py:17
  93.7 2.7 %collective-permute-start.4 = (bf16[4,32,1152]{2,1,0:T(8,128)(2,1)S(1)}, bf16[4,32,1152]{2,1,0:T(8,128)(2,1)S(1)}, u32[]{:S(2)}, u32[]{:S(2)}) collective-permute-start(bf16[4,32,1152]{2,1,0:T(8,128)(2,1)S(1)} %bitcast.105), channel_id=1, source_target_pairs={{0,480},{32,0},{64,32},{96,64},{128,96},{160,128},{192,160},{224,1... | collective-permute-start | bytes 884744 | tf_op jit(solution)/shard_map/ppermute | solution.py:35
  96.5 3.8 %collective-permute-start.5 = (bf16[4,32,1152]{2,1,0:T(8,128)(2,1)S(1)}, bf16[4,32,1152]{2,1,0:T(8,128)(2,1)S(1)}, u32[]{:S(2)}, u32[]{:S(2)}) collective-permute-start(bf16[4,32,1152]{2,1,0:T(8,128)(2,1)S(1)} %bitcast.104), channel_id=1, source_target_pairs={{0,32},{32,64},{64,96},{96,128},{128,160},{160,192},{192,224},{224... | collective-permute-start | bytes 884744 | tf_op jit(solution)/shard_map/ppermute | solution.py:35
  100.3 3.4 %collective-permute-start.6 = (bf16[4,32,1152]{2,1,0:T(8,128)(2,1)S(1)}, bf16[4,32,1152]{2,1,0:T(8,128)(2,1)}, u32[]{:S(2)}, u32[]{:S(2)}) collective-permute-start(bf16[4,32,1152]{2,1,0:T(8,128)(2,1)S(1)} %bitcast.103), channel_id=1, source_target_pairs={{0,64},{32,96},{64,128},{96,160},{128,192},{160,224},{192,256},{22... | collective-permute-start | bytes 884744 | tf_op jit(solution)/shard_map/ppermute | solution.py:35
  103.8 7.4 %all-to-all-start.2 = ((bf16[32,32,1152]{2,1,0:T(8,128)(2,1)}), bf16[32,32,1152]{2,1,0:T(8,128)(2,1)}, u32[]{:S(2)}, u32[]{:S(2)}) async-start(bf16[32,32,1152]{2,1,0:T(8,128)(2,1)} %bitcast.95), calls=%async_computation.2 | async-start | bytes 4718592 | tf_op jit(solution)/shard_map/all_to_all | solution.py:21
  111.2 6.8 %collective-permute-done.6 = bf16[4,32,1152]{2,1,0:T(8,128)(2,1)} collective-permute-done((bf16[4,32,1152]{2,1,0:T(8,128)(2,1)S(1)}, bf16[4,32,1152]{2,1,0:T(8,128)(2,1)}, u32[]{:S(2)}, u32[]{:S(2)}) %collective-permute-start.6) | collective-permute-done | bytes 294944 | tf_op jit(solution)/shard_map/ppermute | solution.py:35
  119.2 2.5 collective-permute-start.7
  121.7 7.3 %collective-permute-start.9 = (bf16[16,1152]{1,0:T(8,128)(2,1)S(1)}, bf16[16,1152]{1,0:T(8,128)(2,1)S(1)}, u32[]{:S(2)}, u32[]{:S(2)}) collective-permute-start(bf16[16,1152]{1,0:T(8,128)(2,1)S(1)} %get-tuple-element.57), channel_id=1, source_target_pairs={{0,384},{32,416},{64,448},{96,480},{128,0},{160,32},{192,64},{224,... | collective-permute-start | bytes 110600 | tf_op jit(solution)/shard_map/ppermute | solution.py:35
  129.2 2.4 collective-permute-done.9
  131.6 3.8 %collective-permute-start.8 = (bf16[32,1152]{1,0:T(8,128)(2,1)S(1)}, bf16[32,1152]{1,0:T(8,128)(2,1)S(1)}, u32[]{:S(2)}, u32[]{:S(2)}) collective-permute-start(bf16[32,1152]{1,0:T(8,128)(2,1)S(1)} %pad_maximum_fusion.7), channel_id=1, source_target_pairs={{0,128},{32,160},{64,192},{96,224},{128,256},{160,288},{192,320},{... | collective-permute-start | bytes 221192 | tf_op jit(solution)/shard_map/ppermute | solution.py:35
  135.4 6.1 %collective-permute-start.10 = (bf16[32,1152]{1,0:T(8,128)(2,1)S(1)}, bf16[32,1152]{1,0:T(8,128)(2,1)S(1)}, u32[]{:S(2)}, u32[]{:S(2)}) collective-permute-start(bf16[32,1152]{1,0:T(8,128)(2,1)S(1)} %pad_maximum_fusion.8), channel_id=1, source_target_pairs={{0,384},{32,416},{64,448},{96,480},{128,0},{160,32},{192,64},{224,... | collective-permute-start | bytes 221192 | tf_op jit(solution)/shard_map/ppermute | solution.py:35
  143.0 2.0 convert_reduce_fusion
  148.1 8.8 %all-to-all-start.3 = ((bf16[8,32,288]{2,1,0:T(8,128)(2,1)}), bf16[8,32,288]{2,1,0:T(8,128)(2,1)S(1)}, u32[]{:S(2)}, u32[]{:S(2)}) async-start(bf16[8,32,288]{2,1,0:T(8,128)(2,1)} %bitcast.90), calls=%async_computation.3 | async-start | bytes 393216 | tf_op jit(solution)/shard_map/all_to_all | solution.py:21
  157.0 24.7 %all-gather.8.cloned.1.call-done = bf16[1024,544]{0,1:T(8,128)(2,1)} async-done(((bf16[128,544]{0,1:T(8,128)(2,1)}), bf16[1024,544]{0,1:T(8,128)(2,1)}) %all-gather.8.cloned.1.call-update) | async-done | bytes 1114128 | tf_op jit(solution)/shard_map/all_gather | solution.py:113
  181.8 8.7 %all-gather.1 = bf16[8,128,288]{2,0,1:T(8,128)(2,1)S(1)} all-gather(bf16[8,32,288]{2,0,1:T(8,128)(2,1)S(1)} %copy.31), channel_id=3, replica_groups=mesh['run'=4,'place'=4,'replica'=8,'tensor'=4] {'tensor'}, dimensions={1}, use_global_device_ids=true | all-gather | bytes 737280 | tf_op jit(solution)/shard_map/all_gather | solution.py:152
  191.2 2.0 convolution_convert_fusion.5
  194.1 32.4 %all_to_all.30 = bf16[16,80,128]{2,1,0:T(8,128)(2,1)S(1)} all-to-all(bf16[16,80,128]{2,1,0:T(8,128)(2,1)S(1)} %fusion.3), channel_id=1, replica_groups=mesh['run'=4,'place'=4,'replica'=8,'tensor'=4] {'run','place'}, dimensions={0} | all-to-all | bytes 655360 | tf_op jit(solution)/shard_map/all_to_all | solution.py:21
  227.3 5.9 %all-to-all-start.5 = ((bf16[16,80,128]{2,1,0:T(8,128)(2,1)}), bf16[16,80,128]{2,1,0:T(8,128)(2,1)S(1)}, u32[]{:S(2)}, u32[]{:S(2)}) async-start(bf16[16,80,128]{2,1,0:T(8,128)(2,1)} %broadcast_in_dim.17), calls=%async_computation.5 | async-start | bytes 655360 | tf_op jit(solution)/shard_map/all_to_all | solution.py:21
  233.3 8.7 %all-gather.2 = bf16[2,128,1152]{2,1,0:T(8,128)(2,1)S(1)} all-gather(bf16[2,32,1152]{2,1,0:T(8,128)(2,1)S(1)} %pad_maximum_fusion.2), channel_id=4, replica_groups=mesh['run'=4,'place'=4,'replica'=8,'tensor'=4] {'tensor'}, dimensions={1}, use_global_device_ids=true | all-gather | bytes 737280 | tf_op jit(solution)/shard_map/all_gather | solution.py:154
  244.2 10.1 %all-to-all-done.5 = bf16[16,80,128]{2,1,0:T(8,128)(2,1)S(1)} async-done(((bf16[16,80,128]{2,1,0:T(8,128)(2,1)}), bf16[16,80,128]{2,1,0:T(8,128)(2,1)S(1)}, u32[]{:S(2)}, u32[]{:S(2)}) %all-to-all-start.5) | async-done | bytes 327712 | tf_op jit(solution)/shard_map/all_to_all | solution.py:21
  (87 shorter events, 20.2 us)
Async XLA Ops:
  7.2 1.9 copy-start
  7.2 1.9 copy-start.2
  10.4 12.9 %copy-start.3 = (bf16[128,1152]{1,0:T(8,128)(2,1)S(1)}, bf16[128,1152]{1,0:T(8,128)(2,1)}, u32[]{:S(2)}) copy-start(bf16[128,1152]{1,0:T(8,128)(2,1)} %param.8) | copy-start | bytes 884740
  10.4 12.9 %copy-start.5 = (bf16[128,1152]{1,0:T(8,128)(2,1)S(1)}, bf16[128,1152]{1,0:T(8,128)(2,1)}, u32[]{:S(2)}) copy-start(bf16[128,1152]{1,0:T(8,128)(2,1)} %param.11) | copy-start | bytes 884740
  10.4 12.8 %all-to-all-start = ((bf16[4,64,1152]{2,1,0:T(8,128)(2,1)}), bf16[4,64,1152]{2,1,0:T(8,128)(2,1)S(1)}, u32[]{:S(2)}, u32[]{:S(2)}) async-start(bf16[4,64,1152]{2,1,0:T(8,128)(2,1)} %pad_maximum_fusion), calls=%async_computation | async-start | bytes 1179648 | tf_op jit(solution)/shard_map/all_to_all | solution.py:21
  25.3 57.9 %all-to-all-start.1 = ((bf16[32,32,1152]{2,1,0:T(8,128)(2,1)}), bf16[32,32,1152]{2,1,0:T(8,128)(2,1)}, u32[]{:S(2)}, u32[]{:S(2)}) async-start(bf16[32,32,1152]{2,1,0:T(8,128)(2,1)} %broadcast_in_dim.16), calls=%async_computation.1 | async-start | bytes 4718592 | tf_op jit(solution)/shard_map/all_to_all | solution.py:21
  37.2 119.8 %all-gather.6.cloned.1.call-start = ((), (), s32[]{:S(2)}) async-start(), calls=%async_computation.6 | async-start | bytes 1253376 | tf_op jit(solution)/shard_map/all_gather | solution.py:113
  62.7 14.7 %collective-permute-start = (bf16[4,32,1152]{2,1,0:T(8,128)(2,1)S(1)}, bf16[4,32,1152]{2,1,0:T(8,128)(2,1)S(1)}, u32[]{:S(2)}, u32[]{:S(2)}) collective-permute-start(bf16[4,32,1152]{2,1,0:T(8,128)(2,1)S(1)} %bitcast.92), channel_id=1, source_target_pairs={{0,32},{32,64},{64,96},{96,128},{128,160},{160,192},{192,224},{224... | collective-permute-start | bytes 884744 | tf_op jit(solution)/shard_map/ppermute | solution.py:35
  65.0 13.2 %collective-permute-start.1 = (bf16[4,32,1152]{2,1,0:T(8,128)(2,1)S(1)}, bf16[4,32,1152]{2,1,0:T(8,128)(2,1)S(1)}, u32[]{:S(2)}, u32[]{:S(2)}) collective-permute-start(bf16[4,32,1152]{2,1,0:T(8,128)(2,1)S(1)} %bitcast.93), channel_id=1, source_target_pairs={{0,480},{32,0},{64,32},{96,64},{128,96},{160,128},{192,160},{224,1... | collective-permute-start | bytes 884744 | tf_op jit(solution)/shard_map/ppermute | solution.py:35
  70.6 10.1 %collective-permute-start.2 = (bf16[2,32,1152]{2,1,0:T(8,128)(2,1)S(1)}, bf16[2,32,1152]{2,1,0:T(8,128)(2,1)S(1)}, u32[]{:S(2)}, u32[]{:S(2)}) collective-permute-start(bf16[2,32,1152]{2,1,0:T(8,128)(2,1)S(1)} %bitcast.115), channel_id=1, source_target_pairs={{0,448},{32,480},{64,0},{96,32},{128,64},{160,96},{192,128},{224,1... | collective-permute-start | bytes 442376 | tf_op jit(solution)/shard_map/ppermute | solution.py:35
  72.7 9.8 %collective-permute-start.3 = (bf16[2,32,1152]{2,1,0:T(8,128)(2,1)S(1)}, bf16[2,32,1152]{2,1,0:T(8,128)(2,1)S(1)}, u32[]{:S(2)}, u32[]{:S(2)}) collective-permute-start(bf16[2,32,1152]{2,1,0:T(8,128)(2,1)S(1)} %bitcast.114), channel_id=1, source_target_pairs={{0,64},{32,96},{64,128},{96,160},{128,192},{160,224},{192,256},{22... | collective-permute-start | bytes 442376 | tf_op jit(solution)/shard_map/ppermute | solution.py:35
  77.3 104.4 %all-gather.8.cloned.1.call-start = ((), (), s32[]{:S(2)}) async-start(), calls=%async_computation.7 | async-start | bytes 1253376 | tf_op jit(solution)/shard_map/all_gather | solution.py:113
  83.2 4.3 %copy-start.7 = (bf16[16,32,1152]{2,1,0:T(8,128)(2,1)S(1)}, bf16[16,32,1152]{2,1,0:T(8,128)(2,1)}, u32[]{:S(2)}) copy-start(bf16[16,32,1152]{2,1,0:T(8,128)(2,1)} %constant_dynamic-update-slice_fusion) | copy-start | bytes 3538948
  93.7 17.4 %collective-permute-start.4 = (bf16[4,32,1152]{2,1,0:T(8,128)(2,1)S(1)}, bf16[4,32,1152]{2,1,0:T(8,128)(2,1)S(1)}, u32[]{:S(2)}, u32[]{:S(2)}) collective-permute-start(bf16[4,32,1152]{2,1,0:T(8,128)(2,1)S(1)} %bitcast.105), channel_id=1, source_target_pairs={{0,480},{32,0},{64,32},{96,64},{128,96},{160,128},{192,160},{224,1... | collective-permute-start | bytes 884744 | tf_op jit(solution)/shard_map/ppermute | solution.py:35
  96.5 14.7 %collective-permute-start.5 = (bf16[4,32,1152]{2,1,0:T(8,128)(2,1)S(1)}, bf16[4,32,1152]{2,1,0:T(8,128)(2,1)S(1)}, u32[]{:S(2)}, u32[]{:S(2)}) collective-permute-start(bf16[4,32,1152]{2,1,0:T(8,128)(2,1)S(1)} %bitcast.104), channel_id=1, source_target_pairs={{0,32},{32,64},{64,96},{96,128},{128,160},{160,192},{192,224},{224... | collective-permute-start | bytes 884744 | tf_op jit(solution)/shard_map/ppermute | solution.py:35
  100.3 17.7 %collective-permute-start.6 = (bf16[4,32,1152]{2,1,0:T(8,128)(2,1)S(1)}, bf16[4,32,1152]{2,1,0:T(8,128)(2,1)}, u32[]{:S(2)}, u32[]{:S(2)}) collective-permute-start(bf16[4,32,1152]{2,1,0:T(8,128)(2,1)S(1)} %bitcast.103), channel_id=1, source_target_pairs={{0,64},{32,96},{64,128},{96,160},{128,192},{160,224},{192,256},{22... | collective-permute-start | bytes 884744 | tf_op jit(solution)/shard_map/ppermute | solution.py:35
  103.8 39.2 %all-to-all-start.2 = ((bf16[32,32,1152]{2,1,0:T(8,128)(2,1)}), bf16[32,32,1152]{2,1,0:T(8,128)(2,1)}, u32[]{:S(2)}, u32[]{:S(2)}) async-start(bf16[32,32,1152]{2,1,0:T(8,128)(2,1)} %bitcast.95), calls=%async_computation.2 | async-start | bytes 4718592 | tf_op jit(solution)/shard_map/all_to_all | solution.py:21
  119.2 10.0 %collective-permute-start.7 = (bf16[16,1152]{1,0:T(8,128)(2,1)S(1)}, bf16[16,1152]{1,0:T(8,128)(2,1)S(1)}, u32[]{:S(2)}, u32[]{:S(2)}) collective-permute-start(bf16[16,1152]{1,0:T(8,128)(2,1)S(1)} %get-tuple-element.56), channel_id=1, source_target_pairs={{0,128},{32,160},{64,192},{96,224},{128,256},{160,288},{192,320},{... | collective-permute-start | bytes 110600 | tf_op jit(solution)/shard_map/ppermute | solution.py:35
  121.7 9.9 %collective-permute-start.9 = (bf16[16,1152]{1,0:T(8,128)(2,1)S(1)}, bf16[16,1152]{1,0:T(8,128)(2,1)S(1)}, u32[]{:S(2)}, u32[]{:S(2)}) collective-permute-start(bf16[16,1152]{1,0:T(8,128)(2,1)S(1)} %get-tuple-element.57), channel_id=1, source_target_pairs={{0,384},{32,416},{64,448},{96,480},{128,0},{160,32},{192,64},{224,... | collective-permute-start | bytes 110600 | tf_op jit(solution)/shard_map/ppermute | solution.py:35
  131.6 13.4 %collective-permute-start.8 = (bf16[32,1152]{1,0:T(8,128)(2,1)S(1)}, bf16[32,1152]{1,0:T(8,128)(2,1)S(1)}, u32[]{:S(2)}, u32[]{:S(2)}) collective-permute-start(bf16[32,1152]{1,0:T(8,128)(2,1)S(1)} %pad_maximum_fusion.7), channel_id=1, source_target_pairs={{0,128},{32,160},{64,192},{96,224},{128,256},{160,288},{192,320},{... | collective-permute-start | bytes 221192 | tf_op jit(solution)/shard_map/ppermute | solution.py:35
  135.4 11.1 %copy-start.4 = (bf16[128,1152]{1,0:T(8,128)(2,1)S(1)}, bf16[128,1152]{1,0:T(8,128)(2,1)}, u32[]{:S(2)}) copy-start(bf16[128,1152]{1,0:T(8,128)(2,1)} %param.8) | copy-start | bytes 884740
  135.4 11.1 %copy-start.6 = (bf16[128,1152]{1,0:T(8,128)(2,1)S(1)}, bf16[128,1152]{1,0:T(8,128)(2,1)}, u32[]{:S(2)}) copy-start(bf16[128,1152]{1,0:T(8,128)(2,1)} %param.11) | copy-start | bytes 884740
  135.4 11.1 %collective-permute-start.10 = (bf16[32,1152]{1,0:T(8,128)(2,1)S(1)}, bf16[32,1152]{1,0:T(8,128)(2,1)S(1)}, u32[]{:S(2)}, u32[]{:S(2)}) collective-permute-start(bf16[32,1152]{1,0:T(8,128)(2,1)S(1)} %pad_maximum_fusion.8), channel_id=1, source_target_pairs={{0,384},{32,416},{64,448},{96,480},{128,0},{160,32},{192,64},{224,... | collective-permute-start | bytes 221192 | tf_op jit(solution)/shard_map/ppermute | solution.py:35
  148.1 33.6 %all-to-all-start.3 = ((bf16[8,32,288]{2,1,0:T(8,128)(2,1)}), bf16[8,32,288]{2,1,0:T(8,128)(2,1)S(1)}, u32[]{:S(2)}, u32[]{:S(2)}) async-start(bf16[8,32,288]{2,1,0:T(8,128)(2,1)} %bitcast.90), calls=%async_computation.3 | async-start | bytes 393216 | tf_op jit(solution)/shard_map/all_to_all | solution.py:21
  191.2 2.1 copy-start.8
  227.3 27.0 %all-to-all-start.5 = ((bf16[16,80,128]{2,1,0:T(8,128)(2,1)}), bf16[16,80,128]{2,1,0:T(8,128)(2,1)S(1)}, u32[]{:S(2)}, u32[]{:S(2)}) async-start(bf16[16,80,128]{2,1,0:T(8,128)(2,1)} %broadcast_in_dim.17), calls=%async_computation.5 | async-start | bytes 655360 | tf_op jit(solution)/shard_map/all_to_all | solution.py:21
  233.3 9.8 %copy-start.1 = (bf16[544,1152]{1,0:T(8,128)(2,1)S(1)}, bf16[544,1152]{1,0:T(8,128)(2,1)}, u32[]{:S(2)}) copy-start(bf16[544,1152]{1,0:T(8,128)(2,1)} %param.10) | copy-start | bytes 3760132
Sparse Core Ops, SparseCore 0:
  77.4 44.6 all-gather.5
  124.1 57.5 all-gather.7
